TPU v7x, 32 devices: a whole 2x2x4 slice. The times are simulated.
32 devices in a mesh: dp: 4 (over y, core), table: 8 (over z, x).
Axes of the slice: x: 2, y: 2, z: 4, core: 2. Of those that a mesh axis runs over, the one named last changes fastest.
Arguments:
- bag_slots: int32 [16384, 32], P(('dp', 'table')), may hold values from -1 to 767
- labels: float32 [16384], P(('dp', 'table')), may hold values from 0 to 1
- cold_ids: int32 [32, 8, 32], P(('dp', 'table')), may hold values from 0 to 1023
- cold_count: int32 [32, 8], P(('dp', 'table')), may hold values from 1 to 32, 128 in all within a row
- table: float32 [8192, 256], P('table'), may hold values from -1.8 to 1.8
- adagrad_sum: float32 [8192], P('table'), may hold values from 0.1 to 10
- hot_ids: int32 [512], P('table'), may hold values from 0 to 1023
- w_in: bfloat16 [256, 4096], replicated, may hold values from -0.375 to 0.375
- w_out: bfloat16 [4096], replicated, may hold values from -0.09375 to 0.09375
Outputs:
- new_table: float32 [8192, 256], P('table')
- new_sum: float32 [8192], P('table')
Inputs may be any that keep to these rules, and one draw needn't show every extreme that they name: `bag_slots`: -1 marks an empty bag entry. `cold_count`: each reader's counts sum to 128.
All inputs are finite; a program needn't handle non-finite values.
Results may differ from a plain program's by a relative error of at most 0.0045.
The roundings to bfloat16 on the way count: a program that leaves them out, or rounds other values in their place, can miss the bound.
Values may be sent and summed in bfloat16 or wider, within the bound.
No kernel may reach another device: no remote copies, remote signals or barrier semaphores. Data moves between devices by JAX's collectives and lax.ppermute only.
A program may use at most 64 MiB of HBM per device.

v0:
```python
import jax
import jax.numpy as jnp
from jax import lax
from jax.sharding import PartitionSpec as P

learning_rate = 0.3


def adagrad_step(own_table, own_sum, grad):
    new_sum = own_sum + jnp.mean(grad * grad, axis=1)
    new_table = own_table - learning_rate * grad / jnp.sqrt(new_sum)[:, None]
    return (new_table, new_sum)


def per_device(bag_slots, labels, cold_ids, cold_count, table, adagrad_sum, hot_ids, w_in, w_out):
    owners = lax.axis_size("table")
    hot_dev = hot_ids.shape[0]
    slot_cap = cold_ids.shape[2]
    batch = bag_slots.shape[0]
    width = table.shape[1]
    hot_cols = owners * hot_dev
    vocab_size = owners * (hot_dev + slot_cap)
    table_bf = table.astype(jnp.bfloat16)
    hot_rows = table_bf[hot_ids]
    sample_ids = jnp.broadcast_to(jnp.arange(batch, dtype=jnp.int32)[:, None], bag_slots.shape)
    column_ids = jnp.where(bag_slots < 0, vocab_size, bag_slots)
    incidence = (
        jnp.zeros((batch, vocab_size), jnp.bfloat16)
        .at[sample_ids, column_ids]
        .add(jnp.ones(bag_slots.shape, jnp.bfloat16), mode="drop")
    )
    hot_incidence = incidence[:, :hot_cols]
    cold_incidence = incidence[:, hot_cols:]
    asked_ids = lax.all_to_all(cold_ids[0], "table", split_axis=0, concat_axis=0, tiled=True)
    served = table_bf[asked_ids]
    fetched = lax.all_to_all(served, "table", split_axis=0, concat_axis=0, tiled=True)
    live_mask = jnp.arange(slot_cap, dtype=jnp.int32)[None, :] < cold_count[0][:, None]
    fetched = jnp.where(live_mask[..., None], fetched, jnp.zeros_like(fetched))
    cold_pooled = jnp.dot(
        cold_incidence, fetched.reshape(-1, width), preferred_element_type=jnp.float32
    )
    columns = hot_incidence
    pooled = (
        cold_pooled
        + jnp.dot(
            columns,
            lax.all_gather(hot_rows, "table", axis=0, tiled=True),
            preferred_element_type=jnp.float32,
        )
    ).astype(jnp.bfloat16)
    pre_act = jnp.dot(pooled, w_in, preferred_element_type=jnp.float32)
    hidden = jax.nn.relu(pre_act).astype(jnp.bfloat16)
    logit = jnp.dot(hidden, w_out, preferred_element_type=jnp.float32)
    dlogit = jax.nn.sigmoid(logit) - labels
    dhidden = (dlogit[:, None] * w_out.astype(jnp.float32)[None, :] * (pre_act > 0)).astype(
        jnp.bfloat16
    )
    dpooled = lax.dot_general(
        dhidden, w_in, (((1,), (1,)), ((), ())), preferred_element_type=jnp.float32
    ).astype(jnp.bfloat16)
    columns = hot_incidence
    hot_grad = lax.psum_scatter(
        lax.dot_general(
            columns, dpooled, (((0,), (0,)), ((), ())), preferred_element_type=jnp.float32
        ).astype(jnp.bfloat16),
        "table",
        scatter_dimension=0,
        tiled=True,
    ).astype(jnp.float32)
    cold_term = lax.dot_general(
        cold_incidence, dpooled, (((0,), (0,)), ((), ())), preferred_element_type=jnp.float32
    )
    cold_term = jnp.where(live_mask[..., None], cold_term.reshape(owners, slot_cap, width), 0.0)
    returned = lax.all_to_all(
        cold_term.astype(jnp.bfloat16), "table", split_axis=0, concat_axis=0, tiled=True
    ).astype(cold_term.dtype)
    grad = jnp.zeros(table.shape, jnp.float32).at[hot_ids].add(hot_grad)
    grad = grad.at[asked_ids.reshape(-1)].add(returned.reshape(-1, width))
    total_grad = lax.psum(grad.astype(jnp.bfloat16), "dp").astype(jnp.float32)
    new_table, new_sum = adagrad_step(table, adagrad_sum, total_grad)
    return (new_table, new_sum)


def solution(mesh):
    placed = (
        P(("dp", "table"), None),
        P(("dp", "table")),
        P(("dp", "table"), None, None),
        P(("dp", "table"), None),
        P("table", None),
        P("table"),
        P("table"),
        P(),
        P(),
    )
    return jax.shard_map(
        per_device,
        mesh=mesh,
        in_specs=placed,
        out_specs=(P("table", None), P("table")),
        check_vma=False,
    )
```

profile of v0, /device:TPU:0, one launch (start us, length us, event | category | flops | bytes accessed | tf_op | source)
XLA Modules:
  0.0 309.4 jit_solution(2245355269902386737)
XLA Ops:
  7.2 7.4 %all-to-all-start = ((s32[8,1,32]{2,1,0:T(1,128)}), s32[8,1,32]{2,1,0:T(1,128)S(1)}, u32[]{:S(2)}, u32[]{:S(2)}) async-start(s32[8,1,32]{2,1,0:T(1,128)} %bitcast.26), calls=%async_computation | async-start | bytes 8192 | tf_op jit(solution)/shard_map/all_to_all | solution.py:34
  17.0 1.3 convert_element_type.35
  20.1 33.5 %all-gather = bf16[512,256]{1,0:T(8,128)(2,1)} all-gather(bf16[64,256]{1,0:T(8,128)(2,1)S(1)} %gather_fusion.1), channel_id=2, replica_groups=mesh['dp'=4,'table'=8] {'table'}, dimensions={0}, use_global_device_ids=true | all-gather | bytes 294912 | tf_op jit(solution)/shard_map/all_gather | solution.py:47
  53.9 113.6 %scatter_custom_fusion.2 = bf16[393216]{0:T(1024)(128)(2,1)} fusion(s32[16384]{0:T(1024)S(1)} %reshape.161, bf16[16384]{0:T(1024)(128)(2,1)S(1)} %broadcast.91, bf16[]{:T(256)} %constant.12.clone.1), kind=kCustom, calls=%fused_computation.28 | custom fusion | flops 16384 | bytes 786434
  167.6 1.8 reshape.126
  169.5 1.8 gather_fusion
  171.3 5.5 %all-to-all-start.1 = ((bf16[8,32,256]{2,1,0:T(8,128)(2,1)}), bf16[8,32,256]{2,1,0:T(8,128)(2,1)}, u32[]{:S(2)}, u32[]{:S(2)}) async-start(bf16[8,32,256]{2,1,0:T(8,128)(2,1)} %bitcast.4), calls=%async_computation.1 | async-start | bytes 262144 | tf_op jit(solution)/shard_map/all_to_all | solution.py:36
  176.8 1.2 fusion.15
  179.3 4.9 %all-to-all-done.1 = bf16[8,32,256]{2,1,0:T(8,128)(2,1)} async-done(((bf16[8,32,256]{2,1,0:T(8,128)(2,1)}), bf16[8,32,256]{2,1,0:T(8,128)(2,1)}, u32[]{:S(2)}, u32[]{:S(2)}) %all-to-all-start.1) | async-done | bytes 131104 | tf_op jit(solution)/shard_map/all_to_all | solution.py:36
  184.2 1.0 broadcast_select_fusion
  185.2 4.6 %fusion.8 = f32[512,4096]{1,0:T(8,128)} fusion(bf16[256,4096]{1,0:T(8,128)(2,1)S(1)} %copy-done, f32[512,256]{1,0:T(8,128)S(1)} %fusion.15, bf16[256,256]{1,0:T(8,128)(2,1)S(1)} %bitcast.21, bf16[512,768]{1,0:T(8,128)(2,1)S(1)} %reshape.126), kind=kOutput, calls=%fused_computation.19 | convolution fusion | flops 1141112832 | bytes 11403264 | tf_op jit(solution)/shard_map/dot_general | solution.py:51
  189.8 4.7 %fusion = f32[1,512]{1,0:T(1,128)S(1)} fusion(bf16[4096,1]{0,1:T(2,128)(2,1)S(1)} %reshape.171, f32[512,4096]{1,0:T(8,128)} %fusion.8), kind=kOutput, calls=%fused_computation.7 | convolution fusion | flops 8388608 | bytes 8398848 | tf_op jit(solution)/shard_map/dot_general | solution.py:53
  194.6 1.0 copy-done.1
  195.6 1.4 fusion.6
  197.7 1.0 convolution_convert_fusion
  198.8 1.3 fusion.21
  200.9 3.4 %all-to-all-start.2 = ((bf16[8,32,256]{2,1,0:T(8,128)(2,1)}), bf16[8,32,256]{2,1,0:T(8,128)(2,1)S(1)}, u32[]{:S(2)}, u32[]{:S(2)}) async-start(bf16[8,32,256]{2,1,0:T(8,128)(2,1)} %select_convert_fusion.4), calls=%async_computation.3 | async-start | bytes 262144 | tf_op jit(solution)/shard_map/all_to_all | solution.py:74
  205.5 52.4 %reduce-scatter.2.cloned.1.call-done = bf16[64,256]{1,0:T(8,128)(2,1)} async-done(((bf16[512,256]{1,0:T(8,128)(2,1)}), bf16[64,256]{1,0:T(8,128)(2,1)}) %reduce-scatter.2.cloned.1.call-update) | async-done | bytes 32784 | tf_op jit(solution)/shard_map/reduce_scatter | solution.py:62
  257.9 2.1 scatter_custom_fusion
  260.1 4.0 %scatter_custom_fusion.1 = f32[1024,256]{1,0:T(8,128)} fusion(f32[1024,256]{1,0:T(8,128)} %scatter_custom_fusion, s32[256]{0:T(256)S(1)} %bitcast.27, bf16[256,256]{1,0:T(8,128)(2,1)S(1)} %bitcast.22), kind=kCustom, calls=%fused_computation.30 | custom fusion | flops 131072 | bytes 1179648 | tf_op jit(solution)/shard_map/scatter-add | solution.py:78
  264.1 2.1 convert_element_type.44
  266.2 32.3 %all-reduce.2.cloned.1.call-done = bf16[1024,256]{1,0:T(8,128)(2,1)} async-done(((bf16[1024,256]{1,0:T(8,128)(2,1)}), bf16[1024,256]{1,0:T(8,128)(2,1)}) %all-reduce.2.cloned.1.call-update) | async-done | bytes 524304 | tf_op jit(solution)/shard_map/psum | solution.py:79
  298.4 1.3 fusion.11
  300.3 2.2 fusion.10
  (59 shorter events, 9.2 us)
Async XLA Ops:
  7.2 178.0 %copy-start = (bf16[256,4096]{1,0:T(8,128)(2,1)S(1)}, bf16[256,4096]{1,0:T(8,128)(2,1)}, u32[]{:S(2)}) copy-start(bf16[256,4096]{1,0:T(8,128)(2,1)} %param.16) | copy-start | bytes 6291460
  7.2 170.9 %copy-start.7 = (bf16[4096]{0:T(1024)(128)(2,1)S(1)}, bf16[4096]{0:T(1024)(128)(2,1)}, u32[]{:S(2)}) copy-start(bf16[4096]{0:T(1024)(128)(2,1)} %param.17) | copy-start | bytes 24580
  7.2 171.5 %copy-start.13 = (s32[1,8]{1,0:T(1,128)S(1)}, s32[1,8]{1,0:T(1,128)}, u32[]{:S(2)}) copy-start(s32[1,8]{1,0:T(1,128)} %param.12) | copy-start | bytes 100
  7.2 162.2 %all-to-all-start = ((s32[8,1,32]{2,1,0:T(1,128)}), s32[8,1,32]{2,1,0:T(1,128)S(1)}, u32[]{:S(2)}, u32[]{:S(2)}) async-start(s32[8,1,32]{2,1,0:T(1,128)} %bitcast.26), calls=%async_computation | async-start | bytes 8192 | tf_op jit(solution)/shard_map/all_to_all | solution.py:34
  18.9 0.5 copy-start.12
  169.3 25.2 %copy-start.3 = (bf16[512,768]{1,0:T(8,128)(2,1)}, bf16[512,768]{1,0:T(8,128)(2,1)S(1)}, u32[]{:S(2)}) copy-start(bf16[512,768]{1,0:T(8,128)(2,1)S(1)} %reshape.126) | copy-start | bytes 2359300
  169.4 9.9 %copy-start.5 = (s32[8,1,32]{2,1,0:T(1,128)}, s32[8,1,32]{2,1,0:T(1,128)S(1)}, u32[]{:S(2)}) copy-start(s32[8,1,32]{2,1,0:T(1,128)S(1)} %all-to-all-done) | copy-start | bytes 3076
  171.3 12.9 %all-to-all-start.1 = ((bf16[8,32,256]{2,1,0:T(8,128)(2,1)}), bf16[8,32,256]{2,1,0:T(8,128)(2,1)}, u32[]{:S(2)}, u32[]{:S(2)}) async-start(bf16[8,32,256]{2,1,0:T(8,128)(2,1)} %bitcast.4), calls=%async_computation.1 | async-start | bytes 262144 | tf_op jit(solution)/shard_map/all_to_all | solution.py:36
  176.7 81.2 %reduce-scatter.2.cloned.1.call-start = ((), (), s32[]{:S(2)}) async-start(), calls=%async_computation.4 | async-start | bytes 294912 | tf_op jit(solution)/shard_map/reduce_scatter | solution.py:62
  189.8 4.7 %copy-start.11 = (f32[512]{0:T(512)S(1)}, f32[512]{0:T(512)}, u32[]{:S(2)}) copy-start(f32[512]{0:T(512)} %param.10) | copy-start | bytes 6148
  189.8 5.8 %copy-start.1 = (f32[512,4096]{1,0:T(8,128)S(1)}, f32[512,4096]{1,0:T(8,128)}, u32[]{:S(2)}) copy-start(f32[512,4096]{1,0:T(8,128)} %fusion.8) | copy-start | bytes 25165828
  189.8 5.8 %copy-start.8 = (f32[4096]{0:T(1024)S(1)}, f32[4096]{0:T(1024)}, u32[]{:S(2)}) copy-start(f32[4096]{0:T(1024)} %convert_element_type.38) | copy-start | bytes 49156
  195.6 2.1 copy-start.4
  195.6 4.5 %copy-start.9 = (pred[8,32]{1,0:T(8,128)(4,1)S(1)}, pred[8,32]{1,0:T(8,128)(4,1)}, u32[]{:S(2)}) copy-start(pred[8,32]{1,0:T(8,128)(4,1)} %iota_compare_fusion) | copy-start | bytes 772
  195.6 9.2 %copy-start.6 = (s32[8,1,32]{2,1,0:T(1,128)S(1)}, s32[8,1,32]{2,1,0:T(1,128)}, u32[]{:S(2)}) copy-start(s32[8,1,32]{2,1,0:T(1,128)} %copy-done.5) | copy-start | bytes 3076
  195.6 104.1 %copy-start.10 = (f32[1024]{0:T(1024)S(1)}, f32[1024]{0:T(1024)}, u32[]{:S(2)}) copy-start(f32[1024]{0:T(1024)} %param.14) | copy-start | bytes 12292
  197.0 0.7 copy-start.14
  197.7 102.6 %copy-start.2 = (f32[1024,256]{1,0:T(8,128)S(1)}, f32[1024,256]{1,0:T(8,128)}, u32[]{:S(2)}) copy-start(f32[1024,256]{1,0:T(8,128)} %param.13) | copy-start | bytes 3145732
  200.9 59.2 %all-to-all-start.2 = ((bf16[8,32,256]{2,1,0:T(8,128)(2,1)}), bf16[8,32,256]{2,1,0:T(8,128)(2,1)S(1)}, u32[]{:S(2)}, u32[]{:S(2)}) async-start(bf16[8,32,256]{2,1,0:T(8,128)(2,1)} %select_convert_fusion.4), calls=%async_computation.3 | async-start | bytes 262144 | tf_op jit(solution)/shard_map/all_to_all | solution.py:74
  204.2 94.2 %all-reduce.2.cloned.1.call-start = ((), (), s32[]{:S(2)}) async-start(), calls=%async_computation.5 | async-start | bytes 1048576 | tf_op jit(solution)/shard_map/psum | solution.py:79
Sparse Core Ops, SparseCore 0:
  198.9 59.0 reduce-scatter.1
  266.3 32.1 all-reduce.1
where the time goes:
time: 310 us; the launch traced here: 309 us
  other arithmetic  134 us (43%)
  waiting for transfers between devices  89.6 us (29%)
  blocking collectives  33.5 us (11%)
  starting transfers between devices  16.3 us (5%)
  matrix products  14.3 us (5%)
  between operations  14.3 us (5%)
  local copies, waits for them, and re-layouts  7.46 us (2%)
    unnamed x4, other arithmetic  115 us
    reduce_scatter x1, waiting for transfers between devices, per_device(): lax.psum_scatter(lax.dot_general(columns, dpooled, (((0,), (0,)), ((), ()...  52.4 us
    all_gather x1, blocking collectives, per_device(): lax.all_gather(hot_rows, 'table', axis=0, tiled=True)  33.5 us
    psum x1, waiting for transfers between devices, per_device(): total_grad = lax.psum(grad.astype(jnp.bfloat16), 'dp').astype(jnp.float32)  32.3 us
    all_to_all x1, starting transfers between devices, per_device(): lax.all_to_all(cold_ids[0], 'table', split_axis=0, concat_axis=0, tiled=T...  7.4 us
  transfers between devices with their start and end apart: 5, of which 3 were waited for; matrix products, arithmetic and copies ran while one was open for 42% of the time, Pallas kernels for 0%

commit v1 on v0

v1 whole, which is shorter than its diff:
```python
import functools

import jax
import jax.numpy as jnp
from jax import lax
from jax.experimental import pallas as pl
from jax.experimental.pallas import tpu as pltpu
from jax.sharding import PartitionSpec as P

learning_rate = 0.3
f32, bf16, i32 = jnp.float32, jnp.bfloat16, jnp.int32
VMEM = pl.BlockSpec(memory_space=pltpu.VMEM)
SMEM = pl.BlockSpec(memory_space=pltpu.SMEM)
FIELDS = 4
FIELD_BITS = 8
TAIL = 16


def call(body, outs, operands, scratch=(), in_specs=None, flops=0, moved=0):
    return pl.pallas_call(
        body,
        out_shape=outs,
        in_specs=in_specs or [VMEM] * len(operands),
        out_specs=jax.tree.map(lambda _: VMEM, outs),
        scratch_shapes=list(scratch),
        compiler_params=pltpu.CompilerParams(vmem_limit_bytes=48 * 1024 * 1024),
        cost_estimate=pl.CostEstimate(flops=flops, bytes_accessed=moved, transcendentals=0),
    )(*operands)


def lanes(pieces):
    return jnp.concatenate(pieces, axis=1)


def incidence_body(hot_dev, slot_cap, count_ref, slots_ref, inc_ref, inc_t_ref):
    vocab, batch = inc_t_ref.shape
    block = hot_dev + slot_cap
    owners = vocab // block
    field = vocab // FIELDS
    step = 128
    row = lax.broadcasted_iota(i32, (field, step), 0)
    for start in range(0, batch, step):
        slots = slots_ref[start:start + step, :].T
        cold = slots - owners * hot_dev
        hot_column = (slots // hot_dev) * block + slots % hot_dev
        cold_column = (cold // slot_cap) * block + hot_dev + cold % slot_cap
        column = jnp.where(cold < 0, hot_column, cold_column)
        key = jnp.where(slots < 0, -1, column % field)
        unit = jnp.left_shift(jnp.ones_like(slots), FIELD_BITS * (column // field))
        packed = jnp.zeros((field, step), i32)
        for entry in range(slots.shape[0]):
            packed += jnp.where(row == key[entry:entry + 1, :], unit[entry:entry + 1, :], 0)
        for k in range(FIELDS):
            part = jnp.right_shift(packed, FIELD_BITS * k) & (2**FIELD_BITS - 1)
            inc_t_ref[k * field:(k + 1) * field, start:start + step] = part.astype(f32).astype(bf16)
    place = lax.broadcasted_iota(i32, (block, batch), 0)
    for owner in range(owners):
        rows = pl.ds(owner * block, block)
        live = place < hot_dev + count_ref[0, owner]
        inc_t_ref[rows, :] = jnp.where(live, inc_t_ref[rows, :].astype(f32), 0.0).astype(bf16)
    inc_ref[...] = inc_t_ref[...].T


def serve_body(asked_ref, hot_ref, table_ref, out_ref, pick):
    owners, slot_cap = asked_ref.shape
    hot_dev = hot_ref.shape[1]
    rows = table_ref.shape[0]
    hot_column = jnp.broadcast_to(hot_ref[...], (8, hot_dev)).T[:, 0:1]
    asked = asked_ref[...].T
    pick[0:hot_dev, :] = (lax.broadcasted_iota(i32, (hot_dev, rows), 1) == hot_column).astype(f32).astype(bf16)
    row = lax.broadcasted_iota(i32, (slot_cap, rows), 1)
    for t in range(owners):
        at = hot_dev + t * slot_cap
        pick[at:at + slot_cap, :] = (row == asked[:, t:t + 1]).astype(f32).astype(bf16)
    picked = jnp.dot(pick[...], table_ref[...].astype(bf16), preferred_element_type=f32).astype(bf16)
    for t in range(owners):
        at = hot_dev + t * slot_cap
        out_ref[t, 0:hot_dev, :] = picked[0:hot_dev]
        out_ref[t, hot_dev:, :] = picked[at:at + slot_cap]


def top_body(labels_ref, inc_ref, inc_t_ref, rows_ref, w_in_ref, w_out_ref, out_ref, gated, dhidden):
    batch = inc_ref.shape[0]
    hidden_units = w_in_ref.shape[1]
    step = 512
    pooled = jnp.dot(inc_ref[...], rows_ref[...], preferred_element_type=f32).astype(bf16)
    total = jnp.zeros((batch, 128), f32)
    for start in range(0, hidden_units, step):
        cols = slice(start, start + step)
        pre_act = jnp.dot(pooled, w_in_ref[:, cols], preferred_element_type=f32)
        w_out = w_out_ref[:, cols].astype(f32)
        hidden = jnp.maximum(pre_act, 0.0).astype(bf16).astype(f32)
        gated[:, cols] = jnp.where(pre_act > 0, w_out, 0.0).astype(bf16)
        term = hidden * w_out
        for k in range(0, step, 128):
            total += term[:, k:k + 128]
    logit = jnp.sum(total, axis=1, keepdims=True)
    labels = labels_ref[...].T
    labels = jnp.concatenate([labels[:, k:k + 1] for k in range(labels.shape[1])], axis=0)
    dlogit = jax.nn.sigmoid(logit) - labels
    dhidden[...] = (dlogit * gated[...].astype(f32)).astype(bf16)
    dpooled = lax.dot_general(
        dhidden[...], w_in_ref[...], (((1,), (1,)), ((), ())), preferred_element_type=f32
    ).astype(bf16)
    out_ref[...] = jnp.dot(inc_t_ref[...], dpooled, preferred_element_type=f32).astype(bf16)


def collect_body(asked_ref, back_ref, out_ref):
    owners, slot_cap = asked_ref.shape
    hot_dev = back_ref.shape[1] - slot_cap
    out_ref[0:hot_dev, :] = jnp.sum(back_ref[:, 0:hot_dev, :].astype(f32), axis=0).astype(bf16)
    for t in range(owners):
        at = hot_dev + t * slot_cap
        out_ref[at:at + slot_cap, :] = back_ref[t, hot_dev:, :]
    asked = lanes([asked_ref[t:t + 1, :] for t in range(owners)])
    digit = lax.broadcasted_iota(i32, (TAIL, asked.shape[1]), 0)
    digits = jnp.where(digit == 0, asked >> 8, jnp.where(digit == 1, asked & 255, 0))
    out_ref[hot_dev + owners * slot_cap:, :] = digits.astype(f32).astype(bf16)


def adagrad(table, own_sum, grad):
    new_sum = own_sum + jnp.sum(grad * grad, axis=1, keepdims=True) * (1.0 / grad.shape[1])
    return table - grad * (learning_rate / jnp.sqrt(new_sum)), new_sum


def update_body(hot_ref, sum_ref, table_ref, *refs):
    groups = len(refs) - 4
    part_refs, (new_table_ref, new_sum_ref, held, sums) = refs[:groups], refs[groups:]
    hot_dev = hot_ref.shape[1]
    size = part_refs[0].shape[0]
    cold = size - hot_dev - TAIL
    rows, width = table_ref.shape
    me = lax.axis_index("dp")
    for s in range(groups):
        held[pl.ds(pl.multiple_of((me ^ s) * size, 16), size), :] = part_refs[s][...]
    hot = jnp.concatenate([held[g * size:g * size + hot_dev, :] for g in range(groups)], axis=0)
    hot_ids = lanes([hot_ref[...]] * groups)
    cold_ids = []
    for g in range(groups):
        digits = held[g * size + hot_dev + cold:(g + 1) * size, :].astype(f32).astype(i32)
        cold_ids.append(digits[0:1, :] * 256 + digits[1:2, :])
    own_sum = sum_ref[...].T
    step = 128
    for k in range(rows // step):
        at = slice(k * step, (k + 1) * step)

        def pick(ids):
            row = lax.broadcasted_iota(i32, (step, ids.shape[1]), 0) + k * step
            return (row == ids).astype(f32).astype(bf16)

        grad = jnp.dot(pick(hot_ids), hot, preferred_element_type=f32)
        for g in range(groups):
            part = held[g * size + hot_dev:g * size + hot_dev + cold, :]
            grad += jnp.dot(pick(cold_ids[g]), part, preferred_element_type=f32)
        new_table_ref[at, :], sums[:, k:k + 1] = adagrad(table_ref[at, :], own_sum[:, k:k + 1], grad)
    new_sum_ref[...] = sums[...].T


def dense_body(hot_ref, asked_ref, back_ref, out_ref):
    owners, slot_cap = asked_ref.shape
    hot_dev = hot_ref.shape[1]
    rows = out_ref.shape[0]

    def pick(ids):
        return (lax.broadcasted_iota(i32, (rows, ids.shape[1]), 0) == ids).astype(f32).astype(bf16)

    hot = jnp.sum(back_ref[:, 0:hot_dev, :].astype(f32), axis=0).astype(bf16)
    grad = jnp.dot(pick(hot_ref[...]), hot, preferred_element_type=f32)
    for t in range(owners):
        grad += jnp.dot(pick(asked_ref[t:t + 1, :]), back_ref[t, hot_dev:, :], preferred_element_type=f32)
    out_ref[...] = grad.astype(bf16)


def exchange(x):
    return lax.all_to_all(x, "table", split_axis=0, concat_axis=0, tiled=True)


def per_device(bag_slots, labels, cold_ids, cold_count, table, adagrad_sum, hot_ids, w_in, w_out):
    owners = lax.axis_size("table")
    groups = lax.axis_size("dp")
    hot_dev = hot_ids.shape[0]
    slot_cap = cold_ids.shape[2]
    batch = bag_slots.shape[0]
    rows, width = table.shape
    hidden_units = w_in.shape[1]
    block = hot_dev + slot_cap
    vocab = owners * block
    shape = jax.ShapeDtypeStruct

    hot_row = hot_ids.reshape(1, hot_dev)
    asked = exchange(cold_ids[0])
    inc, inc_t = call(
        functools.partial(incidence_body, hot_dev, slot_cap),
        (shape((batch, vocab), bf16), shape((vocab, batch), bf16)),
        (cold_count, bag_slots),
        in_specs=[SMEM, VMEM],
    )
    served = call(
        serve_body,
        shape((owners, block, width), bf16),
        (asked, hot_row, table),
        [pltpu.VMEM((hot_dev + owners * slot_cap, rows), bf16)],
    )
    fetched = exchange(served)
    slot_grad = call(
        top_body,
        shape((vocab, width), bf16),
        (labels.reshape(-1, 128), inc, inc_t, fetched.reshape(vocab, width), w_in, w_out.reshape(1, -1)),
        [pltpu.VMEM((batch, hidden_units), bf16), pltpu.VMEM((batch, hidden_units), bf16)],
    )
    returned = exchange(slot_grad.reshape(owners, block, width))
    size = hot_dev + owners * slot_cap + TAIL
    if groups & (groups - 1) == 0 and groups * size <= 2 * rows and owners * slot_cap == width:
        part = call(collect_body, shape((size, width), bf16), (asked, returned))
        parts = {0: part}
        bit = groups // 2
        while bit:
            swap = [(g, g ^ bit) for g in range(groups)]
            parts.update({s ^ bit: lax.ppermute(x, "dp", swap) for s, x in list(parts.items())})
            bit //= 2
        new_table, new_sum = call(
            update_body,
            (shape((rows, width), f32), shape((rows // 128, 128), f32)),
            (hot_row, adagrad_sum.reshape(-1, 128), table) + tuple(parts[s] for s in range(groups)),
            [pltpu.VMEM((groups * size, width), bf16), pltpu.VMEM((128, rows // 128), f32)],
        )
        return new_table, new_sum.reshape(rows)
    grad = call(dense_body, shape((rows, width), bf16), (hot_row, asked, returned))
    grad = lax.psum(grad, "dp").astype(f32)
    new_table, new_sum = adagrad(table, adagrad_sum[:, None], grad)
    return new_table, new_sum[:, 0]


def solution(mesh):
    placed = (
        P(("dp", "table"), None),
        P(("dp", "table")),
        P(("dp", "table"), None, None),
        P(("dp", "table"), None),
        P("table", None),
        P("table"),
        P("table"),
        P(),
        P(),
    )
    return jax.shard_map(
        per_device,
        mesh=mesh,
        in_specs=placed,
        out_specs=(P("table", None), P("table")),
        check_vma=False,
    )
```

time: 310 us -> 64 us (0.21)
  other arithmetic: 134 us -> 0 us
  waiting for transfers between devices: 89.6 us -> 11 us
  matrix products: 14.3 us -> 0 us
  between operations: 14.3 us -> 0.73 us
  Pallas kernels: 0 us -> 12.3 us
  starting transfers between devices: 16.3 us -> 5.04 us
  blocking collectives: 33.5 us -> 28.5 us
    unnamed x4 -> x0, other arithmetic: 115 us -> none
    reduce_scatter x1 -> x0, waiting for transfers between devices: 52.4 us -> none  [per_device(): lax.psum_scatter(lax.dot_general(columns, dpooled, (((0,), (0,)), ((), ()...]
    all_gather x1 -> x0, blocking collectives: 33.5 us -> none  [per_device(): lax.all_gather(hot_rows, 'table', axis=0, tiled=True)]
    psum x1 -> x0, waiting for transfers between devices: 32.3 us -> none  [per_device(): total_grad = lax.psum(grad.astype(jnp.bfloat16), 'dp').astype(jnp.float32)]
    all_to_all x0 -> x2, blocking collectives: none -> 28.5 us  [exchange(): return lax.all_to_all(x, 'table', split_axis=0, concat_axis=0, tiled=True)]
    dot_general x6 -> x0, matrix products: 14.3 us -> none  [the longest x1 4.71 us: per_device(): logit = jnp.dot(hidden, w_out, preferred_element_type=jnp.float32)]
    all_to_all x3 -> x1, starting transfers between devices: 16.2 us -> 3.45 us  [exchange(): return lax.all_to_all(x, 'table', split_axis=0, concat_axis=0, tiled=True)]
    pallas_call x0 -> x5, Pallas kernels: none -> 12.3 us  [call(): pl.pallas_call(body, out_shape=outs, in_specs=in_specs or [VMEM] * len(op...]
  transfers between devices with their start and end apart: 5 -> 4, of which waited for: 3 -> 3; matrix products, arithmetic and copies ran while one was open for 42% -> 0% of each run, Pallas kernels for 0% -> 5%
where the time goes in v1:
time: 64 us; the launch traced here: 63.5 us
  blocking collectives  28.5 us (45%)
  Pallas kernels  12.3 us (19%)
  waiting for transfers between devices  11 us (17%)
  local copies, waits for them, and re-layouts  5.97 us (9%)
  starting transfers between devices  5.04 us (8%)
  between operations  0.73 us (1%)
    all_to_all x2, blocking collectives, exchange(): return lax.all_to_all(x, 'table', split_axis=0, concat_axis=0, tiled=True)  28.5 us
    pallas_call x5, Pallas kernels, call(): pl.pallas_call(body, out_shape=outs, in_specs=in_specs or [VMEM] * len(op...  12.3 us
    unnamed x29, local copies, waits for them, and re-layouts  5.96 us
    all_to_all x1, waiting for transfers between devices, exchange(): return lax.all_to_all(x, 'table', split_axis=0, concat_axis=0, tiled=True)  5.76 us
    ppermute x3, waiting for transfers between devices, per_device(): lax.ppermute(x, 'dp', swap)  5.27 us
    all_to_all x1, starting transfers between devices, exchange(): return lax.all_to_all(x, 'table', split_axis=0, concat_axis=0, tiled=True)  3.45 us
    ppermute x3, starting transfers between devices, per_device(): lax.ppermute(x, 'dp', swap)  1.59 us
  transfers between devices with their start and end apart: 4, of which 3 were waited for; matrix products, arithmetic and copies ran while one was open for 0% of the time, Pallas kernels for 5%

profile of v1, /device:TPU:0, one launch (start us, length us, event | category | flops | bytes accessed | tf_op | source)
XLA Modules:
  0.0 63.5 jit_solution(462565928495962744)
XLA Ops:
  0.6 13.7 %all_to_all.21 = s32[8,1,32]{2,1,0:T(1,128)S(1)} all-to-all(s32[8,1,32]{2,1,0:T(1,128)} %bitcast.16), channel_id=1, replica_groups=mesh['dp'=4,'table'=8] {'table'}, dimensions={0} | all-to-all | bytes 2048 | tf_op jit(solution)/shard_map/all_to_all | solution.py:175
  14.3 1.2 %copy-done = f32[1024,256]{1,0:T(8,128)S(1)} copy-done((f32[1024,256]{1,0:T(8,128)S(1)}, f32[1024,256]{1,0:T(8,128)}, u32[]{:S(2)}) %copy-start) | copy-done | bytes 1048600
  15.5 0.7 %copy-done.8 = s32[64]{0:T(128)S(1)} copy-done((s32[64]{0:T(128)S(1)}, s32[64]{0:T(128)}, u32[]{:S(2)}) %copy-start.8) | copy-done | bytes 280
  16.2 1.2 %shard_map.105 = bf16[8,96,256]{2,1,0:T(8,128)(2,1)} custom-call(s32[8,32]{1,0:T(8,128)S(1)} %bitcast.10, s32[1,64]{1,0:T(1,128)S(1)} %bitcast.13, f32[1024,256]{1,0:T(8,128)S(1)} %copy-done), custom_call_target="tpu_custom_call" | custom-call | tf_op jit(solution)/shard_map/pallas_call | solution.py:20
  17.4 0.6 copy-done.5
  18.0 3.5 %all-to-all-start.1 = ((bf16[8,96,256]{2,1,0:T(8,128)(2,1)}), bf16[8,96,256]{2,1,0:T(8,128)(2,1)S(1)}, u32[]{:S(2)}, u32[]{:S(2)}) async-start(bf16[8,96,256]{2,1,0:T(8,128)(2,1)} %shard_map.105), calls=%async_computation.1 | async-start | bytes 786432 | tf_op jit(solution)/shard_map/all_to_all | solution.py:175
  21.5 0.1 copy.12.slots_ref
  21.6 0.0 copy-start.11
  21.6 0.7 %copy-done.11 = s32[1,8]{1,0:T(1,128)S(1)} copy-done((s32[1,8]{1,0:T(1,128)S(1)}, s32[1,8]{1,0:T(1,128)}, u32[]{:S(2)}) %copy-start.11) | copy-done | bytes 56
  22.3 3.0 %shard_map.104 = (bf16[512,768]{1,0:T(8,128)(2,1)S(1)}, bf16[768,512]{1,0:T(8,128)(2,1)S(1)}) custom-call(s32[1,8]{1,0:T(1,128)S(1)} %copy-done.11, s32[512,32]{1,0:T(8,128)S(1)} %copy.12.slots_ref), custom_call_target="tpu_custom_call" | custom-call | tf_op jit(solution)/shard_map/pallas_call | solution.py:20
  25.3 0.0 copy-start.3
  25.3 0.9 %copy-done.3 = bf16[768,512]{1,0:T(8,128)(2,1)} copy-done((bf16[768,512]{1,0:T(8,128)(2,1)}, bf16[768,512]{1,0:T(8,128)(2,1)S(1)}, u32[]{:S(2)}) %copy-start.3) | copy-done | bytes 786456
  26.1 5.8 %all-to-all-done.1 = bf16[8,96,256]{2,1,0:T(8,128)(2,1)S(1)} async-done(((bf16[8,96,256]{2,1,0:T(8,128)(2,1)}), bf16[8,96,256]{2,1,0:T(8,128)(2,1)S(1)}, u32[]{:S(2)}, u32[]{:S(2)}) %all-to-all-start.1) | async-done | bytes 393248 | tf_op jit(solution)/shard_map/all_to_all | solution.py:175
  31.9 1.1 %copy-done.4 = bf16[768,512]{1,0:T(8,128)(2,1)S(1)} copy-done((bf16[768,512]{1,0:T(8,128)(2,1)S(1)}, bf16[768,512]{1,0:T(8,128)(2,1)}, u32[]{:S(2)}) %copy-start.4) | copy-done | bytes 786456
  33.0 0.7 %copy-done.10 = f32[512]{0:T(512)S(1)} copy-done((f32[512]{0:T(512)S(1)}, f32[512]{0:T(512)}, u32[]{:S(2)}) %copy-start.10) | copy-done | bytes 2072
  33.7 5.7 %shard_map.106 = bf16[768,256]{1,0:T(8,128)(2,1)S(1)} custom-call(f32[4,128]{1,0:T(4,128)S(1)} %bitcast.15, bf16[512,768]{1,0:T(8,128)(2,1)S(1)} %get-tuple-element.6.inc_ref, bf16[768,512]{1,0:T(8,128)(2,1)S(1)} %copy-done.4, bf16[768,256]{1,0:T(8,128)(2,1)S(1)} %bitcast.8, bf16[256,4096]{1,0:T(8,128)(2,1)S(1)} %copy-done.2, ...), custom_call_target="tpu_custom_call" | custom-call | tf_op jit(solution)/shard_map/pallas_call | solution.py:20
  39.4 14.8 %all_to_all.22.back_ref = bf16[8,96,256]{2,1,0:T(8,128)(2,1)S(1)} all-to-all(bf16[8,96,256]{2,1,0:T(8,128)(2,1)S(1)} %bitcast.9), channel_id=1, replica_groups=mesh['dp'=4,'table'=8] {'table'}, dimensions={0} | all-to-all | bytes 786432 | tf_op jit(solution)/shard_map/all_to_all | solution.py:175
  54.2 0.1 shard_map.107.refs_0_
  54.3 1.6 %collective-permute-start.1 = (bf16[336,256]{1,0:T(8,128)(2,1)S(1)}, bf16[336,256]{1,0:T(8,128)(2,1)S(1)}, u32[]{:S(2)}, u32[]{:S(2)}) collective-permute-start(bf16[336,256]{1,0:T(8,128)(2,1)S(1)} %shard_map.107.refs_0_), channel_id=1, source_target_pairs={{0,16},{8,24},{16,0},{24,8},{1,17},{9,25},{17,1},{25,9},{2,18},{10... | collective-permute-start | bytes 516104 | tf_op jit(solution)/shard_map/ppermute | solution.py:219
  55.9 0.0 collective-permute-start
  55.9 3.9 %collective-permute-done.1.refs_2_ = bf16[336,256]{1,0:T(8,128)(2,1)S(1)} collective-permute-done((bf16[336,256]{1,0:T(8,128)(2,1)S(1)}, bf16[336,256]{1,0:T(8,128)(2,1)S(1)}, u32[]{:S(2)}, u32[]{:S(2)}) %collective-permute-start.1) | collective-permute-done | bytes 172064 | tf_op jit(solution)/shard_map/ppermute | solution.py:219
  59.8 0.0 collective-permute-start.2
  59.8 1.4 %collective-permute-done.2.refs_3_ = bf16[336,256]{1,0:T(8,128)(2,1)S(1)} collective-permute-done((bf16[336,256]{1,0:T(8,128)(2,1)S(1)}, bf16[336,256]{1,0:T(8,128)(2,1)S(1)}, u32[]{:S(2)}, u32[]{:S(2)}) %collective-permute-start.2) | collective-permute-done | bytes 172064 | tf_op jit(solution)/shard_map/ppermute | solution.py:219
  61.2 2.3 %shard_map.108 = (f32[1024,256]{1,0:T(8,128)}, f32[8,128]{1,0:T(8,128)}) custom-call(s32[1,64]{1,0:T(1,128)S(1)} %bitcast.14, f32[8,128]{1,0:T(8,128)S(1)} %bitcast.12, f32[1024,256]{1,0:T(8,128)S(1)} %copy-done.1, bf16[336,256]{1,0:T(8,128)(2,1)S(1)} %shard_map.107.refs_0_, bf16[336,256]{1,0:T(8,128)(2,1)S(1)} %collective-permute-done.refs_1_, ...), custom_call_target="tpu_custom_call" | custom-call | tf_op jit(solution)/shard_map/pallas_call | solution.py:20
  (21 shorter events, 0.0 us)
Async XLA Ops:
  0.6 20.8 %copy-start.13 = (bf16[4096]{0:T(1024)(128)(2,1)S(1)}, bf16[4096]{0:T(1024)(128)(2,1)}, u32[]{:S(2)}) copy-start(bf16[4096]{0:T(1024)(128)(2,1)} %param.17) | copy-start | bytes 24580
  14.3 1.2 %copy-start = (f32[1024,256]{1,0:T(8,128)S(1)}, f32[1024,256]{1,0:T(8,128)}, u32[]{:S(2)}) copy-start(f32[1024,256]{1,0:T(8,128)} %table_ref.3) | copy-start | bytes 3145732
  15.5 0.7 %copy-start.8 = (s32[64]{0:T(128)S(1)}, s32[64]{0:T(128)}, u32[]{:S(2)}) copy-start(s32[64]{0:T(128)} %param.15) | copy-start | bytes 772
  16.2 5.3 %copy-start.12 = (s32[512,32]{0,1:T(8,128)S(1)}, s32[512,32]{0,1:T(8,128)}, u32[]{:S(2)}) copy-start(s32[512,32]{0,1:T(8,128)} %param.9) | copy-start | bytes 196612
  16.2 15.7 %copy-start.2 = (bf16[256,4096]{1,0:T(8,128)(2,1)S(1)}, bf16[256,4096]{1,0:T(8,128)(2,1)}, u32[]{:S(2)}) copy-start(bf16[256,4096]{1,0:T(8,128)(2,1)} %w_in_ref.1) | copy-start | bytes 6291460
  17.4 0.6 copy-start.5
  18.0 13.9 %all-to-all-start.1 = ((bf16[8,96,256]{2,1,0:T(8,128)(2,1)}), bf16[8,96,256]{2,1,0:T(8,128)(2,1)S(1)}, u32[]{:S(2)}, u32[]{:S(2)}) async-start(bf16[8,96,256]{2,1,0:T(8,128)(2,1)} %shard_map.105), calls=%async_computation.1 | async-start | bytes 786432 | tf_op jit(solution)/shard_map/all_to_all | solution.py:175
  21.6 0.7 %copy-start.11 = (s32[1,8]{1,0:T(1,128)S(1)}, s32[1,8]{1,0:T(1,128)}, u32[]{:S(2)}) copy-start(s32[1,8]{1,0:T(1,128)} %count_ref.1) | copy-start | bytes 100
  25.3 0.9 %copy-start.3 = (bf16[768,512]{1,0:T(8,128)(2,1)}, bf16[768,512]{1,0:T(8,128)(2,1)S(1)}, u32[]{:S(2)}) copy-start(bf16[768,512]{1,0:T(8,128)(2,1)S(1)} %get-tuple-element.7.inc_t_ref) | copy-start | bytes 2359300
  31.9 1.1 %copy-start.4 = (bf16[768,512]{1,0:T(8,128)(2,1)S(1)}, bf16[768,512]{1,0:T(8,128)(2,1)}, u32[]{:S(2)}) copy-start(bf16[768,512]{1,0:T(8,128)(2,1)} %copy-done.3) | copy-start | bytes 2359300
  33.0 0.7 %copy-start.10 = (f32[512]{0:T(512)S(1)}, f32[512]{0:T(512)}, u32[]{:S(2)}) copy-start(f32[512]{0:T(512)} %param.10) | copy-start | bytes 6148
  33.7 20.5 %copy-start.6 = (s32[8,1,32]{2,1,0:T(1,128)S(1)}, s32[8,1,32]{2,1,0:T(1,128)}, u32[]{:S(2)}) copy-start(s32[8,1,32]{2,1,0:T(1,128)} %copy-done.5) | copy-start | bytes 3076
  33.7 27.4 %copy-start.1 = (f32[1024,256]{1,0:T(8,128)S(1)}, f32[1024,256]{1,0:T(8,128)}, u32[]{:S(2)}) copy-start(f32[1024,256]{1,0:T(8,128)} %table_ref.3) | copy-start | bytes 3145732
  33.7 27.4 %copy-start.7 = (f32[1024]{0:T(1024)S(1)}, f32[1024]{0:T(1024)}, u32[]{:S(2)}) copy-start(f32[1024]{0:T(1024)} %param.14) | copy-start | bytes 12292
  33.7 27.4 %copy-start.9 = (s32[64]{0:T(128)S(1)}, s32[64]{0:T(128)}, u32[]{:S(2)}) copy-start(s32[64]{0:T(128)} %param.15) | copy-start | bytes 772
  54.3 5.5 %collective-permute-start.1 = (bf16[336,256]{1,0:T(8,128)(2,1)S(1)}, bf16[336,256]{1,0:T(8,128)(2,1)S(1)}, u32[]{:S(2)}, u32[]{:S(2)}) collective-permute-start(bf16[336,256]{1,0:T(8,128)(2,1)S(1)} %shard_map.107.refs_0_), channel_id=1, source_target_pairs={{0,16},{8,24},{16,0},{24,8},{1,17},{9,25},{17,1},{25,9},{2,18},{10... | collective-permute-start | bytes 516104 | tf_op jit(solution)/shard_map/ppermute | solution.py:219
  55.9 3.9 %collective-permute-start = (bf16[336,256]{1,0:T(8,128)(2,1)S(1)}, bf16[336,256]{1,0:T(8,128)(2,1)S(1)}, u32[]{:S(2)}, u32[]{:S(2)}) collective-permute-start(bf16[336,256]{1,0:T(8,128)(2,1)S(1)} %shard_map.107.refs_0_), channel_id=1, source_target_pairs={{0,8},{8,0},{16,24},{24,16},{1,9},{9,1},{17,25},{25,17},{2,10},{10... | collective-permute-start | bytes 516104 | tf_op jit(solution)/shard_map/ppermute | solution.py:219
  59.8 1.4 %collective-permute-start.2 = (bf16[336,256]{1,0:T(8,128)(2,1)S(1)}, bf16[336,256]{1,0:T(8,128)(2,1)S(1)}, u32[]{:S(2)}, u32[]{:S(2)}) collective-permute-start(bf16[336,256]{1,0:T(8,128)(2,1)S(1)} %collective-permute-done.1.refs_2_), channel_id=1, source_target_pairs={{0,8},{8,0},{16,24},{24,16},{1,9},{9,1},{17,25},{25,17},{2,10},{10... | collective-permute-start | bytes 516104 | tf_op jit(solution)/shard_map/ppermute | solution.py:219

commit v2 on v1

--- a/solution.py
+++ b/solution.py
@@ -16,15 +16,14 @@
 TAIL = 16
 
 
-def call(body, outs, operands, scratch=(), in_specs=None, flops=0, moved=0):
+def call(body, outs, operands, scratch=(), in_specs=None, mib=12):
     return pl.pallas_call(
         body,
         out_shape=outs,
         in_specs=in_specs or [VMEM] * len(operands),
         out_specs=jax.tree.map(lambda _: VMEM, outs),
         scratch_shapes=list(scratch),
-        compiler_params=pltpu.CompilerParams(vmem_limit_bytes=48 * 1024 * 1024),
-        cost_estimate=pl.CostEstimate(flops=flops, bytes_accessed=moved, transcendentals=0),
+        compiler_params=pltpu.CompilerParams(vmem_limit_bytes=mib * 1024 * 1024),
     )(*operands)
 
 
@@ -32,77 +31,81 @@
     return jnp.concatenate(pieces, axis=1)
 
 
-def incidence_body(hot_dev, slot_cap, count_ref, slots_ref, inc_ref, inc_t_ref):
+def one_hot(ids, shape, axis, start=0):
+    return (lax.broadcasted_iota(i32, shape, axis) + start == ids).astype(f32).astype(bf16)
+
+
+def incidence_body(hot_cols, slot_cap, count_ref, slots_ref, inc_ref, inc_t_ref):
     vocab, batch = inc_t_ref.shape
-    block = hot_dev + slot_cap
-    owners = vocab // block
     field = vocab // FIELDS
     step = 128
     row = lax.broadcasted_iota(i32, (field, step), 0)
     for start in range(0, batch, step):
-        slots = slots_ref[start:start + step, :].T
-        cold = slots - owners * hot_dev
-        hot_column = (slots // hot_dev) * block + slots % hot_dev
-        cold_column = (cold // slot_cap) * block + hot_dev + cold % slot_cap
-        column = jnp.where(cold < 0, hot_column, cold_column)
-        key = jnp.where(slots < 0, -1, column % field)
-        unit = jnp.left_shift(jnp.ones_like(slots), FIELD_BITS * (column // field))
+        slots = slots_ref[:, start:start + step]
+        key = jnp.where(slots < 0, -1, slots % field)
+        unit = jnp.left_shift(jnp.ones_like(slots), FIELD_BITS * (slots // field))
         packed = jnp.zeros((field, step), i32)
         for entry in range(slots.shape[0]):
             packed += jnp.where(row == key[entry:entry + 1, :], unit[entry:entry + 1, :], 0)
         for k in range(FIELDS):
             part = jnp.right_shift(packed, FIELD_BITS * k) & (2**FIELD_BITS - 1)
             inc_t_ref[k * field:(k + 1) * field, start:start + step] = part.astype(f32).astype(bf16)
-    place = lax.broadcasted_iota(i32, (block, batch), 0)
-    for owner in range(owners):
-        rows = pl.ds(owner * block, block)
-        live = place < hot_dev + count_ref[0, owner]
-        inc_t_ref[rows, :] = jnp.where(live, inc_t_ref[rows, :].astype(f32), 0.0).astype(bf16)
+    place = lax.broadcasted_iota(i32, (slot_cap, batch), 0)
+    for owner in range((vocab - hot_cols) // slot_cap):
+        rows = pl.ds(hot_cols + owner * slot_cap, slot_cap)
+        inc_t_ref[rows, :] = jnp.where(place < count_ref[0, owner], inc_t_ref[rows, :].astype(f32), 0.0).astype(bf16)
     inc_ref[...] = inc_t_ref[...].T
 
 
-def serve_body(asked_ref, hot_ref, table_ref, out_ref, pick):
+def serve_hot_body(ids_ref, table_ref, out_ref, table_bf_ref):
+    hot_dev = ids_ref.shape[1]
+    table_bf_ref[...] = table_ref[...].astype(bf16)
+    ids = jnp.broadcast_to(ids_ref[...], (8, hot_dev)).T[:, 0:1]
+    pick = one_hot(ids, (hot_dev, table_ref.shape[0]), 1)
+    picked = jnp.dot(pick, table_bf_ref[...], preferred_element_type=f32).astype(bf16)
+    for t in range(out_ref.shape[0]):
+        out_ref[t] = picked
+
+
+def serve_cold_body(asked_ref, table_ref, out_ref, pick):
     owners, slot_cap = asked_ref.shape
-    hot_dev = hot_ref.shape[1]
-    rows = table_ref.shape[0]
-    hot_column = jnp.broadcast_to(hot_ref[...], (8, hot_dev)).T[:, 0:1]
     asked = asked_ref[...].T
-    pick[0:hot_dev, :] = (lax.broadcasted_iota(i32, (hot_dev, rows), 1) == hot_column).astype(f32).astype(bf16)
-    row = lax.broadcasted_iota(i32, (slot_cap, rows), 1)
-    for t in range(owners):
-        at = hot_dev + t * slot_cap
-        pick[at:at + slot_cap, :] = (row == asked[:, t:t + 1]).astype(f32).astype(bf16)
-    picked = jnp.dot(pick[...], table_ref[...].astype(bf16), preferred_element_type=f32).astype(bf16)
-    for t in range(owners):
-        at = hot_dev + t * slot_cap
-        out_ref[t, 0:hot_dev, :] = picked[0:hot_dev]
-        out_ref[t, hot_dev:, :] = picked[at:at + slot_cap]
-
-
-def top_body(labels_ref, inc_ref, inc_t_ref, rows_ref, w_in_ref, w_out_ref, out_ref, gated, dhidden):
+    for t in range(owners):
+        pick[t * slot_cap:(t + 1) * slot_cap, :] = one_hot(asked[:, t:t + 1], (slot_cap, table_ref.shape[0]), 1)
+    out_ref[...] = jnp.dot(pick[...], table_ref[...], preferred_element_type=f32).astype(bf16)
+
+
+def top_body(labels_ref, inc_ref, inc_t_ref, hot_ref, cold_ref, w_in_ref, w_out_ref, out_ref, gated, dhidden):
     batch = inc_ref.shape[0]
     hidden_units = w_in_ref.shape[1]
+    owners, block, _ = out_ref.shape
+    hot_cols = hot_ref.shape[0]
+    hot_dev = hot_cols // owners
+    slot_cap = block - hot_dev
     step = 512
-    pooled = jnp.dot(inc_ref[...], rows_ref[...], preferred_element_type=f32).astype(bf16)
-    total = jnp.zeros((batch, 128), f32)
+    pooled = jnp.dot(inc_ref[:, 0:hot_cols], hot_ref[...], preferred_element_type=f32)
+    pooled = (pooled + jnp.dot(inc_ref[:, hot_cols:], cold_ref[...], preferred_element_type=f32)).astype(bf16)
+    logit = jnp.zeros((batch, 128), f32)
     for start in range(0, hidden_units, step):
         cols = slice(start, start + step)
         pre_act = jnp.dot(pooled, w_in_ref[:, cols], preferred_element_type=f32)
-        w_out = w_out_ref[:, cols].astype(f32)
-        hidden = jnp.maximum(pre_act, 0.0).astype(bf16).astype(f32)
-        gated[:, cols] = jnp.where(pre_act > 0, w_out, 0.0).astype(bf16)
-        term = hidden * w_out
-        for k in range(0, step, 128):
-            total += term[:, k:k + 128]
-    logit = jnp.sum(total, axis=1, keepdims=True)
+        hidden = jnp.maximum(pre_act, 0.0).astype(bf16)
+        gated[:, cols] = jnp.where(pre_act > 0, w_out_ref[:, cols].astype(f32), 0.0).astype(bf16)
+        w_out = jnp.broadcast_to(w_out_ref[:, cols], (128, step))
+        logit += lax.dot_general(hidden, w_out, (((1,), (1,)), ((), ())), preferred_element_type=f32)
     labels = labels_ref[...].T
     labels = jnp.concatenate([labels[:, k:k + 1] for k in range(labels.shape[1])], axis=0)
     dlogit = jax.nn.sigmoid(logit) - labels
-    dhidden[...] = (dlogit * gated[...].astype(f32)).astype(bf16)
+    for start in range(0, hidden_units, 128):
+        cols = slice(start, start + 128)
+        dhidden[:, cols] = (dlogit * gated[:, cols].astype(f32)).astype(bf16)
     dpooled = lax.dot_general(
         dhidden[...], w_in_ref[...], (((1,), (1,)), ((), ())), preferred_element_type=f32
     ).astype(bf16)
-    out_ref[...] = jnp.dot(inc_t_ref[...], dpooled, preferred_element_type=f32).astype(bf16)
+    grad = jnp.dot(inc_t_ref[...], dpooled, preferred_element_type=f32).astype(bf16)
+    for t in range(owners):
+        out_ref[t, 0:hot_dev, :] = grad[t * hot_dev:(t + 1) * hot_dev]
+        out_ref[t, hot_dev:, :] = grad[hot_cols + t * slot_cap:hot_cols + (t + 1) * slot_cap]
 
 
 def collect_body(asked_ref, back_ref, out_ref):
@@ -190,25 +193,32 @@
     hot_row = hot_ids.reshape(1, hot_dev)
     asked = exchange(cold_ids[0])
     inc, inc_t = call(
-        functools.partial(incidence_body, hot_dev, slot_cap),
+        functools.partial(incidence_body, owners * hot_dev, slot_cap),
         (shape((batch, vocab), bf16), shape((vocab, batch), bf16)),
-        (cold_count, bag_slots),
+        (cold_count, bag_slots.T),
         in_specs=[SMEM, VMEM],
     )
-    served = call(
-        serve_body,
-        shape((owners, block, width), bf16),
-        (asked, hot_row, table),
-        [pltpu.VMEM((hot_dev + owners * slot_cap, rows), bf16)],
-    )
-    fetched = exchange(served)
+    served_hot, table_bf = call(
+        serve_hot_body,
+        (shape((owners, hot_dev, width), bf16), shape((rows, width), bf16)),
+        (hot_row, table),
+    )
+    hot_rows = exchange(served_hot).reshape(-1, width)
+    served_cold = call(
+        serve_cold_body,
+        shape((owners * slot_cap, width), bf16),
+        (asked, table_bf),
+        [pltpu.VMEM((owners * slot_cap, rows), bf16)],
+    )
+    cold_rows = exchange(served_cold.reshape(owners, slot_cap, width)).reshape(-1, width)
     slot_grad = call(
         top_body,
-        shape((vocab, width), bf16),
-        (labels.reshape(-1, 128), inc, inc_t, fetched.reshape(vocab, width), w_in, w_out.reshape(1, -1)),
+        shape((owners, block, width), bf16),
+        (labels.reshape(-1, 128), inc, inc_t, hot_rows, cold_rows, w_in, w_out.reshape(1, -1)),
         [pltpu.VMEM((batch, hidden_units), bf16), pltpu.VMEM((batch, hidden_units), bf16)],
-    )
-    returned = exchange(slot_grad.reshape(owners, block, width))
+        mib=24,
+    )
+    returned = exchange(slot_grad)
     size = hot_dev + owners * slot_cap + TAIL
     if groups & (groups - 1) == 0 and groups * size <= 2 * rows and owners * slot_cap == width:
         part = call(collect_body, shape((size, width), bf16), (asked, returned))

time: 64 us -> 65.6 us (1.025)
  starting transfers between devices: 5.04 us -> 12.4 us
  blocking collectives: 28.5 us -> 21.8 us
  waiting for transfers between devices: 11 us -> 13.4 us
  local copies, waits for them, and re-layouts: 5.97 us -> 3.93 us
    all_to_all x1 -> x2, starting transfers between devices: 3.45 us -> 10.8 us  [exchange(): return lax.all_to_all(x, 'table', split_axis=0, concat_axis=0, tiled=True)]
    all_to_all x2, blocking collectives: 28.5 us -> 21.8 us  [exchange(): return lax.all_to_all(x, 'table', split_axis=0, concat_axis=0, tiled=True)]
    all_to_all x1 -> x2, waiting for transfers between devices: 5.76 us -> 8.1 us  [exchange(): return lax.all_to_all(x, 'table', split_axis=0, concat_axis=0, tiled=True)]
    unnamed x29 -> x24, local copies, waits for them, and re-layouts: 5.96 us -> 3.92 us
    pallas_call x5 -> x6, Pallas kernels: 12.3 us -> 12.9 us  [call(): pl.pallas_call(body, out_shape=outs, in_specs=in_specs or [VMEM] * len(op...]
  transfers between devices with their start and end apart: 4 -> 5, of which waited for: 3 -> 4; matrix products, arithmetic and copies ran while one was open for 0% -> 0% of each run, Pallas kernels for 5% -> 6%
where the time goes in v2:
time: 65.6 us; the launch traced here: 65.1 us
  blocking collectives  21.8 us (33%)
  waiting for transfers between devices  13.4 us (20%)
  Pallas kernels  12.9 us (20%)
  starting transfers between devices  12.4 us (19%)
  local copies, waits for them, and re-layouts  3.93 us (6%)
  between operations  0.74 us (1%)
    all_to_all x2, blocking collectives, exchange(): return lax.all_to_all(x, 'table', split_axis=0, concat_axis=0, tiled=True)  21.8 us
    pallas_call x6, Pallas kernels, call(): pl.pallas_call(body, out_shape=outs, in_specs=in_specs or [VMEM] * len(op...  12.9 us
    all_to_all x2, starting transfers between devices, exchange(): return lax.all_to_all(x, 'table', split_axis=0, concat_axis=0, tiled=True)  10.8 us
    all_to_all x2, waiting for transfers between devices, exchange(): return lax.all_to_all(x, 'table', split_axis=0, concat_axis=0, tiled=True)  8.1 us
    ppermute x3, waiting for transfers between devices, per_device(): lax.ppermute(x, 'dp', swap)  5.29 us
    unnamed x24, local copies, waits for them, and re-layouts  3.92 us
    ppermute x3, starting transfers between devices, per_device(): lax.ppermute(x, 'dp', swap)  1.58 us
  transfers between devices with their start and end apart: 5, of which 4 were waited for; matrix products, arithmetic and copies ran while one was open for 0% of the time, Pallas kernels for 6%

profile of v2, /device:TPU:0, one launch (start us, length us, event | category | flops | bytes accessed | tf_op | source)
XLA Modules:
  0.0 65.1 jit_solution(7235237156078913917)
XLA Ops:
  0.7 7.4 %all-to-all-start = ((s32[8,1,32]{2,1,0:T(1,128)}), s32[8,1,32]{2,1,0:T(1,128)S(1)}, u32[]{:S(2)}, u32[]{:S(2)}) async-start(s32[8,1,32]{2,1,0:T(1,128)} %bitcast.20), calls=%async_computation | async-start | bytes 8192 | tf_op jit(solution)/shard_map/all_to_all | solution.py:178
  8.1 1.2 %copy-done = f32[1024,256]{1,0:T(8,128)S(1)} copy-done((f32[1024,256]{1,0:T(8,128)S(1)}, f32[1024,256]{1,0:T(8,128)}, u32[]{:S(2)}) %copy-start) | copy-done | bytes 1048600
  9.3 0.7 %copy-done.7 = s32[64]{0:T(128)S(1)} copy-done((s32[64]{0:T(128)S(1)}, s32[64]{0:T(128)}, u32[]{:S(2)}) %copy-start.7) | copy-done | bytes 280
  9.9 1.0 %shard_map.105 = (bf16[8,64,256]{2,1,0:T(8,128)(2,1)}, bf16[1024,256]{1,0:T(8,128)(2,1)S(1)}) custom-call(s32[1,64]{1,0:T(1,128)S(1)} %bitcast.17, f32[1024,256]{1,0:T(8,128)S(1)} %copy-done), custom_call_target="tpu_custom_call" | custom-call | tf_op jit(solution)/shard_map/pallas_call | solution.py:20
  11.0 3.5 %all-to-all-done = s32[8,1,32]{2,1,0:T(1,128)S(1)} async-done(((s32[8,1,32]{2,1,0:T(1,128)}), s32[8,1,32]{2,1,0:T(1,128)S(1)}, u32[]{:S(2)}, u32[]{:S(2)}) %all-to-all-start) | async-done | bytes 1056 | tf_op jit(solution)/shard_map/all_to_all | solution.py:178
  14.4 0.4 shard_map.106
  14.9 9.7 %all_to_all.26 = bf16[8,32,256]{2,1,0:T(8,128)(2,1)S(1)} all-to-all(bf16[8,32,256]{2,1,0:T(8,128)(2,1)S(1)} %bitcast.12), channel_id=1, replica_groups=mesh['dp'=4,'table'=8] {'table'}, dimensions={0} | all-to-all | bytes 262144 | tf_op jit(solution)/shard_map/all_to_all | solution.py:178
  24.6 3.4 %all-to-all-start.1 = ((bf16[8,64,256]{2,1,0:T(8,128)(2,1)}), bf16[8,64,256]{2,1,0:T(8,128)(2,1)S(1)}, u32[]{:S(2)}, u32[]{:S(2)}) async-start(bf16[8,64,256]{2,1,0:T(8,128)(2,1)} %get-tuple-element.10), calls=%async_computation.1 | async-start | bytes 524288 | tf_op jit(solution)/shard_map/all_to_all | solution.py:178
  28.1 2.6 %shard_map.104 = (bf16[512,768]{1,0:T(8,128)(2,1)S(1)}, bf16[768,512]{1,0:T(8,128)(2,1)S(1)}) custom-call(s32[1,8]{1,0:T(1,128)S(1)} %copy-done.10, s32[32,512]{1,0:T(8,128)S(1)} %bitcast.13), custom_call_target="tpu_custom_call" | custom-call | tf_op jit(solution)/shard_map/pallas_call | solution.py:20
  30.7 0.0 copy-start.3
  30.7 0.9 %copy-done.3 = bf16[768,512]{1,0:T(8,128)(2,1)} copy-done((bf16[768,512]{1,0:T(8,128)(2,1)}, bf16[768,512]{1,0:T(8,128)(2,1)S(1)}, u32[]{:S(2)}) %copy-start.3) | copy-done | bytes 786456
  31.6 4.6 %all-to-all-done.1 = bf16[8,64,256]{2,1,0:T(8,128)(2,1)S(1)} async-done(((bf16[8,64,256]{2,1,0:T(8,128)(2,1)}), bf16[8,64,256]{2,1,0:T(8,128)(2,1)S(1)}, u32[]{:S(2)}, u32[]{:S(2)}) %all-to-all-start.1) | async-done | bytes 262176 | tf_op jit(solution)/shard_map/all_to_all | solution.py:178
  36.2 0.0 copy-done.9
  36.2 1.1 %copy-done.4 = bf16[768,512]{1,0:T(8,128)(2,1)S(1)} copy-done((bf16[768,512]{1,0:T(8,128)(2,1)S(1)}, bf16[768,512]{1,0:T(8,128)(2,1)}, u32[]{:S(2)}) %copy-start.4) | copy-done | bytes 786456
  37.4 6.4 %shard_map.107 = bf16[8,96,256]{2,1,0:T(8,128)(2,1)S(1)} custom-call(f32[4,128]{1,0:T(4,128)S(1)} %bitcast.19, bf16[512,768]{1,0:T(8,128)(2,1)S(1)} %get-tuple-element.8.inc_ref, bf16[768,512]{1,0:T(8,128)(2,1)S(1)} %copy-done.4, bf16[512,256]{1,0:T(8,128)(2,1)S(1)} %bitcast.10, bf16[256,256]{1,0:T(8,128)(2,1)S(1)} %bitcast.11, ...), custom_call_target="tpu_custom_call" | custom-call | tf_op jit(solution)/shard_map/pallas_call | solution.py:20
  43.8 12.1 %all_to_all.27.back_ref = bf16[8,96,256]{2,1,0:T(8,128)(2,1)S(1)} all-to-all(bf16[8,96,256]{2,1,0:T(8,128)(2,1)S(1)} %shard_map.107), channel_id=1, replica_groups=mesh['dp'=4,'table'=8] {'table'}, dimensions={0} | all-to-all | bytes 786432 | tf_op jit(solution)/shard_map/all_to_all | solution.py:178
  55.9 0.1 shard_map.108.refs_0_
  55.9 1.6 %collective-permute-start.1 = (bf16[336,256]{1,0:T(8,128)(2,1)S(1)}, bf16[336,256]{1,0:T(8,128)(2,1)S(1)}, u32[]{:S(2)}, u32[]{:S(2)}) collective-permute-start(bf16[336,256]{1,0:T(8,128)(2,1)S(1)} %shard_map.108.refs_0_), channel_id=1, source_target_pairs={{0,16},{8,24},{16,0},{24,8},{1,17},{9,25},{17,1},{25,9},{2,18},{10... | collective-permute-start | bytes 516104 | tf_op jit(solution)/shard_map/ppermute | solution.py:229
  57.5 0.0 collective-permute-start
  57.5 3.9 %collective-permute-done.1.refs_2_ = bf16[336,256]{1,0:T(8,128)(2,1)S(1)} collective-permute-done((bf16[336,256]{1,0:T(8,128)(2,1)S(1)}, bf16[336,256]{1,0:T(8,128)(2,1)S(1)}, u32[]{:S(2)}, u32[]{:S(2)}) %collective-permute-start.1) | collective-permute-done | bytes 172064 | tf_op jit(solution)/shard_map/ppermute | solution.py:229
  61.4 0.0 collective-permute-start.2
  61.4 0.0 collective-permute-done.refs_1_
  61.4 1.4 %collective-permute-done.2.refs_3_ = bf16[336,256]{1,0:T(8,128)(2,1)S(1)} collective-permute-done((bf16[336,256]{1,0:T(8,128)(2,1)S(1)}, bf16[336,256]{1,0:T(8,128)(2,1)S(1)}, u32[]{:S(2)}, u32[]{:S(2)}) %collective-permute-start.2) | collective-permute-done | bytes 172064 | tf_op jit(solution)/shard_map/ppermute | solution.py:229
  62.8 2.3 %shard_map.109 = (f32[1024,256]{1,0:T(8,128)}, f32[8,128]{1,0:T(8,128)}) custom-call(s32[1,64]{1,0:T(1,128)S(1)} %bitcast.18, f32[8,128]{1,0:T(8,128)S(1)} %bitcast.16, f32[1024,256]{1,0:T(8,128)S(1)} %copy-done.1, bf16[336,256]{1,0:T(8,128)(2,1)S(1)} %shard_map.108.refs_0_, bf16[336,256]{1,0:T(8,128)(2,1)S(1)} %collective-permute-done.refs_1_, ...), custom_call_target="tpu_custom_call" | custom-call | tf_op jit(solution)/shard_map/pallas_call | solution.py:20
  (19 shorter events, 0.0 us)
Async XLA Ops:
  0.6 27.4 %copy-start.11 = (bf16[4096]{0:T(1024)(128)(2,1)S(1)}, bf16[4096]{0:T(1024)(128)(2,1)}, u32[]{:S(2)}) copy-start(bf16[4096]{0:T(1024)(128)(2,1)} %param.17) | copy-start | bytes 24580
  0.6 27.4 %copy-start.10 = (s32[1,8]{1,0:T(1,128)S(1)}, s32[1,8]{1,0:T(1,128)}, u32[]{:S(2)}) copy-start(s32[1,8]{1,0:T(1,128)} %count_ref.1) | copy-start | bytes 100
  0.7 35.6 %copy-start.9 = (f32[512]{0:T(512)S(1)}, f32[512]{0:T(512)}, u32[]{:S(2)}) copy-start(f32[512]{0:T(512)} %param.10) | copy-start | bytes 6148
  0.7 13.8 %all-to-all-start = ((s32[8,1,32]{2,1,0:T(1,128)}), s32[8,1,32]{2,1,0:T(1,128)S(1)}, u32[]{:S(2)}, u32[]{:S(2)}) async-start(s32[8,1,32]{2,1,0:T(1,128)} %bitcast.20), calls=%async_computation | async-start | bytes 8192 | tf_op jit(solution)/shard_map/all_to_all | solution.py:178
  8.1 1.2 %copy-start = (f32[1024,256]{1,0:T(8,128)S(1)}, f32[1024,256]{1,0:T(8,128)}, u32[]{:S(2)}) copy-start(f32[1024,256]{1,0:T(8,128)} %table_ref.3) | copy-start | bytes 3145732
  9.3 0.7 %copy-start.7 = (s32[64]{0:T(128)S(1)}, s32[64]{0:T(128)}, u32[]{:S(2)}) copy-start(s32[64]{0:T(128)} %param.15) | copy-start | bytes 772
  9.9 18.1 %copy-start.5 = (s32[512,32]{0,1:T(8,128)S(1)}, s32[512,32]{0,1:T(8,128)}, u32[]{:S(2)}) copy-start(s32[512,32]{0,1:T(8,128)} %param.9) | copy-start | bytes 196612
  9.9 26.3 %copy-start.2 = (bf16[256,4096]{1,0:T(8,128)(2,1)S(1)}, bf16[256,4096]{1,0:T(8,128)(2,1)}, u32[]{:S(2)}) copy-start(bf16[256,4096]{1,0:T(8,128)(2,1)} %w_in_ref.1) | copy-start | bytes 6291460
  24.6 11.6 %all-to-all-start.1 = ((bf16[8,64,256]{2,1,0:T(8,128)(2,1)}), bf16[8,64,256]{2,1,0:T(8,128)(2,1)S(1)}, u32[]{:S(2)}, u32[]{:S(2)}) async-start(bf16[8,64,256]{2,1,0:T(8,128)(2,1)} %get-tuple-element.10), calls=%async_computation.1 | async-start | bytes 524288 | tf_op jit(solution)/shard_map/all_to_all | solution.py:178
  30.7 0.9 %copy-start.3 = (bf16[768,512]{1,0:T(8,128)(2,1)}, bf16[768,512]{1,0:T(8,128)(2,1)S(1)}, u32[]{:S(2)}) copy-start(bf16[768,512]{1,0:T(8,128)(2,1)S(1)} %get-tuple-element.9.inc_t_ref) | copy-start | bytes 2359300
  36.2 1.1 %copy-start.4 = (bf16[768,512]{1,0:T(8,128)(2,1)S(1)}, bf16[768,512]{1,0:T(8,128)(2,1)}, u32[]{:S(2)}) copy-start(bf16[768,512]{1,0:T(8,128)(2,1)} %copy-done.3) | copy-start | bytes 2359300
  37.3 25.5 %copy-start.1 = (f32[1024,256]{1,0:T(8,128)S(1)}, f32[1024,256]{1,0:T(8,128)}, u32[]{:S(2)}) copy-start(f32[1024,256]{1,0:T(8,128)} %table_ref.3) | copy-start | bytes 3145732
  37.3 25.5 %copy-start.6 = (f32[1024]{0:T(1024)S(1)}, f32[1024]{0:T(1024)}, u32[]{:S(2)}) copy-start(f32[1024]{0:T(1024)} %param.14) | copy-start | bytes 12292
  37.4 25.5 %copy-start.8 = (s32[64]{0:T(128)S(1)}, s32[64]{0:T(128)}, u32[]{:S(2)}) copy-start(s32[64]{0:T(128)} %param.15) | copy-start | bytes 772
  55.9 5.5 %collective-permute-start.1 = (bf16[336,256]{1,0:T(8,128)(2,1)S(1)}, bf16[336,256]{1,0:T(8,128)(2,1)S(1)}, u32[]{:S(2)}, u32[]{:S(2)}) collective-permute-start(bf16[336,256]{1,0:T(8,128)(2,1)S(1)} %shard_map.108.refs_0_), channel_id=1, source_target_pairs={{0,16},{8,24},{16,0},{24,8},{1,17},{9,25},{17,1},{25,9},{2,18},{10... | collective-permute-start | bytes 516104 | tf_op jit(solution)/shard_map/ppermute | solution.py:229
  57.5 3.9 %collective-permute-start = (bf16[336,256]{1,0:T(8,128)(2,1)S(1)}, bf16[336,256]{1,0:T(8,128)(2,1)S(1)}, u32[]{:S(2)}, u32[]{:S(2)}) collective-permute-start(bf16[336,256]{1,0:T(8,128)(2,1)S(1)} %shard_map.108.refs_0_), channel_id=1, source_target_pairs={{0,8},{8,0},{16,24},{24,16},{1,9},{9,1},{17,25},{25,17},{2,10},{10... | collective-permute-start | bytes 516104 | tf_op jit(solution)/shard_map/ppermute | solution.py:229
  61.4 1.4 %collective-permute-start.2 = (bf16[336,256]{1,0:T(8,128)(2,1)S(1)}, bf16[336,256]{1,0:T(8,128)(2,1)S(1)}, u32[]{:S(2)}, u32[]{:S(2)}) collective-permute-start(bf16[336,256]{1,0:T(8,128)(2,1)S(1)} %collective-permute-done.1.refs_2_), channel_id=1, source_target_pairs={{0,8},{8,0},{16,24},{24,16},{1,9},{9,1},{17,25},{25,17},{2,10},{10... | collective-permute-start | bytes 516104 | tf_op jit(solution)/shard_map/ppermute | solution.py:229

commit v3 on v2

v3 whole, which is shorter than its diff:
```python
import functools

import jax
import jax.numpy as jnp
from jax import lax
from jax.experimental import pallas as pl
from jax.experimental.pallas import tpu as pltpu
from jax.sharding import PartitionSpec as P

learning_rate = 0.3
f32, bf16, i32 = jnp.float32, jnp.bfloat16, jnp.int32
VMEM = pl.BlockSpec(memory_space=pltpu.VMEM)
SMEM = pl.BlockSpec(memory_space=pltpu.SMEM)
FIELDS = 4
FIELD_BITS = 8
TAIL = 16


def call(body, outs, operands, scratch=(), in_specs=None, mib=12):
    return pl.pallas_call(
        body,
        out_shape=outs,
        in_specs=in_specs or [VMEM] * len(operands),
        out_specs=jax.tree.map(lambda _: VMEM, outs),
        scratch_shapes=list(scratch),
        compiler_params=pltpu.CompilerParams(vmem_limit_bytes=mib * 1024 * 1024),
    )(*operands)


def lanes(pieces):
    return jnp.concatenate(pieces, axis=1)


def one_hot(ids, shape, axis, start=0):
    return (lax.broadcasted_iota(i32, shape, axis) + start == ids).astype(f32).astype(bf16)


def incidence_body(hot_cols, slot_cap, count_ref, slots_ref, inc_ref, inc_t_ref):
    vocab, batch = inc_t_ref.shape
    field = vocab // FIELDS
    step = 128
    row = lax.broadcasted_iota(i32, (field, step), 0)
    for start in range(0, batch, step):
        slots = slots_ref[:, start:start + step]
        key = jnp.where(slots < 0, -1, slots % field)
        unit = jnp.left_shift(jnp.ones_like(slots), FIELD_BITS * (slots // field))
        packed = jnp.zeros((field, step), i32)
        for entry in range(slots.shape[0]):
            packed += jnp.where(row == key[entry:entry + 1, :], unit[entry:entry + 1, :], 0)
        for k in range(FIELDS):
            part = jnp.right_shift(packed, FIELD_BITS * k) & (2**FIELD_BITS - 1)
            inc_t_ref[k * field:(k + 1) * field, start:start + step] = part.astype(f32).astype(bf16)
    place = lax.broadcasted_iota(i32, (slot_cap, batch), 0)
    for owner in range((vocab - hot_cols) // slot_cap):
        rows = pl.ds(hot_cols + owner * slot_cap, slot_cap)
        inc_t_ref[rows, :] = jnp.where(place < count_ref[0, owner], inc_t_ref[rows, :].astype(f32), 0.0).astype(bf16)
    inc_ref[...] = inc_t_ref[...].T


def core():
    return lax.rem(lax.axis_index("dp"), 2)


def half_rows(owner, hot_dev, which):
    half = hot_dev // 2
    return pl.ds(pl.multiple_of(owner * hot_dev + which * half, half), half)


def pick_hot_body(ids_ref, table_ref, hot_ref, table_bf_ref):
    hot_dev = ids_ref.shape[1]
    table_bf_ref[...] = table_ref[...].astype(bf16)
    ids = jnp.broadcast_to(ids_ref[...], (8, hot_dev)).T[:, 0:1]
    pick = one_hot(ids, (hot_dev, table_ref.shape[0]), 1)
    hot_ref[...] = jnp.dot(pick, table_bf_ref[...], preferred_element_type=f32).astype(bf16)


def serve_body(asked_ref, hot_ref, table_ref, out_ref, pick):
    owners, slot_cap = asked_ref.shape
    hot_dev = hot_ref.shape[0]
    asked = asked_ref[...].T
    for t in range(owners):
        pick[t * slot_cap:(t + 1) * slot_cap, :] = one_hot(asked[:, t:t + 1], (slot_cap, table_ref.shape[0]), 1)
    picked = jnp.dot(pick[...], table_ref[...], preferred_element_type=f32).astype(bf16)
    hot = hot_ref[half_rows(0, hot_dev, core()), :]
    for t in range(owners):
        out_ref[t, 0:hot_dev // 2, :] = hot
        out_ref[t, hot_dev // 2:, :] = picked[t * slot_cap:(t + 1) * slot_cap]


def first_rows_body(rows_ref, out_ref):
    out_ref[...] = rows_ref[:, 0:out_ref.shape[1], :]


def top_body(labels_ref, inc_ref, inc_t_ref, own_ref, mate_ref, w_in_ref, w_out_ref, part_ref, send_ref, gated, rows):
    batch = inc_ref.shape[0]
    hidden_units, width = w_in_ref.shape[1], w_in_ref.shape[0]
    owners, half, _ = send_ref.shape
    hot_dev = 2 * half
    hot_cols = owners * hot_dev
    slot_cap = part_ref.shape[1] - half
    me = core()
    for t in range(owners):
        rows[half_rows(t, hot_dev, me), :] = own_ref[t, 0:half, :]
        rows[half_rows(t, hot_dev, 1 - me), :] = mate_ref[t, 0:half, :]
        rows[hot_cols + t * slot_cap:hot_cols + (t + 1) * slot_cap, :] = own_ref[t, half:, :]
    labels = labels_ref[...].T
    labels = jnp.concatenate([labels[:, k:k + 1] for k in range(labels.shape[1])], axis=0)
    pooled = jnp.dot(inc_ref[...], rows[...], preferred_element_type=f32).astype(bf16)
    size, step, wide = batch // 2, 512, 2048
    dpooled = []
    for at in range(0, batch, size):
        samples = slice(at, at + size)
        total = jnp.zeros((size, 128), f32)
        for start in range(0, hidden_units, step):
            cols = slice(start, start + step)
            pre_act = jnp.dot(pooled[samples], w_in_ref[:, cols], preferred_element_type=f32)
            w_out = w_out_ref[:, cols].astype(f32)
            gated[samples, cols] = jnp.where(pre_act > 0, w_out, 0.0).astype(bf16)
            term = jnp.maximum(pre_act, 0.0).astype(bf16).astype(f32) * w_out
            for k in range(0, step, 128):
                total += term[:, k:k + 128]
        logit = jnp.sum(total, axis=1, keepdims=True)
        dlogit = jnp.broadcast_to(jax.nn.sigmoid(logit) - labels[samples], (size, 128))
        grad = jnp.zeros((size, width), f32)
        for start in range(0, hidden_units, wide):
            dhidden = lanes([
                (dlogit * gated[samples, k:k + 128].astype(f32)).astype(bf16) for k in range(start, start + wide, 128)
            ])
            grad += lax.dot_general(
                dhidden, w_in_ref[:, start:start + wide], (((1,), (1,)), ((), ())), preferred_element_type=f32
            )
        dpooled.append(grad.astype(bf16))
    dpooled = jnp.concatenate(dpooled, axis=0)
    rows[...] = jnp.dot(inc_t_ref[...], dpooled, preferred_element_type=f32).astype(bf16)
    for t in range(owners):
        send_ref[t] = rows[half_rows(t, hot_dev, 1 - me), :]
        part_ref[t, 0:half, :] = rows[half_rows(t, hot_dev, me), :]
        part_ref[t, half:, :] = rows[hot_cols + t * slot_cap:hot_cols + (t + 1) * slot_cap, :]


def add_hot_body(part_ref, got_ref, out_ref):
    half = got_ref.shape[1]
    out_ref[:, 0:half, :] = (part_ref[:, 0:half, :].astype(f32) + got_ref[...].astype(f32)).astype(bf16)
    out_ref[:, half:, :] = part_ref[:, half:, :]


def collect_body(asked_ref, back_ref, out_ref):
    owners, slot_cap = asked_ref.shape
    half = back_ref.shape[1] - slot_cap
    out_ref[0:half, :] = jnp.sum(back_ref[:, 0:half, :].astype(f32), axis=0).astype(bf16)
    for t in range(owners):
        out_ref[half + t * slot_cap:half + (t + 1) * slot_cap, :] = back_ref[t, half:, :]
    asked = lanes([asked_ref[t:t + 1, :] for t in range(owners)])
    digit = lax.broadcasted_iota(i32, (TAIL, asked.shape[1]), 0)
    digits = jnp.where(digit == 0, asked >> 8, jnp.where(digit == 1, asked & 255, 0))
    out_ref[half + owners * slot_cap:, :] = digits.astype(f32).astype(bf16)


def hot_half(hot_ref, which):
    half = hot_ref.shape[1] // 2
    return jnp.where(which == 0, hot_ref[:, 0:half], hot_ref[:, half:])


def row_grads(which, hot_ref, part_refs, held, put, rows):
    size = part_refs[0].shape[0]
    half = hot_ref.shape[1] // 2
    me = lax.div(lax.axis_index("dp"), 2)
    count = len(part_refs)
    for s in range(count):
        held[pl.ds(pl.multiple_of((me ^ s) * size, 16), size), :] = part_refs[s][...]
    hot = jnp.concatenate([held[g * size:g * size + half, :] for g in range(count)], axis=0)
    ids = [lanes([hot_half(hot_ref, which)] * count)]
    parts = [hot]
    for g in range(count):
        digits = held[(g + 1) * size - TAIL:(g + 1) * size, :].astype(f32).astype(i32)
        ids.append(digits[0:1, :] * 256 + digits[1:2, :])
        parts.append(held[g * size + half:(g + 1) * size - TAIL, :])
    step = 128
    for start in range(0, rows, step):
        grad = 0.0
        for k in range(len(ids)):
            pick = one_hot(ids[k], (step, ids[k].shape[1]), 0, start)
            grad += jnp.dot(pick, parts[k], preferred_element_type=f32)
        put(slice(start, start + step), grad)


def own_grad_body(hot_ref, *refs):
    part_refs, (out_ref, held) = refs[:-2], refs[-2:]

    def put(at, grad):
        out_ref[at, :] = grad

    row_grads(core(), hot_ref, part_refs, held, put, out_ref.shape[0])


def adagrad(table, own_sum, grad):
    new_sum = own_sum + jnp.sum(grad * grad, axis=1, keepdims=True) * (1.0 / grad.shape[1])
    return table - grad * (learning_rate / jnp.sqrt(new_sum)), new_sum


def update_body(hot_ref, sum_ref, table_ref, grad_ref, *refs):
    part_refs, (new_table_ref, new_sum_ref, held, sums) = refs[:-4], refs[-4:]
    own_sum = sum_ref[...].T

    def put(at, grad):
        k = at.start // 128
        new_table_ref[at, :], sums[:, k:k + 1] = adagrad(
            table_ref[at, :], own_sum[:, k:k + 1], grad_ref[at, :] + grad
        )

    row_grads(1 - core(), hot_ref, part_refs, held, put, table_ref.shape[0])
    new_sum_ref[...] = sums[...].T


def dense_body(hot_ref, asked_ref, back_ref, out_ref):
    owners, slot_cap = asked_ref.shape
    half = back_ref.shape[1] - slot_cap
    rows = out_ref.shape[0]
    hot = jnp.sum(back_ref[:, 0:half, :].astype(f32), axis=0).astype(bf16)
    grad = jnp.dot(one_hot(hot_half(hot_ref, core()), (rows, half), 0), hot, preferred_element_type=f32)
    for t in range(owners):
        pick = one_hot(asked_ref[t:t + 1, :], (rows, slot_cap), 0)
        grad += jnp.dot(pick, back_ref[t, half:, :], preferred_element_type=f32)
    out_ref[...] = grad.astype(bf16)


def exchange(x):
    return lax.all_to_all(x, "table", split_axis=0, concat_axis=0, tiled=True)


def swap(x, bit):
    return lax.ppermute(x, "dp", [(g, g ^ bit) for g in range(lax.axis_size("dp"))])


def per_device(bag_slots, labels, cold_ids, cold_count, table, adagrad_sum, hot_ids, w_in, w_out):
    owners = lax.axis_size("table")
    groups = lax.axis_size("dp")
    hot_dev = hot_ids.shape[0]
    slot_cap = cold_ids.shape[2]
    batch = bag_slots.shape[0]
    rows, width = table.shape
    hidden_units = w_in.shape[1]
    half = hot_dev // 2
    vocab = owners * (hot_dev + slot_cap)
    shape = jax.ShapeDtypeStruct

    hot_row = hot_ids.reshape(1, hot_dev)
    asked = exchange(cold_ids[0])
    inc, inc_t = call(
        functools.partial(incidence_body, owners * hot_dev, slot_cap),
        (shape((batch, vocab), bf16), shape((vocab, batch), bf16)),
        (cold_count, bag_slots.T),
        in_specs=[SMEM, VMEM],
    )
    hot, table_bf = call(pick_hot_body, (shape((hot_dev, width), bf16), shape((rows, width), bf16)), (hot_row, table))
    served = call(
        serve_body,
        shape((owners, half + slot_cap, width), bf16),
        (asked, hot, table_bf),
        [pltpu.VMEM((owners * slot_cap, rows), bf16)],
    )
    own_rows, inc, inc_t = lax.optimization_barrier((exchange(served), inc, inc_t))
    mate_rows = swap(call(first_rows_body, shape((owners, half, width), bf16), (own_rows,)), 1)
    part, to_mate = call(
        top_body,
        (shape((owners, half + slot_cap, width), bf16), shape((owners, half, width), bf16)),
        (labels.reshape(-1, 128), inc, inc_t, own_rows, mate_rows, w_in, w_out.reshape(1, -1)),
        [pltpu.VMEM((batch, hidden_units), bf16), pltpu.VMEM((vocab, width), bf16)],
        mib=24,
    )
    summed = call(add_hot_body, shape(part.shape, bf16), (part, swap(to_mate, 1)))
    returned = exchange(summed)
    size = half + owners * slot_cap + TAIL
    if groups & (groups - 1) == 0 and groups * size <= 2 * rows and owners * slot_cap == width:
        parts = {0: call(collect_body, shape((size, width), bf16), (asked, returned))}
        bit = groups // 2
        while bit > 1:
            parts.update({s ^ bit: swap(x, bit) for s, x in list(parts.items())})
            bit //= 2
        near = [parts[2 * y] for y in range(groups // 2)]
        far = [swap(x, 1) for x in near]
        held = pltpu.VMEM((groups // 2 * size, width), bf16)
        grad = call(own_grad_body, shape((rows, width), f32), (hot_row, *near), [held])
        new_table, new_sum = call(
            update_body,
            (shape((rows, width), f32), shape((rows // 128, 128), f32)),
            (hot_row, adagrad_sum.reshape(-1, 128), table, grad, *far),
            [held, pltpu.VMEM((128, rows // 128), f32)],
        )
        return new_table, new_sum.reshape(rows)
    grad = call(dense_body, shape((rows, width), bf16), (hot_row, asked, returned))
    grad = lax.psum(grad, "dp").astype(f32)
    new_table, new_sum = adagrad(table, adagrad_sum[:, None], grad)
    return new_table, new_sum[:, 0]


def solution(mesh):
    placed = (
        P(("dp", "table"), None),
        P(("dp", "table")),
        P(("dp", "table"), None, None),
        P(("dp", "table"), None),
        P("table", None),
        P("table"),
        P("table"),
        P(),
        P(),
    )
    return jax.shard_map(
        per_device,
        mesh=mesh,
        in_specs=placed,
        out_specs=(P("table", None), P("table")),
        check_vma=False,
    )
```

time: 65.6 us -> 57.6 us (0.88)
  blocking collectives: 21.8 us -> 12.1 us
  waiting for transfers between devices: 13.4 us -> 15.7 us
  Pallas kernels: 12.9 us -> 11.9 us
    all_to_all x2 -> x1, blocking collectives: 21.8 us -> 12.1 us  [exchange(): return lax.all_to_all(x, 'table', split_axis=0, concat_axis=0, tiled=True)]
    ppermute x3 -> x5, waiting for transfers between devices: 5.29 us -> 6.91 us  [swap(): lax.ppermute(x, 'dp', [(g, g ^ bit) for g in range(lax.axis_size('dp'))])]
    pallas_call x6 -> x9, Pallas kernels: 12.9 us -> 11.9 us  [call(): pl.pallas_call(body, out_shape=outs, in_specs=in_specs or [VMEM] * len(op...]
    all_to_all x2, waiting for transfers between devices: 8.1 us -> 8.83 us  [exchange(): return lax.all_to_all(x, 'table', split_axis=0, concat_axis=0, tiled=True)]
    ppermute x3 -> x5, starting transfers between devices: 1.58 us -> 1.86 us  [swap(): lax.ppermute(x, 'dp', [(g, g ^ bit) for g in range(lax.axis_size('dp'))])]
  transfers between devices with their start and end apart: 5 -> 7, of which waited for: 4 -> 6; matrix products, arithmetic and copies ran while one was open for 0% -> 0% of each run, Pallas kernels for 6% -> 6%
where the time goes in v3:
time: 57.6 us; the launch traced here: 57.2 us
  waiting for transfers between devices  15.7 us (27%)
  starting transfers between devices  12.7 us (22%)
  blocking collectives  12.1 us (21%)
  Pallas kernels  11.9 us (21%)
  local copies, waits for them, and re-layouts  3.93 us (7%)
  between operations  0.78 us (1%)
    all_to_all x1, blocking collectives, exchange(): return lax.all_to_all(x, 'table', split_axis=0, concat_axis=0, tiled=True)  12.1 us
    pallas_call x9, Pallas kernels, call(): pl.pallas_call(body, out_shape=outs, in_specs=in_specs or [VMEM] * len(op...  11.9 us
    all_to_all x2, starting transfers between devices, exchange(): return lax.all_to_all(x, 'table', split_axis=0, concat_axis=0, tiled=True)  10.8 us
    all_to_all x2, waiting for transfers between devices, exchange(): return lax.all_to_all(x, 'table', split_axis=0, concat_axis=0, tiled=True)  8.83 us
    ppermute x5, waiting for transfers between devices, swap(): lax.ppermute(x, 'dp', [(g, g ^ bit) for g in range(lax.axis_size('dp'))])  6.91 us
    unnamed x24, local copies, waits for them, and re-layouts  3.92 us
    ppermute x5, starting transfers between devices, swap(): lax.ppermute(x, 'dp', [(g, g ^ bit) for g in range(lax.axis_size('dp'))])  1.86 us
  transfers between devices with their start and end apart: 7, of which 6 were waited for; matrix products, arithmetic and copies ran while one was open for 0% of the time, Pallas kernels for 6%

profile of v3, /device:TPU:0, one launch (start us, length us, event | category | flops | bytes accessed | tf_op | source)
XLA Modules:
  0.0 57.2 jit_solution(580072612762562518)
XLA Ops:
  0.7 7.4 %all-to-all-start = ((s32[8,1,32]{2,1,0:T(1,128)}), s32[8,1,32]{2,1,0:T(1,128)S(1)}, u32[]{:S(2)}, u32[]{:S(2)}) async-start(s32[8,1,32]{2,1,0:T(1,128)} %bitcast.15), calls=%async_computation | async-start | bytes 8192 | tf_op jit(solution)/shard_map/all_to_all | solution.py:228
  8.1 1.2 %copy-done = f32[1024,256]{1,0:T(8,128)S(1)} copy-done((f32[1024,256]{1,0:T(8,128)S(1)}, f32[1024,256]{1,0:T(8,128)}, u32[]{:S(2)}) %copy-start) | copy-done | bytes 1048600
  9.3 0.7 %copy-done.6 = s32[64]{0:T(128)S(1)} copy-done((s32[64]{0:T(128)S(1)}, s32[64]{0:T(128)}, u32[]{:S(2)}) %copy-start.6) | copy-done | bytes 280
  9.9 0.3 shard_map.104
  10.3 4.2 %all-to-all-done = s32[8,1,32]{2,1,0:T(1,128)S(1)} async-done(((s32[8,1,32]{2,1,0:T(1,128)}), s32[8,1,32]{2,1,0:T(1,128)S(1)}, u32[]{:S(2)}, u32[]{:S(2)}) %all-to-all-start) | async-done | bytes 1056 | tf_op jit(solution)/shard_map/all_to_all | solution.py:228
  14.4 1.2 %shard_map.105 = bf16[8,64,256]{2,1,0:T(8,128)(2,1)} custom-call(s32[8,32]{1,0:T(8,128)S(1)} %bitcast.8, bf16[64,256]{1,0:T(8,128)(2,1)S(1)} %get-tuple-element.13.hot_ref, bf16[1024,256]{1,0:T(8,128)(2,1)S(1)} %get-tuple-element.14.table_ref), custom_call_target="tpu_custom_call" | custom-call | tf_op jit(solution)/shard_map/pallas_call | solution.py:20
  15.6 3.4 %all-to-all-start.1 = ((bf16[8,64,256]{2,1,0:T(8,128)(2,1)}), bf16[8,64,256]{2,1,0:T(8,128)(2,1)S(1)}, u32[]{:S(2)}, u32[]{:S(2)}) async-start(bf16[8,64,256]{2,1,0:T(8,128)(2,1)} %shard_map.105), calls=%async_computation.1 | async-start | bytes 524288 | tf_op jit(solution)/shard_map/all_to_all | solution.py:228
  19.0 2.6 %shard_map.106 = (bf16[512,768]{1,0:T(8,128)(2,1)S(1)}, bf16[768,512]{1,0:T(8,128)(2,1)S(1)}) custom-call(s32[1,8]{1,0:T(1,128)S(1)} %copy-done.10, s32[32,512]{1,0:T(8,128)S(1)} %bitcast.7), custom_call_target="tpu_custom_call" | custom-call | tf_op jit(solution)/shard_map/pallas_call | solution.py:20
  21.7 0.9 %copy-done.3 = bf16[768,512]{1,0:T(8,128)(2,1)} copy-done((bf16[768,512]{1,0:T(8,128)(2,1)}, bf16[768,512]{1,0:T(8,128)(2,1)S(1)}, u32[]{:S(2)}) %copy-start.3) | copy-done | bytes 786456
  22.5 4.6 %all-to-all-done.1.rows_ref.own_ref = bf16[8,64,256]{2,1,0:T(8,128)(2,1)S(1)} async-done(((bf16[8,64,256]{2,1,0:T(8,128)(2,1)}), bf16[8,64,256]{2,1,0:T(8,128)(2,1)S(1)}, u32[]{:S(2)}, u32[]{:S(2)}) %all-to-all-start.1) | async-done | bytes 262176 | tf_op jit(solution)/shard_map/all_to_all | solution.py:228
  27.2 0.1 collective-permute-start
  27.3 1.3 %collective-permute-done.mate_ref = bf16[8,32,256]{2,1,0:T(8,128)(2,1)S(1)} collective-permute-done((bf16[8,32,256]{2,1,0:T(8,128)(2,1)S(1)}, bf16[8,32,256]{2,1,0:T(8,128)(2,1)S(1)}, u32[]{:S(2)}, u32[]{:S(2)}) %collective-permute-start) | collective-permute-done | bytes 131104 | tf_op jit(solution)/shard_map/ppermute | solution.py:232
  28.6 1.1 %copy-done.4 = bf16[768,512]{1,0:T(8,128)(2,1)S(1)} copy-done((bf16[768,512]{1,0:T(8,128)(2,1)S(1)}, bf16[768,512]{1,0:T(8,128)(2,1)}, u32[]{:S(2)}) %copy-start.4) | copy-done | bytes 786456
  29.8 4.8 %shard_map.108 = (bf16[8,64,256]{2,1,0:T(8,128)(2,1)S(1)}, bf16[8,32,256]{2,1,0:T(8,128)(2,1)S(1)}) custom-call(f32[4,128]{1,0:T(4,128)S(1)} %bitcast.14, bf16[512,768]{1,0:T(8,128)(2,1)S(1)} %get-tuple-element.17.inc_ref, bf16[768,512]{1,0:T(8,128)(2,1)S(1)} %copy-done.4, bf16[8,64,256]{2,1,0:T(8,128)(2,1)S(1)} %all-to-all-done.1.rows_ref.own_ref, ...), custom_call_target="tpu_custom_call" | custom-call | tf_op jit(solution)/shard_map/pallas_call | solution.py:20
  34.5 0.0 copy-start.1
  34.6 0.2 collective-permute-start.1
  34.8 1.2 %collective-permute-done.1.got_ref = bf16[8,32,256]{2,1,0:T(8,128)(2,1)S(1)} collective-permute-done((bf16[8,32,256]{2,1,0:T(8,128)(2,1)S(1)}, bf16[8,32,256]{2,1,0:T(8,128)(2,1)S(1)}, u32[]{:S(2)}, u32[]{:S(2)}) %collective-permute-start.1) | collective-permute-done | bytes 131104 | tf_op jit(solution)/shard_map/ppermute | solution.py:232
  36.0 12.1 %all_to_all.21.back_ref = bf16[8,64,256]{2,1,0:T(8,128)(2,1)S(1)} all-to-all(bf16[8,64,256]{2,1,0:T(8,128)(2,1)S(1)} %shard_map.109), channel_id=1, replica_groups=mesh['dp'=4,'table'=8] {'table'}, dimensions={0} | all-to-all | bytes 524288 | tf_op jit(solution)/shard_map/all_to_all | solution.py:228
  48.1 0.1 shard_map.110.refs_0_
  48.2 1.6 %collective-permute-start.2 = (bf16[304,256]{1,0:T(8,128)(2,1)S(1)}, bf16[304,256]{1,0:T(8,128)(2,1)S(1)}, u32[]{:S(2)}, u32[]{:S(2)}) collective-permute-start(bf16[304,256]{1,0:T(8,128)(2,1)S(1)} %shard_map.110.refs_0_), channel_id=1, source_target_pairs={{0,16},{8,24},{16,0},{24,8},{1,17},{9,25},{17,1},{25,9},{2,18},{10... | collective-permute-start | bytes 466952 | tf_op jit(solution)/shard_map/ppermute | solution.py:232
  49.8 3.7 %collective-permute-done.2.refs_1_ = bf16[304,256]{1,0:T(8,128)(2,1)S(1)} collective-permute-done((bf16[304,256]{1,0:T(8,128)(2,1)S(1)}, bf16[304,256]{1,0:T(8,128)(2,1)S(1)}, u32[]{:S(2)}, u32[]{:S(2)}) %collective-permute-start.2) | collective-permute-done | bytes 155680 | tf_op jit(solution)/shard_map/ppermute | solution.py:232
  53.5 0.7 %shard_map.111.grad_ref = f32[1024,256]{1,0:T(8,128)S(1)} custom-call(s32[1,64]{1,0:T(1,128)S(1)} %bitcast.11, bf16[304,256]{1,0:T(8,128)(2,1)S(1)} %shard_map.110.refs_0_, bf16[304,256]{1,0:T(8,128)(2,1)S(1)} %collective-permute-done.2.refs_1_), custom_call_target="tpu_custom_call" | custom-call | tf_op jit(solution)/shard_map/pallas_call | solution.py:20
  54.2 0.7 %collective-permute-done.4.refs_1_ = bf16[304,256]{1,0:T(8,128)(2,1)S(1)} collective-permute-done((bf16[304,256]{1,0:T(8,128)(2,1)S(1)}, bf16[304,256]{1,0:T(8,128)(2,1)S(1)}, u32[]{:S(2)}, u32[]{:S(2)}) %collective-permute-start.4) | collective-permute-done | bytes 155680 | tf_op jit(solution)/shard_map/ppermute | solution.py:232
  54.9 2.3 %shard_map.112 = (f32[1024,256]{1,0:T(8,128)}, f32[8,128]{1,0:T(8,128)}) custom-call(s32[1,64]{1,0:T(1,128)S(1)} %bitcast.12, f32[8,128]{1,0:T(8,128)S(1)} %bitcast.13, f32[1024,256]{1,0:T(8,128)S(1)} %copy-done.1, f32[1024,256]{1,0:T(8,128)S(1)} %shard_map.111.grad_ref, bf16[304,256]{1,0:T(8,128)(2,1)S(1)} %collective-permute-done.3.refs_0_, ...), custom_call_target="tpu_custom_call" | custom-call | tf_op jit(solution)/shard_map/pallas_call | solution.py:20
  (25 shorter events, 0.1 us)
Async XLA Ops:
  0.6 18.4 %copy-start.10 = (s32[1,8]{1,0:T(1,128)S(1)}, s32[1,8]{1,0:T(1,128)}, u32[]{:S(2)}) copy-start(s32[1,8]{1,0:T(1,128)} %count_ref.1) | copy-start | bytes 100
  0.6 26.6 %copy-start.11 = (bf16[4096]{0:T(1024)(128)(2,1)S(1)}, bf16[4096]{0:T(1024)(128)(2,1)}, u32[]{:S(2)}) copy-start(bf16[4096]{0:T(1024)(128)(2,1)} %param.17) | copy-start | bytes 24580
  0.7 28.0 %copy-start.9 = (f32[512]{0:T(512)S(1)}, f32[512]{0:T(512)}, u32[]{:S(2)}) copy-start(f32[512]{0:T(512)} %param.10) | copy-start | bytes 6148
  0.7 13.8 %all-to-all-start = ((s32[8,1,32]{2,1,0:T(1,128)}), s32[8,1,32]{2,1,0:T(1,128)S(1)}, u32[]{:S(2)}, u32[]{:S(2)}) async-start(s32[8,1,32]{2,1,0:T(1,128)} %bitcast.15), calls=%async_computation | async-start | bytes 8192 | tf_op jit(solution)/shard_map/all_to_all | solution.py:228
  8.1 1.2 %copy-start = (f32[1024,256]{1,0:T(8,128)S(1)}, f32[1024,256]{1,0:T(8,128)}, u32[]{:S(2)}) copy-start(f32[1024,256]{1,0:T(8,128)} %table_ref.3) | copy-start | bytes 3145732
  9.3 0.7 %copy-start.6 = (s32[64]{0:T(128)S(1)}, s32[64]{0:T(128)}, u32[]{:S(2)}) copy-start(s32[64]{0:T(128)} %param.15) | copy-start | bytes 772
  9.9 9.1 %copy-start.5 = (s32[512,32]{0,1:T(8,128)S(1)}, s32[512,32]{0,1:T(8,128)}, u32[]{:S(2)}) copy-start(s32[512,32]{0,1:T(8,128)} %param.9) | copy-start | bytes 196612
  9.9 18.7 %copy-start.2 = (bf16[256,4096]{1,0:T(8,128)(2,1)S(1)}, bf16[256,4096]{1,0:T(8,128)(2,1)}, u32[]{:S(2)}) copy-start(bf16[256,4096]{1,0:T(8,128)(2,1)} %w_in_ref.1) | copy-start | bytes 6291460
  15.6 11.6 %all-to-all-start.1 = ((bf16[8,64,256]{2,1,0:T(8,128)(2,1)}), bf16[8,64,256]{2,1,0:T(8,128)(2,1)S(1)}, u32[]{:S(2)}, u32[]{:S(2)}) async-start(bf16[8,64,256]{2,1,0:T(8,128)(2,1)} %shard_map.105), calls=%async_computation.1 | async-start | bytes 524288 | tf_op jit(solution)/shard_map/all_to_all | solution.py:228
  21.7 0.9 %copy-start.3 = (bf16[768,512]{1,0:T(8,128)(2,1)}, bf16[768,512]{1,0:T(8,128)(2,1)S(1)}, u32[]{:S(2)}) copy-start(bf16[768,512]{1,0:T(8,128)(2,1)S(1)} %get-tuple-element.18.inc_t_ref) | copy-start | bytes 2359300
  27.2 1.4 %collective-permute-start = (bf16[8,32,256]{2,1,0:T(8,128)(2,1)S(1)}, bf16[8,32,256]{2,1,0:T(8,128)(2,1)S(1)}, u32[]{:S(2)}, u32[]{:S(2)}) collective-permute-start(bf16[8,32,256]{2,1,0:T(8,128)(2,1)S(1)} %shard_map.107), channel_id=1, source_target_pairs={{0,8},{8,0},{16,24},{24,16},{1,9},{9,1},{17,25},{25,17},{2,10},{10... | collective-permute-start | bytes 393224 | tf_op jit(solution)/shard_map/ppermute | solution.py:232
  28.6 1.1 %copy-start.4 = (bf16[768,512]{1,0:T(8,128)(2,1)S(1)}, bf16[768,512]{1,0:T(8,128)(2,1)}, u32[]{:S(2)}) copy-start(bf16[768,512]{1,0:T(8,128)(2,1)} %copy-done.3) | copy-start | bytes 2359300
  29.8 23.7 %copy-start.7 = (s32[64]{0:T(128)S(1)}, s32[64]{0:T(128)}, u32[]{:S(2)}) copy-start(s32[64]{0:T(128)} %param.15) | copy-start | bytes 772
  34.5 20.3 %copy-start.1 = (f32[1024,256]{1,0:T(8,128)S(1)}, f32[1024,256]{1,0:T(8,128)}, u32[]{:S(2)}) copy-start(f32[1024,256]{1,0:T(8,128)} %table_ref.3) | copy-start | bytes 3145732
  34.5 20.3 %copy-start.8 = (f32[1024]{0:T(1024)S(1)}, f32[1024]{0:T(1024)}, u32[]{:S(2)}) copy-start(f32[1024]{0:T(1024)} %param.14) | copy-start | bytes 12292
  34.6 1.4 %collective-permute-start.1 = (bf16[8,32,256]{2,1,0:T(8,128)(2,1)S(1)}, bf16[8,32,256]{2,1,0:T(8,128)(2,1)S(1)}, u32[]{:S(2)}, u32[]{:S(2)}) collective-permute-start(bf16[8,32,256]{2,1,0:T(8,128)(2,1)S(1)} %get-tuple-element.21), channel_id=1, source_target_pairs={{0,8},{8,0},{16,24},{24,16},{1,9},{9,1},{17,25},{25,17},{2,10},{10... | collective-permute-start | bytes 393224 | tf_op jit(solution)/shard_map/ppermute | solution.py:232
  48.2 5.3 %collective-permute-start.2 = (bf16[304,256]{1,0:T(8,128)(2,1)S(1)}, bf16[304,256]{1,0:T(8,128)(2,1)S(1)}, u32[]{:S(2)}, u32[]{:S(2)}) collective-permute-start(bf16[304,256]{1,0:T(8,128)(2,1)S(1)} %shard_map.110.refs_0_), channel_id=1, source_target_pairs={{0,16},{8,24},{16,0},{24,8},{1,17},{9,25},{17,1},{25,9},{2,18},{10... | collective-permute-start | bytes 466952 | tf_op jit(solution)/shard_map/ppermute | solution.py:232
  49.8 4.4 %collective-permute-start.3 = (bf16[304,256]{1,0:T(8,128)(2,1)S(1)}, bf16[304,256]{1,0:T(8,128)(2,1)S(1)}, u32[]{:S(2)}, u32[]{:S(2)}) collective-permute-start(bf16[304,256]{1,0:T(8,128)(2,1)S(1)} %shard_map.110.refs_0_), channel_id=1, source_target_pairs={{0,8},{8,0},{16,24},{24,16},{1,9},{9,1},{17,25},{25,17},{2,10},{10... | collective-permute-start | bytes 466952 | tf_op jit(solution)/shard_map/ppermute | solution.py:232
  53.5 1.4 %collective-permute-start.4 = (bf16[304,256]{1,0:T(8,128)(2,1)S(1)}, bf16[304,256]{1,0:T(8,128)(2,1)S(1)}, u32[]{:S(2)}, u32[]{:S(2)}) collective-permute-start(bf16[304,256]{1,0:T(8,128)(2,1)S(1)} %collective-permute-done.2.refs_1_), channel_id=1, source_target_pairs={{0,8},{8,0},{16,24},{24,16},{1,9},{9,1},{17,25},{25,17},{2,10},{10... | collective-permute-start | bytes 466952 | tf_op jit(solution)/shard_map/ppermute | solution.py:232

commit v4 on v3

--- a/solution.py
+++ b/solution.py
@@ -10,18 +10,19 @@
 learning_rate = 0.3
 f32, bf16, i32 = jnp.float32, jnp.bfloat16, jnp.int32
 VMEM = pl.BlockSpec(memory_space=pltpu.VMEM)
+ANY = pl.BlockSpec(memory_space=pl.ANY)
 SMEM = pl.BlockSpec(memory_space=pltpu.SMEM)
 FIELDS = 4
 FIELD_BITS = 8
 TAIL = 16
 
 
-def call(body, outs, operands, scratch=(), in_specs=None, mib=12):
+def call(body, outs, operands, scratch=(), in_specs=None, out_specs=None, mib=12):
     return pl.pallas_call(
         body,
         out_shape=outs,
         in_specs=in_specs or [VMEM] * len(operands),
-        out_specs=jax.tree.map(lambda _: VMEM, outs),
+        out_specs=out_specs or jax.tree.map(lambda _: VMEM, outs),
         scratch_shapes=list(scratch),
         compiler_params=pltpu.CompilerParams(vmem_limit_bytes=mib * 1024 * 1024),
     )(*operands)
@@ -74,30 +75,36 @@
     hot_ref[...] = jnp.dot(pick, table_bf_ref[...], preferred_element_type=f32).astype(bf16)
 
 
-def serve_body(asked_ref, hot_ref, table_ref, out_ref, pick):
+def serve_body(asked_ref, hot_ref, table_ref, out_ref, pick, hot, cold, sems):
     owners, slot_cap = asked_ref.shape
-    hot_dev = hot_ref.shape[0]
+    half = hot.shape[0]
+    hot[...] = hot_ref[half_rows(0, 2 * half, core()), :]
+    copies = [pltpu.make_async_copy(hot, out_ref.at[t, 0:half], sems.at[t]) for t in range(owners)]
+    for copy in copies:
+        copy.start()
     asked = asked_ref[...].T
     for t in range(owners):
         pick[t * slot_cap:(t + 1) * slot_cap, :] = one_hot(asked[:, t:t + 1], (slot_cap, table_ref.shape[0]), 1)
-    picked = jnp.dot(pick[...], table_ref[...], preferred_element_type=f32).astype(bf16)
-    hot = hot_ref[half_rows(0, hot_dev, core()), :]
-    for t in range(owners):
-        out_ref[t, 0:hot_dev // 2, :] = hot
-        out_ref[t, hot_dev // 2:, :] = picked[t * slot_cap:(t + 1) * slot_cap]
+    cold[...] = jnp.dot(pick[...], table_ref[...], preferred_element_type=f32).astype(bf16)
+    for t in range(owners):
+        rows = cold.at[t * slot_cap:(t + 1) * slot_cap]
+        copies.append(pltpu.make_async_copy(rows, out_ref.at[t, half:half + slot_cap], sems.at[owners + t]))
+        copies[-1].start()
+    for copy in copies:
+        copy.wait()
 
 
 def first_rows_body(rows_ref, out_ref):
     out_ref[...] = rows_ref[:, 0:out_ref.shape[1], :]
 
 
-def top_body(labels_ref, inc_ref, inc_t_ref, own_ref, mate_ref, w_in_ref, w_out_ref, part_ref, send_ref, gated, rows):
+def top_body(labels_ref, inc_ref, own_ref, mate_ref, w_in_ref, w_out_ref, out_ref, gated, rows):
     batch = inc_ref.shape[0]
     hidden_units, width = w_in_ref.shape[1], w_in_ref.shape[0]
-    owners, half, _ = send_ref.shape
+    owners, half, _ = mate_ref.shape
     hot_dev = 2 * half
     hot_cols = owners * hot_dev
-    slot_cap = part_ref.shape[1] - half
+    slot_cap = own_ref.shape[1] - half
     me = core()
     for t in range(owners):
         rows[half_rows(t, hot_dev, me), :] = own_ref[t, 0:half, :]
@@ -107,7 +114,6 @@
     labels = jnp.concatenate([labels[:, k:k + 1] for k in range(labels.shape[1])], axis=0)
     pooled = jnp.dot(inc_ref[...], rows[...], preferred_element_type=f32).astype(bf16)
     size, step, wide = batch // 2, 512, 2048
-    dpooled = []
     for at in range(0, batch, size):
         samples = slice(at, at + size)
         total = jnp.zeros((size, 128), f32)
@@ -129,9 +135,16 @@
             grad += lax.dot_general(
                 dhidden, w_in_ref[:, start:start + wide], (((1,), (1,)), ((), ())), preferred_element_type=f32
             )
-        dpooled.append(grad.astype(bf16))
-    dpooled = jnp.concatenate(dpooled, axis=0)
-    rows[...] = jnp.dot(inc_t_ref[...], dpooled, preferred_element_type=f32).astype(bf16)
+        out_ref[samples, :] = grad.astype(bf16)
+
+
+def slot_grads_body(inc_t_ref, dpooled_ref, part_ref, send_ref, rows):
+    owners, half, _ = send_ref.shape
+    hot_dev = 2 * half
+    hot_cols = owners * hot_dev
+    slot_cap = part_ref.shape[1] - half
+    me = core()
+    rows[...] = jnp.dot(inc_t_ref[...], dpooled_ref[...], preferred_element_type=f32).astype(bf16)
     for t in range(owners):
         send_ref[t] = rows[half_rows(t, hot_dev, 1 - me), :]
         part_ref[t, 0:half, :] = rows[half_rows(t, hot_dev, me), :]
@@ -199,17 +212,20 @@
 
 
 def update_body(hot_ref, sum_ref, table_ref, grad_ref, *refs):
-    part_refs, (new_table_ref, new_sum_ref, held, sums) = refs[:-4], refs[-4:]
+    part_refs, (new_table_ref, new_sum_ref, held, sums, staged, sems) = refs[:-6], refs[-6:]
     own_sum = sum_ref[...].T
+    copies = []
 
     def put(at, grad):
         k = at.start // 128
-        new_table_ref[at, :], sums[:, k:k + 1] = adagrad(
-            table_ref[at, :], own_sum[:, k:k + 1], grad_ref[at, :] + grad
-        )
+        staged[at, :], sums[:, k:k + 1] = adagrad(table_ref[at, :], own_sum[:, k:k + 1], grad_ref[at, :] + grad)
+        copies.append(pltpu.make_async_copy(staged.at[at], new_table_ref.at[at], sems.at[k]))
+        copies[k].start()
 
     row_grads(1 - core(), hot_ref, part_refs, held, put, table_ref.shape[0])
     new_sum_ref[...] = sums[...].T
+    for copy in copies:
+        copy.wait()
 
 
 def dense_body(hot_ref, asked_ref, back_ref, out_ref):
@@ -257,16 +273,28 @@
         serve_body,
         shape((owners, half + slot_cap, width), bf16),
         (asked, hot, table_bf),
-        [pltpu.VMEM((owners * slot_cap, rows), bf16)],
+        [
+            pltpu.VMEM((owners * slot_cap, rows), bf16),
+            pltpu.VMEM((half, width), bf16),
+            pltpu.VMEM((owners * slot_cap, width), bf16),
+            pltpu.SemaphoreType.DMA((2 * owners,)),
+        ],
+        out_specs=ANY,
     )
     own_rows, inc, inc_t = lax.optimization_barrier((exchange(served), inc, inc_t))
     mate_rows = swap(call(first_rows_body, shape((owners, half, width), bf16), (own_rows,)), 1)
-    part, to_mate = call(
+    dpooled = call(
         top_body,
-        (shape((owners, half + slot_cap, width), bf16), shape((owners, half, width), bf16)),
-        (labels.reshape(-1, 128), inc, inc_t, own_rows, mate_rows, w_in, w_out.reshape(1, -1)),
+        shape((batch, width), bf16),
+        (labels.reshape(-1, 128), inc, own_rows, mate_rows, w_in, w_out.reshape(1, -1)),
         [pltpu.VMEM((batch, hidden_units), bf16), pltpu.VMEM((vocab, width), bf16)],
         mib=24,
+    )
+    part, to_mate = call(
+        slot_grads_body,
+        (shape((owners, half + slot_cap, width), bf16), shape((owners, half, width), bf16)),
+        (inc_t, dpooled),
+        [pltpu.VMEM((vocab, width), bf16)],
     )
     summed = call(add_hot_body, shape(part.shape, bf16), (part, swap(to_mate, 1)))
     returned = exchange(summed)
@@ -285,7 +313,13 @@
             update_body,
             (shape((rows, width), f32), shape((rows // 128, 128), f32)),
             (hot_row, adagrad_sum.reshape(-1, 128), table, grad, *far),
-            [held, pltpu.VMEM((128, rows // 128), f32)],
+            [
+                held,
+                pltpu.VMEM((128, rows // 128), f32),
+                pltpu.VMEM((rows, width), f32),
+                pltpu.SemaphoreType.DMA((rows // 128,)),
+            ],
+            out_specs=(ANY, VMEM),
         )
         return new_table, new_sum.reshape(rows)
     grad = call(dense_body, shape((rows, width), bf16), (hot_row, asked, returned))

time: 57.6 us -> 58.2 us (1.010)
  Pallas kernels: 11.9 us -> 12.5 us
    pallas_call x9 -> x10, Pallas kernels: 11.9 us -> 12.5 us  [call(): pl.pallas_call(body, out_shape=outs, in_specs=in_specs or [VMEM] * len(op...]
where the time goes in v4:
time: 58.2 us; the launch traced here: 57.8 us
  waiting for transfers between devices  15.7 us (27%)
  starting transfers between devices  12.7 us (22%)
  Pallas kernels  12.5 us (21%)
  blocking collectives  12.1 us (21%)
  local copies, waits for them, and re-layouts  3.94 us (7%)
  between operations  0.8 us (1%)
    pallas_call x10, Pallas kernels, call(): pl.pallas_call(body, out_shape=outs, in_specs=in_specs or [VMEM] * len(op...  12.5 us
    all_to_all x1, blocking collectives, exchange(): return lax.all_to_all(x, 'table', split_axis=0, concat_axis=0, tiled=True)  12.1 us
    all_to_all x2, starting transfers between devices, exchange(): return lax.all_to_all(x, 'table', split_axis=0, concat_axis=0, tiled=True)  10.8 us
    all_to_all x2, waiting for transfers between devices, exchange(): return lax.all_to_all(x, 'table', split_axis=0, concat_axis=0, tiled=True)  8.83 us
    ppermute x5, waiting for transfers between devices, swap(): lax.ppermute(x, 'dp', [(g, g ^ bit) for g in range(lax.axis_size('dp'))])  6.88 us
    unnamed x24, local copies, waits for them, and re-layouts  3.92 us
    ppermute x5, starting transfers between devices, swap(): lax.ppermute(x, 'dp', [(g, g ^ bit) for g in range(lax.axis_size('dp'))])  1.88 us
  transfers between devices with their start and end apart: 7, of which 6 were waited for; matrix products, arithmetic and copies ran while one was open for 0% of the time, Pallas kernels for 6%

profile of v4, /device:TPU:0, one launch (start us, length us, event | category | flops | bytes accessed | tf_op | source)
XLA Modules:
  0.0 57.8 jit_solution(1892627707050587437)
XLA Ops:
  0.7 7.4 %all-to-all-start = ((s32[8,1,32]{2,1,0:T(1,128)}), s32[8,1,32]{2,1,0:T(1,128)S(1)}, u32[]{:S(2)}, u32[]{:S(2)}) async-start(s32[8,1,32]{2,1,0:T(1,128)} %bitcast.15), calls=%async_computation | async-start | bytes 8192 | tf_op jit(solution)/shard_map/all_to_all | solution.py:244
  8.1 1.2 %copy-done = f32[1024,256]{1,0:T(8,128)S(1)} copy-done((f32[1024,256]{1,0:T(8,128)S(1)}, f32[1024,256]{1,0:T(8,128)}, u32[]{:S(2)}) %copy-start) | copy-done | bytes 1048600
  9.3 0.7 %copy-done.6 = s32[64]{0:T(128)S(1)} copy-done((s32[64]{0:T(128)S(1)}, s32[64]{0:T(128)}, u32[]{:S(2)}) %copy-start.6) | copy-done | bytes 280
  9.9 0.3 shard_map.104
  10.3 4.2 %all-to-all-done = s32[8,1,32]{2,1,0:T(1,128)S(1)} async-done(((s32[8,1,32]{2,1,0:T(1,128)}), s32[8,1,32]{2,1,0:T(1,128)S(1)}, u32[]{:S(2)}, u32[]{:S(2)}) %all-to-all-start) | async-done | bytes 1056 | tf_op jit(solution)/shard_map/all_to_all | solution.py:244
  14.4 1.2 %shard_map.105 = bf16[8,64,256]{2,1,0:T(8,128)(2,1)} custom-call(s32[8,32]{1,0:T(8,128)S(1)} %bitcast.8, bf16[64,256]{1,0:T(8,128)(2,1)S(1)} %get-tuple-element.13.hot_ref, bf16[1024,256]{1,0:T(8,128)(2,1)S(1)} %get-tuple-element.14.table_ref), custom_call_target="tpu_custom_call" | custom-call | tf_op jit(solution)/shard_map/pallas_call | solution.py:21
  15.7 3.4 %all-to-all-start.1 = ((bf16[8,64,256]{2,1,0:T(8,128)(2,1)}), bf16[8,64,256]{2,1,0:T(8,128)(2,1)S(1)}, u32[]{:S(2)}, u32[]{:S(2)}) async-start(bf16[8,64,256]{2,1,0:T(8,128)(2,1)} %shard_map.105), calls=%async_computation.1 | async-start | bytes 524288 | tf_op jit(solution)/shard_map/all_to_all | solution.py:244
  19.1 2.6 %shard_map.106 = (bf16[512,768]{1,0:T(8,128)(2,1)S(1)}, bf16[768,512]{1,0:T(8,128)(2,1)S(1)}) custom-call(s32[1,8]{1,0:T(1,128)S(1)} %copy-done.10, s32[32,512]{1,0:T(8,128)S(1)} %bitcast.7), custom_call_target="tpu_custom_call" | custom-call | tf_op jit(solution)/shard_map/pallas_call | solution.py:21
  21.8 0.9 %copy-done.3 = bf16[512,768]{1,0:T(8,128)(2,1)} copy-done((bf16[512,768]{1,0:T(8,128)(2,1)}, bf16[512,768]{1,0:T(8,128)(2,1)S(1)}, u32[]{:S(2)}) %copy-start.3) | copy-done | bytes 786456
  22.6 4.6 %all-to-all-done.1.rows_ref.own_ref = bf16[8,64,256]{2,1,0:T(8,128)(2,1)S(1)} async-done(((bf16[8,64,256]{2,1,0:T(8,128)(2,1)}), bf16[8,64,256]{2,1,0:T(8,128)(2,1)S(1)}, u32[]{:S(2)}, u32[]{:S(2)}) %all-to-all-start.1) | async-done | bytes 262176 | tf_op jit(solution)/shard_map/all_to_all | solution.py:244
  27.3 0.1 collective-permute-start
  27.4 1.3 %collective-permute-done.mate_ref = bf16[8,32,256]{2,1,0:T(8,128)(2,1)S(1)} collective-permute-done((bf16[8,32,256]{2,1,0:T(8,128)(2,1)S(1)}, bf16[8,32,256]{2,1,0:T(8,128)(2,1)S(1)}, u32[]{:S(2)}, u32[]{:S(2)}) %collective-permute-start) | collective-permute-done | bytes 131104 | tf_op jit(solution)/shard_map/ppermute | solution.py:248
  28.7 1.1 %copy-done.4 = bf16[512,768]{1,0:T(8,128)(2,1)S(1)} copy-done((bf16[512,768]{1,0:T(8,128)(2,1)S(1)}, bf16[512,768]{1,0:T(8,128)(2,1)}, u32[]{:S(2)}) %copy-start.4) | copy-done | bytes 786456
  29.9 4.5 %shard_map.108.dpooled_ref = bf16[512,256]{1,0:T(8,128)(2,1)S(1)} custom-call(f32[4,128]{1,0:T(4,128)S(1)} %bitcast.14, bf16[512,768]{1,0:T(8,128)(2,1)S(1)} %copy-done.4, bf16[8,64,256]{2,1,0:T(8,128)(2,1)S(1)} %all-to-all-done.1.rows_ref.own_ref, bf16[8,32,256]{2,1,0:T(8,128)(2,1)S(1)} %collective-permute-done.mate_ref, bf16[256,4096]{1,0:T(8,128)(2,1)S(1)} %copy-done.2, ...), custom_call_target="tpu_custom_call" | custom-call | tf_op jit(solution)/shard_map/pallas_call | solution.py:21
  34.4 0.4 shard_map.109
  34.8 0.2 collective-permute-start.1
  35.0 1.2 %collective-permute-done.1.got_ref = bf16[8,32,256]{2,1,0:T(8,128)(2,1)S(1)} collective-permute-done((bf16[8,32,256]{2,1,0:T(8,128)(2,1)S(1)}, bf16[8,32,256]{2,1,0:T(8,128)(2,1)S(1)}, u32[]{:S(2)}, u32[]{:S(2)}) %collective-permute-start.1) | collective-permute-done | bytes 131104 | tf_op jit(solution)/shard_map/ppermute | solution.py:248
  36.2 12.1 %all_to_all.21.back_ref = bf16[8,64,256]{2,1,0:T(8,128)(2,1)S(1)} all-to-all(bf16[8,64,256]{2,1,0:T(8,128)(2,1)S(1)} %shard_map.110), channel_id=1, replica_groups=mesh['dp'=4,'table'=8] {'table'}, dimensions={0} | all-to-all | bytes 524288 | tf_op jit(solution)/shard_map/all_to_all | solution.py:244
  48.4 0.1 shard_map.111.refs_0_
  48.5 1.6 %collective-permute-start.2 = (bf16[304,256]{1,0:T(8,128)(2,1)S(1)}, bf16[304,256]{1,0:T(8,128)(2,1)S(1)}, u32[]{:S(2)}, u32[]{:S(2)}) collective-permute-start(bf16[304,256]{1,0:T(8,128)(2,1)S(1)} %shard_map.111.refs_0_), channel_id=1, source_target_pairs={{0,16},{8,24},{16,0},{24,8},{1,17},{9,25},{17,1},{25,9},{2,18},{10... | collective-permute-start | bytes 466952 | tf_op jit(solution)/shard_map/ppermute | solution.py:248
  50.0 3.7 %collective-permute-done.2.refs_1_ = bf16[304,256]{1,0:T(8,128)(2,1)S(1)} collective-permute-done((bf16[304,256]{1,0:T(8,128)(2,1)S(1)}, bf16[304,256]{1,0:T(8,128)(2,1)S(1)}, u32[]{:S(2)}, u32[]{:S(2)}) %collective-permute-start.2) | collective-permute-done | bytes 155680 | tf_op jit(solution)/shard_map/ppermute | solution.py:248
  53.7 0.7 %shard_map.112.grad_ref = f32[1024,256]{1,0:T(8,128)S(1)} custom-call(s32[1,64]{1,0:T(1,128)S(1)} %bitcast.11, bf16[304,256]{1,0:T(8,128)(2,1)S(1)} %shard_map.111.refs_0_, bf16[304,256]{1,0:T(8,128)(2,1)S(1)} %collective-permute-done.2.refs_1_), custom_call_target="tpu_custom_call" | custom-call | tf_op jit(solution)/shard_map/pallas_call | solution.py:21
  54.4 0.7 %collective-permute-done.4.refs_1_ = bf16[304,256]{1,0:T(8,128)(2,1)S(1)} collective-permute-done((bf16[304,256]{1,0:T(8,128)(2,1)S(1)}, bf16[304,256]{1,0:T(8,128)(2,1)S(1)}, u32[]{:S(2)}, u32[]{:S(2)}) %collective-permute-start.4) | collective-permute-done | bytes 155680 | tf_op jit(solution)/shard_map/ppermute | solution.py:248
  55.1 2.7 %shard_map.113 = (f32[1024,256]{1,0:T(8,128)}, f32[8,128]{1,0:T(8,128)}) custom-call(s32[1,64]{1,0:T(1,128)S(1)} %bitcast.12, f32[8,128]{1,0:T(8,128)S(1)} %bitcast.13, f32[1024,256]{1,0:T(8,128)S(1)} %copy-done.1, f32[1024,256]{1,0:T(8,128)S(1)} %shard_map.112.grad_ref, bf16[304,256]{1,0:T(8,128)(2,1)S(1)} %collective-permute-done.3.refs_0_, ...), custom_call_target="tpu_custom_call" | custom-call | tf_op jit(solution)/shard_map/pallas_call | solution.py:21
  (26 shorter events, 0.1 us)
Async XLA Ops:
  0.6 18.5 %copy-start.10 = (s32[1,8]{1,0:T(1,128)S(1)}, s32[1,8]{1,0:T(1,128)}, u32[]{:S(2)}) copy-start(s32[1,8]{1,0:T(1,128)} %count_ref.1) | copy-start | bytes 100
  0.6 26.7 %copy-start.11 = (bf16[4096]{0:T(1024)(128)(2,1)S(1)}, bf16[4096]{0:T(1024)(128)(2,1)}, u32[]{:S(2)}) copy-start(bf16[4096]{0:T(1024)(128)(2,1)} %param.17) | copy-start | bytes 24580
  0.7 28.1 %copy-start.9 = (f32[512]{0:T(512)S(1)}, f32[512]{0:T(512)}, u32[]{:S(2)}) copy-start(f32[512]{0:T(512)} %param.10) | copy-start | bytes 6148
  0.7 13.8 %all-to-all-start = ((s32[8,1,32]{2,1,0:T(1,128)}), s32[8,1,32]{2,1,0:T(1,128)S(1)}, u32[]{:S(2)}, u32[]{:S(2)}) async-start(s32[8,1,32]{2,1,0:T(1,128)} %bitcast.15), calls=%async_computation | async-start | bytes 8192 | tf_op jit(solution)/shard_map/all_to_all | solution.py:244
  8.1 1.2 %copy-start = (f32[1024,256]{1,0:T(8,128)S(1)}, f32[1024,256]{1,0:T(8,128)}, u32[]{:S(2)}) copy-start(f32[1024,256]{1,0:T(8,128)} %table_ref.3) | copy-start | bytes 3145732
  9.3 0.7 %copy-start.6 = (s32[64]{0:T(128)S(1)}, s32[64]{0:T(128)}, u32[]{:S(2)}) copy-start(s32[64]{0:T(128)} %param.15) | copy-start | bytes 772
  9.9 9.2 %copy-start.5 = (s32[512,32]{0,1:T(8,128)S(1)}, s32[512,32]{0,1:T(8,128)}, u32[]{:S(2)}) copy-start(s32[512,32]{0,1:T(8,128)} %param.9) | copy-start | bytes 196612
  9.9 18.8 %copy-start.2 = (bf16[256,4096]{1,0:T(8,128)(2,1)S(1)}, bf16[256,4096]{1,0:T(8,128)(2,1)}, u32[]{:S(2)}) copy-start(bf16[256,4096]{1,0:T(8,128)(2,1)} %w_in_ref.1) | copy-start | bytes 6291460
  15.7 11.6 %all-to-all-start.1 = ((bf16[8,64,256]{2,1,0:T(8,128)(2,1)}), bf16[8,64,256]{2,1,0:T(8,128)(2,1)S(1)}, u32[]{:S(2)}, u32[]{:S(2)}) async-start(bf16[8,64,256]{2,1,0:T(8,128)(2,1)} %shard_map.105), calls=%async_computation.1 | async-start | bytes 524288 | tf_op jit(solution)/shard_map/all_to_all | solution.py:244
  21.8 0.9 %copy-start.3 = (bf16[512,768]{1,0:T(8,128)(2,1)}, bf16[512,768]{1,0:T(8,128)(2,1)S(1)}, u32[]{:S(2)}) copy-start(bf16[512,768]{1,0:T(8,128)(2,1)S(1)} %get-tuple-element.18.inc_ref) | copy-start | bytes 2359300
  27.3 1.4 %collective-permute-start = (bf16[8,32,256]{2,1,0:T(8,128)(2,1)S(1)}, bf16[8,32,256]{2,1,0:T(8,128)(2,1)S(1)}, u32[]{:S(2)}, u32[]{:S(2)}) collective-permute-start(bf16[8,32,256]{2,1,0:T(8,128)(2,1)S(1)} %shard_map.107), channel_id=1, source_target_pairs={{0,8},{8,0},{16,24},{24,16},{1,9},{9,1},{17,25},{25,17},{2,10},{10... | collective-permute-start | bytes 393224 | tf_op jit(solution)/shard_map/ppermute | solution.py:248
  28.7 1.1 %copy-start.4 = (bf16[512,768]{1,0:T(8,128)(2,1)S(1)}, bf16[512,768]{1,0:T(8,128)(2,1)}, u32[]{:S(2)}) copy-start(bf16[512,768]{1,0:T(8,128)(2,1)} %copy-done.3) | copy-start | bytes 2359300
  34.4 19.4 %copy-start.7 = (s32[64]{0:T(128)S(1)}, s32[64]{0:T(128)}, u32[]{:S(2)}) copy-start(s32[64]{0:T(128)} %param.15) | copy-start | bytes 772
  34.4 20.7 %copy-start.1 = (f32[1024,256]{1,0:T(8,128)S(1)}, f32[1024,256]{1,0:T(8,128)}, u32[]{:S(2)}) copy-start(f32[1024,256]{1,0:T(8,128)} %table_ref.3) | copy-start | bytes 3145732
  34.4 20.7 %copy-start.8 = (f32[1024]{0:T(1024)S(1)}, f32[1024]{0:T(1024)}, u32[]{:S(2)}) copy-start(f32[1024]{0:T(1024)} %param.14) | copy-start | bytes 12292
  34.8 1.4 %collective-permute-start.1 = (bf16[8,32,256]{2,1,0:T(8,128)(2,1)S(1)}, bf16[8,32,256]{2,1,0:T(8,128)(2,1)S(1)}, u32[]{:S(2)}, u32[]{:S(2)}) collective-permute-start(bf16[8,32,256]{2,1,0:T(8,128)(2,1)S(1)} %get-tuple-element.21), channel_id=1, source_target_pairs={{0,8},{8,0},{16,24},{24,16},{1,9},{9,1},{17,25},{25,17},{2,10},{10... | collective-permute-start | bytes 393224 | tf_op jit(solution)/shard_map/ppermute | solution.py:248
  48.5 5.3 %collective-permute-start.2 = (bf16[304,256]{1,0:T(8,128)(2,1)S(1)}, bf16[304,256]{1,0:T(8,128)(2,1)S(1)}, u32[]{:S(2)}, u32[]{:S(2)}) collective-permute-start(bf16[304,256]{1,0:T(8,128)(2,1)S(1)} %shard_map.111.refs_0_), channel_id=1, source_target_pairs={{0,16},{8,24},{16,0},{24,8},{1,17},{9,25},{17,1},{25,9},{2,18},{10... | collective-permute-start | bytes 466952 | tf_op jit(solution)/shard_map/ppermute | solution.py:248
  50.0 4.4 %collective-permute-start.3 = (bf16[304,256]{1,0:T(8,128)(2,1)S(1)}, bf16[304,256]{1,0:T(8,128)(2,1)S(1)}, u32[]{:S(2)}, u32[]{:S(2)}) collective-permute-start(bf16[304,256]{1,0:T(8,128)(2,1)S(1)} %shard_map.111.refs_0_), channel_id=1, source_target_pairs={{0,8},{8,0},{16,24},{24,16},{1,9},{9,1},{17,25},{25,17},{2,10},{10... | collective-permute-start | bytes 466952 | tf_op jit(solution)/shard_map/ppermute | solution.py:248
  53.7 1.4 %collective-permute-start.4 = (bf16[304,256]{1,0:T(8,128)(2,1)S(1)}, bf16[304,256]{1,0:T(8,128)(2,1)S(1)}, u32[]{:S(2)}, u32[]{:S(2)}) collective-permute-start(bf16[304,256]{1,0:T(8,128)(2,1)S(1)} %collective-permute-done.2.refs_1_), channel_id=1, source_target_pairs={{0,8},{8,0},{16,24},{24,16},{1,9},{9,1},{17,25},{25,17},{2,10},{10... | collective-permute-start | bytes 466952 | tf_op jit(solution)/shard_map/ppermute | solution.py:248

commit v5 on v4

--- a/solution.py
+++ b/solution.py
@@ -10,7 +10,7 @@
 learning_rate = 0.3
 f32, bf16, i32 = jnp.float32, jnp.bfloat16, jnp.int32
 VMEM = pl.BlockSpec(memory_space=pltpu.VMEM)
-ANY = pl.BlockSpec(memory_space=pl.ANY)
+HBM = pl.BlockSpec(memory_space=pltpu.HBM)
 SMEM = pl.BlockSpec(memory_space=pltpu.SMEM)
 FIELDS = 4
 FIELD_BITS = 8
@@ -36,7 +36,7 @@
     return (lax.broadcasted_iota(i32, shape, axis) + start == ids).astype(f32).astype(bf16)
 
 
-def incidence_body(hot_cols, slot_cap, count_ref, slots_ref, inc_ref, inc_t_ref):
+def incidence_body(hot_cols, slot_cap, count_ref, slots_ref, inc_t_ref):
     vocab, batch = inc_t_ref.shape
     field = vocab // FIELDS
     step = 128
@@ -55,7 +55,10 @@
     for owner in range((vocab - hot_cols) // slot_cap):
         rows = pl.ds(hot_cols + owner * slot_cap, slot_cap)
         inc_t_ref[rows, :] = jnp.where(place < count_ref[0, owner], inc_t_ref[rows, :].astype(f32), 0.0).astype(bf16)
-    inc_ref[...] = inc_t_ref[...].T
+
+
+def transpose_body(x_ref, out_ref):
+    out_ref[...] = x_ref[...].T
 
 
 def core():
@@ -67,31 +70,33 @@
     return pl.ds(pl.multiple_of(owner * hot_dev + which * half, half), half)
 
 
-def pick_hot_body(ids_ref, table_ref, hot_ref, table_bf_ref):
-    hot_dev = ids_ref.shape[1]
-    table_bf_ref[...] = table_ref[...].astype(bf16)
-    ids = jnp.broadcast_to(ids_ref[...], (8, hot_dev)).T[:, 0:1]
-    pick = one_hot(ids, (hot_dev, table_ref.shape[0]), 1)
-    hot_ref[...] = jnp.dot(pick, table_bf_ref[...], preferred_element_type=f32).astype(bf16)
-
-
-def serve_body(asked_ref, hot_ref, table_ref, out_ref, pick, hot, cold, sems):
-    owners, slot_cap = asked_ref.shape
-    half = hot.shape[0]
-    hot[...] = hot_ref[half_rows(0, 2 * half, core()), :]
-    copies = [pltpu.make_async_copy(hot, out_ref.at[t, 0:half], sems.at[t]) for t in range(owners)]
+def pick_hot_body(ids_ref, table_ref, hot_ref, table_bf_ref, ids, table, sems):
+    copies = [pltpu.make_async_copy(ids_ref, ids, sems.at[0]), pltpu.make_async_copy(table_ref, table, sems.at[1])]
     for copy in copies:
         copy.start()
-    asked = asked_ref[...].T
-    for t in range(owners):
-        pick[t * slot_cap:(t + 1) * slot_cap, :] = one_hot(asked[:, t:t + 1], (slot_cap, table_ref.shape[0]), 1)
-    cold[...] = jnp.dot(pick[...], table_ref[...], preferred_element_type=f32).astype(bf16)
-    for t in range(owners):
-        rows = cold.at[t * slot_cap:(t + 1) * slot_cap]
-        copies.append(pltpu.make_async_copy(rows, out_ref.at[t, half:half + slot_cap], sems.at[owners + t]))
-        copies[-1].start()
     for copy in copies:
         copy.wait()
+    hot_dev = ids.shape[1]
+    table_bf_ref[...] = table[...].astype(bf16)
+    column = jnp.broadcast_to(ids[...], (8, hot_dev)).T[:, 0:1]
+    pick = one_hot(column, (hot_dev, table.shape[0]), 1)
+    hot_ref[...] = jnp.dot(pick, table_bf_ref[...], preferred_element_type=f32).astype(bf16)
+
+
+def serve_body(asked_ref, hot_ref, table_ref, out_ref, pick, staged, sem):
+    owners, slot_cap = asked_ref.shape
+    hot_dev = hot_ref.shape[0]
+    asked = asked_ref[...].T
+    for t in range(owners):
+        pick[t * slot_cap:(t + 1) * slot_cap, :] = one_hot(asked[:, t:t + 1], (slot_cap, table_ref.shape[0]), 1)
+    picked = jnp.dot(pick[...], table_ref[...], preferred_element_type=f32).astype(bf16)
+    hot = hot_ref[half_rows(0, hot_dev, core()), :]
+    for t in range(owners):
+        staged[t, 0:hot_dev // 2, :] = hot
+        staged[t, hot_dev // 2:, :] = picked[t * slot_cap:(t + 1) * slot_cap]
+    copy = pltpu.make_async_copy(staged, out_ref, sem)
+    copy.start()
+    copy.wait()
 
 
 def first_rows_body(rows_ref, out_ref):
@@ -214,13 +219,16 @@
 def update_body(hot_ref, sum_ref, table_ref, grad_ref, *refs):
     part_refs, (new_table_ref, new_sum_ref, held, sums, staged, sems) = refs[:-6], refs[-6:]
     own_sum = sum_ref[...].T
+    piece = table_ref.shape[0] // 2
     copies = []
 
     def put(at, grad):
         k = at.start // 128
         staged[at, :], sums[:, k:k + 1] = adagrad(table_ref[at, :], own_sum[:, k:k + 1], grad_ref[at, :] + grad)
-        copies.append(pltpu.make_async_copy(staged.at[at], new_table_ref.at[at], sems.at[k]))
-        copies[k].start()
+        if at.stop % piece == 0:
+            done = slice(at.stop - piece, at.stop)
+            copies.append(pltpu.make_async_copy(staged.at[done], new_table_ref.at[done], sems.at[len(copies)]))
+            copies[-1].start()
 
     row_grads(1 - core(), hot_ref, part_refs, held, put, table_ref.shape[0])
     new_sum_ref[...] = sums[...].T
@@ -262,24 +270,30 @@
 
     hot_row = hot_ids.reshape(1, hot_dev)
     asked = exchange(cold_ids[0])
-    inc, inc_t = call(
+    inc_t = call(
         functools.partial(incidence_body, owners * hot_dev, slot_cap),
-        (shape((batch, vocab), bf16), shape((vocab, batch), bf16)),
+        shape((vocab, batch), bf16),
         (cold_count, bag_slots.T),
         in_specs=[SMEM, VMEM],
     )
-    hot, table_bf = call(pick_hot_body, (shape((hot_dev, width), bf16), shape((rows, width), bf16)), (hot_row, table))
+    inc = call(transpose_body, shape((batch, vocab), bf16), (inc_t,))
+    hot, table_bf = call(
+        pick_hot_body,
+        (shape((hot_dev, width), bf16), shape((rows, width), bf16)),
+        (hot_row, table),
+        [pltpu.VMEM((1, hot_dev), i32), pltpu.VMEM((rows, width), f32), pltpu.SemaphoreType.DMA((2,))],
+        in_specs=[HBM, HBM],
+    )
     served = call(
         serve_body,
         shape((owners, half + slot_cap, width), bf16),
         (asked, hot, table_bf),
         [
             pltpu.VMEM((owners * slot_cap, rows), bf16),
-            pltpu.VMEM((half, width), bf16),
-            pltpu.VMEM((owners * slot_cap, width), bf16),
-            pltpu.SemaphoreType.DMA((2 * owners,)),
+            pltpu.VMEM((owners, half + slot_cap, width), bf16),
+            pltpu.SemaphoreType.DMA,
         ],
-        out_specs=ANY,
+        out_specs=HBM,
     )
     own_rows, inc, inc_t = lax.optimization_barrier((exchange(served), inc, inc_t))
     mate_rows = swap(call(first_rows_body, shape((owners, half, width), bf16), (own_rows,)), 1)
@@ -317,9 +331,9 @@
                 held,
                 pltpu.VMEM((128, rows // 128), f32),
                 pltpu.VMEM((rows, width), f32),
-                pltpu.SemaphoreType.DMA((rows // 128,)),
+                pltpu.SemaphoreType.DMA((2,)),
             ],
-            out_specs=(ANY, VMEM),
+            out_specs=(HBM, VMEM),
         )
         return new_table, new_sum.reshape(rows)
     grad = call(dense_body, shape((rows, width), bf16), (hot_row, asked, returned))

time: 58.2 us -> 58.5 us (level)
  Pallas kernels: 12.5 us -> 13.1 us
    pallas_call x10 -> x11, Pallas kernels: 12.5 us -> 13.1 us  [call(): pl.pallas_call(body, out_shape=outs, in_specs=in_specs or [VMEM] * len(op...]
    unnamed x24 -> x20, local copies, waits for them, and re-layouts: 3.92 us -> 3.5 us
  transfers between devices with their start and end apart: 7 -> 7, of which waited for: 6 -> 6; matrix products, arithmetic and copies ran while one was open for 0% -> 0% of each run, Pallas kernels for 6% -> 7%
where the time goes in v5:
time: 58.5 us; the launch traced here: 58.1 us
  waiting for transfers between devices  16 us (27%)
  Pallas kernels  13.1 us (22%)
  starting transfers between devices  12.6 us (22%)
  blocking collectives  12.1 us (21%)
  local copies, waits for them, and re-layouts  3.52 us (6%)
  between operations  0.79 us (1%)
    pallas_call x11, Pallas kernels, call(): pl.pallas_call(body, out_shape=outs, in_specs=in_specs or [VMEM] * len(op...  13.1 us
    all_to_all x1, blocking collectives, exchange(): return lax.all_to_all(x, 'table', split_axis=0, concat_axis=0, tiled=True)  12.1 us
    all_to_all x2, starting transfers between devices, exchange(): return lax.all_to_all(x, 'table', split_axis=0, concat_axis=0, tiled=True)  10.7 us
    all_to_all x2, waiting for transfers between devices, exchange(): return lax.all_to_all(x, 'table', split_axis=0, concat_axis=0, tiled=True)  9.06 us
    ppermute x5, waiting for transfers between devices, swap(): lax.ppermute(x, 'dp', [(g, g ^ bit) for g in range(lax.axis_size('dp'))])  6.9 us
    unnamed x20, local copies, waits for them, and re-layouts  3.5 us
    ppermute x5, starting transfers between devices, swap(): lax.ppermute(x, 'dp', [(g, g ^ bit) for g in range(lax.axis_size('dp'))])  1.86 us
  transfers between devices with their start and end apart: 7, of which 6 were waited for; matrix products, arithmetic and copies ran while one was open for 0% of the time, Pallas kernels for 7%

profile of v5, /device:TPU:0, one launch (start us, length us, event | category | flops | bytes accessed | tf_op | source)
XLA Modules:
  0.0 58.1 jit_solution(875049798570901805)
XLA Ops:
  0.6 7.3 %all-to-all-start = ((s32[8,1,32]{2,1,0:T(1,128)}), s32[8,1,32]{2,1,0:T(1,128)S(1)}, u32[]{:S(2)}, u32[]{:S(2)}) async-start(s32[8,1,32]{2,1,0:T(1,128)} %bitcast.15), calls=%async_computation | async-start | bytes 8192 | tf_op jit(solution)/shard_map/all_to_all | solution.py:252
  7.9 1.2 %copy-done = f32[1024,256]{1,0:T(8,128)S(1)} copy-done((f32[1024,256]{1,0:T(8,128)S(1)}, f32[1024,256]{1,0:T(8,128)}, u32[]{:S(2)}) %copy-start) | copy-done | bytes 1048600
  9.1 0.7 %copy-done.4 = s32[64]{0:T(128)S(1)} copy-done((s32[64]{0:T(128)S(1)}, s32[64]{0:T(128)}, u32[]{:S(2)}) %copy-start.4) | copy-done | bytes 280
  9.8 0.4 shard_map.104
  10.2 4.1 %all-to-all-done = s32[8,1,32]{2,1,0:T(1,128)S(1)} async-done(((s32[8,1,32]{2,1,0:T(1,128)}), s32[8,1,32]{2,1,0:T(1,128)S(1)}, u32[]{:S(2)}, u32[]{:S(2)}) %all-to-all-start) | async-done | bytes 1056 | tf_op jit(solution)/shard_map/all_to_all | solution.py:252
  14.3 1.2 %shard_map.105 = bf16[8,64,256]{2,1,0:T(8,128)(2,1)} custom-call(s32[8,32]{1,0:T(8,128)S(1)} %bitcast.8, bf16[64,256]{1,0:T(8,128)(2,1)S(1)} %get-tuple-element.11.hot_ref, bf16[1024,256]{1,0:T(8,128)(2,1)S(1)} %get-tuple-element.12.table_ref), custom_call_target="tpu_custom_call" | custom-call | tf_op jit(solution)/shard_map/pallas_call | solution.py:21
  15.5 3.4 %all-to-all-start.1 = ((bf16[8,64,256]{2,1,0:T(8,128)(2,1)}), bf16[8,64,256]{2,1,0:T(8,128)(2,1)S(1)}, u32[]{:S(2)}, u32[]{:S(2)}) async-start(bf16[8,64,256]{2,1,0:T(8,128)(2,1)} %shard_map.105), calls=%async_computation.1 | async-start | bytes 524288 | tf_op jit(solution)/shard_map/all_to_all | solution.py:252
  18.9 2.9 %shard_map.106.x_ref.inc_t_ref = bf16[768,512]{1,0:T(8,128)(2,1)S(1)} custom-call(s32[1,8]{1,0:T(1,128)S(1)} %copy-done.8, s32[32,512]{1,0:T(8,128)S(1)} %bitcast.7), custom_call_target="tpu_custom_call" | custom-call | tf_op jit(solution)/shard_map/pallas_call | solution.py:21
  21.8 0.3 shard_map.107.inc_ref
  22.1 5.0 %all-to-all-done.1.rows_ref.own_ref = bf16[8,64,256]{2,1,0:T(8,128)(2,1)S(1)} async-done(((bf16[8,64,256]{2,1,0:T(8,128)(2,1)}), bf16[8,64,256]{2,1,0:T(8,128)(2,1)S(1)}, u32[]{:S(2)}, u32[]{:S(2)}) %all-to-all-start.1) | async-done | bytes 262176 | tf_op jit(solution)/shard_map/all_to_all | solution.py:252
  27.1 0.1 collective-permute-start
  27.2 1.3 %collective-permute-done.mate_ref = bf16[8,32,256]{2,1,0:T(8,128)(2,1)S(1)} collective-permute-done((bf16[8,32,256]{2,1,0:T(8,128)(2,1)S(1)}, bf16[8,32,256]{2,1,0:T(8,128)(2,1)S(1)}, u32[]{:S(2)}, u32[]{:S(2)}) %collective-permute-start) | collective-permute-done | bytes 131104 | tf_op jit(solution)/shard_map/ppermute | solution.py:256
  28.5 1.6 %copy-done.2 = bf16[256,4096]{1,0:T(8,128)(2,1)S(1)} copy-done((bf16[256,4096]{1,0:T(8,128)(2,1)S(1)}, bf16[256,4096]{1,0:T(8,128)(2,1)}, u32[]{:S(2)}) %copy-start.2) | copy-done | bytes 2097176
  30.1 4.5 %shard_map.109.dpooled_ref = bf16[512,256]{1,0:T(8,128)(2,1)S(1)} custom-call(f32[4,128]{1,0:T(4,128)S(1)} %bitcast.14, bf16[512,768]{1,0:T(8,128)(2,1)S(1)} %shard_map.107.inc_ref, bf16[8,64,256]{2,1,0:T(8,128)(2,1)S(1)} %all-to-all-done.1.rows_ref.own_ref, bf16[8,32,256]{2,1,0:T(8,128)(2,1)S(1)} %collective-permute-done.mate_ref, ...), custom_call_target="tpu_custom_call" | custom-call | tf_op jit(solution)/shard_map/pallas_call | solution.py:21
  34.6 0.4 shard_map.110
  35.0 0.2 collective-permute-start.1
  35.2 1.2 %collective-permute-done.1.got_ref = bf16[8,32,256]{2,1,0:T(8,128)(2,1)S(1)} collective-permute-done((bf16[8,32,256]{2,1,0:T(8,128)(2,1)S(1)}, bf16[8,32,256]{2,1,0:T(8,128)(2,1)S(1)}, u32[]{:S(2)}, u32[]{:S(2)}) %collective-permute-start.1) | collective-permute-done | bytes 131104 | tf_op jit(solution)/shard_map/ppermute | solution.py:256
  36.5 12.1 %all_to_all.21.back_ref = bf16[8,64,256]{2,1,0:T(8,128)(2,1)S(1)} all-to-all(bf16[8,64,256]{2,1,0:T(8,128)(2,1)S(1)} %shard_map.111), channel_id=1, replica_groups=mesh['dp'=4,'table'=8] {'table'}, dimensions={0} | all-to-all | bytes 524288 | tf_op jit(solution)/shard_map/all_to_all | solution.py:252
  48.6 0.1 shard_map.112.refs_0_
  48.7 1.6 %collective-permute-start.2 = (bf16[304,256]{1,0:T(8,128)(2,1)S(1)}, bf16[304,256]{1,0:T(8,128)(2,1)S(1)}, u32[]{:S(2)}, u32[]{:S(2)}) collective-permute-start(bf16[304,256]{1,0:T(8,128)(2,1)S(1)} %shard_map.112.refs_0_), channel_id=1, source_target_pairs={{0,16},{8,24},{16,0},{24,8},{1,17},{9,25},{17,1},{25,9},{2,18},{10... | collective-permute-start | bytes 466952 | tf_op jit(solution)/shard_map/ppermute | solution.py:256
  50.2 3.7 %collective-permute-done.2.refs_1_ = bf16[304,256]{1,0:T(8,128)(2,1)S(1)} collective-permute-done((bf16[304,256]{1,0:T(8,128)(2,1)S(1)}, bf16[304,256]{1,0:T(8,128)(2,1)S(1)}, u32[]{:S(2)}, u32[]{:S(2)}) %collective-permute-start.2) | collective-permute-done | bytes 155680 | tf_op jit(solution)/shard_map/ppermute | solution.py:256
  54.0 0.7 %shard_map.113.grad_ref = f32[1024,256]{1,0:T(8,128)S(1)} custom-call(s32[1,64]{1,0:T(1,128)S(1)} %bitcast.11, bf16[304,256]{1,0:T(8,128)(2,1)S(1)} %shard_map.112.refs_0_, bf16[304,256]{1,0:T(8,128)(2,1)S(1)} %collective-permute-done.2.refs_1_), custom_call_target="tpu_custom_call" | custom-call | tf_op jit(solution)/shard_map/pallas_call | solution.py:21
  54.6 0.7 %collective-permute-done.4.refs_1_ = bf16[304,256]{1,0:T(8,128)(2,1)S(1)} collective-permute-done((bf16[304,256]{1,0:T(8,128)(2,1)S(1)}, bf16[304,256]{1,0:T(8,128)(2,1)S(1)}, u32[]{:S(2)}, u32[]{:S(2)}) %collective-permute-start.4) | collective-permute-done | bytes 155680 | tf_op jit(solution)/shard_map/ppermute | solution.py:256
  55.3 2.7 %shard_map.114 = (f32[1024,256]{1,0:T(8,128)}, f32[8,128]{1,0:T(8,128)}) custom-call(s32[1,64]{1,0:T(1,128)S(1)} %bitcast.12, f32[8,128]{1,0:T(8,128)S(1)} %bitcast.13, f32[1024,256]{1,0:T(8,128)S(1)} %copy-done.1, f32[1024,256]{1,0:T(8,128)S(1)} %shard_map.113.grad_ref, bf16[304,256]{1,0:T(8,128)(2,1)S(1)} %collective-permute-done.3.refs_0_, ...), custom_call_target="tpu_custom_call" | custom-call | tf_op jit(solution)/shard_map/pallas_call | solution.py:21
  (23 shorter events, 0.1 us)
Async XLA Ops:
  0.6 18.3 %copy-start.8 = (s32[1,8]{1,0:T(1,128)S(1)}, s32[1,8]{1,0:T(1,128)}, u32[]{:S(2)}) copy-start(s32[1,8]{1,0:T(1,128)} %count_ref.1) | copy-start | bytes 100
  0.6 13.7 %all-to-all-start = ((s32[8,1,32]{2,1,0:T(1,128)}), s32[8,1,32]{2,1,0:T(1,128)S(1)}, u32[]{:S(2)}, u32[]{:S(2)}) async-start(s32[8,1,32]{2,1,0:T(1,128)} %bitcast.15), calls=%async_computation | async-start | bytes 8192 | tf_op jit(solution)/shard_map/all_to_all | solution.py:252
  7.9 1.2 %copy-start = (f32[1024,256]{1,0:T(8,128)S(1)}, f32[1024,256]{1,0:T(8,128)}, u32[]{:S(2)}) copy-start(f32[1024,256]{1,0:T(8,128)} %table_ref.3) | copy-start | bytes 3145732
  9.1 0.7 %copy-start.4 = (s32[64]{0:T(128)S(1)}, s32[64]{0:T(128)}, u32[]{:S(2)}) copy-start(s32[64]{0:T(128)} %param.15) | copy-start | bytes 772
  9.8 9.1 %copy-start.3 = (s32[512,32]{0,1:T(8,128)S(1)}, s32[512,32]{0,1:T(8,128)}, u32[]{:S(2)}) copy-start(s32[512,32]{0,1:T(8,128)} %param.9) | copy-start | bytes 196612
  10.2 16.9 %copy-start.9 = (bf16[4096]{0:T(1024)(128)(2,1)S(1)}, bf16[4096]{0:T(1024)(128)(2,1)}, u32[]{:S(2)}) copy-start(bf16[4096]{0:T(1024)(128)(2,1)} %param.17) | copy-start | bytes 24580
  14.3 14.2 %copy-start.7 = (f32[512]{0:T(512)S(1)}, f32[512]{0:T(512)}, u32[]{:S(2)}) copy-start(f32[512]{0:T(512)} %param.10) | copy-start | bytes 6148
  15.5 11.6 %all-to-all-start.1 = ((bf16[8,64,256]{2,1,0:T(8,128)(2,1)}), bf16[8,64,256]{2,1,0:T(8,128)(2,1)S(1)}, u32[]{:S(2)}, u32[]{:S(2)}) async-start(bf16[8,64,256]{2,1,0:T(8,128)(2,1)} %shard_map.105), calls=%async_computation.1 | async-start | bytes 524288 | tf_op jit(solution)/shard_map/all_to_all | solution.py:252
  27.1 1.4 %collective-permute-start = (bf16[8,32,256]{2,1,0:T(8,128)(2,1)S(1)}, bf16[8,32,256]{2,1,0:T(8,128)(2,1)S(1)}, u32[]{:S(2)}, u32[]{:S(2)}) collective-permute-start(bf16[8,32,256]{2,1,0:T(8,128)(2,1)S(1)} %shard_map.108), channel_id=1, source_target_pairs={{0,8},{8,0},{16,24},{24,16},{1,9},{9,1},{17,25},{25,17},{2,10},{10... | collective-permute-start | bytes 393224 | tf_op jit(solution)/shard_map/ppermute | solution.py:256
  28.5 1.6 %copy-start.2 = (bf16[256,4096]{1,0:T(8,128)(2,1)S(1)}, bf16[256,4096]{1,0:T(8,128)(2,1)}, u32[]{:S(2)}) copy-start(bf16[256,4096]{1,0:T(8,128)(2,1)} %w_in_ref.1) | copy-start | bytes 6291460
  34.6 19.4 %copy-start.5 = (s32[64]{0:T(128)S(1)}, s32[64]{0:T(128)}, u32[]{:S(2)}) copy-start(s32[64]{0:T(128)} %param.15) | copy-start | bytes 772
  34.6 20.8 %copy-start.1 = (f32[1024,256]{1,0:T(8,128)S(1)}, f32[1024,256]{1,0:T(8,128)}, u32[]{:S(2)}) copy-start(f32[1024,256]{1,0:T(8,128)} %table_ref.3) | copy-start | bytes 3145732
  34.6 20.7 %copy-start.6 = (f32[1024]{0:T(1024)S(1)}, f32[1024]{0:T(1024)}, u32[]{:S(2)}) copy-start(f32[1024]{0:T(1024)} %param.14) | copy-start | bytes 12292
  35.0 1.4 %collective-permute-start.1 = (bf16[8,32,256]{2,1,0:T(8,128)(2,1)S(1)}, bf16[8,32,256]{2,1,0:T(8,128)(2,1)S(1)}, u32[]{:S(2)}, u32[]{:S(2)}) collective-permute-start(bf16[8,32,256]{2,1,0:T(8,128)(2,1)S(1)} %get-tuple-element.17), channel_id=1, source_target_pairs={{0,8},{8,0},{16,24},{24,16},{1,9},{9,1},{17,25},{25,17},{2,10},{10... | collective-permute-start | bytes 393224 | tf_op jit(solution)/shard_map/ppermute | solution.py:256
  48.7 5.3 %collective-permute-start.2 = (bf16[304,256]{1,0:T(8,128)(2,1)S(1)}, bf16[304,256]{1,0:T(8,128)(2,1)S(1)}, u32[]{:S(2)}, u32[]{:S(2)}) collective-permute-start(bf16[304,256]{1,0:T(8,128)(2,1)S(1)} %shard_map.112.refs_0_), channel_id=1, source_target_pairs={{0,16},{8,24},{16,0},{24,8},{1,17},{9,25},{17,1},{25,9},{2,18},{10... | collective-permute-start | bytes 466952 | tf_op jit(solution)/shard_map/ppermute | solution.py:256
  50.2 4.4 %collective-permute-start.3 = (bf16[304,256]{1,0:T(8,128)(2,1)S(1)}, bf16[304,256]{1,0:T(8,128)(2,1)S(1)}, u32[]{:S(2)}, u32[]{:S(2)}) collective-permute-start(bf16[304,256]{1,0:T(8,128)(2,1)S(1)} %shard_map.112.refs_0_), channel_id=1, source_target_pairs={{0,8},{8,0},{16,24},{24,16},{1,9},{9,1},{17,25},{25,17},{2,10},{10... | collective-permute-start | bytes 466952 | tf_op jit(solution)/shard_map/ppermute | solution.py:256
  54.0 1.4 %collective-permute-start.4 = (bf16[304,256]{1,0:T(8,128)(2,1)S(1)}, bf16[304,256]{1,0:T(8,128)(2,1)S(1)}, u32[]{:S(2)}, u32[]{:S(2)}) collective-permute-start(bf16[304,256]{1,0:T(8,128)(2,1)S(1)} %collective-permute-done.2.refs_1_), channel_id=1, source_target_pairs={{0,8},{8,0},{16,24},{24,16},{1,9},{9,1},{17,25},{25,17},{2,10},{10... | collective-permute-start | bytes 466952 | tf_op jit(solution)/shard_map/ppermute | solution.py:256

commit v6 on v5

--- a/solution.py
+++ b/solution.py
@@ -1,4 +1,5 @@
 import functools
+import math
 
 import jax
 import jax.numpy as jnp
@@ -17,14 +18,16 @@
 TAIL = 16
 
 
-def call(body, outs, operands, scratch=(), in_specs=None, out_specs=None, mib=12):
+def call(body, outs, operands, scratch=(), in_specs=None, out_specs=None):
+    held = jax.tree.leaves((outs, operands)) + [x for x in scratch if getattr(x, "memory_space", None) == pltpu.VMEM]
+    limit = sum(math.prod(x.shape) * jnp.dtype(x.dtype).itemsize for x in held) + 4 * 1024 * 1024
     return pl.pallas_call(
         body,
         out_shape=outs,
         in_specs=in_specs or [VMEM] * len(operands),
         out_specs=out_specs or jax.tree.map(lambda _: VMEM, outs),
         scratch_shapes=list(scratch),
-        compiler_params=pltpu.CompilerParams(vmem_limit_bytes=mib * 1024 * 1024),
+        compiler_params=pltpu.CompilerParams(vmem_limit_bytes=limit),
     )(*operands)
 
 
@@ -119,15 +122,17 @@
     labels = jnp.concatenate([labels[:, k:k + 1] for k in range(labels.shape[1])], axis=0)
     pooled = jnp.dot(inc_ref[...], rows[...], preferred_element_type=f32).astype(bf16)
     size, step, wide = batch // 2, 512, 2048
+    w_out = w_out_ref[...].astype(f32)
+    w_out = [lanes([w_out[k:k + 1, :] for k in range(r, r + step // 128)]) for r in range(0, hidden_units // 128, step // 128)]
     for at in range(0, batch, size):
         samples = slice(at, at + size)
         total = jnp.zeros((size, 128), f32)
         for start in range(0, hidden_units, step):
             cols = slice(start, start + step)
             pre_act = jnp.dot(pooled[samples], w_in_ref[:, cols], preferred_element_type=f32)
-            w_out = w_out_ref[:, cols].astype(f32)
-            gated[samples, cols] = jnp.where(pre_act > 0, w_out, 0.0).astype(bf16)
-            term = jnp.maximum(pre_act, 0.0).astype(bf16).astype(f32) * w_out
+            own = w_out[start // step]
+            gated[samples, cols] = jnp.where(pre_act > 0, own, 0.0).astype(bf16)
+            term = jnp.maximum(pre_act, 0.0).astype(bf16).astype(f32) * own
             for k in range(0, step, 128):
                 total += term[:, k:k + 128]
         logit = jnp.sum(total, axis=1, keepdims=True)
@@ -211,27 +216,30 @@
     row_grads(core(), hot_ref, part_refs, held, put, out_ref.shape[0])
 
 
-def adagrad(table, own_sum, grad):
-    new_sum = own_sum + jnp.sum(grad * grad, axis=1, keepdims=True) * (1.0 / grad.shape[1])
-    return table - grad * (learning_rate / jnp.sqrt(new_sum)), new_sum
-
-
 def update_body(hot_ref, sum_ref, table_ref, grad_ref, *refs):
-    part_refs, (new_table_ref, new_sum_ref, held, sums, staged, sems) = refs[:-6], refs[-6:]
-    own_sum = sum_ref[...].T
-    piece = table_ref.shape[0] // 2
-    copies = []
+    part_refs, (new_table_ref, new_sum_ref, held, squares, grads, staged, sums, sems) = refs[:-8], refs[-8:]
+    rows, width = table_ref.shape
+    step = 128
 
     def put(at, grad):
-        k = at.start // 128
-        staged[at, :], sums[:, k:k + 1] = adagrad(table_ref[at, :], own_sum[:, k:k + 1], grad_ref[at, :] + grad)
-        if at.stop % piece == 0:
-            done = slice(at.stop - piece, at.stop)
+        grad = grad_ref[at, :] + grad
+        grads[at, :] = grad
+        squares[:, at.start // step:at.stop // step] = jnp.sum(grad * grad, axis=1, keepdims=True)
+
+    row_grads(1 - core(), hot_ref, part_refs, held, put, rows)
+    new_sum = sum_ref[...] + squares[...].T * (1.0 / width)
+    sums[...] = new_sum
+    copies = [pltpu.make_async_copy(sums, new_sum_ref, sems.at[0])]
+    copies[0].start()
+    scale = (learning_rate / jnp.sqrt(new_sum)).T
+    for start in range(0, rows, step):
+        at = slice(start, start + step)
+        k = start // step
+        staged[at, :] = table_ref[at, :] - grads[at, :] * scale[:, k:k + 1]
+        if at.stop % (rows // 2) == 0:
+            done = slice(at.stop - rows // 2, at.stop)
             copies.append(pltpu.make_async_copy(staged.at[done], new_table_ref.at[done], sems.at[len(copies)]))
             copies[-1].start()
-
-    row_grads(1 - core(), hot_ref, part_refs, held, put, table_ref.shape[0])
-    new_sum_ref[...] = sums[...].T
     for copy in copies:
         copy.wait()
 
@@ -300,9 +308,8 @@
     dpooled = call(
         top_body,
         shape((batch, width), bf16),
-        (labels.reshape(-1, 128), inc, own_rows, mate_rows, w_in, w_out.reshape(1, -1)),
+        (labels.reshape(-1, 128), inc, own_rows, mate_rows, w_in, w_out.reshape(-1, 128)),
         [pltpu.VMEM((batch, hidden_units), bf16), pltpu.VMEM((vocab, width), bf16)],
-        mib=24,
     )
     part, to_mate = call(
         slot_grads_body,
@@ -331,15 +338,17 @@
                 held,
                 pltpu.VMEM((128, rows // 128), f32),
                 pltpu.VMEM((rows, width), f32),
-                pltpu.SemaphoreType.DMA((2,)),
+                pltpu.VMEM((rows, width), f32),
+                pltpu.VMEM((rows // 128, 128), f32),
+                pltpu.SemaphoreType.DMA((3,)),
             ],
-            out_specs=(HBM, VMEM),
+            out_specs=(HBM, HBM),
         )
         return new_table, new_sum.reshape(rows)
     grad = call(dense_body, shape((rows, width), bf16), (hot_row, asked, returned))
     grad = lax.psum(grad, "dp").astype(f32)
-    new_table, new_sum = adagrad(table, adagrad_sum[:, None], grad)
-    return new_table, new_sum[:, 0]
+    new_sum = adagrad_sum + jnp.mean(grad * grad, axis=1)
+    return table - learning_rate * grad / jnp.sqrt(new_sum)[:, None], new_sum
 
 
 def solution(mesh):

time: 58.5 us -> 57.8 us (0.988)
  Pallas kernels: 13.1 us -> 12.5 us
    pallas_call x11, Pallas kernels: 13.1 us -> 12.5 us  [call(): pl.pallas_call(body, out_shape=outs, in_specs=in_specs or [VMEM] * len(op...]
where the time goes in v6:
time: 57.8 us; the launch traced here: 57.4 us
  waiting for transfers between devices  16 us (28%)
  starting transfers between devices  12.6 us (22%)
  Pallas kernels  12.5 us (22%)
  blocking collectives  12.1 us (21%)
  local copies, waits for them, and re-layouts  3.51 us (6%)
  between operations  0.78 us (1%)
    pallas_call x11, Pallas kernels, call(): pl.pallas_call(body, out_shape=outs, in_specs=in_specs or [VMEM] * len(op...  12.5 us
    all_to_all x1, blocking collectives, exchange(): return lax.all_to_all(x, 'table', split_axis=0, concat_axis=0, tiled=True)  12.1 us
    all_to_all x2, starting transfers between devices, exchange(): return lax.all_to_all(x, 'table', split_axis=0, concat_axis=0, tiled=True)  10.7 us
    all_to_all x2, waiting for transfers between devices, exchange(): return lax.all_to_all(x, 'table', split_axis=0, concat_axis=0, tiled=True)  9.05 us
    ppermute x5, waiting for transfers between devices, swap(): lax.ppermute(x, 'dp', [(g, g ^ bit) for g in range(lax.axis_size('dp'))])  6.93 us
    unnamed x20, local copies, waits for them, and re-layouts  3.51 us
    ppermute x5, starting transfers between devices, swap(): lax.ppermute(x, 'dp', [(g, g ^ bit) for g in range(lax.axis_size('dp'))])  1.86 us
  transfers between devices with their start and end apart: 7, of which 6 were waited for; matrix products, arithmetic and copies ran while one was open for 0% of the time, Pallas kernels for 7%

profile of v6, /device:TPU:0, one launch (start us, length us, event | category | flops | bytes accessed | tf_op | source)
XLA Modules:
  0.0 57.4 jit_solution(5640888571174337783)
XLA Ops:
  0.6 7.3 %all-to-all-start = ((s32[8,1,32]{2,1,0:T(1,128)}), s32[8,1,32]{2,1,0:T(1,128)S(1)}, u32[]{:S(2)}, u32[]{:S(2)}) async-start(s32[8,1,32]{2,1,0:T(1,128)} %bitcast.17), calls=%async_computation | async-start | bytes 8192 | tf_op jit(solution)/shard_map/all_to_all | solution.py:260
  7.9 1.2 %copy-done = f32[1024,256]{1,0:T(8,128)S(1)} copy-done((f32[1024,256]{1,0:T(8,128)S(1)}, f32[1024,256]{1,0:T(8,128)}, u32[]{:S(2)}) %copy-start) | copy-done | bytes 1048600
  9.1 0.7 %copy-done.5 = s32[64]{0:T(128)S(1)} copy-done((s32[64]{0:T(128)S(1)}, s32[64]{0:T(128)}, u32[]{:S(2)}) %copy-start.5) | copy-done | bytes 280
  9.8 0.4 shard_map.104
  10.2 4.1 %all-to-all-done = s32[8,1,32]{2,1,0:T(1,128)S(1)} async-done(((s32[8,1,32]{2,1,0:T(1,128)}), s32[8,1,32]{2,1,0:T(1,128)S(1)}, u32[]{:S(2)}, u32[]{:S(2)}) %all-to-all-start) | async-done | bytes 1056 | tf_op jit(solution)/shard_map/all_to_all | solution.py:260
  14.3 1.2 %shard_map.105 = bf16[8,64,256]{2,1,0:T(8,128)(2,1)} custom-call(s32[8,32]{1,0:T(8,128)S(1)} %bitcast.9, bf16[64,256]{1,0:T(8,128)(2,1)S(1)} %get-tuple-element.11.hot_ref, bf16[1024,256]{1,0:T(8,128)(2,1)S(1)} %get-tuple-element.12.table_ref), custom_call_target="tpu_custom_call" | custom-call | tf_op jit(solution)/shard_map/pallas_call | solution.py:24
  15.5 3.4 %all-to-all-start.1 = ((bf16[8,64,256]{2,1,0:T(8,128)(2,1)}), bf16[8,64,256]{2,1,0:T(8,128)(2,1)S(1)}, u32[]{:S(2)}, u32[]{:S(2)}) async-start(bf16[8,64,256]{2,1,0:T(8,128)(2,1)} %shard_map.105), calls=%async_computation.1 | async-start | bytes 524288 | tf_op jit(solution)/shard_map/all_to_all | solution.py:260
  18.9 2.9 %shard_map.106.x_ref.inc_t_ref = bf16[768,512]{1,0:T(8,128)(2,1)S(1)} custom-call(s32[1,8]{1,0:T(1,128)S(1)} %copy-done.9, s32[32,512]{1,0:T(8,128)S(1)} %bitcast.8), custom_call_target="tpu_custom_call" | custom-call | tf_op jit(solution)/shard_map/pallas_call | solution.py:24
  21.8 0.3 shard_map.107.inc_ref
  22.1 5.0 %all-to-all-done.1.rows_ref.own_ref = bf16[8,64,256]{2,1,0:T(8,128)(2,1)S(1)} async-done(((bf16[8,64,256]{2,1,0:T(8,128)(2,1)}), bf16[8,64,256]{2,1,0:T(8,128)(2,1)S(1)}, u32[]{:S(2)}, u32[]{:S(2)}) %all-to-all-start.1) | async-done | bytes 262176 | tf_op jit(solution)/shard_map/all_to_all | solution.py:260
  27.1 0.1 collective-permute-start
  27.1 1.3 %collective-permute-done.mate_ref = bf16[8,32,256]{2,1,0:T(8,128)(2,1)S(1)} collective-permute-done((bf16[8,32,256]{2,1,0:T(8,128)(2,1)S(1)}, bf16[8,32,256]{2,1,0:T(8,128)(2,1)S(1)}, u32[]{:S(2)}, u32[]{:S(2)}) %collective-permute-start) | collective-permute-done | bytes 131104 | tf_op jit(solution)/shard_map/ppermute | solution.py:264
  28.5 1.6 %copy-done.2 = bf16[256,4096]{1,0:T(8,128)(2,1)S(1)} copy-done((bf16[256,4096]{1,0:T(8,128)(2,1)S(1)}, bf16[256,4096]{1,0:T(8,128)(2,1)}, u32[]{:S(2)}) %copy-start.2) | copy-done | bytes 2097176
  30.1 4.4 %shard_map.109.dpooled_ref = bf16[512,256]{1,0:T(8,128)(2,1)S(1)} custom-call(f32[4,128]{1,0:T(4,128)S(1)} %bitcast.16, bf16[512,768]{1,0:T(8,128)(2,1)S(1)} %shard_map.107.inc_ref, bf16[8,64,256]{2,1,0:T(8,128)(2,1)S(1)} %all-to-all-done.1.rows_ref.own_ref, bf16[8,32,256]{2,1,0:T(8,128)(2,1)S(1)} %collective-permute-done.mate_ref, ...), custom_call_target="tpu_custom_call" | custom-call | tf_op jit(solution)/shard_map/pallas_call | solution.py:24
  34.5 0.4 shard_map.110
  34.9 0.2 collective-permute-start.1
  35.2 1.2 %collective-permute-done.1.got_ref = bf16[8,32,256]{2,1,0:T(8,128)(2,1)S(1)} collective-permute-done((bf16[8,32,256]{2,1,0:T(8,128)(2,1)S(1)}, bf16[8,32,256]{2,1,0:T(8,128)(2,1)S(1)}, u32[]{:S(2)}, u32[]{:S(2)}) %collective-permute-start.1) | collective-permute-done | bytes 131104 | tf_op jit(solution)/shard_map/ppermute | solution.py:264
  36.4 12.1 %all_to_all.21.back_ref = bf16[8,64,256]{2,1,0:T(8,128)(2,1)S(1)} all-to-all(bf16[8,64,256]{2,1,0:T(8,128)(2,1)S(1)} %shard_map.111), channel_id=1, replica_groups=mesh['dp'=4,'table'=8] {'table'}, dimensions={0} | all-to-all | bytes 524288 | tf_op jit(solution)/shard_map/all_to_all | solution.py:260
  48.5 0.1 shard_map.112.refs_0_
  48.6 1.6 %collective-permute-start.2 = (bf16[304,256]{1,0:T(8,128)(2,1)S(1)}, bf16[304,256]{1,0:T(8,128)(2,1)S(1)}, u32[]{:S(2)}, u32[]{:S(2)}) collective-permute-start(bf16[304,256]{1,0:T(8,128)(2,1)S(1)} %shard_map.112.refs_0_), channel_id=1, source_target_pairs={{0,16},{8,24},{16,0},{24,8},{1,17},{9,25},{17,1},{25,9},{2,18},{10... | collective-permute-start | bytes 466952 | tf_op jit(solution)/shard_map/ppermute | solution.py:264
  50.2 3.7 %collective-permute-done.2.refs_1_ = bf16[304,256]{1,0:T(8,128)(2,1)S(1)} collective-permute-done((bf16[304,256]{1,0:T(8,128)(2,1)S(1)}, bf16[304,256]{1,0:T(8,128)(2,1)S(1)}, u32[]{:S(2)}, u32[]{:S(2)}) %collective-permute-start.2) | collective-permute-done | bytes 155680 | tf_op jit(solution)/shard_map/ppermute | solution.py:264
  53.9 0.7 %shard_map.113.grad_ref = f32[1024,256]{1,0:T(8,128)S(1)} custom-call(s32[1,64]{1,0:T(1,128)S(1)} %bitcast.13, bf16[304,256]{1,0:T(8,128)(2,1)S(1)} %shard_map.112.refs_0_, bf16[304,256]{1,0:T(8,128)(2,1)S(1)} %collective-permute-done.2.refs_1_), custom_call_target="tpu_custom_call" | custom-call | tf_op jit(solution)/shard_map/pallas_call | solution.py:24
  54.6 0.7 %collective-permute-done.4.refs_1_ = bf16[304,256]{1,0:T(8,128)(2,1)S(1)} collective-permute-done((bf16[304,256]{1,0:T(8,128)(2,1)S(1)}, bf16[304,256]{1,0:T(8,128)(2,1)S(1)}, u32[]{:S(2)}, u32[]{:S(2)}) %collective-permute-start.4) | collective-permute-done | bytes 155680 | tf_op jit(solution)/shard_map/ppermute | solution.py:264
  55.3 2.2 %shard_map.114 = (f32[1024,256]{1,0:T(8,128)}, f32[8,128]{1,0:T(8,128)}) custom-call(s32[1,64]{1,0:T(1,128)S(1)} %bitcast.14, f32[8,128]{1,0:T(8,128)S(1)} %bitcast.15, f32[1024,256]{1,0:T(8,128)S(1)} %copy-done.1, f32[1024,256]{1,0:T(8,128)S(1)} %shard_map.113.grad_ref, bf16[304,256]{1,0:T(8,128)(2,1)S(1)} %collective-permute-done.3.refs_0_, ...), custom_call_target="tpu_custom_call" | custom-call | tf_op jit(solution)/shard_map/pallas_call | solution.py:24
  (22 shorter events, 0.1 us)
Async XLA Ops:
  0.6 18.3 %copy-start.9 = (s32[1,8]{1,0:T(1,128)S(1)}, s32[1,8]{1,0:T(1,128)}, u32[]{:S(2)}) copy-start(s32[1,8]{1,0:T(1,128)} %count_ref.1) | copy-start | bytes 100
  0.6 13.7 %all-to-all-start = ((s32[8,1,32]{2,1,0:T(1,128)}), s32[8,1,32]{2,1,0:T(1,128)S(1)}, u32[]{:S(2)}, u32[]{:S(2)}) async-start(s32[8,1,32]{2,1,0:T(1,128)} %bitcast.17), calls=%async_computation | async-start | bytes 8192 | tf_op jit(solution)/shard_map/all_to_all | solution.py:260
  7.9 1.2 %copy-start = (f32[1024,256]{1,0:T(8,128)S(1)}, f32[1024,256]{1,0:T(8,128)}, u32[]{:S(2)}) copy-start(f32[1024,256]{1,0:T(8,128)} %table_ref.3) | copy-start | bytes 3145732
  9.1 0.7 %copy-start.5 = (s32[64]{0:T(128)S(1)}, s32[64]{0:T(128)}, u32[]{:S(2)}) copy-start(s32[64]{0:T(128)} %param.15) | copy-start | bytes 772
  9.8 9.1 %copy-start.3 = (s32[512,32]{0,1:T(8,128)S(1)}, s32[512,32]{0,1:T(8,128)}, u32[]{:S(2)}) copy-start(s32[512,32]{0,1:T(8,128)} %param.9) | copy-start | bytes 196612
  10.2 18.3 %copy-start.4 = (bf16[4096]{0:T(1024)(128)(2,1)S(1)}, bf16[4096]{0:T(1024)(128)(2,1)}, u32[]{:S(2)}) copy-start(bf16[4096]{0:T(1024)(128)(2,1)} %param.17) | copy-start | bytes 24580
  10.2 18.3 %copy-start.8 = (f32[512]{0:T(512)S(1)}, f32[512]{0:T(512)}, u32[]{:S(2)}) copy-start(f32[512]{0:T(512)} %param.10) | copy-start | bytes 6148
  15.5 11.6 %all-to-all-start.1 = ((bf16[8,64,256]{2,1,0:T(8,128)(2,1)}), bf16[8,64,256]{2,1,0:T(8,128)(2,1)S(1)}, u32[]{:S(2)}, u32[]{:S(2)}) async-start(bf16[8,64,256]{2,1,0:T(8,128)(2,1)} %shard_map.105), calls=%async_computation.1 | async-start | bytes 524288 | tf_op jit(solution)/shard_map/all_to_all | solution.py:260
  27.1 1.4 %collective-permute-start = (bf16[8,32,256]{2,1,0:T(8,128)(2,1)S(1)}, bf16[8,32,256]{2,1,0:T(8,128)(2,1)S(1)}, u32[]{:S(2)}, u32[]{:S(2)}) collective-permute-start(bf16[8,32,256]{2,1,0:T(8,128)(2,1)S(1)} %shard_map.108), channel_id=1, source_target_pairs={{0,8},{8,0},{16,24},{24,16},{1,9},{9,1},{17,25},{25,17},{2,10},{10... | collective-permute-start | bytes 393224 | tf_op jit(solution)/shard_map/ppermute | solution.py:264
  28.5 1.6 %copy-start.2 = (bf16[256,4096]{1,0:T(8,128)(2,1)S(1)}, bf16[256,4096]{1,0:T(8,128)(2,1)}, u32[]{:S(2)}) copy-start(bf16[256,4096]{1,0:T(8,128)(2,1)} %w_in_ref.1) | copy-start | bytes 6291460
  34.5 19.4 %copy-start.6 = (s32[64]{0:T(128)S(1)}, s32[64]{0:T(128)}, u32[]{:S(2)}) copy-start(s32[64]{0:T(128)} %param.15) | copy-start | bytes 772
  34.5 20.7 %copy-start.1 = (f32[1024,256]{1,0:T(8,128)S(1)}, f32[1024,256]{1,0:T(8,128)}, u32[]{:S(2)}) copy-start(f32[1024,256]{1,0:T(8,128)} %table_ref.3) | copy-start | bytes 3145732
  34.5 20.7 %copy-start.7 = (f32[1024]{0:T(1024)S(1)}, f32[1024]{0:T(1024)}, u32[]{:S(2)}) copy-start(f32[1024]{0:T(1024)} %param.14) | copy-start | bytes 12292
  34.9 1.4 %collective-permute-start.1 = (bf16[8,32,256]{2,1,0:T(8,128)(2,1)S(1)}, bf16[8,32,256]{2,1,0:T(8,128)(2,1)S(1)}, u32[]{:S(2)}, u32[]{:S(2)}) collective-permute-start(bf16[8,32,256]{2,1,0:T(8,128)(2,1)S(1)} %get-tuple-element.17), channel_id=1, source_target_pairs={{0,8},{8,0},{16,24},{24,16},{1,9},{9,1},{17,25},{25,17},{2,10},{10... | collective-permute-start | bytes 393224 | tf_op jit(solution)/shard_map/ppermute | solution.py:264
  48.6 5.3 %collective-permute-start.2 = (bf16[304,256]{1,0:T(8,128)(2,1)S(1)}, bf16[304,256]{1,0:T(8,128)(2,1)S(1)}, u32[]{:S(2)}, u32[]{:S(2)}) collective-permute-start(bf16[304,256]{1,0:T(8,128)(2,1)S(1)} %shard_map.112.refs_0_), channel_id=1, source_target_pairs={{0,16},{8,24},{16,0},{24,8},{1,17},{9,25},{17,1},{25,9},{2,18},{10... | collective-permute-start | bytes 466952 | tf_op jit(solution)/shard_map/ppermute | solution.py:264
  50.2 4.4 %collective-permute-start.3 = (bf16[304,256]{1,0:T(8,128)(2,1)S(1)}, bf16[304,256]{1,0:T(8,128)(2,1)S(1)}, u32[]{:S(2)}, u32[]{:S(2)}) collective-permute-start(bf16[304,256]{1,0:T(8,128)(2,1)S(1)} %shard_map.112.refs_0_), channel_id=1, source_target_pairs={{0,8},{8,0},{16,24},{24,16},{1,9},{9,1},{17,25},{25,17},{2,10},{10... | collective-permute-start | bytes 466952 | tf_op jit(solution)/shard_map/ppermute | solution.py:264
  53.9 1.4 %collective-permute-start.4 = (bf16[304,256]{1,0:T(8,128)(2,1)S(1)}, bf16[304,256]{1,0:T(8,128)(2,1)S(1)}, u32[]{:S(2)}, u32[]{:S(2)}) collective-permute-start(bf16[304,256]{1,0:T(8,128)(2,1)S(1)} %collective-permute-done.2.refs_1_), channel_id=1, source_target_pairs={{0,8},{8,0},{16,24},{24,16},{1,9},{9,1},{17,25},{25,17},{2,10},{10... | collective-permute-start | bytes 466952 | tf_op jit(solution)/shard_map/ppermute | solution.py:264

commit v7 on v6

--- a/solution.py
+++ b/solution.py
@@ -39,7 +39,7 @@
     return (lax.broadcasted_iota(i32, shape, axis) + start == ids).astype(f32).astype(bf16)
 
 
-def incidence_body(hot_cols, slot_cap, count_ref, slots_ref, inc_t_ref):
+def incidence_body(hot_cols, slot_cap, count_ref, slots_ref, out_ref, inc_t_ref):
     vocab, batch = inc_t_ref.shape
     field = vocab // FIELDS
     step = 128
@@ -58,10 +58,7 @@
     for owner in range((vocab - hot_cols) // slot_cap):
         rows = pl.ds(hot_cols + owner * slot_cap, slot_cap)
         inc_t_ref[rows, :] = jnp.where(place < count_ref[0, owner], inc_t_ref[rows, :].astype(f32), 0.0).astype(bf16)
-
-
-def transpose_body(x_ref, out_ref):
-    out_ref[...] = x_ref[...].T
+    out_ref[...] = inc_t_ref[...].T
 
 
 def core():
@@ -106,7 +103,7 @@
     out_ref[...] = rows_ref[:, 0:out_ref.shape[1], :]
 
 
-def top_body(labels_ref, inc_ref, own_ref, mate_ref, w_in_ref, w_out_ref, out_ref, gated, rows):
+def top_body(labels_ref, inc_ref, own_ref, mate_ref, w_in_ref, w_out_ref, out_ref, gated, rows, pooled, total, dlogit):
     batch = inc_ref.shape[0]
     hidden_units, width = w_in_ref.shape[1], w_in_ref.shape[0]
     owners, half, _ = mate_ref.shape
@@ -114,47 +111,58 @@
     hot_cols = owners * hot_dev
     slot_cap = own_ref.shape[1] - half
     me = core()
-    for t in range(owners):
-        rows[half_rows(t, hot_dev, me), :] = own_ref[t, 0:half, :]
-        rows[half_rows(t, hot_dev, 1 - me), :] = mate_ref[t, 0:half, :]
-        rows[hot_cols + t * slot_cap:hot_cols + (t + 1) * slot_cap, :] = own_ref[t, half:, :]
-    labels = labels_ref[...].T
-    labels = jnp.concatenate([labels[:, k:k + 1] for k in range(labels.shape[1])], axis=0)
-    pooled = jnp.dot(inc_ref[...], rows[...], preferred_element_type=f32).astype(bf16)
-    size, step, wide = batch // 2, 512, 2048
-    w_out = w_out_ref[...].astype(f32)
-    w_out = [lanes([w_out[k:k + 1, :] for k in range(r, r + step // 128)]) for r in range(0, hidden_units // 128, step // 128)]
-    for at in range(0, batch, size):
-        samples = slice(at, at + size)
-        total = jnp.zeros((size, 128), f32)
+    step, wide = 512, 2048
+
+    def stage(body):
+        pl.when(me >= 0)(body)
+
+    @stage
+    def pool():
+        for t in range(owners):
+            rows[half_rows(t, hot_dev, me), :] = own_ref[t, 0:half, :]
+            rows[half_rows(t, hot_dev, 1 - me), :] = mate_ref[t, 0:half, :]
+            rows[hot_cols + t * slot_cap:hot_cols + (t + 1) * slot_cap, :] = own_ref[t, half:, :]
+        pooled[...] = jnp.dot(inc_ref[...], rows[...], preferred_element_type=f32).astype(bf16)
+
+    @stage
+    def forward():
+        w_out = w_out_ref[...].astype(f32)
+        acc = jnp.zeros((batch, 128), f32)
         for start in range(0, hidden_units, step):
             cols = slice(start, start + step)
-            pre_act = jnp.dot(pooled[samples], w_in_ref[:, cols], preferred_element_type=f32)
-            own = w_out[start // step]
-            gated[samples, cols] = jnp.where(pre_act > 0, own, 0.0).astype(bf16)
+            pre_act = jnp.dot(pooled[...], w_in_ref[:, cols], preferred_element_type=f32)
+            own = lanes([w_out[k:k + 1, :] for k in range(start // 128, (start + step) // 128)])
+            gated[:, cols] = jnp.where(pre_act > 0, own, 0.0).astype(bf16)
             term = jnp.maximum(pre_act, 0.0).astype(bf16).astype(f32) * own
             for k in range(0, step, 128):
-                total += term[:, k:k + 128]
-        logit = jnp.sum(total, axis=1, keepdims=True)
-        dlogit = jnp.broadcast_to(jax.nn.sigmoid(logit) - labels[samples], (size, 128))
-        grad = jnp.zeros((size, width), f32)
+                acc += term[:, k:k + 128]
+        total[...] = acc
+
+    @stage
+    def backward():
+        blocks = batch // 128
+        logit = lanes([jnp.sum(total[k * 128:(k + 1) * 128, :], axis=1, keepdims=True) for k in range(blocks)])
+        delta = jax.nn.sigmoid(logit) - labels_ref[...].T
+        for k in range(blocks):
+            dlogit[k * 128:(k + 1) * 128, :] = jnp.broadcast_to(delta[:, k:k + 1], (128, 128))
+        grad = jnp.zeros((batch, width), f32)
         for start in range(0, hidden_units, wide):
             dhidden = lanes([
-                (dlogit * gated[samples, k:k + 128].astype(f32)).astype(bf16) for k in range(start, start + wide, 128)
+                (dlogit[...] * gated[:, k:k + 128].astype(f32)).astype(bf16) for k in range(start, start + wide, 128)
             ])
             grad += lax.dot_general(
                 dhidden, w_in_ref[:, start:start + wide], (((1,), (1,)), ((), ())), preferred_element_type=f32
             )
-        out_ref[samples, :] = grad.astype(bf16)
-
-
-def slot_grads_body(inc_t_ref, dpooled_ref, part_ref, send_ref, rows):
+        out_ref[...] = grad.astype(bf16)
+
+
+def slot_grads_body(inc_ref, dpooled_ref, part_ref, send_ref, rows):
     owners, half, _ = send_ref.shape
     hot_dev = 2 * half
     hot_cols = owners * hot_dev
     slot_cap = part_ref.shape[1] - half
     me = core()
-    rows[...] = jnp.dot(inc_t_ref[...], dpooled_ref[...], preferred_element_type=f32).astype(bf16)
+    rows[...] = jnp.dot(inc_ref[...].T, dpooled_ref[...], preferred_element_type=f32).astype(bf16)
     for t in range(owners):
         send_ref[t] = rows[half_rows(t, hot_dev, 1 - me), :]
         part_ref[t, 0:half, :] = rows[half_rows(t, hot_dev, me), :]
@@ -184,7 +192,7 @@
     return jnp.where(which == 0, hot_ref[:, 0:half], hot_ref[:, half:])
 
 
-def row_grads(which, hot_ref, part_refs, held, put, rows):
+def row_grads(which, hot_ref, part_refs, held, put, pieces):
     size = part_refs[0].shape[0]
     half = hot_ref.shape[1] // 2
     me = lax.div(lax.axis_index("dp"), 2)
@@ -199,12 +207,14 @@
         ids.append(digits[0:1, :] * 256 + digits[1:2, :])
         parts.append(held[g * size + half:(g + 1) * size - TAIL, :])
     step = 128
-    for start in range(0, rows, step):
-        grad = 0.0
-        for k in range(len(ids)):
-            pick = one_hot(ids[k], (step, ids[k].shape[1]), 0, start)
-            grad += jnp.dot(pick, parts[k], preferred_element_type=f32)
-        put(slice(start, start + step), grad)
+    for piece, done in pieces:
+        for start in range(piece.start, piece.stop, step):
+            grad = 0.0
+            for k in range(len(ids)):
+                pick = one_hot(ids[k], (step, ids[k].shape[1]), 0, start)
+                grad += jnp.dot(pick, parts[k], preferred_element_type=f32)
+            put(slice(start, start + step), grad)
+        done(piece)
 
 
 def own_grad_body(hot_ref, *refs):
@@ -213,7 +223,7 @@
     def put(at, grad):
         out_ref[at, :] = grad
 
-    row_grads(core(), hot_ref, part_refs, held, put, out_ref.shape[0])
+    row_grads(core(), hot_ref, part_refs, held, put, [(slice(0, out_ref.shape[0]), lambda piece: None)])
 
 
 def update_body(hot_ref, sum_ref, table_ref, grad_ref, *refs):
@@ -226,20 +236,24 @@
         grads[at, :] = grad
         squares[:, at.start // step:at.stop // step] = jnp.sum(grad * grad, axis=1, keepdims=True)
 
-    row_grads(1 - core(), hot_ref, part_refs, held, put, rows)
-    new_sum = sum_ref[...] + squares[...].T * (1.0 / width)
-    sums[...] = new_sum
-    copies = [pltpu.make_async_copy(sums, new_sum_ref, sems.at[0])]
-    copies[0].start()
-    scale = (learning_rate / jnp.sqrt(new_sum)).T
-    for start in range(0, rows, step):
-        at = slice(start, start + step)
-        k = start // step
-        staged[at, :] = table_ref[at, :] - grads[at, :] * scale[:, k:k + 1]
-        if at.stop % (rows // 2) == 0:
-            done = slice(at.stop - rows // 2, at.stop)
-            copies.append(pltpu.make_async_copy(staged.at[done], new_table_ref.at[done], sems.at[len(copies)]))
-            copies[-1].start()
+    copies = []
+
+    def done(piece):
+        lines = slice(piece.start // step, piece.stop // step)
+        new_sum = sum_ref[lines, :] + squares[:, lines].T * (1.0 / width)
+        sums[lines, :] = new_sum
+        scale = (learning_rate / jnp.sqrt(new_sum)).T
+        for start in range(piece.start, piece.stop, step):
+            at = slice(start, start + step)
+            k = (start - piece.start) // step
+            staged[at, :] = table_ref[at, :] - grads[at, :] * scale[:, k:k + 1]
+        copies.append(pltpu.make_async_copy(staged.at[piece], new_table_ref.at[piece], sems.at[len(copies)]))
+        copies[-1].start()
+
+    middle = rows // 2
+    row_grads(1 - core(), hot_ref, part_refs, held, put, [(slice(0, middle), done), (slice(middle, rows), done)])
+    copies.append(pltpu.make_async_copy(sums, new_sum_ref, sems.at[len(copies)]))
+    copies[-1].start()
     for copy in copies:
         copy.wait()
 
@@ -278,13 +292,13 @@
 
     hot_row = hot_ids.reshape(1, hot_dev)
     asked = exchange(cold_ids[0])
-    inc_t = call(
+    inc = call(
         functools.partial(incidence_body, owners * hot_dev, slot_cap),
-        shape((vocab, batch), bf16),
+        shape((batch, vocab), bf16),
         (cold_count, bag_slots.T),
+        [pltpu.VMEM((vocab, batch), bf16)],
         in_specs=[SMEM, VMEM],
     )
-    inc = call(transpose_body, shape((batch, vocab), bf16), (inc_t,))
     hot, table_bf = call(
         pick_hot_body,
         (shape((hot_dev, width), bf16), shape((rows, width), bf16)),
@@ -303,18 +317,24 @@
         ],
         out_specs=HBM,
     )
-    own_rows, inc, inc_t = lax.optimization_barrier((exchange(served), inc, inc_t))
+    own_rows, inc = lax.optimization_barrier((exchange(served), inc))
     mate_rows = swap(call(first_rows_body, shape((owners, half, width), bf16), (own_rows,)), 1)
     dpooled = call(
         top_body,
         shape((batch, width), bf16),
         (labels.reshape(-1, 128), inc, own_rows, mate_rows, w_in, w_out.reshape(-1, 128)),
-        [pltpu.VMEM((batch, hidden_units), bf16), pltpu.VMEM((vocab, width), bf16)],
+        [
+            pltpu.VMEM((batch, hidden_units), bf16),
+            pltpu.VMEM((vocab, width), bf16),
+            pltpu.VMEM((batch, width), bf16),
+            pltpu.VMEM((batch, 128), f32),
+            pltpu.VMEM((batch, 128), f32),
+        ],
     )
     part, to_mate = call(
         slot_grads_body,
         (shape((owners, half + slot_cap, width), bf16), shape((owners, half, width), bf16)),
-        (inc_t, dpooled),
+        (inc, dpooled),
         [pltpu.VMEM((vocab, width), bf16)],
     )
     summed = call(add_hot_body, shape(part.shape, bf16), (part, swap(to_mate, 1)))

time: 57.8 us -> 57.3 us (level)
  local copies, waits for them, and re-layouts: 3.51 us -> 1.92 us
  waiting for transfers between devices: 16 us -> 16.6 us
    unnamed x20, local copies, waits for them, and re-layouts: 3.51 us -> 1.92 us
    all_to_all x2, waiting for transfers between devices: 9.05 us -> 9.63 us  [exchange(): return lax.all_to_all(x, 'table', split_axis=0, concat_axis=0, tiled=True)]
    pallas_call x11 -> x10, Pallas kernels: 12.5 us -> 12.9 us  [call(): pl.pallas_call(body, out_shape=outs, in_specs=in_specs or [VMEM] * len(op...]
  transfers between devices with their start and end apart: 7 -> 7, of which waited for: 6 -> 6; matrix products, arithmetic and copies ran while one was open for 0% -> 0% of each run, Pallas kernels for 7% -> 6%
where the time goes in v7:
time: 57.3 us; the launch traced here: 56.9 us
  waiting for transfers between devices  16.6 us (29%)
  Pallas kernels  12.9 us (23%)
  starting transfers between devices  12.7 us (22%)
  blocking collectives  12.1 us (21%)
  local copies, waits for them, and re-layouts  1.92 us (3%)
  between operations  0.77 us (1%)
    pallas_call x10, Pallas kernels, call(): pl.pallas_call(body, out_shape=outs, in_specs=in_specs or [VMEM] * len(op...  12.9 us
    all_to_all x1, blocking collectives, exchange(): return lax.all_to_all(x, 'table', split_axis=0, concat_axis=0, tiled=True)  12.1 us
    all_to_all x2, starting transfers between devices, exchange(): return lax.all_to_all(x, 'table', split_axis=0, concat_axis=0, tiled=True)  10.8 us
    all_to_all x2, waiting for transfers between devices, exchange(): return lax.all_to_all(x, 'table', split_axis=0, concat_axis=0, tiled=True)  9.63 us
    ppermute x5, waiting for transfers between devices, swap(): lax.ppermute(x, 'dp', [(g, g ^ bit) for g in range(lax.axis_size('dp'))])  6.95 us
    unnamed x20, local copies, waits for them, and re-layouts  1.92 us
    ppermute x5, starting transfers between devices, swap(): lax.ppermute(x, 'dp', [(g, g ^ bit) for g in range(lax.axis_size('dp'))])  1.85 us
  transfers between devices with their start and end apart: 7, of which 6 were waited for; matrix products, arithmetic and copies ran while one was open for 0% of the time, Pallas kernels for 6%

profile of v7, /device:TPU:0, one launch (start us, length us, event | category | flops | bytes accessed | tf_op | source)
XLA Modules:
  0.0 56.9 jit_solution(16381738938986148229)
XLA Ops:
  0.7 7.4 %all-to-all-start = ((s32[8,1,32]{2,1,0:T(1,128)}), s32[8,1,32]{2,1,0:T(1,128)S(1)}, u32[]{:S(2)}, u32[]{:S(2)}) async-start(s32[8,1,32]{2,1,0:T(1,128)} %bitcast.17), calls=%async_computation | async-start | bytes 8192 | tf_op jit(solution)/shard_map/all_to_all | solution.py:274
  8.1 1.2 %copy-done = f32[1024,256]{1,0:T(8,128)S(1)} copy-done((f32[1024,256]{1,0:T(8,128)S(1)}, f32[1024,256]{1,0:T(8,128)}, u32[]{:S(2)}) %copy-start) | copy-done | bytes 1048600
  9.3 0.7 %copy-done.5 = s32[64]{0:T(128)S(1)} copy-done((s32[64]{0:T(128)S(1)}, s32[64]{0:T(128)}, u32[]{:S(2)}) %copy-start.5) | copy-done | bytes 280
  9.9 0.4 shard_map.104
  10.4 4.1 %all-to-all-done = s32[8,1,32]{2,1,0:T(1,128)S(1)} async-done(((s32[8,1,32]{2,1,0:T(1,128)}), s32[8,1,32]{2,1,0:T(1,128)S(1)}, u32[]{:S(2)}, u32[]{:S(2)}) %all-to-all-start) | async-done | bytes 1056 | tf_op jit(solution)/shard_map/all_to_all | solution.py:274
  14.4 1.2 %shard_map.105 = bf16[8,64,256]{2,1,0:T(8,128)(2,1)} custom-call(s32[8,32]{1,0:T(8,128)S(1)} %bitcast.9, bf16[64,256]{1,0:T(8,128)(2,1)S(1)} %get-tuple-element.10.hot_ref, bf16[1024,256]{1,0:T(8,128)(2,1)S(1)} %get-tuple-element.11.table_ref), custom_call_target="tpu_custom_call" | custom-call | tf_op jit(solution)/shard_map/pallas_call | solution.py:24
  15.6 3.4 %all-to-all-start.1 = ((bf16[8,64,256]{2,1,0:T(8,128)(2,1)}), bf16[8,64,256]{2,1,0:T(8,128)(2,1)S(1)}, u32[]{:S(2)}, u32[]{:S(2)}) async-start(bf16[8,64,256]{2,1,0:T(8,128)(2,1)} %shard_map.105), calls=%async_computation.1 | async-start | bytes 524288 | tf_op jit(solution)/shard_map/all_to_all | solution.py:274
  19.1 2.6 %shard_map.106.inc_ref = bf16[512,768]{1,0:T(8,128)(2,1)S(1)} custom-call(s32[1,8]{1,0:T(1,128)S(1)} %copy-done.9, s32[32,512]{1,0:T(8,128)S(1)} %bitcast.8), custom_call_target="tpu_custom_call" | custom-call | tf_op jit(solution)/shard_map/pallas_call | solution.py:24
  21.7 5.5 %all-to-all-done.1.rows_ref.own_ref = bf16[8,64,256]{2,1,0:T(8,128)(2,1)S(1)} async-done(((bf16[8,64,256]{2,1,0:T(8,128)(2,1)}), bf16[8,64,256]{2,1,0:T(8,128)(2,1)S(1)}, u32[]{:S(2)}, u32[]{:S(2)}) %all-to-all-start.1) | async-done | bytes 262176 | tf_op jit(solution)/shard_map/all_to_all | solution.py:274
  27.2 0.1 collective-permute-start
  27.3 1.3 %collective-permute-done.mate_ref = bf16[8,32,256]{2,1,0:T(8,128)(2,1)S(1)} collective-permute-done((bf16[8,32,256]{2,1,0:T(8,128)(2,1)S(1)}, bf16[8,32,256]{2,1,0:T(8,128)(2,1)S(1)}, u32[]{:S(2)}, u32[]{:S(2)}) %collective-permute-start) | collective-permute-done | bytes 131104 | tf_op jit(solution)/shard_map/ppermute | solution.py:278
  28.6 5.2 %shard_map.108.dpooled_ref = bf16[512,256]{1,0:T(8,128)(2,1)S(1)} custom-call(f32[4,128]{1,0:T(4,128)S(1)} %bitcast.16, bf16[512,768]{1,0:T(8,128)(2,1)S(1)} %shard_map.106.inc_ref, bf16[8,64,256]{2,1,0:T(8,128)(2,1)S(1)} %all-to-all-done.1.rows_ref.own_ref, bf16[8,32,256]{2,1,0:T(8,128)(2,1)S(1)} %collective-permute-done.mate_ref, ...), custom_call_target="tpu_custom_call" | custom-call | tf_op jit(solution)/shard_map/pallas_call | solution.py:24
  33.8 0.0 copy-start.1
  33.8 0.0 copy-start.7
  33.8 0.4 shard_map.109
  34.3 0.2 collective-permute-start.1
  34.5 1.2 %collective-permute-done.1.got_ref = bf16[8,32,256]{2,1,0:T(8,128)(2,1)S(1)} collective-permute-done((bf16[8,32,256]{2,1,0:T(8,128)(2,1)S(1)}, bf16[8,32,256]{2,1,0:T(8,128)(2,1)S(1)}, u32[]{:S(2)}, u32[]{:S(2)}) %collective-permute-start.1) | collective-permute-done | bytes 131104 | tf_op jit(solution)/shard_map/ppermute | solution.py:278
  35.7 12.1 %all_to_all.21.back_ref = bf16[8,64,256]{2,1,0:T(8,128)(2,1)S(1)} all-to-all(bf16[8,64,256]{2,1,0:T(8,128)(2,1)S(1)} %shard_map.110), channel_id=1, replica_groups=mesh['dp'=4,'table'=8] {'table'}, dimensions={0} | all-to-all | bytes 524288 | tf_op jit(solution)/shard_map/all_to_all | solution.py:274
  47.9 0.1 shard_map.111.refs_0_
  47.9 1.6 %collective-permute-start.2 = (bf16[304,256]{1,0:T(8,128)(2,1)S(1)}, bf16[304,256]{1,0:T(8,128)(2,1)S(1)}, u32[]{:S(2)}, u32[]{:S(2)}) collective-permute-start(bf16[304,256]{1,0:T(8,128)(2,1)S(1)} %shard_map.111.refs_0_), channel_id=1, source_target_pairs={{0,16},{8,24},{16,0},{24,8},{1,17},{9,25},{17,1},{25,9},{2,18},{10... | collective-permute-start | bytes 466952 | tf_op jit(solution)/shard_map/ppermute | solution.py:278
  49.5 3.7 %collective-permute-done.2.refs_1_ = bf16[304,256]{1,0:T(8,128)(2,1)S(1)} collective-permute-done((bf16[304,256]{1,0:T(8,128)(2,1)S(1)}, bf16[304,256]{1,0:T(8,128)(2,1)S(1)}, u32[]{:S(2)}, u32[]{:S(2)}) %collective-permute-start.2) | collective-permute-done | bytes 155680 | tf_op jit(solution)/shard_map/ppermute | solution.py:278
  53.2 0.7 %shard_map.112.grad_ref = f32[1024,256]{1,0:T(8,128)S(1)} custom-call(s32[1,64]{1,0:T(1,128)S(1)} %bitcast.13, bf16[304,256]{1,0:T(8,128)(2,1)S(1)} %shard_map.111.refs_0_, bf16[304,256]{1,0:T(8,128)(2,1)S(1)} %collective-permute-done.2.refs_1_), custom_call_target="tpu_custom_call" | custom-call | tf_op jit(solution)/shard_map/pallas_call | solution.py:24
  53.9 0.7 %collective-permute-done.4.refs_1_ = bf16[304,256]{1,0:T(8,128)(2,1)S(1)} collective-permute-done((bf16[304,256]{1,0:T(8,128)(2,1)S(1)}, bf16[304,256]{1,0:T(8,128)(2,1)S(1)}, u32[]{:S(2)}, u32[]{:S(2)}) %collective-permute-start.4) | collective-permute-done | bytes 155680 | tf_op jit(solution)/shard_map/ppermute | solution.py:278
  54.6 2.3 %shard_map.113 = (f32[1024,256]{1,0:T(8,128)}, f32[8,128]{1,0:T(8,128)}) custom-call(s32[1,64]{1,0:T(1,128)S(1)} %bitcast.14, f32[8,128]{1,0:T(8,128)S(1)} %bitcast.15, f32[1024,256]{1,0:T(8,128)S(1)} %copy-done.1, f32[1024,256]{1,0:T(8,128)S(1)} %shard_map.112.grad_ref, bf16[304,256]{1,0:T(8,128)(2,1)S(1)} %collective-permute-done.3.refs_0_, ...), custom_call_target="tpu_custom_call" | custom-call | tf_op jit(solution)/shard_map/pallas_call | solution.py:24
  (21 shorter events, 0.1 us)
Async XLA Ops:
  0.6 18.4 %copy-start.9 = (s32[1,8]{1,0:T(1,128)S(1)}, s32[1,8]{1,0:T(1,128)}, u32[]{:S(2)}) copy-start(s32[1,8]{1,0:T(1,128)} %count_ref.1) | copy-start | bytes 100
  0.6 28.0 %copy-start.4 = (bf16[4096]{0:T(1024)(128)(2,1)S(1)}, bf16[4096]{0:T(1024)(128)(2,1)}, u32[]{:S(2)}) copy-start(bf16[4096]{0:T(1024)(128)(2,1)} %param.17) | copy-start | bytes 24580
  0.7 28.0 %copy-start.8 = (f32[512]{0:T(512)S(1)}, f32[512]{0:T(512)}, u32[]{:S(2)}) copy-start(f32[512]{0:T(512)} %param.10) | copy-start | bytes 6148
  0.7 13.8 %all-to-all-start = ((s32[8,1,32]{2,1,0:T(1,128)}), s32[8,1,32]{2,1,0:T(1,128)S(1)}, u32[]{:S(2)}, u32[]{:S(2)}) async-start(s32[8,1,32]{2,1,0:T(1,128)} %bitcast.17), calls=%async_computation | async-start | bytes 8192 | tf_op jit(solution)/shard_map/all_to_all | solution.py:274
  8.1 1.2 %copy-start = (f32[1024,256]{1,0:T(8,128)S(1)}, f32[1024,256]{1,0:T(8,128)}, u32[]{:S(2)}) copy-start(f32[1024,256]{1,0:T(8,128)} %table_ref.3) | copy-start | bytes 3145732
  9.3 0.7 %copy-start.5 = (s32[64]{0:T(128)S(1)}, s32[64]{0:T(128)}, u32[]{:S(2)}) copy-start(s32[64]{0:T(128)} %param.15) | copy-start | bytes 772
  9.9 9.1 %copy-start.3 = (s32[512,32]{0,1:T(8,128)S(1)}, s32[512,32]{0,1:T(8,128)}, u32[]{:S(2)}) copy-start(s32[512,32]{0,1:T(8,128)} %param.9) | copy-start | bytes 196612
  9.9 18.7 %copy-start.2 = (bf16[256,4096]{1,0:T(8,128)(2,1)S(1)}, bf16[256,4096]{1,0:T(8,128)(2,1)}, u32[]{:S(2)}) copy-start(bf16[256,4096]{1,0:T(8,128)(2,1)} %w_in_ref.1) | copy-start | bytes 6291460
  15.6 11.6 %all-to-all-start.1 = ((bf16[8,64,256]{2,1,0:T(8,128)(2,1)}), bf16[8,64,256]{2,1,0:T(8,128)(2,1)S(1)}, u32[]{:S(2)}, u32[]{:S(2)}) async-start(bf16[8,64,256]{2,1,0:T(8,128)(2,1)} %shard_map.105), calls=%async_computation.1 | async-start | bytes 524288 | tf_op jit(solution)/shard_map/all_to_all | solution.py:274
  27.2 1.4 %collective-permute-start = (bf16[8,32,256]{2,1,0:T(8,128)(2,1)S(1)}, bf16[8,32,256]{2,1,0:T(8,128)(2,1)S(1)}, u32[]{:S(2)}, u32[]{:S(2)}) collective-permute-start(bf16[8,32,256]{2,1,0:T(8,128)(2,1)S(1)} %shard_map.107), channel_id=1, source_target_pairs={{0,8},{8,0},{16,24},{24,16},{1,9},{9,1},{17,25},{25,17},{2,10},{10... | collective-permute-start | bytes 393224 | tf_op jit(solution)/shard_map/ppermute | solution.py:278
  33.8 19.4 %copy-start.6 = (s32[64]{0:T(128)S(1)}, s32[64]{0:T(128)}, u32[]{:S(2)}) copy-start(s32[64]{0:T(128)} %param.15) | copy-start | bytes 772
  33.8 20.8 %copy-start.1 = (f32[1024,256]{1,0:T(8,128)S(1)}, f32[1024,256]{1,0:T(8,128)}, u32[]{:S(2)}) copy-start(f32[1024,256]{1,0:T(8,128)} %table_ref.3) | copy-start | bytes 3145732
  33.8 20.8 %copy-start.7 = (f32[1024]{0:T(1024)S(1)}, f32[1024]{0:T(1024)}, u32[]{:S(2)}) copy-start(f32[1024]{0:T(1024)} %param.14) | copy-start | bytes 12292
  34.3 1.4 %collective-permute-start.1 = (bf16[8,32,256]{2,1,0:T(8,128)(2,1)S(1)}, bf16[8,32,256]{2,1,0:T(8,128)(2,1)S(1)}, u32[]{:S(2)}, u32[]{:S(2)}) collective-permute-start(bf16[8,32,256]{2,1,0:T(8,128)(2,1)S(1)} %get-tuple-element.15), channel_id=1, source_target_pairs={{0,8},{8,0},{16,24},{24,16},{1,9},{9,1},{17,25},{25,17},{2,10},{10... | collective-permute-start | bytes 393224 | tf_op jit(solution)/shard_map/ppermute | solution.py:278
  47.9 5.3 %collective-permute-start.2 = (bf16[304,256]{1,0:T(8,128)(2,1)S(1)}, bf16[304,256]{1,0:T(8,128)(2,1)S(1)}, u32[]{:S(2)}, u32[]{:S(2)}) collective-permute-start(bf16[304,256]{1,0:T(8,128)(2,1)S(1)} %shard_map.111.refs_0_), channel_id=1, source_target_pairs={{0,16},{8,24},{16,0},{24,8},{1,17},{9,25},{17,1},{25,9},{2,18},{10... | collective-permute-start | bytes 466952 | tf_op jit(solution)/shard_map/ppermute | solution.py:278
  49.5 4.4 %collective-permute-start.3 = (bf16[304,256]{1,0:T(8,128)(2,1)S(1)}, bf16[304,256]{1,0:T(8,128)(2,1)S(1)}, u32[]{:S(2)}, u32[]{:S(2)}) collective-permute-start(bf16[304,256]{1,0:T(8,128)(2,1)S(1)} %shard_map.111.refs_0_), channel_id=1, source_target_pairs={{0,8},{8,0},{16,24},{24,16},{1,9},{9,1},{17,25},{25,17},{2,10},{10... | collective-permute-start | bytes 466952 | tf_op jit(solution)/shard_map/ppermute | solution.py:278
  53.2 1.4 %collective-permute-start.4 = (bf16[304,256]{1,0:T(8,128)(2,1)S(1)}, bf16[304,256]{1,0:T(8,128)(2,1)S(1)}, u32[]{:S(2)}, u32[]{:S(2)}) collective-permute-start(bf16[304,256]{1,0:T(8,128)(2,1)S(1)} %collective-permute-done.2.refs_1_), channel_id=1, source_target_pairs={{0,8},{8,0},{16,24},{24,16},{1,9},{9,1},{17,25},{25,17},{2,10},{10... | collective-permute-start | bytes 466952 | tf_op jit(solution)/shard_map/ppermute | solution.py:278

commit v8 on v6

--- a/solution.py
+++ b/solution.py
@@ -39,7 +39,7 @@
     return (lax.broadcasted_iota(i32, shape, axis) + start == ids).astype(f32).astype(bf16)
 
 
-def incidence_body(hot_cols, slot_cap, count_ref, slots_ref, inc_t_ref):
+def incidence_body(hot_cols, slot_cap, count_ref, slots_ref, out_ref, inc_t_ref):
     vocab, batch = inc_t_ref.shape
     field = vocab // FIELDS
     step = 128
@@ -58,10 +58,7 @@
     for owner in range((vocab - hot_cols) // slot_cap):
         rows = pl.ds(hot_cols + owner * slot_cap, slot_cap)
         inc_t_ref[rows, :] = jnp.where(place < count_ref[0, owner], inc_t_ref[rows, :].astype(f32), 0.0).astype(bf16)
-
-
-def transpose_body(x_ref, out_ref):
-    out_ref[...] = x_ref[...].T
+    out_ref[...] = inc_t_ref[...].T
 
 
 def core():
@@ -106,7 +103,7 @@
     out_ref[...] = rows_ref[:, 0:out_ref.shape[1], :]
 
 
-def top_body(labels_ref, inc_ref, own_ref, mate_ref, w_in_ref, w_out_ref, out_ref, gated, rows):
+def top_body(labels_ref, inc_ref, own_ref, mate_ref, w_in_ref, w_out_ref, out_ref, gated, rows, pooled, total, dlogit):
     batch = inc_ref.shape[0]
     hidden_units, width = w_in_ref.shape[1], w_in_ref.shape[0]
     owners, half, _ = mate_ref.shape
@@ -114,33 +111,36 @@
     hot_cols = owners * hot_dev
     slot_cap = own_ref.shape[1] - half
     me = core()
+    size, step, wide = batch // 2, 512, 2048
+    blocks = [slice(at, at + size) for at in range(0, batch, size)]
     for t in range(owners):
         rows[half_rows(t, hot_dev, me), :] = own_ref[t, 0:half, :]
         rows[half_rows(t, hot_dev, 1 - me), :] = mate_ref[t, 0:half, :]
         rows[hot_cols + t * slot_cap:hot_cols + (t + 1) * slot_cap, :] = own_ref[t, half:, :]
-    labels = labels_ref[...].T
-    labels = jnp.concatenate([labels[:, k:k + 1] for k in range(labels.shape[1])], axis=0)
-    pooled = jnp.dot(inc_ref[...], rows[...], preferred_element_type=f32).astype(bf16)
-    size, step, wide = batch // 2, 512, 2048
+    pooled[...] = jnp.dot(inc_ref[...], rows[...], preferred_element_type=f32).astype(bf16)
     w_out = w_out_ref[...].astype(f32)
-    w_out = [lanes([w_out[k:k + 1, :] for k in range(r, r + step // 128)]) for r in range(0, hidden_units // 128, step // 128)]
-    for at in range(0, batch, size):
-        samples = slice(at, at + size)
-        total = jnp.zeros((size, 128), f32)
+    for samples in blocks:
+        acc = jnp.zeros((size, 128), f32)
         for start in range(0, hidden_units, step):
             cols = slice(start, start + step)
-            pre_act = jnp.dot(pooled[samples], w_in_ref[:, cols], preferred_element_type=f32)
-            own = w_out[start // step]
+            pre_act = jnp.dot(pooled[samples, :], w_in_ref[:, cols], preferred_element_type=f32)
+            own = lanes([w_out[k:k + 1, :] for k in range(start // 128, (start + step) // 128)])
             gated[samples, cols] = jnp.where(pre_act > 0, own, 0.0).astype(bf16)
             term = jnp.maximum(pre_act, 0.0).astype(bf16).astype(f32) * own
             for k in range(0, step, 128):
-                total += term[:, k:k + 128]
-        logit = jnp.sum(total, axis=1, keepdims=True)
-        dlogit = jnp.broadcast_to(jax.nn.sigmoid(logit) - labels[samples], (size, 128))
+                acc += term[:, k:k + 128]
+        total[samples, :] = acc
+    lines = [slice(at, at + 128) for at in range(0, batch, 128)]
+    logit = lanes([jnp.sum(total[line, :], axis=1, keepdims=True) for line in lines])
+    delta = jax.nn.sigmoid(logit) - labels_ref[...].T
+    for k, line in enumerate(lines):
+        dlogit[line, :] = jnp.broadcast_to(delta[:, k:k + 1], (128, 128))
+    for samples in blocks:
+        scale = dlogit[samples, :]
         grad = jnp.zeros((size, width), f32)
         for start in range(0, hidden_units, wide):
             dhidden = lanes([
-                (dlogit * gated[samples, k:k + 128].astype(f32)).astype(bf16) for k in range(start, start + wide, 128)
+                (scale * gated[samples, k:k + 128].astype(f32)).astype(bf16) for k in range(start, start + wide, 128)
             ])
             grad += lax.dot_general(
                 dhidden, w_in_ref[:, start:start + wide], (((1,), (1,)), ((), ())), preferred_element_type=f32
@@ -148,13 +148,13 @@
         out_ref[samples, :] = grad.astype(bf16)
 
 
-def slot_grads_body(inc_t_ref, dpooled_ref, part_ref, send_ref, rows):
+def slot_grads_body(inc_ref, dpooled_ref, part_ref, send_ref, rows):
     owners, half, _ = send_ref.shape
     hot_dev = 2 * half
     hot_cols = owners * hot_dev
     slot_cap = part_ref.shape[1] - half
     me = core()
-    rows[...] = jnp.dot(inc_t_ref[...], dpooled_ref[...], preferred_element_type=f32).astype(bf16)
+    rows[...] = jnp.dot(inc_ref[...].T, dpooled_ref[...], preferred_element_type=f32).astype(bf16)
     for t in range(owners):
         send_ref[t] = rows[half_rows(t, hot_dev, 1 - me), :]
         part_ref[t, 0:half, :] = rows[half_rows(t, hot_dev, me), :]
@@ -229,17 +229,17 @@
     row_grads(1 - core(), hot_ref, part_refs, held, put, rows)
     new_sum = sum_ref[...] + squares[...].T * (1.0 / width)
     sums[...] = new_sum
-    copies = [pltpu.make_async_copy(sums, new_sum_ref, sems.at[0])]
-    copies[0].start()
     scale = (learning_rate / jnp.sqrt(new_sum)).T
     for start in range(0, rows, step):
         at = slice(start, start + step)
         k = start // step
         staged[at, :] = table_ref[at, :] - grads[at, :] * scale[:, k:k + 1]
-        if at.stop % (rows // 2) == 0:
-            done = slice(at.stop - rows // 2, at.stop)
-            copies.append(pltpu.make_async_copy(staged.at[done], new_table_ref.at[done], sems.at[len(copies)]))
-            copies[-1].start()
+    copies = [
+        pltpu.make_async_copy(staged, new_table_ref, sems.at[0]),
+        pltpu.make_async_copy(sums, new_sum_ref, sems.at[1]),
+    ]
+    for copy in copies:
+        copy.start()
     for copy in copies:
         copy.wait()
 
@@ -278,13 +278,13 @@
 
     hot_row = hot_ids.reshape(1, hot_dev)
     asked = exchange(cold_ids[0])
-    inc_t = call(
+    inc = call(
         functools.partial(incidence_body, owners * hot_dev, slot_cap),
-        shape((vocab, batch), bf16),
+        shape((batch, vocab), bf16),
         (cold_count, bag_slots.T),
+        [pltpu.VMEM((vocab, batch), bf16)],
         in_specs=[SMEM, VMEM],
     )
-    inc = call(transpose_body, shape((batch, vocab), bf16), (inc_t,))
     hot, table_bf = call(
         pick_hot_body,
         (shape((hot_dev, width), bf16), shape((rows, width), bf16)),
@@ -303,18 +303,24 @@
         ],
         out_specs=HBM,
     )
-    own_rows, inc, inc_t = lax.optimization_barrier((exchange(served), inc, inc_t))
+    own_rows, inc = lax.optimization_barrier((exchange(served), inc))
     mate_rows = swap(call(first_rows_body, shape((owners, half, width), bf16), (own_rows,)), 1)
     dpooled = call(
         top_body,
         shape((batch, width), bf16),
         (labels.reshape(-1, 128), inc, own_rows, mate_rows, w_in, w_out.reshape(-1, 128)),
-        [pltpu.VMEM((batch, hidden_units), bf16), pltpu.VMEM((vocab, width), bf16)],
+        [
+            pltpu.VMEM((batch, hidden_units), bf16),
+            pltpu.VMEM((vocab, width), bf16),
+            pltpu.VMEM((batch, width), bf16),
+            pltpu.VMEM((batch, 128), f32),
+            pltpu.VMEM((batch, 128), f32),
+        ],
     )
     part, to_mate = call(
         slot_grads_body,
         (shape((owners, half + slot_cap, width), bf16), shape((owners, half, width), bf16)),
-        (inc_t, dpooled),
+        (inc, dpooled),
         [pltpu.VMEM((vocab, width), bf16)],
     )
     summed = call(add_hot_body, shape(part.shape, bf16), (part, swap(to_mate, 1)))
@@ -340,7 +346,7 @@
                 pltpu.VMEM((rows, width), f32),
                 pltpu.VMEM((rows, width), f32),
                 pltpu.VMEM((rows // 128, 128), f32),
-                pltpu.SemaphoreType.DMA((3,)),
+                pltpu.SemaphoreType.DMA((2,)),
             ],
             out_specs=(HBM, HBM),
         )

time: 57.8 us -> 56.2 us (0.972)
  local copies, waits for them, and re-layouts: 3.51 us -> 1.92 us
  Pallas kernels: 12.5 us -> 11.7 us
  waiting for transfers between devices: 16 us -> 16.6 us
    unnamed x20, local copies, waits for them, and re-layouts: 3.51 us -> 1.92 us
    pallas_call x11 -> x10, Pallas kernels: 12.5 us -> 11.7 us  [call(): pl.pallas_call(body, out_shape=outs, in_specs=in_specs or [VMEM] * len(op...]
    all_to_all x2, waiting for transfers between devices: 9.05 us -> 9.63 us  [exchange(): return lax.all_to_all(x, 'table', split_axis=0, concat_axis=0, tiled=True)]
where the time goes in v8:
time: 56.2 us; the launch traced here: 55.8 us
  waiting for transfers between devices  16.6 us (30%)
  starting transfers between devices  12.7 us (23%)
  blocking collectives  12.1 us (22%)
  Pallas kernels  11.7 us (21%)
  local copies, waits for them, and re-layouts  1.92 us (3%)
  between operations  0.77 us (1%)
    all_to_all x1, blocking collectives, exchange(): return lax.all_to_all(x, 'table', split_axis=0, concat_axis=0, tiled=True)  12.1 us
    pallas_call x10, Pallas kernels, call(): pl.pallas_call(body, out_shape=outs, in_specs=in_specs or [VMEM] * len(op...  11.7 us
    all_to_all x2, starting transfers between devices, exchange(): return lax.all_to_all(x, 'table', split_axis=0, concat_axis=0, tiled=True)  10.8 us
    all_to_all x2, waiting for transfers between devices, exchange(): return lax.all_to_all(x, 'table', split_axis=0, concat_axis=0, tiled=True)  9.63 us
    ppermute x5, waiting for transfers between devices, swap(): lax.ppermute(x, 'dp', [(g, g ^ bit) for g in range(lax.axis_size('dp'))])  6.94 us
    unnamed x20, local copies, waits for them, and re-layouts  1.92 us
    ppermute x5, starting transfers between devices, swap(): lax.ppermute(x, 'dp', [(g, g ^ bit) for g in range(lax.axis_size('dp'))])  1.86 us
  transfers between devices with their start and end apart: 7, of which 6 were waited for; matrix products, arithmetic and copies ran while one was open for 0% of the time, Pallas kernels for 7%

profile of v8, /device:TPU:0, one launch (start us, length us, event | category | flops | bytes accessed | tf_op | source)
XLA Modules:
  0.0 55.8 jit_solution(12955690520779915972)
XLA Ops:
  0.7 7.4 %all-to-all-start = ((s32[8,1,32]{2,1,0:T(1,128)}), s32[8,1,32]{2,1,0:T(1,128)S(1)}, u32[]{:S(2)}, u32[]{:S(2)}) async-start(s32[8,1,32]{2,1,0:T(1,128)} %bitcast.17), calls=%async_computation | async-start | bytes 8192 | tf_op jit(solution)/shard_map/all_to_all | solution.py:260
  8.1 1.2 %copy-done = f32[1024,256]{1,0:T(8,128)S(1)} copy-done((f32[1024,256]{1,0:T(8,128)S(1)}, f32[1024,256]{1,0:T(8,128)}, u32[]{:S(2)}) %copy-start) | copy-done | bytes 1048600
  9.3 0.7 %copy-done.5 = s32[64]{0:T(128)S(1)} copy-done((s32[64]{0:T(128)S(1)}, s32[64]{0:T(128)}, u32[]{:S(2)}) %copy-start.5) | copy-done | bytes 280
  9.9 0.4 shard_map.104
  10.4 4.1 %all-to-all-done = s32[8,1,32]{2,1,0:T(1,128)S(1)} async-done(((s32[8,1,32]{2,1,0:T(1,128)}), s32[8,1,32]{2,1,0:T(1,128)S(1)}, u32[]{:S(2)}, u32[]{:S(2)}) %all-to-all-start) | async-done | bytes 1056 | tf_op jit(solution)/shard_map/all_to_all | solution.py:260
  14.4 1.2 %shard_map.105 = bf16[8,64,256]{2,1,0:T(8,128)(2,1)} custom-call(s32[8,32]{1,0:T(8,128)S(1)} %bitcast.9, bf16[64,256]{1,0:T(8,128)(2,1)S(1)} %get-tuple-element.10.hot_ref, bf16[1024,256]{1,0:T(8,128)(2,1)S(1)} %get-tuple-element.11.table_ref), custom_call_target="tpu_custom_call" | custom-call | tf_op jit(solution)/shard_map/pallas_call | solution.py:24
  15.6 3.4 %all-to-all-start.1 = ((bf16[8,64,256]{2,1,0:T(8,128)(2,1)}), bf16[8,64,256]{2,1,0:T(8,128)(2,1)S(1)}, u32[]{:S(2)}, u32[]{:S(2)}) async-start(bf16[8,64,256]{2,1,0:T(8,128)(2,1)} %shard_map.105), calls=%async_computation.1 | async-start | bytes 524288 | tf_op jit(solution)/shard_map/all_to_all | solution.py:260
  19.1 2.6 %shard_map.106.inc_ref = bf16[512,768]{1,0:T(8,128)(2,1)S(1)} custom-call(s32[1,8]{1,0:T(1,128)S(1)} %copy-done.9, s32[32,512]{1,0:T(8,128)S(1)} %bitcast.8), custom_call_target="tpu_custom_call" | custom-call | tf_op jit(solution)/shard_map/pallas_call | solution.py:24
  21.7 5.5 %all-to-all-done.1.rows_ref.own_ref = bf16[8,64,256]{2,1,0:T(8,128)(2,1)S(1)} async-done(((bf16[8,64,256]{2,1,0:T(8,128)(2,1)}), bf16[8,64,256]{2,1,0:T(8,128)(2,1)S(1)}, u32[]{:S(2)}, u32[]{:S(2)}) %all-to-all-start.1) | async-done | bytes 262176 | tf_op jit(solution)/shard_map/all_to_all | solution.py:260
  27.2 0.1 collective-permute-start
  27.3 1.3 %collective-permute-done.mate_ref = bf16[8,32,256]{2,1,0:T(8,128)(2,1)S(1)} collective-permute-done((bf16[8,32,256]{2,1,0:T(8,128)(2,1)S(1)}, bf16[8,32,256]{2,1,0:T(8,128)(2,1)S(1)}, u32[]{:S(2)}, u32[]{:S(2)}) %collective-permute-start) | collective-permute-done | bytes 131104 | tf_op jit(solution)/shard_map/ppermute | solution.py:264
  28.6 4.2 %shard_map.108.dpooled_ref = bf16[512,256]{1,0:T(8,128)(2,1)S(1)} custom-call(f32[4,128]{1,0:T(4,128)S(1)} %bitcast.16, bf16[512,768]{1,0:T(8,128)(2,1)S(1)} %shard_map.106.inc_ref, bf16[8,64,256]{2,1,0:T(8,128)(2,1)S(1)} %all-to-all-done.1.rows_ref.own_ref, bf16[8,32,256]{2,1,0:T(8,128)(2,1)S(1)} %collective-permute-done.mate_ref, ...), custom_call_target="tpu_custom_call" | custom-call | tf_op jit(solution)/shard_map/pallas_call | solution.py:24
  32.8 0.0 copy-start.6
  32.8 0.0 copy-start.7
  32.8 0.4 shard_map.109
  33.3 0.2 collective-permute-start.1
  33.5 1.2 %collective-permute-done.1.got_ref = bf16[8,32,256]{2,1,0:T(8,128)(2,1)S(1)} collective-permute-done((bf16[8,32,256]{2,1,0:T(8,128)(2,1)S(1)}, bf16[8,32,256]{2,1,0:T(8,128)(2,1)S(1)}, u32[]{:S(2)}, u32[]{:S(2)}) %collective-permute-start.1) | collective-permute-done | bytes 131104 | tf_op jit(solution)/shard_map/ppermute | solution.py:264
  34.7 12.1 %all_to_all.21.back_ref = bf16[8,64,256]{2,1,0:T(8,128)(2,1)S(1)} all-to-all(bf16[8,64,256]{2,1,0:T(8,128)(2,1)S(1)} %shard_map.110), channel_id=1, replica_groups=mesh['dp'=4,'table'=8] {'table'}, dimensions={0} | all-to-all | bytes 524288 | tf_op jit(solution)/shard_map/all_to_all | solution.py:260
  46.9 0.1 shard_map.111.refs_0_
  47.0 1.6 %collective-permute-start.2 = (bf16[304,256]{1,0:T(8,128)(2,1)S(1)}, bf16[304,256]{1,0:T(8,128)(2,1)S(1)}, u32[]{:S(2)}, u32[]{:S(2)}) collective-permute-start(bf16[304,256]{1,0:T(8,128)(2,1)S(1)} %shard_map.111.refs_0_), channel_id=1, source_target_pairs={{0,16},{8,24},{16,0},{24,8},{1,17},{9,25},{17,1},{25,9},{2,18},{10... | collective-permute-start | bytes 466952 | tf_op jit(solution)/shard_map/ppermute | solution.py:264
  48.5 3.7 %collective-permute-done.2.refs_1_ = bf16[304,256]{1,0:T(8,128)(2,1)S(1)} collective-permute-done((bf16[304,256]{1,0:T(8,128)(2,1)S(1)}, bf16[304,256]{1,0:T(8,128)(2,1)S(1)}, u32[]{:S(2)}, u32[]{:S(2)}) %collective-permute-start.2) | collective-permute-done | bytes 155680 | tf_op jit(solution)/shard_map/ppermute | solution.py:264
  52.2 0.7 %shard_map.112.grad_ref = f32[1024,256]{1,0:T(8,128)S(1)} custom-call(s32[1,64]{1,0:T(1,128)S(1)} %bitcast.13, bf16[304,256]{1,0:T(8,128)(2,1)S(1)} %shard_map.111.refs_0_, bf16[304,256]{1,0:T(8,128)(2,1)S(1)} %collective-permute-done.2.refs_1_), custom_call_target="tpu_custom_call" | custom-call | tf_op jit(solution)/shard_map/pallas_call | solution.py:24
  52.9 0.7 %collective-permute-done.4.refs_1_ = bf16[304,256]{1,0:T(8,128)(2,1)S(1)} collective-permute-done((bf16[304,256]{1,0:T(8,128)(2,1)S(1)}, bf16[304,256]{1,0:T(8,128)(2,1)S(1)}, u32[]{:S(2)}, u32[]{:S(2)}) %collective-permute-start.4) | collective-permute-done | bytes 155680 | tf_op jit(solution)/shard_map/ppermute | solution.py:264
  53.6 2.2 %shard_map.113 = (f32[1024,256]{1,0:T(8,128)}, f32[8,128]{1,0:T(8,128)}) custom-call(s32[1,64]{1,0:T(1,128)S(1)} %bitcast.14, f32[8,128]{1,0:T(8,128)S(1)} %bitcast.15, f32[1024,256]{1,0:T(8,128)S(1)} %copy-done.1, f32[1024,256]{1,0:T(8,128)S(1)} %shard_map.112.grad_ref, bf16[304,256]{1,0:T(8,128)(2,1)S(1)} %collective-permute-done.3.refs_0_, ...), custom_call_target="tpu_custom_call" | custom-call | tf_op jit(solution)/shard_map/pallas_call | solution.py:24
  (21 shorter events, 0.1 us)
Async XLA Ops:
  0.6 18.4 %copy-start.9 = (s32[1,8]{1,0:T(1,128)S(1)}, s32[1,8]{1,0:T(1,128)}, u32[]{:S(2)}) copy-start(s32[1,8]{1,0:T(1,128)} %count_ref.1) | copy-start | bytes 100
  0.6 28.0 %copy-start.4 = (bf16[4096]{0:T(1024)(128)(2,1)S(1)}, bf16[4096]{0:T(1024)(128)(2,1)}, u32[]{:S(2)}) copy-start(bf16[4096]{0:T(1024)(128)(2,1)} %param.17) | copy-start | bytes 24580
  0.7 28.0 %copy-start.8 = (f32[512]{0:T(512)S(1)}, f32[512]{0:T(512)}, u32[]{:S(2)}) copy-start(f32[512]{0:T(512)} %param.10) | copy-start | bytes 6148
  0.7 13.8 %all-to-all-start = ((s32[8,1,32]{2,1,0:T(1,128)}), s32[8,1,32]{2,1,0:T(1,128)S(1)}, u32[]{:S(2)}, u32[]{:S(2)}) async-start(s32[8,1,32]{2,1,0:T(1,128)} %bitcast.17), calls=%async_computation | async-start | bytes 8192 | tf_op jit(solution)/shard_map/all_to_all | solution.py:260
  8.1 1.2 %copy-start = (f32[1024,256]{1,0:T(8,128)S(1)}, f32[1024,256]{1,0:T(8,128)}, u32[]{:S(2)}) copy-start(f32[1024,256]{1,0:T(8,128)} %table_ref.3) | copy-start | bytes 3145732
  9.3 0.7 %copy-start.5 = (s32[64]{0:T(128)S(1)}, s32[64]{0:T(128)}, u32[]{:S(2)}) copy-start(s32[64]{0:T(128)} %param.15) | copy-start | bytes 772
  9.9 9.1 %copy-start.3 = (s32[512,32]{0,1:T(8,128)S(1)}, s32[512,32]{0,1:T(8,128)}, u32[]{:S(2)}) copy-start(s32[512,32]{0,1:T(8,128)} %param.9) | copy-start | bytes 196612
  9.9 18.7 %copy-start.2 = (bf16[256,4096]{1,0:T(8,128)(2,1)S(1)}, bf16[256,4096]{1,0:T(8,128)(2,1)}, u32[]{:S(2)}) copy-start(bf16[256,4096]{1,0:T(8,128)(2,1)} %w_in_ref.1) | copy-start | bytes 6291460
  15.6 11.6 %all-to-all-start.1 = ((bf16[8,64,256]{2,1,0:T(8,128)(2,1)}), bf16[8,64,256]{2,1,0:T(8,128)(2,1)S(1)}, u32[]{:S(2)}, u32[]{:S(2)}) async-start(bf16[8,64,256]{2,1,0:T(8,128)(2,1)} %shard_map.105), calls=%async_computation.1 | async-start | bytes 524288 | tf_op jit(solution)/shard_map/all_to_all | solution.py:260
  27.2 1.4 %collective-permute-start = (bf16[8,32,256]{2,1,0:T(8,128)(2,1)S(1)}, bf16[8,32,256]{2,1,0:T(8,128)(2,1)S(1)}, u32[]{:S(2)}, u32[]{:S(2)}) collective-permute-start(bf16[8,32,256]{2,1,0:T(8,128)(2,1)S(1)} %shard_map.107), channel_id=1, source_target_pairs={{0,8},{8,0},{16,24},{24,16},{1,9},{9,1},{17,25},{25,17},{2,10},{10... | collective-permute-start | bytes 393224 | tf_op jit(solution)/shard_map/ppermute | solution.py:264
  32.8 19.4 %copy-start.6 = (s32[64]{0:T(128)S(1)}, s32[64]{0:T(128)}, u32[]{:S(2)}) copy-start(s32[64]{0:T(128)} %param.15) | copy-start | bytes 772
  32.8 20.8 %copy-start.1 = (f32[1024,256]{1,0:T(8,128)S(1)}, f32[1024,256]{1,0:T(8,128)}, u32[]{:S(2)}) copy-start(f32[1024,256]{1,0:T(8,128)} %table_ref.3) | copy-start | bytes 3145732
  32.8 20.8 %copy-start.7 = (f32[1024]{0:T(1024)S(1)}, f32[1024]{0:T(1024)}, u32[]{:S(2)}) copy-start(f32[1024]{0:T(1024)} %param.14) | copy-start | bytes 12292
  33.3 1.4 %collective-permute-start.1 = (bf16[8,32,256]{2,1,0:T(8,128)(2,1)S(1)}, bf16[8,32,256]{2,1,0:T(8,128)(2,1)S(1)}, u32[]{:S(2)}, u32[]{:S(2)}) collective-permute-start(bf16[8,32,256]{2,1,0:T(8,128)(2,1)S(1)} %get-tuple-element.15), channel_id=1, source_target_pairs={{0,8},{8,0},{16,24},{24,16},{1,9},{9,1},{17,25},{25,17},{2,10},{10... | collective-permute-start | bytes 393224 | tf_op jit(solution)/shard_map/ppermute | solution.py:264
  47.0 5.3 %collective-permute-start.2 = (bf16[304,256]{1,0:T(8,128)(2,1)S(1)}, bf16[304,256]{1,0:T(8,128)(2,1)S(1)}, u32[]{:S(2)}, u32[]{:S(2)}) collective-permute-start(bf16[304,256]{1,0:T(8,128)(2,1)S(1)} %shard_map.111.refs_0_), channel_id=1, source_target_pairs={{0,16},{8,24},{16,0},{24,8},{1,17},{9,25},{17,1},{25,9},{2,18},{10... | collective-permute-start | bytes 466952 | tf_op jit(solution)/shard_map/ppermute | solution.py:264
  48.5 4.4 %collective-permute-start.3 = (bf16[304,256]{1,0:T(8,128)(2,1)S(1)}, bf16[304,256]{1,0:T(8,128)(2,1)S(1)}, u32[]{:S(2)}, u32[]{:S(2)}) collective-permute-start(bf16[304,256]{1,0:T(8,128)(2,1)S(1)} %shard_map.111.refs_0_), channel_id=1, source_target_pairs={{0,8},{8,0},{16,24},{24,16},{1,9},{9,1},{17,25},{25,17},{2,10},{10... | collective-permute-start | bytes 466952 | tf_op jit(solution)/shard_map/ppermute | solution.py:264
  52.2 1.4 %collective-permute-start.4 = (bf16[304,256]{1,0:T(8,128)(2,1)S(1)}, bf16[304,256]{1,0:T(8,128)(2,1)S(1)}, u32[]{:S(2)}, u32[]{:S(2)}) collective-permute-start(bf16[304,256]{1,0:T(8,128)(2,1)S(1)} %collective-permute-done.2.refs_1_), channel_id=1, source_target_pairs={{0,8},{8,0},{16,24},{24,16},{1,9},{9,1},{17,25},{25,17},{2,10},{10... | collective-permute-start | bytes 466952 | tf_op jit(solution)/shard_map/ppermute | solution.py:264

commit v9 on v8

--- a/solution.py
+++ b/solution.py
@@ -39,15 +39,22 @@
     return (lax.broadcasted_iota(i32, shape, axis) + start == ids).astype(f32).astype(bf16)
 
 
-def incidence_body(hot_cols, slot_cap, count_ref, slots_ref, out_ref, inc_t_ref):
+def incidence_body(hot_dev, slot_cap, count_ref, slots_ref, out_ref, inc_t_ref):
     vocab, batch = inc_t_ref.shape
+    owners = vocab // (hot_dev + slot_cap)
+    half = hot_dev // 2
+    hot_cols = owners * hot_dev
+    me = core()
     field = vocab // FIELDS
     step = 128
     row = lax.broadcasted_iota(i32, (field, step), 0)
     for start in range(0, batch, step):
         slots = slots_ref[:, start:start + step]
-        key = jnp.where(slots < 0, -1, slots % field)
-        unit = jnp.left_shift(jnp.ones_like(slots), FIELD_BITS * (slots // field))
+        place = slots % hot_dev
+        hot = jnp.where(place // half == me, 0, owners * half) + (slots // hot_dev) * half + place % half
+        column = jnp.where(slots < hot_cols, hot, slots)
+        key = jnp.where(slots < 0, -1, column % field)
+        unit = jnp.left_shift(jnp.ones_like(slots), FIELD_BITS * (column // field))
         packed = jnp.zeros((field, step), i32)
         for entry in range(slots.shape[0]):
             packed += jnp.where(row == key[entry:entry + 1, :], unit[entry:entry + 1, :], 0)
@@ -55,7 +62,7 @@
             part = jnp.right_shift(packed, FIELD_BITS * k) & (2**FIELD_BITS - 1)
             inc_t_ref[k * field:(k + 1) * field, start:start + step] = part.astype(f32).astype(bf16)
     place = lax.broadcasted_iota(i32, (slot_cap, batch), 0)
-    for owner in range((vocab - hot_cols) // slot_cap):
+    for owner in range(owners):
         rows = pl.ds(hot_cols + owner * slot_cap, slot_cap)
         inc_t_ref[rows, :] = jnp.where(place < count_ref[0, owner], inc_t_ref[rows, :].astype(f32), 0.0).astype(bf16)
     out_ref[...] = inc_t_ref[...].T
@@ -63,11 +70,6 @@
 
 def core():
     return lax.rem(lax.axis_index("dp"), 2)
-
-
-def half_rows(owner, hot_dev, which):
-    half = hot_dev // 2
-    return pl.ds(pl.multiple_of(owner * hot_dev + which * half, half), half)
 
 
 def pick_hot_body(ids_ref, table_ref, hot_ref, table_bf_ref, ids, table, sems):
@@ -90,10 +92,11 @@
     for t in range(owners):
         pick[t * slot_cap:(t + 1) * slot_cap, :] = one_hot(asked[:, t:t + 1], (slot_cap, table_ref.shape[0]), 1)
     picked = jnp.dot(pick[...], table_ref[...], preferred_element_type=f32).astype(bf16)
-    hot = hot_ref[half_rows(0, hot_dev, core()), :]
-    for t in range(owners):
-        staged[t, 0:hot_dev // 2, :] = hot
-        staged[t, hot_dev // 2:, :] = picked[t * slot_cap:(t + 1) * slot_cap]
+    half = hot_dev // 2
+    hot = hot_ref[pl.ds(pl.multiple_of(core() * half, half), half), :]
+    for t in range(owners):
+        staged[t, 0:half, :] = hot
+        staged[t, half:, :] = picked[t * slot_cap:(t + 1) * slot_cap]
     copy = pltpu.make_async_copy(staged, out_ref, sem)
     copy.start()
     copy.wait()
@@ -103,20 +106,18 @@
     out_ref[...] = rows_ref[:, 0:out_ref.shape[1], :]
 
 
-def top_body(labels_ref, inc_ref, own_ref, mate_ref, w_in_ref, w_out_ref, out_ref, gated, rows, pooled, total, dlogit):
+def top_body(labels_ref, inc_ref, own_ref, mate_ref, w_in_ref, w_out_ref, out_ref, hidden, rows, pooled, total, dlogit):
     batch = inc_ref.shape[0]
     hidden_units, width = w_in_ref.shape[1], w_in_ref.shape[0]
     owners, half, _ = mate_ref.shape
-    hot_dev = 2 * half
-    hot_cols = owners * hot_dev
+    hot_half = owners * half
     slot_cap = own_ref.shape[1] - half
-    me = core()
     size, step, wide = batch // 2, 512, 2048
     blocks = [slice(at, at + size) for at in range(0, batch, size)]
-    for t in range(owners):
-        rows[half_rows(t, hot_dev, me), :] = own_ref[t, 0:half, :]
-        rows[half_rows(t, hot_dev, 1 - me), :] = mate_ref[t, 0:half, :]
-        rows[hot_cols + t * slot_cap:hot_cols + (t + 1) * slot_cap, :] = own_ref[t, half:, :]
+    rows[hot_half:2 * hot_half, :] = mate_ref[...].reshape(hot_half, width)
+    for t in range(owners):
+        rows[t * half:(t + 1) * half, :] = own_ref[t, 0:half, :]
+        rows[2 * hot_half + t * slot_cap:2 * hot_half + (t + 1) * slot_cap, :] = own_ref[t, half:, :]
     pooled[...] = jnp.dot(inc_ref[...], rows[...], preferred_element_type=f32).astype(bf16)
     w_out = w_out_ref[...].astype(f32)
     for samples in blocks:
@@ -125,8 +126,9 @@
             cols = slice(start, start + step)
             pre_act = jnp.dot(pooled[samples, :], w_in_ref[:, cols], preferred_element_type=f32)
             own = lanes([w_out[k:k + 1, :] for k in range(start // 128, (start + step) // 128)])
-            gated[samples, cols] = jnp.where(pre_act > 0, own, 0.0).astype(bf16)
-            term = jnp.maximum(pre_act, 0.0).astype(bf16).astype(f32) * own
+            act = jnp.maximum(pre_act, 0.0).astype(bf16)
+            hidden[samples, cols] = act
+            term = act.astype(f32) * own
             for k in range(0, step, 128):
                 acc += term[:, k:k + 128]
         total[samples, :] = acc
@@ -140,7 +142,10 @@
         grad = jnp.zeros((size, width), f32)
         for start in range(0, hidden_units, wide):
             dhidden = lanes([
-                (scale * gated[samples, k:k + 128].astype(f32)).astype(bf16) for k in range(start, start + wide, 128)
+                jnp.where(
+                    hidden[samples, k:k + 128].astype(f32) > 0, scale * w_out[k // 128:k // 128 + 1, :], 0.0
+                ).astype(bf16)
+                for k in range(start, start + wide, 128)
             ])
             grad += lax.dot_general(
                 dhidden, w_in_ref[:, start:start + wide], (((1,), (1,)), ((), ())), preferred_element_type=f32
@@ -148,23 +153,27 @@
         out_ref[samples, :] = grad.astype(bf16)
 
 
-def slot_grads_body(inc_ref, dpooled_ref, part_ref, send_ref, rows):
-    owners, half, _ = send_ref.shape
-    hot_dev = 2 * half
-    hot_cols = owners * hot_dev
-    slot_cap = part_ref.shape[1] - half
-    me = core()
-    rows[...] = jnp.dot(inc_ref[...].T, dpooled_ref[...], preferred_element_type=f32).astype(bf16)
-    for t in range(owners):
-        send_ref[t] = rows[half_rows(t, hot_dev, 1 - me), :]
-        part_ref[t, 0:half, :] = rows[half_rows(t, hot_dev, me), :]
-        part_ref[t, half:, :] = rows[hot_cols + t * slot_cap:hot_cols + (t + 1) * slot_cap, :]
-
-
-def add_hot_body(part_ref, got_ref, out_ref):
-    half = got_ref.shape[1]
-    out_ref[:, 0:half, :] = (part_ref[:, 0:half, :].astype(f32) + got_ref[...].astype(f32)).astype(bf16)
-    out_ref[:, half:, :] = part_ref[:, half:, :]
+def mate_grads_body(inc_ref, dpooled_ref, out_ref):
+    hot_half = out_ref.shape[0]
+    out_ref[...] = jnp.dot(
+        inc_ref[:, hot_half:2 * hot_half].T, dpooled_ref[...], preferred_element_type=f32
+    ).astype(bf16)
+
+
+def own_grads_body(inc_ref, dpooled_ref, hot_ref, cold_ref):
+    hot_half = hot_ref.shape[0]
+    dpooled = dpooled_ref[...]
+    hot_ref[...] = jnp.dot(inc_ref[:, 0:hot_half].T, dpooled, preferred_element_type=f32)
+    cold_ref[...] = jnp.dot(inc_ref[:, 2 * hot_half:].T, dpooled, preferred_element_type=f32).astype(bf16)
+
+
+def pack_grads_body(hot_ref, got_ref, cold_ref, out_ref):
+    owners, half, width = got_ref.shape
+    hot = hot_ref[...] + got_ref[...].reshape(owners * half, width).astype(f32)
+    slot_cap = out_ref.shape[1] - half
+    for t in range(owners):
+        out_ref[t, 0:half, :] = hot[t * half:(t + 1) * half].astype(bf16)
+        out_ref[t, half:, :] = cold_ref[t * slot_cap:(t + 1) * slot_cap, :]
 
 
 def collect_body(asked_ref, back_ref, out_ref):
@@ -279,7 +288,7 @@
     hot_row = hot_ids.reshape(1, hot_dev)
     asked = exchange(cold_ids[0])
     inc = call(
-        functools.partial(incidence_body, owners * hot_dev, slot_cap),
+        functools.partial(incidence_body, hot_dev, slot_cap),
         shape((batch, vocab), bf16),
         (cold_count, bag_slots.T),
         [pltpu.VMEM((vocab, batch), bf16)],
@@ -317,13 +326,15 @@
             pltpu.VMEM((batch, 128), f32),
         ],
     )
-    part, to_mate = call(
-        slot_grads_body,
-        (shape((owners, half + slot_cap, width), bf16), shape((owners, half, width), bf16)),
+    hot_half = owners * half
+    to_mate = call(mate_grads_body, shape((hot_half, width), bf16), (inc, dpooled))
+    got = swap(to_mate.reshape(owners, half, width), 1)
+    hot_grads, cold_grads = call(
+        own_grads_body,
+        (shape((hot_half, width), f32), shape((owners * slot_cap, width), bf16)),
         (inc, dpooled),
-        [pltpu.VMEM((vocab, width), bf16)],
-    )
-    summed = call(add_hot_body, shape(part.shape, bf16), (part, swap(to_mate, 1)))
+    )
+    summed = call(pack_grads_body, shape((owners, half + slot_cap, width), bf16), (hot_grads, got, cold_grads))
     returned = exchange(summed)
     size = half + owners * slot_cap + TAIL
     if groups & (groups - 1) == 0 and groups * size <= 2 * rows and owners * slot_cap == width:

time: 56.2 us -> 55.5 us (0.988)
    pallas_call x10 -> x11, Pallas kernels: 11.7 us -> 11.5 us  [call(): pl.pallas_call(body, out_shape=outs, in_specs=in_specs or [VMEM] * len(op...]
where the time goes in v9:
time: 55.5 us; the launch traced here: 55.1 us
  waiting for transfers between devices  16.1 us (29%)
  starting transfers between devices  12.7 us (23%)
  blocking collectives  12.1 us (22%)
  Pallas kernels  11.5 us (21%)
  local copies, waits for them, and re-layouts  1.92 us (3%)
  between operations  0.78 us (1%)
    all_to_all x1, blocking collectives, exchange(): return lax.all_to_all(x, 'table', split_axis=0, concat_axis=0, tiled=True)  12.1 us
    pallas_call x11, Pallas kernels, call(): pl.pallas_call(body, out_shape=outs, in_specs=in_specs or [VMEM] * len(op...  11.5 us
    all_to_all x2, starting transfers between devices, exchange(): return lax.all_to_all(x, 'table', split_axis=0, concat_axis=0, tiled=True)  10.8 us
    all_to_all x2, waiting for transfers between devices, exchange(): return lax.all_to_all(x, 'table', split_axis=0, concat_axis=0, tiled=True)  9.49 us
    ppermute x5, waiting for transfers between devices, swap(): lax.ppermute(x, 'dp', [(g, g ^ bit) for g in range(lax.axis_size('dp'))])  6.62 us
    unnamed x20, local copies, waits for them, and re-layouts  1.92 us
    ppermute x5, starting transfers between devices, swap(): lax.ppermute(x, 'dp', [(g, g ^ bit) for g in range(lax.axis_size('dp'))])  1.84 us
  transfers between devices with their start and end apart: 7, of which 6 were waited for; matrix products, arithmetic and copies ran while one was open for 0% of the time, Pallas kernels for 7%

profile of v9, /device:TPU:0, one launch (start us, length us, event | category | flops | bytes accessed | tf_op | source)
XLA Modules:
  0.0 55.1 jit_solution(14527924080816437017)
XLA Ops:
  0.7 7.4 %all-to-all-start = ((s32[8,1,32]{2,1,0:T(1,128)}), s32[8,1,32]{2,1,0:T(1,128)S(1)}, u32[]{:S(2)}, u32[]{:S(2)}) async-start(s32[8,1,32]{2,1,0:T(1,128)} %bitcast.19), calls=%async_computation | async-start | bytes 8192 | tf_op jit(solution)/shard_map/all_to_all | solution.py:269
  8.1 1.2 %copy-done = f32[1024,256]{1,0:T(8,128)S(1)} copy-done((f32[1024,256]{1,0:T(8,128)S(1)}, f32[1024,256]{1,0:T(8,128)}, u32[]{:S(2)}) %copy-start) | copy-done | bytes 1048600
  9.3 0.7 %copy-done.5 = s32[64]{0:T(128)S(1)} copy-done((s32[64]{0:T(128)S(1)}, s32[64]{0:T(128)}, u32[]{:S(2)}) %copy-start.5) | copy-done | bytes 280
  9.9 0.4 shard_map.104
  10.4 4.1 %all-to-all-done = s32[8,1,32]{2,1,0:T(1,128)S(1)} async-done(((s32[8,1,32]{2,1,0:T(1,128)}), s32[8,1,32]{2,1,0:T(1,128)S(1)}, u32[]{:S(2)}, u32[]{:S(2)}) %all-to-all-start) | async-done | bytes 1056 | tf_op jit(solution)/shard_map/all_to_all | solution.py:269
  14.4 1.2 %shard_map.105 = bf16[8,64,256]{2,1,0:T(8,128)(2,1)} custom-call(s32[8,32]{1,0:T(8,128)S(1)} %bitcast.11, bf16[64,256]{1,0:T(8,128)(2,1)S(1)} %get-tuple-element.10.hot_ref, bf16[1024,256]{1,0:T(8,128)(2,1)S(1)} %get-tuple-element.11.table_ref), custom_call_target="tpu_custom_call" | custom-call | tf_op jit(solution)/shard_map/pallas_call | solution.py:24
  15.6 3.4 %all-to-all-start.1 = ((bf16[8,64,256]{2,1,0:T(8,128)(2,1)}), bf16[8,64,256]{2,1,0:T(8,128)(2,1)S(1)}, u32[]{:S(2)}, u32[]{:S(2)}) async-start(bf16[8,64,256]{2,1,0:T(8,128)(2,1)} %shard_map.105), calls=%async_computation.1 | async-start | bytes 524288 | tf_op jit(solution)/shard_map/all_to_all | solution.py:269
  19.1 2.7 %shard_map.106.inc_ref = bf16[512,768]{1,0:T(8,128)(2,1)S(1)} custom-call(s32[1,8]{1,0:T(1,128)S(1)} %copy-done.9, s32[32,512]{1,0:T(8,128)S(1)} %bitcast.10), custom_call_target="tpu_custom_call" | custom-call | tf_op jit(solution)/shard_map/pallas_call | solution.py:24
  21.8 5.4 %all-to-all-done.1.rows_ref.own_ref = bf16[8,64,256]{2,1,0:T(8,128)(2,1)S(1)} async-done(((bf16[8,64,256]{2,1,0:T(8,128)(2,1)}), bf16[8,64,256]{2,1,0:T(8,128)(2,1)S(1)}, u32[]{:S(2)}, u32[]{:S(2)}) %all-to-all-start.1) | async-done | bytes 262176 | tf_op jit(solution)/shard_map/all_to_all | solution.py:269
  27.2 0.1 collective-permute-start
  27.3 1.3 %collective-permute-done.mate_ref = bf16[8,32,256]{2,1,0:T(8,128)(2,1)S(1)} collective-permute-done((bf16[8,32,256]{2,1,0:T(8,128)(2,1)S(1)}, bf16[8,32,256]{2,1,0:T(8,128)(2,1)S(1)}, u32[]{:S(2)}, u32[]{:S(2)}) %collective-permute-start) | collective-permute-done | bytes 131104 | tf_op jit(solution)/shard_map/ppermute | solution.py:273
  28.6 3.7 %shard_map.108.dpooled_ref = bf16[512,256]{1,0:T(8,128)(2,1)S(1)} custom-call(f32[4,128]{1,0:T(4,128)S(1)} %bitcast.18, bf16[512,768]{1,0:T(8,128)(2,1)S(1)} %shard_map.106.inc_ref, bf16[8,64,256]{2,1,0:T(8,128)(2,1)S(1)} %all-to-all-done.1.rows_ref.own_ref, bf16[8,32,256]{2,1,0:T(8,128)(2,1)S(1)} %collective-permute-done.mate_ref, ...), custom_call_target="tpu_custom_call" | custom-call | tf_op jit(solution)/shard_map/pallas_call | solution.py:24
  32.4 0.0 copy-start.6
  32.4 0.3 shard_map.110
  32.7 0.2 collective-permute-start.1
  32.9 0.3 shard_map.109
  33.2 0.9 %collective-permute-done.1.got_ref = bf16[8,32,256]{2,1,0:T(8,128)(2,1)S(1)} collective-permute-done((bf16[8,32,256]{2,1,0:T(8,128)(2,1)S(1)}, bf16[8,32,256]{2,1,0:T(8,128)(2,1)S(1)}, u32[]{:S(2)}, u32[]{:S(2)}) %collective-permute-start.1) | collective-permute-done | bytes 131104 | tf_op jit(solution)/shard_map/ppermute | solution.py:273
  34.1 12.1 %all_to_all.21.back_ref = bf16[8,64,256]{2,1,0:T(8,128)(2,1)S(1)} all-to-all(bf16[8,64,256]{2,1,0:T(8,128)(2,1)S(1)} %shard_map.111), channel_id=1, replica_groups=mesh['dp'=4,'table'=8] {'table'}, dimensions={0} | all-to-all | bytes 524288 | tf_op jit(solution)/shard_map/all_to_all | solution.py:269
  46.2 0.1 shard_map.112.refs_0_
  46.3 1.6 %collective-permute-start.2 = (bf16[304,256]{1,0:T(8,128)(2,1)S(1)}, bf16[304,256]{1,0:T(8,128)(2,1)S(1)}, u32[]{:S(2)}, u32[]{:S(2)}) collective-permute-start(bf16[304,256]{1,0:T(8,128)(2,1)S(1)} %shard_map.112.refs_0_), channel_id=1, source_target_pairs={{0,16},{8,24},{16,0},{24,8},{1,17},{9,25},{17,1},{25,9},{2,18},{10... | collective-permute-start | bytes 466952 | tf_op jit(solution)/shard_map/ppermute | solution.py:273
  47.9 3.7 %collective-permute-done.2.refs_1_ = bf16[304,256]{1,0:T(8,128)(2,1)S(1)} collective-permute-done((bf16[304,256]{1,0:T(8,128)(2,1)S(1)}, bf16[304,256]{1,0:T(8,128)(2,1)S(1)}, u32[]{:S(2)}, u32[]{:S(2)}) %collective-permute-start.2) | collective-permute-done | bytes 155680 | tf_op jit(solution)/shard_map/ppermute | solution.py:273
  51.6 0.7 %shard_map.113.grad_ref = f32[1024,256]{1,0:T(8,128)S(1)} custom-call(s32[1,64]{1,0:T(1,128)S(1)} %bitcast.15, bf16[304,256]{1,0:T(8,128)(2,1)S(1)} %shard_map.112.refs_0_, bf16[304,256]{1,0:T(8,128)(2,1)S(1)} %collective-permute-done.2.refs_1_), custom_call_target="tpu_custom_call" | custom-call | tf_op jit(solution)/shard_map/pallas_call | solution.py:24
  52.3 0.7 %collective-permute-done.4.refs_1_ = bf16[304,256]{1,0:T(8,128)(2,1)S(1)} collective-permute-done((bf16[304,256]{1,0:T(8,128)(2,1)S(1)}, bf16[304,256]{1,0:T(8,128)(2,1)S(1)}, u32[]{:S(2)}, u32[]{:S(2)}) %collective-permute-start.4) | collective-permute-done | bytes 155680 | tf_op jit(solution)/shard_map/ppermute | solution.py:273
  53.0 2.1 %shard_map.114 = (f32[1024,256]{1,0:T(8,128)}, f32[8,128]{1,0:T(8,128)}) custom-call(s32[1,64]{1,0:T(1,128)S(1)} %bitcast.16, f32[8,128]{1,0:T(8,128)S(1)} %bitcast.17, f32[1024,256]{1,0:T(8,128)S(1)} %copy-done.1, f32[1024,256]{1,0:T(8,128)S(1)} %shard_map.113.grad_ref, bf16[304,256]{1,0:T(8,128)(2,1)S(1)} %collective-permute-done.3.refs_0_, ...), custom_call_target="tpu_custom_call" | custom-call | tf_op jit(solution)/shard_map/pallas_call | solution.py:24
  (22 shorter events, 0.1 us)
Async XLA Ops:
  0.6 18.4 %copy-start.9 = (s32[1,8]{1,0:T(1,128)S(1)}, s32[1,8]{1,0:T(1,128)}, u32[]{:S(2)}) copy-start(s32[1,8]{1,0:T(1,128)} %count_ref.1) | copy-start | bytes 100
  0.6 28.0 %copy-start.4 = (bf16[4096]{0:T(1024)(128)(2,1)S(1)}, bf16[4096]{0:T(1024)(128)(2,1)}, u32[]{:S(2)}) copy-start(bf16[4096]{0:T(1024)(128)(2,1)} %param.17) | copy-start | bytes 24580
  0.7 28.0 %copy-start.8 = (f32[512]{0:T(512)S(1)}, f32[512]{0:T(512)}, u32[]{:S(2)}) copy-start(f32[512]{0:T(512)} %param.10) | copy-start | bytes 6148
  0.7 13.8 %all-to-all-start = ((s32[8,1,32]{2,1,0:T(1,128)}), s32[8,1,32]{2,1,0:T(1,128)S(1)}, u32[]{:S(2)}, u32[]{:S(2)}) async-start(s32[8,1,32]{2,1,0:T(1,128)} %bitcast.19), calls=%async_computation | async-start | bytes 8192 | tf_op jit(solution)/shard_map/all_to_all | solution.py:269
  8.1 1.2 %copy-start = (f32[1024,256]{1,0:T(8,128)S(1)}, f32[1024,256]{1,0:T(8,128)}, u32[]{:S(2)}) copy-start(f32[1024,256]{1,0:T(8,128)} %table_ref.3) | copy-start | bytes 3145732
  9.3 0.7 %copy-start.5 = (s32[64]{0:T(128)S(1)}, s32[64]{0:T(128)}, u32[]{:S(2)}) copy-start(s32[64]{0:T(128)} %param.15) | copy-start | bytes 772
  9.9 9.1 %copy-start.3 = (s32[512,32]{0,1:T(8,128)S(1)}, s32[512,32]{0,1:T(8,128)}, u32[]{:S(2)}) copy-start(s32[512,32]{0,1:T(8,128)} %param.9) | copy-start | bytes 196612
  9.9 18.7 %copy-start.2 = (bf16[256,4096]{1,0:T(8,128)(2,1)S(1)}, bf16[256,4096]{1,0:T(8,128)(2,1)}, u32[]{:S(2)}) copy-start(bf16[256,4096]{1,0:T(8,128)(2,1)} %w_in_ref.1) | copy-start | bytes 6291460
  15.6 11.6 %all-to-all-start.1 = ((bf16[8,64,256]{2,1,0:T(8,128)(2,1)}), bf16[8,64,256]{2,1,0:T(8,128)(2,1)S(1)}, u32[]{:S(2)}, u32[]{:S(2)}) async-start(bf16[8,64,256]{2,1,0:T(8,128)(2,1)} %shard_map.105), calls=%async_computation.1 | async-start | bytes 524288 | tf_op jit(solution)/shard_map/all_to_all | solution.py:269
  27.2 1.4 %collective-permute-start = (bf16[8,32,256]{2,1,0:T(8,128)(2,1)S(1)}, bf16[8,32,256]{2,1,0:T(8,128)(2,1)S(1)}, u32[]{:S(2)}, u32[]{:S(2)}) collective-permute-start(bf16[8,32,256]{2,1,0:T(8,128)(2,1)S(1)} %shard_map.107), channel_id=1, source_target_pairs={{0,8},{8,0},{16,24},{24,16},{1,9},{9,1},{17,25},{25,17},{2,10},{10... | collective-permute-start | bytes 393224 | tf_op jit(solution)/shard_map/ppermute | solution.py:273
  32.4 19.2 %copy-start.6 = (s32[64]{0:T(128)S(1)}, s32[64]{0:T(128)}, u32[]{:S(2)}) copy-start(s32[64]{0:T(128)} %param.15) | copy-start | bytes 772
  32.6 20.3 %copy-start.1 = (f32[1024,256]{1,0:T(8,128)S(1)}, f32[1024,256]{1,0:T(8,128)}, u32[]{:S(2)}) copy-start(f32[1024,256]{1,0:T(8,128)} %table_ref.3) | copy-start | bytes 3145732
  32.7 20.3 %copy-start.7 = (f32[1024]{0:T(1024)S(1)}, f32[1024]{0:T(1024)}, u32[]{:S(2)}) copy-start(f32[1024]{0:T(1024)} %param.14) | copy-start | bytes 12292
  32.7 1.4 %collective-permute-start.1 = (bf16[8,32,256]{2,1,0:T(8,128)(2,1)S(1)}, bf16[8,32,256]{2,1,0:T(8,128)(2,1)S(1)}, u32[]{:S(2)}, u32[]{:S(2)}) collective-permute-start(bf16[8,32,256]{2,1,0:T(8,128)(2,1)S(1)} %bitcast.9), channel_id=1, source_target_pairs={{0,8},{8,0},{16,24},{24,16},{1,9},{9,1},{17,25},{25,17},{2,10},{10... | collective-permute-start | bytes 393224 | tf_op jit(solution)/shard_map/ppermute | solution.py:273
  46.3 5.3 %collective-permute-start.2 = (bf16[304,256]{1,0:T(8,128)(2,1)S(1)}, bf16[304,256]{1,0:T(8,128)(2,1)S(1)}, u32[]{:S(2)}, u32[]{:S(2)}) collective-permute-start(bf16[304,256]{1,0:T(8,128)(2,1)S(1)} %shard_map.112.refs_0_), channel_id=1, source_target_pairs={{0,16},{8,24},{16,0},{24,8},{1,17},{9,25},{17,1},{25,9},{2,18},{10... | collective-permute-start | bytes 466952 | tf_op jit(solution)/shard_map/ppermute | solution.py:273
  47.9 4.4 %collective-permute-start.3 = (bf16[304,256]{1,0:T(8,128)(2,1)S(1)}, bf16[304,256]{1,0:T(8,128)(2,1)S(1)}, u32[]{:S(2)}, u32[]{:S(2)}) collective-permute-start(bf16[304,256]{1,0:T(8,128)(2,1)S(1)} %shard_map.112.refs_0_), channel_id=1, source_target_pairs={{0,8},{8,0},{16,24},{24,16},{1,9},{9,1},{17,25},{25,17},{2,10},{10... | collective-permute-start | bytes 466952 | tf_op jit(solution)/shard_map/ppermute | solution.py:273
  51.6 1.4 %collective-permute-start.4 = (bf16[304,256]{1,0:T(8,128)(2,1)S(1)}, bf16[304,256]{1,0:T(8,128)(2,1)S(1)}, u32[]{:S(2)}, u32[]{:S(2)}) collective-permute-start(bf16[304,256]{1,0:T(8,128)(2,1)S(1)} %collective-permute-done.2.refs_1_), channel_id=1, source_target_pairs={{0,8},{8,0},{16,24},{24,16},{1,9},{9,1},{17,25},{25,17},{2,10},{10... | collective-permute-start | bytes 466952 | tf_op jit(solution)/shard_map/ppermute | solution.py:273

commit v10 on v9

--- a/solution.py
+++ b/solution.py
@@ -39,13 +39,13 @@
     return (lax.broadcasted_iota(i32, shape, axis) + start == ids).astype(f32).astype(bf16)
 
 
-def incidence_body(hot_dev, slot_cap, count_ref, slots_ref, out_ref, inc_t_ref):
-    vocab, batch = inc_t_ref.shape
-    owners = vocab // (hot_dev + slot_cap)
+def count_body(hot_dev, count_ref, slots_ref, packed_ref):
+    field, batch = packed_ref.shape
+    owners = count_ref.shape[1]
+    slot_cap = FIELDS * field // owners - hot_dev
     half = hot_dev // 2
     hot_cols = owners * hot_dev
     me = core()
-    field = vocab // FIELDS
     step = 128
     row = lax.broadcasted_iota(i32, (field, step), 0)
     for start in range(0, batch, step):
@@ -53,18 +53,24 @@
         place = slots % hot_dev
         hot = jnp.where(place // half == me, 0, owners * half) + (slots // hot_dev) * half + place % half
         column = jnp.where(slots < hot_cols, hot, slots)
-        key = jnp.where(slots < 0, -1, column % field)
+        cold = slots - hot_cols
+        live = slots >= 0
+        for t in range(owners):
+            at = cold - t * slot_cap
+            live = live & ((at < count_ref[0, t]) | (at >= slot_cap))
+        key = jnp.where(live, column % field, -1)
         unit = jnp.left_shift(jnp.ones_like(slots), FIELD_BITS * (column // field))
         packed = jnp.zeros((field, step), i32)
         for entry in range(slots.shape[0]):
             packed += jnp.where(row == key[entry:entry + 1, :], unit[entry:entry + 1, :], 0)
-        for k in range(FIELDS):
-            part = jnp.right_shift(packed, FIELD_BITS * k) & (2**FIELD_BITS - 1)
-            inc_t_ref[k * field:(k + 1) * field, start:start + step] = part.astype(f32).astype(bf16)
-    place = lax.broadcasted_iota(i32, (slot_cap, batch), 0)
-    for owner in range(owners):
-        rows = pl.ds(hot_cols + owner * slot_cap, slot_cap)
-        inc_t_ref[rows, :] = jnp.where(place < count_ref[0, owner], inc_t_ref[rows, :].astype(f32), 0.0).astype(bf16)
+        packed_ref[:, start:start + step] = packed
+
+
+def incidence_body(packed_ref, out_ref, inc_t_ref):
+    field = packed_ref.shape[0]
+    for k in range(FIELDS):
+        part = jnp.right_shift(packed_ref[...], FIELD_BITS * k) & (2**FIELD_BITS - 1)
+        inc_t_ref[k * field:(k + 1) * field, :] = part.astype(f32).astype(bf16)
     out_ref[...] = inc_t_ref[...].T
 
 
@@ -85,21 +91,17 @@
     hot_ref[...] = jnp.dot(pick, table_bf_ref[...], preferred_element_type=f32).astype(bf16)
 
 
-def serve_body(asked_ref, hot_ref, table_ref, out_ref, pick, staged, sem):
+def serve_body(asked_ref, hot_ref, table_ref, out_ref, pick):
     owners, slot_cap = asked_ref.shape
-    hot_dev = hot_ref.shape[0]
+    half = hot_ref.shape[0] // 2
     asked = asked_ref[...].T
     for t in range(owners):
         pick[t * slot_cap:(t + 1) * slot_cap, :] = one_hot(asked[:, t:t + 1], (slot_cap, table_ref.shape[0]), 1)
     picked = jnp.dot(pick[...], table_ref[...], preferred_element_type=f32).astype(bf16)
-    half = hot_dev // 2
     hot = hot_ref[pl.ds(pl.multiple_of(core() * half, half), half), :]
     for t in range(owners):
-        staged[t, 0:half, :] = hot
-        staged[t, half:, :] = picked[t * slot_cap:(t + 1) * slot_cap]
-    copy = pltpu.make_async_copy(staged, out_ref, sem)
-    copy.start()
-    copy.wait()
+        out_ref[t, 0:half, :] = hot
+        out_ref[t, half:, :] = picked[t * slot_cap:(t + 1) * slot_cap]
 
 
 def first_rows_body(rows_ref, out_ref):
@@ -233,10 +235,12 @@
     def put(at, grad):
         grad = grad_ref[at, :] + grad
         grads[at, :] = grad
-        squares[:, at.start // step:at.stop // step] = jnp.sum(grad * grad, axis=1, keepdims=True)
+        square = grad * grad
+        square = sum(square[:, k:k + 128] for k in range(0, width, 128)).T
+        squares[at.start // step:at.stop // step, :] = jnp.sum(square, axis=0, keepdims=True)
 
     row_grads(1 - core(), hot_ref, part_refs, held, put, rows)
-    new_sum = sum_ref[...] + squares[...].T * (1.0 / width)
+    new_sum = sum_ref[...] + squares[...] * (1.0 / width)
     sums[...] = new_sum
     scale = (learning_rate / jnp.sqrt(new_sum)).T
     for start in range(0, rows, step):
@@ -287,13 +291,13 @@
 
     hot_row = hot_ids.reshape(1, hot_dev)
     asked = exchange(cold_ids[0])
-    inc = call(
-        functools.partial(incidence_body, hot_dev, slot_cap),
-        shape((batch, vocab), bf16),
+    packed = call(
+        functools.partial(count_body, hot_dev),
+        shape((vocab // FIELDS, batch), i32),
         (cold_count, bag_slots.T),
-        [pltpu.VMEM((vocab, batch), bf16)],
         in_specs=[SMEM, VMEM],
     )
+    asked, packed = lax.optimization_barrier((asked, packed))
     hot, table_bf = call(
         pick_hot_body,
         (shape((hot_dev, width), bf16), shape((rows, width), bf16)),
@@ -305,15 +309,13 @@
         serve_body,
         shape((owners, half + slot_cap, width), bf16),
         (asked, hot, table_bf),
-        [
-            pltpu.VMEM((owners * slot_cap, rows), bf16),
-            pltpu.VMEM((owners, half + slot_cap, width), bf16),
-            pltpu.SemaphoreType.DMA,
-        ],
-        out_specs=HBM,
-    )
-    own_rows, inc = lax.optimization_barrier((exchange(served), inc))
-    mate_rows = swap(call(first_rows_body, shape((owners, half, width), bf16), (own_rows,)), 1)
+        [pltpu.VMEM((owners * slot_cap, rows), bf16)],
+    )
+    own_rows = exchange(served)
+    first_rows = call(first_rows_body, shape((owners, half, width), bf16), (own_rows,))
+    first_rows, packed = lax.optimization_barrier((first_rows, packed))
+    mate_rows = swap(first_rows, 1)
+    inc = call(incidence_body, shape((batch, vocab), bf16), (packed,), [pltpu.VMEM((vocab, batch), bf16)])
     dpooled = call(
         top_body,
         shape((batch, width), bf16),
@@ -353,7 +355,7 @@
             (hot_row, adagrad_sum.reshape(-1, 128), table, grad, *far),
             [
                 held,
-                pltpu.VMEM((128, rows // 128), f32),
+                pltpu.VMEM((rows // 128, 128), f32),
                 pltpu.VMEM((rows, width), f32),
                 pltpu.VMEM((rows, width), f32),
                 pltpu.VMEM((rows // 128, 128), f32),

time: 55.5 us -> 57.5 us (1.036)
  blocking collectives: 12.1 us -> 26.6 us
  waiting for transfers between devices: 16.1 us -> 6.51 us
  starting transfers between devices: 12.7 us -> 9.1 us
  local copies, waits for them, and re-layouts: 1.92 us -> 3.4 us
  Pallas kernels: 11.5 us -> 10.8 us
    all_to_all x1 -> x2, blocking collectives: 12.1 us -> 26.6 us  [exchange(): return lax.all_to_all(x, 'table', split_axis=0, concat_axis=0, tiled=True)]
    all_to_all x2 -> x1, waiting for transfers between devices: 9.49 us -> 0.16 us  [exchange(): return lax.all_to_all(x, 'table', split_axis=0, concat_axis=0, tiled=True)]
    all_to_all x2 -> x1, starting transfers between devices: 10.8 us -> 7.26 us  [exchange(): return lax.all_to_all(x, 'table', split_axis=0, concat_axis=0, tiled=True)]
    unnamed x20, local copies, waits for them, and re-layouts: 1.92 us -> 3.4 us
    pallas_call x11 -> x12, Pallas kernels: 11.5 us -> 10.8 us  [call(): pl.pallas_call(body, out_shape=outs, in_specs=in_specs or [VMEM] * len(op...]
  transfers between devices with their start and end apart: 7 -> 6, of which waited for: 6 -> 5; matrix products, arithmetic and copies ran while one was open for 0% -> 0% of each run, Pallas kernels for 7% -> 7%
where the time goes in v10:
time: 57.5 us; the launch traced here: 57.1 us
  blocking collectives  26.6 us (46%)
  Pallas kernels  10.8 us (19%)
  starting transfers between devices  9.1 us (16%)
  waiting for transfers between devices  6.51 us (11%)
  local copies, waits for them, and re-layouts  3.4 us (6%)
  between operations  0.75 us (1%)
    all_to_all x2, blocking collectives, exchange(): return lax.all_to_all(x, 'table', split_axis=0, concat_axis=0, tiled=True)  26.6 us
    pallas_call x12, Pallas kernels, call(): pl.pallas_call(body, out_shape=outs, in_specs=in_specs or [VMEM] * len(op...  10.8 us
    all_to_all x1, starting transfers between devices, exchange(): return lax.all_to_all(x, 'table', split_axis=0, concat_axis=0, tiled=True)  7.26 us
    ppermute x5, waiting for transfers between devices, swap(): lax.ppermute(x, 'dp', [(g, g ^ bit) for g in range(lax.axis_size('dp'))])  6.36 us
    unnamed x20, local copies, waits for them, and re-layouts  3.4 us
    ppermute x5, starting transfers between devices, swap(): lax.ppermute(x, 'dp', [(g, g ^ bit) for g in range(lax.axis_size('dp'))])  1.84 us
  transfers between devices with their start and end apart: 6, of which 5 were waited for; matrix products, arithmetic and copies ran while one was open for 0% of the time, Pallas kernels for 7%

profile of v10, /device:TPU:0, one launch (start us, length us, event | category | flops | bytes accessed | tf_op | source)
XLA Modules:
  0.0 57.1 jit_solution(8761598581055047199)
XLA Ops:
  0.6 7.3 %all-to-all-start = ((s32[8,1,32]{2,1,0:T(1,128)}), s32[8,1,32]{2,1,0:T(1,128)S(1)}, u32[]{:S(2)}, u32[]{:S(2)}) async-start(s32[8,1,32]{2,1,0:T(1,128)} %bitcast.19), calls=%async_computation | async-start | bytes 8192 | tf_op jit(solution)/shard_map/all_to_all | solution.py:273
  7.9 0.8 %copy-done.3 = s32[512,32]{0,1:T(8,128)S(1)} copy-done((s32[512,32]{0,1:T(8,128)S(1)}, s32[512,32]{0,1:T(8,128)}, u32[]{:S(2)}) %copy-start.3) | copy-done | bytes 65560
  8.7 0.7 %copy-done.9 = s32[1,8]{1,0:T(1,128)S(1)} copy-done((s32[1,8]{1,0:T(1,128)S(1)}, s32[1,8]{1,0:T(1,128)}, u32[]{:S(2)}) %copy-start.9) | copy-done | bytes 56
  9.4 2.4 %shard_map.104.packed_ref = s32[192,512]{1,0:T(8,128)S(1)} custom-call(s32[1,8]{1,0:T(1,128)S(1)} %copy-done.9, s32[32,512]{1,0:T(8,128)S(1)} %bitcast.10), custom_call_target="tpu_custom_call" | custom-call | tf_op jit(solution)/shard_map/pallas_call | solution.py:24
  11.8 1.2 %copy-done = f32[1024,256]{1,0:T(8,128)S(1)} copy-done((f32[1024,256]{1,0:T(8,128)S(1)}, f32[1024,256]{1,0:T(8,128)}, u32[]{:S(2)}) %copy-start) | copy-done | bytes 1048600
  13.0 0.7 %copy-done.5 = s32[64]{0:T(128)S(1)} copy-done((s32[64]{0:T(128)S(1)}, s32[64]{0:T(128)}, u32[]{:S(2)}) %copy-start.5) | copy-done | bytes 280
  13.7 0.4 shard_map.105
  14.1 0.2 all-to-all-done
  14.3 0.4 shard_map.106
  14.7 14.2 %all_to_all.22.rows_ref.own_ref = bf16[8,64,256]{2,1,0:T(8,128)(2,1)S(1)} all-to-all(bf16[8,64,256]{2,1,0:T(8,128)(2,1)S(1)} %shard_map.106), channel_id=1, replica_groups=mesh['dp'=4,'table'=8] {'table'}, dimensions={0} | all-to-all | bytes 524288 | tf_op jit(solution)/shard_map/all_to_all | solution.py:273
  29.0 0.3 shard_map.108.inc_ref
  29.2 1.1 %collective-permute-done.mate_ref = bf16[8,32,256]{2,1,0:T(8,128)(2,1)S(1)} collective-permute-done((bf16[8,32,256]{2,1,0:T(8,128)(2,1)S(1)}, bf16[8,32,256]{2,1,0:T(8,128)(2,1)S(1)}, u32[]{:S(2)}, u32[]{:S(2)}) %collective-permute-start) | collective-permute-done | bytes 131104 | tf_op jit(solution)/shard_map/ppermute | solution.py:277
  30.3 3.8 %shard_map.109.dpooled_ref = bf16[512,256]{1,0:T(8,128)(2,1)S(1)} custom-call(f32[4,128]{1,0:T(4,128)S(1)} %bitcast.18, bf16[512,768]{1,0:T(8,128)(2,1)S(1)} %shard_map.108.inc_ref, bf16[8,64,256]{2,1,0:T(8,128)(2,1)S(1)} %all_to_all.22.rows_ref.own_ref, bf16[8,32,256]{2,1,0:T(8,128)(2,1)S(1)} %collective-permute-done.mate_ref, ...), custom_call_target="tpu_custom_call" | custom-call | tf_op jit(solution)/shard_map/pallas_call | solution.py:24
  34.1 0.3 shard_map.111
  34.4 0.2 collective-permute-start.1
  34.6 0.3 shard_map.110
  34.9 0.9 %collective-permute-done.1.got_ref = bf16[8,32,256]{2,1,0:T(8,128)(2,1)S(1)} collective-permute-done((bf16[8,32,256]{2,1,0:T(8,128)(2,1)S(1)}, bf16[8,32,256]{2,1,0:T(8,128)(2,1)S(1)}, u32[]{:S(2)}, u32[]{:S(2)}) %collective-permute-start.1) | collective-permute-done | bytes 131104 | tf_op jit(solution)/shard_map/ppermute | solution.py:277
  35.8 12.5 %all_to_all.23.back_ref = bf16[8,64,256]{2,1,0:T(8,128)(2,1)S(1)} all-to-all(bf16[8,64,256]{2,1,0:T(8,128)(2,1)S(1)} %shard_map.112), channel_id=1, replica_groups=mesh['dp'=4,'table'=8] {'table'}, dimensions={0} | all-to-all | bytes 524288 | tf_op jit(solution)/shard_map/all_to_all | solution.py:273
  48.3 0.1 shard_map.113.refs_0_
  48.4 1.6 %collective-permute-start.2 = (bf16[304,256]{1,0:T(8,128)(2,1)S(1)}, bf16[304,256]{1,0:T(8,128)(2,1)S(1)}, u32[]{:S(2)}, u32[]{:S(2)}) collective-permute-start(bf16[304,256]{1,0:T(8,128)(2,1)S(1)} %shard_map.113.refs_0_), channel_id=1, source_target_pairs={{0,16},{8,24},{16,0},{24,8},{1,17},{9,25},{17,1},{25,9},{2,18},{10... | collective-permute-start | bytes 466952 | tf_op jit(solution)/shard_map/ppermute | solution.py:277
  49.9 3.7 %collective-permute-done.2.refs_1_ = bf16[304,256]{1,0:T(8,128)(2,1)S(1)} collective-permute-done((bf16[304,256]{1,0:T(8,128)(2,1)S(1)}, bf16[304,256]{1,0:T(8,128)(2,1)S(1)}, u32[]{:S(2)}, u32[]{:S(2)}) %collective-permute-start.2) | collective-permute-done | bytes 155680 | tf_op jit(solution)/shard_map/ppermute | solution.py:277
  53.7 0.7 %shard_map.114.grad_ref = f32[1024,256]{1,0:T(8,128)S(1)} custom-call(s32[1,64]{1,0:T(1,128)S(1)} %bitcast.15, bf16[304,256]{1,0:T(8,128)(2,1)S(1)} %shard_map.113.refs_0_, bf16[304,256]{1,0:T(8,128)(2,1)S(1)} %collective-permute-done.2.refs_1_), custom_call_target="tpu_custom_call" | custom-call | tf_op jit(solution)/shard_map/pallas_call | solution.py:24
  54.3 0.7 %collective-permute-done.4.refs_1_ = bf16[304,256]{1,0:T(8,128)(2,1)S(1)} collective-permute-done((bf16[304,256]{1,0:T(8,128)(2,1)S(1)}, bf16[304,256]{1,0:T(8,128)(2,1)S(1)}, u32[]{:S(2)}, u32[]{:S(2)}) %collective-permute-start.4) | collective-permute-done | bytes 155680 | tf_op jit(solution)/shard_map/ppermute | solution.py:277
  55.0 2.1 %shard_map.115 = (f32[1024,256]{1,0:T(8,128)}, f32[8,128]{1,0:T(8,128)}) custom-call(s32[1,64]{1,0:T(1,128)S(1)} %bitcast.16, f32[8,128]{1,0:T(8,128)S(1)} %bitcast.17, f32[1024,256]{1,0:T(8,128)S(1)} %copy-done.1, f32[1024,256]{1,0:T(8,128)S(1)} %shard_map.114.grad_ref, bf16[304,256]{1,0:T(8,128)(2,1)S(1)} %collective-permute-done.3.refs_0_, ...), custom_call_target="tpu_custom_call" | custom-call | tf_op jit(solution)/shard_map/pallas_call | solution.py:24
  (22 shorter events, 0.2 us)
Async XLA Ops:
  0.6 13.7 %all-to-all-start = ((s32[8,1,32]{2,1,0:T(1,128)}), s32[8,1,32]{2,1,0:T(1,128)S(1)}, u32[]{:S(2)}, u32[]{:S(2)}) async-start(s32[8,1,32]{2,1,0:T(1,128)} %bitcast.19), calls=%async_computation | async-start | bytes 8192 | tf_op jit(solution)/shard_map/all_to_all | solution.py:273
  7.9 0.8 %copy-start.3 = (s32[512,32]{0,1:T(8,128)S(1)}, s32[512,32]{0,1:T(8,128)}, u32[]{:S(2)}) copy-start(s32[512,32]{0,1:T(8,128)} %param.9) | copy-start | bytes 196612
  8.7 0.7 %copy-start.9 = (s32[1,8]{1,0:T(1,128)S(1)}, s32[1,8]{1,0:T(1,128)}, u32[]{:S(2)}) copy-start(s32[1,8]{1,0:T(1,128)} %count_ref.1) | copy-start | bytes 100
  11.8 1.2 %copy-start = (f32[1024,256]{1,0:T(8,128)S(1)}, f32[1024,256]{1,0:T(8,128)}, u32[]{:S(2)}) copy-start(f32[1024,256]{1,0:T(8,128)} %table_ref.3) | copy-start | bytes 3145732
  13.0 0.7 %copy-start.5 = (s32[64]{0:T(128)S(1)}, s32[64]{0:T(128)}, u32[]{:S(2)}) copy-start(s32[64]{0:T(128)} %param.15) | copy-start | bytes 772
  13.7 16.6 %copy-start.2 = (bf16[256,4096]{1,0:T(8,128)(2,1)S(1)}, bf16[256,4096]{1,0:T(8,128)(2,1)}, u32[]{:S(2)}) copy-start(bf16[256,4096]{1,0:T(8,128)(2,1)} %w_in_ref.1) | copy-start | bytes 6291460
  13.7 16.6 %copy-start.4 = (bf16[4096]{0:T(1024)(128)(2,1)S(1)}, bf16[4096]{0:T(1024)(128)(2,1)}, u32[]{:S(2)}) copy-start(bf16[4096]{0:T(1024)(128)(2,1)} %param.17) | copy-start | bytes 24580
  13.7 16.6 %copy-start.8 = (f32[512]{0:T(512)S(1)}, f32[512]{0:T(512)}, u32[]{:S(2)}) copy-start(f32[512]{0:T(512)} %param.10) | copy-start | bytes 6148
  28.9 1.4 %collective-permute-start = (bf16[8,32,256]{2,1,0:T(8,128)(2,1)S(1)}, bf16[8,32,256]{2,1,0:T(8,128)(2,1)S(1)}, u32[]{:S(2)}, u32[]{:S(2)}) collective-permute-start(bf16[8,32,256]{2,1,0:T(8,128)(2,1)S(1)} %shard_map.107), channel_id=1, source_target_pairs={{0,8},{8,0},{16,24},{24,16},{1,9},{9,1},{17,25},{25,17},{2,10},{10... | collective-permute-start | bytes 393224 | tf_op jit(solution)/shard_map/ppermute | solution.py:277
  34.1 19.6 %copy-start.6 = (s32[64]{0:T(128)S(1)}, s32[64]{0:T(128)}, u32[]{:S(2)}) copy-start(s32[64]{0:T(128)} %param.15) | copy-start | bytes 772
  34.4 20.7 %copy-start.1 = (f32[1024,256]{1,0:T(8,128)S(1)}, f32[1024,256]{1,0:T(8,128)}, u32[]{:S(2)}) copy-start(f32[1024,256]{1,0:T(8,128)} %table_ref.3) | copy-start | bytes 3145732
  34.4 20.7 %copy-start.7 = (f32[1024]{0:T(1024)S(1)}, f32[1024]{0:T(1024)}, u32[]{:S(2)}) copy-start(f32[1024]{0:T(1024)} %param.14) | copy-start | bytes 12292
  34.4 1.4 %collective-permute-start.1 = (bf16[8,32,256]{2,1,0:T(8,128)(2,1)S(1)}, bf16[8,32,256]{2,1,0:T(8,128)(2,1)S(1)}, u32[]{:S(2)}, u32[]{:S(2)}) collective-permute-start(bf16[8,32,256]{2,1,0:T(8,128)(2,1)S(1)} %bitcast.9), channel_id=1, source_target_pairs={{0,8},{8,0},{16,24},{24,16},{1,9},{9,1},{17,25},{25,17},{2,10},{10... | collective-permute-start | bytes 393224 | tf_op jit(solution)/shard_map/ppermute | solution.py:277
  48.4 5.3 %collective-permute-start.2 = (bf16[304,256]{1,0:T(8,128)(2,1)S(1)}, bf16[304,256]{1,0:T(8,128)(2,1)S(1)}, u32[]{:S(2)}, u32[]{:S(2)}) collective-permute-start(bf16[304,256]{1,0:T(8,128)(2,1)S(1)} %shard_map.113.refs_0_), channel_id=1, source_target_pairs={{0,16},{8,24},{16,0},{24,8},{1,17},{9,25},{17,1},{25,9},{2,18},{10... | collective-permute-start | bytes 466952 | tf_op jit(solution)/shard_map/ppermute | solution.py:277
  49.9 4.4 %collective-permute-start.3 = (bf16[304,256]{1,0:T(8,128)(2,1)S(1)}, bf16[304,256]{1,0:T(8,128)(2,1)S(1)}, u32[]{:S(2)}, u32[]{:S(2)}) collective-permute-start(bf16[304,256]{1,0:T(8,128)(2,1)S(1)} %shard_map.113.refs_0_), channel_id=1, source_target_pairs={{0,8},{8,0},{16,24},{24,16},{1,9},{9,1},{17,25},{25,17},{2,10},{10... | collective-permute-start | bytes 466952 | tf_op jit(solution)/shard_map/ppermute | solution.py:277
  53.7 1.4 %collective-permute-start.4 = (bf16[304,256]{1,0:T(8,128)(2,1)S(1)}, bf16[304,256]{1,0:T(8,128)(2,1)S(1)}, u32[]{:S(2)}, u32[]{:S(2)}) collective-permute-start(bf16[304,256]{1,0:T(8,128)(2,1)S(1)} %collective-permute-done.2.refs_1_), channel_id=1, source_target_pairs={{0,8},{8,0},{16,24},{24,16},{1,9},{9,1},{17,25},{25,17},{2,10},{10... | collective-permute-start | bytes 466952 | tf_op jit(solution)/shard_map/ppermute | solution.py:277

commit v11 on v9

--- a/solution.py
+++ b/solution.py
@@ -112,7 +112,7 @@
     owners, half, _ = mate_ref.shape
     hot_half = owners * half
     slot_cap = own_ref.shape[1] - half
-    size, step, wide = batch // 2, 512, 2048
+    size, step, wide = batch // 2, 512, 1024
     blocks = [slice(at, at + size) for at in range(0, batch, size)]
     rows[hot_half:2 * hot_half, :] = mate_ref[...].reshape(hot_half, width)
     for t in range(owners):
@@ -126,7 +126,7 @@
             cols = slice(start, start + step)
             pre_act = jnp.dot(pooled[samples, :], w_in_ref[:, cols], preferred_element_type=f32)
             own = lanes([w_out[k:k + 1, :] for k in range(start // 128, (start + step) // 128)])
-            act = jnp.maximum(pre_act, 0.0).astype(bf16)
+            act = jnp.maximum(pre_act.astype(bf16), jnp.zeros((), bf16))
             hidden[samples, cols] = act
             term = act.astype(f32) * own
             for k in range(0, step, 128):
@@ -193,50 +193,51 @@
     return jnp.where(which == 0, hot_ref[:, 0:half], hot_ref[:, half:])
 
 
-def row_grads(which, hot_ref, part_refs, held, put, rows):
-    size = part_refs[0].shape[0]
+def row_grads(which, hot_ref, part_refs, put, rows):
     half = hot_ref.shape[1] // 2
-    me = lax.div(lax.axis_index("dp"), 2)
-    count = len(part_refs)
-    for s in range(count):
-        held[pl.ds(pl.multiple_of((me ^ s) * size, 16), size), :] = part_refs[s][...]
-    hot = jnp.concatenate([held[g * size:g * size + half, :] for g in range(count)], axis=0)
-    ids = [lanes([hot_half(hot_ref, which)] * count)]
-    parts = [hot]
-    for g in range(count):
-        digits = held[(g + 1) * size - TAIL:(g + 1) * size, :].astype(f32).astype(i32)
-        ids.append(digits[0:1, :] * 256 + digits[1:2, :])
-        parts.append(held[g * size + half:(g + 1) * size - TAIL, :])
+    hot_ids = hot_half(hot_ref, which)
+    cold_ids = []
+    for part_ref in part_refs:
+        digits = part_ref[part_ref.shape[0] - TAIL:, :].astype(f32).astype(i32)
+        cold_ids.append(digits[0:1, :] * 256 + digits[1:2, :])
     step = 128
     for start in range(0, rows, step):
-        grad = 0.0
-        for k in range(len(ids)):
-            pick = one_hot(ids[k], (step, ids[k].shape[1]), 0, start)
-            grad += jnp.dot(pick, parts[k], preferred_element_type=f32)
-        put(slice(start, start + step), grad)
-
-
-def own_grad_body(hot_ref, *refs):
-    part_refs, (out_ref, held) = refs[:-2], refs[-2:]
-
-    def put(at, grad):
-        out_ref[at, :] = grad
-
-    row_grads(core(), hot_ref, part_refs, held, put, out_ref.shape[0])
-
-
-def update_body(hot_ref, sum_ref, table_ref, grad_ref, *refs):
-    part_refs, (new_table_ref, new_sum_ref, held, squares, grads, staged, sums, sems) = refs[:-8], refs[-8:]
+        hot_pick = one_hot(hot_ids, (step, half), 0, start)
+        grads = []
+        for ids, part_ref in zip(cold_ids, part_refs):
+            pick = one_hot(ids, (step, ids.shape[1]), 0, start)
+            hot = jnp.dot(hot_pick, part_ref[0:half, :], preferred_element_type=f32)
+            grads.append(hot + jnp.dot(pick, part_ref[half:part_ref.shape[0] - TAIL, :], preferred_element_type=f32))
+        put(slice(start, start + step), grads)
+
+
+def near_grads_body(hot_ref, *refs):
+    near_refs, (far_ref, sum_ref, far_sum_ref) = refs[:-3], refs[-3:]
+
+    def put_near(at, grads):
+        sum_ref[at, :] = grads[0] + grads[1]
+
+    def put_far(at, grads):
+        far_sum_ref[at, :] = grads[0]
+
+    row_grads(core(), hot_ref, near_refs, put_near, sum_ref.shape[0])
+    row_grads(1 - core(), hot_ref, [far_ref], put_far, sum_ref.shape[0])
+
+
+def update_body(hot_ref, sum_ref, table_ref, near_ref, far_ref, part_ref, *refs):
+    new_table_ref, new_sum_ref, squares, grads, staged, sums, sems = refs
     rows, width = table_ref.shape
     step = 128
 
-    def put(at, grad):
-        grad = grad_ref[at, :] + grad
+    def put(at, parts):
+        grad = near_ref[at, :] + (far_ref[at, :] + parts[0])
         grads[at, :] = grad
-        squares[:, at.start // step:at.stop // step] = jnp.sum(grad * grad, axis=1, keepdims=True)
-
-    row_grads(1 - core(), hot_ref, part_refs, held, put, rows)
-    new_sum = sum_ref[...] + squares[...].T * (1.0 / width)
+        square = grad * grad
+        square = sum(square[:, k:k + 128] for k in range(0, width, 128)).T
+        squares[at.start // step:at.stop // step, :] = jnp.sum(square, axis=0, keepdims=True)
+
+    row_grads(1 - core(), hot_ref, [part_ref], put, rows)
+    new_sum = sum_ref[...] + squares[...] * (1.0 / width)
     sums[...] = new_sum
     scale = (learning_rate / jnp.sqrt(new_sum)).T
     for start in range(0, rows, step):
@@ -337,23 +338,18 @@
     summed = call(pack_grads_body, shape((owners, half + slot_cap, width), bf16), (hot_grads, got, cold_grads))
     returned = exchange(summed)
     size = half + owners * slot_cap + TAIL
-    if groups & (groups - 1) == 0 and groups * size <= 2 * rows and owners * slot_cap == width:
-        parts = {0: call(collect_body, shape((size, width), bf16), (asked, returned))}
-        bit = groups // 2
-        while bit > 1:
-            parts.update({s ^ bit: swap(x, bit) for s, x in list(parts.items())})
-            bit //= 2
-        near = [parts[2 * y] for y in range(groups // 2)]
-        far = [swap(x, 1) for x in near]
-        held = pltpu.VMEM((groups // 2 * size, width), bf16)
-        grad = call(own_grad_body, shape((rows, width), f32), (hot_row, *near), [held])
+    if groups == 4 and 2 * size <= rows and owners * slot_cap == width:
+        own = call(collect_body, shape((size, width), bf16), (asked, returned))
+        beside = swap(own, 2)
+        far_own, far_beside = swap(own, 1), swap(beside, 1)
+        dense = shape((rows, width), f32)
+        near, far = call(near_grads_body, (dense, dense), (hot_row, own, beside, far_own))
         new_table, new_sum = call(
             update_body,
-            (shape((rows, width), f32), shape((rows // 128, 128), f32)),
-            (hot_row, adagrad_sum.reshape(-1, 128), table, grad, *far),
+            (dense, shape((rows // 128, 128), f32)),
+            (hot_row, adagrad_sum.reshape(-1, 128), table, near, far, far_beside),
             [
-                held,
-                pltpu.VMEM((128, rows // 128), f32),
+                pltpu.VMEM((rows // 128, 128), f32),
                 pltpu.VMEM((rows, width), f32),
                 pltpu.VMEM((rows, width), f32),
                 pltpu.VMEM((rows // 128, 128), f32),

time: 55.5 us -> 55.1 us (level)
  transfers between devices with their start and end apart: 7 -> 7, of which waited for: 6 -> 6; matrix products, arithmetic and copies ran while one was open for 0% -> 0% of each run, Pallas kernels for 7% -> 8%
where the time goes in v11:
time: 55.1 us; the launch traced here: 54.7 us
  waiting for transfers between devices  15.8 us (29%)
  starting transfers between devices  12.7 us (23%)
  blocking collectives  12.1 us (22%)
  Pallas kernels  11.4 us (21%)
  local copies, waits for them, and re-layouts  1.92 us (3%)
  between operations  0.78 us (1%)
    all_to_all x1, blocking collectives, exchange(): return lax.all_to_all(x, 'table', split_axis=0, concat_axis=0, tiled=True)  12.1 us
    pallas_call x11, Pallas kernels, call(): pl.pallas_call(body, out_shape=outs, in_specs=in_specs or [VMEM] * len(op...  11.4 us
    all_to_all x2, starting transfers between devices, exchange(): return lax.all_to_all(x, 'table', split_axis=0, concat_axis=0, tiled=True)  10.8 us
    all_to_all x2, waiting for transfers between devices, exchange(): return lax.all_to_all(x, 'table', split_axis=0, concat_axis=0, tiled=True)  9.49 us
    ppermute x5, waiting for transfers between devices, swap(): lax.ppermute(x, 'dp', [(g, g ^ bit) for g in range(lax.axis_size('dp'))])  6.3 us
    unnamed x20, local copies, waits for them, and re-layouts  1.92 us
    ppermute x5, starting transfers between devices, swap(): lax.ppermute(x, 'dp', [(g, g ^ bit) for g in range(lax.axis_size('dp'))])  1.84 us
  transfers between devices with their start and end apart: 7, of which 6 were waited for; matrix products, arithmetic and copies ran while one was open for 0% of the time, Pallas kernels for 8%

profile of v11, /device:TPU:0, one launch (start us, length us, event | category | flops | bytes accessed | tf_op | source)
XLA Modules:
  0.0 54.7 jit_solution(2823986546627288932)
XLA Ops:
  0.7 7.4 %all-to-all-start = ((s32[8,1,32]{2,1,0:T(1,128)}), s32[8,1,32]{2,1,0:T(1,128)S(1)}, u32[]{:S(2)}, u32[]{:S(2)}) async-start(s32[8,1,32]{2,1,0:T(1,128)} %bitcast.19), calls=%async_computation | async-start | bytes 8192 | tf_op jit(solution)/shard_map/all_to_all | solution.py:270
  8.1 1.2 %copy-done = f32[1024,256]{1,0:T(8,128)S(1)} copy-done((f32[1024,256]{1,0:T(8,128)S(1)}, f32[1024,256]{1,0:T(8,128)}, u32[]{:S(2)}) %copy-start) | copy-done | bytes 1048600
  9.3 0.7 %copy-done.5 = s32[64]{0:T(128)S(1)} copy-done((s32[64]{0:T(128)S(1)}, s32[64]{0:T(128)}, u32[]{:S(2)}) %copy-start.5) | copy-done | bytes 280
  9.9 0.4 shard_map.104
  10.4 4.1 %all-to-all-done = s32[8,1,32]{2,1,0:T(1,128)S(1)} async-done(((s32[8,1,32]{2,1,0:T(1,128)}), s32[8,1,32]{2,1,0:T(1,128)S(1)}, u32[]{:S(2)}, u32[]{:S(2)}) %all-to-all-start) | async-done | bytes 1056 | tf_op jit(solution)/shard_map/all_to_all | solution.py:270
  14.4 1.2 %shard_map.105 = bf16[8,64,256]{2,1,0:T(8,128)(2,1)} custom-call(s32[8,32]{1,0:T(8,128)S(1)} %bitcast.11, bf16[64,256]{1,0:T(8,128)(2,1)S(1)} %get-tuple-element.12.hot_ref, bf16[1024,256]{1,0:T(8,128)(2,1)S(1)} %get-tuple-element.13.table_ref), custom_call_target="tpu_custom_call" | custom-call | tf_op jit(solution)/shard_map/pallas_call | solution.py:24
  15.6 3.4 %all-to-all-start.1 = ((bf16[8,64,256]{2,1,0:T(8,128)(2,1)}), bf16[8,64,256]{2,1,0:T(8,128)(2,1)S(1)}, u32[]{:S(2)}, u32[]{:S(2)}) async-start(bf16[8,64,256]{2,1,0:T(8,128)(2,1)} %shard_map.105), calls=%async_computation.1 | async-start | bytes 524288 | tf_op jit(solution)/shard_map/all_to_all | solution.py:270
  19.1 2.7 %shard_map.106.inc_ref = bf16[512,768]{1,0:T(8,128)(2,1)S(1)} custom-call(s32[1,8]{1,0:T(1,128)S(1)} %copy-done.9, s32[32,512]{1,0:T(8,128)S(1)} %bitcast.10), custom_call_target="tpu_custom_call" | custom-call | tf_op jit(solution)/shard_map/pallas_call | solution.py:24
  21.8 5.4 %all-to-all-done.1.rows_ref.own_ref = bf16[8,64,256]{2,1,0:T(8,128)(2,1)S(1)} async-done(((bf16[8,64,256]{2,1,0:T(8,128)(2,1)}), bf16[8,64,256]{2,1,0:T(8,128)(2,1)S(1)}, u32[]{:S(2)}, u32[]{:S(2)}) %all-to-all-start.1) | async-done | bytes 262176 | tf_op jit(solution)/shard_map/all_to_all | solution.py:270
  27.2 0.1 collective-permute-start
  27.3 1.3 %collective-permute-done.mate_ref = bf16[8,32,256]{2,1,0:T(8,128)(2,1)S(1)} collective-permute-done((bf16[8,32,256]{2,1,0:T(8,128)(2,1)S(1)}, bf16[8,32,256]{2,1,0:T(8,128)(2,1)S(1)}, u32[]{:S(2)}, u32[]{:S(2)}) %collective-permute-start) | collective-permute-done | bytes 131104 | tf_op jit(solution)/shard_map/ppermute | solution.py:274
  28.6 3.5 %shard_map.108.dpooled_ref = bf16[512,256]{1,0:T(8,128)(2,1)S(1)} custom-call(f32[4,128]{1,0:T(4,128)S(1)} %bitcast.18, bf16[512,768]{1,0:T(8,128)(2,1)S(1)} %shard_map.106.inc_ref, bf16[8,64,256]{2,1,0:T(8,128)(2,1)S(1)} %all-to-all-done.1.rows_ref.own_ref, bf16[8,32,256]{2,1,0:T(8,128)(2,1)S(1)} %collective-permute-done.mate_ref, ...), custom_call_target="tpu_custom_call" | custom-call | tf_op jit(solution)/shard_map/pallas_call | solution.py:24
  32.2 0.0 copy-start.6
  32.2 0.3 shard_map.110
  32.5 0.2 collective-permute-start.1
  32.7 0.3 shard_map.109
  33.1 0.9 %collective-permute-done.1.got_ref = bf16[8,32,256]{2,1,0:T(8,128)(2,1)S(1)} collective-permute-done((bf16[8,32,256]{2,1,0:T(8,128)(2,1)S(1)}, bf16[8,32,256]{2,1,0:T(8,128)(2,1)S(1)}, u32[]{:S(2)}, u32[]{:S(2)}) %collective-permute-start.1) | collective-permute-done | bytes 131104 | tf_op jit(solution)/shard_map/ppermute | solution.py:274
  34.0 12.1 %all_to_all.21.back_ref = bf16[8,64,256]{2,1,0:T(8,128)(2,1)S(1)} all-to-all(bf16[8,64,256]{2,1,0:T(8,128)(2,1)S(1)} %shard_map.111), channel_id=1, replica_groups=mesh['dp'=4,'table'=8] {'table'}, dimensions={0} | all-to-all | bytes 524288 | tf_op jit(solution)/shard_map/all_to_all | solution.py:270
  46.1 0.1 shard_map.112.refs_0_
  46.2 1.6 %collective-permute-start.2 = (bf16[304,256]{1,0:T(8,128)(2,1)S(1)}, bf16[304,256]{1,0:T(8,128)(2,1)S(1)}, u32[]{:S(2)}, u32[]{:S(2)}) collective-permute-start(bf16[304,256]{1,0:T(8,128)(2,1)S(1)} %shard_map.112.refs_0_), channel_id=1, source_target_pairs={{0,16},{8,24},{16,0},{24,8},{1,17},{9,25},{17,1},{25,9},{2,18},{10... | collective-permute-start | bytes 466952 | tf_op jit(solution)/shard_map/ppermute | solution.py:274
  47.7 3.7 %collective-permute-done.2.refs_1_ = bf16[304,256]{1,0:T(8,128)(2,1)S(1)} collective-permute-done((bf16[304,256]{1,0:T(8,128)(2,1)S(1)}, bf16[304,256]{1,0:T(8,128)(2,1)S(1)}, u32[]{:S(2)}, u32[]{:S(2)}) %collective-permute-start.2) | collective-permute-done | bytes 155680 | tf_op jit(solution)/shard_map/ppermute | solution.py:274
  51.4 1.0 %shard_map.113 = (f32[1024,256]{1,0:T(8,128)S(1)}, f32[1024,256]{1,0:T(8,128)S(1)}) custom-call(s32[1,64]{1,0:T(1,128)S(1)} %bitcast.15, bf16[304,256]{1,0:T(8,128)(2,1)S(1)} %shard_map.112.refs_0_, bf16[304,256]{1,0:T(8,128)(2,1)S(1)} %collective-permute-done.2.refs_1_, bf16[304,256]{1,0:T(8,128)(2,1)S(1)} %collective-permute-done.3.refs_2_), custom_call_target="tpu_custom_call" | custom-call | tf_op jit(solution)/shard_map/pallas_call | solution.py:24
  52.4 0.4 collective-permute-done.4.part_ref
  52.8 1.9 %shard_map.114 = (f32[1024,256]{1,0:T(8,128)}, f32[8,128]{1,0:T(8,128)}) custom-call(s32[1,64]{1,0:T(1,128)S(1)} %bitcast.16, f32[8,128]{1,0:T(8,128)S(1)} %bitcast.17, f32[1024,256]{1,0:T(8,128)S(1)} %copy-done.1, f32[1024,256]{1,0:T(8,128)S(1)} %get-tuple-element.18.near_ref, f32[1024,256]{1,0:T(8,128)S(1)} %get-tuple-element.19.far_ref, ...), custom_call_target="tpu_custom_call" | custom-call | tf_op jit(solution)/shard_map/pallas_call | solution.py:24
  (22 shorter events, 0.1 us)
Async XLA Ops:
  0.6 18.4 %copy-start.9 = (s32[1,8]{1,0:T(1,128)S(1)}, s32[1,8]{1,0:T(1,128)}, u32[]{:S(2)}) copy-start(s32[1,8]{1,0:T(1,128)} %count_ref.1) | copy-start | bytes 100
  0.6 28.0 %copy-start.4 = (bf16[4096]{0:T(1024)(128)(2,1)S(1)}, bf16[4096]{0:T(1024)(128)(2,1)}, u32[]{:S(2)}) copy-start(bf16[4096]{0:T(1024)(128)(2,1)} %param.17) | copy-start | bytes 24580
  0.7 28.0 %copy-start.8 = (f32[512]{0:T(512)S(1)}, f32[512]{0:T(512)}, u32[]{:S(2)}) copy-start(f32[512]{0:T(512)} %param.10) | copy-start | bytes 6148
  0.7 13.8 %all-to-all-start = ((s32[8,1,32]{2,1,0:T(1,128)}), s32[8,1,32]{2,1,0:T(1,128)S(1)}, u32[]{:S(2)}, u32[]{:S(2)}) async-start(s32[8,1,32]{2,1,0:T(1,128)} %bitcast.19), calls=%async_computation | async-start | bytes 8192 | tf_op jit(solution)/shard_map/all_to_all | solution.py:270
  8.1 1.2 %copy-start = (f32[1024,256]{1,0:T(8,128)S(1)}, f32[1024,256]{1,0:T(8,128)}, u32[]{:S(2)}) copy-start(f32[1024,256]{1,0:T(8,128)} %table_ref.3) | copy-start | bytes 3145732
  9.3 0.7 %copy-start.5 = (s32[64]{0:T(128)S(1)}, s32[64]{0:T(128)}, u32[]{:S(2)}) copy-start(s32[64]{0:T(128)} %param.15) | copy-start | bytes 772
  9.9 9.1 %copy-start.3 = (s32[512,32]{0,1:T(8,128)S(1)}, s32[512,32]{0,1:T(8,128)}, u32[]{:S(2)}) copy-start(s32[512,32]{0,1:T(8,128)} %param.9) | copy-start | bytes 196612
  9.9 18.7 %copy-start.2 = (bf16[256,4096]{1,0:T(8,128)(2,1)S(1)}, bf16[256,4096]{1,0:T(8,128)(2,1)}, u32[]{:S(2)}) copy-start(bf16[256,4096]{1,0:T(8,128)(2,1)} %w_in_ref.1) | copy-start | bytes 6291460
  15.6 11.6 %all-to-all-start.1 = ((bf16[8,64,256]{2,1,0:T(8,128)(2,1)}), bf16[8,64,256]{2,1,0:T(8,128)(2,1)S(1)}, u32[]{:S(2)}, u32[]{:S(2)}) async-start(bf16[8,64,256]{2,1,0:T(8,128)(2,1)} %shard_map.105), calls=%async_computation.1 | async-start | bytes 524288 | tf_op jit(solution)/shard_map/all_to_all | solution.py:270
  27.2 1.4 %collective-permute-start = (bf16[8,32,256]{2,1,0:T(8,128)(2,1)S(1)}, bf16[8,32,256]{2,1,0:T(8,128)(2,1)S(1)}, u32[]{:S(2)}, u32[]{:S(2)}) collective-permute-start(bf16[8,32,256]{2,1,0:T(8,128)(2,1)S(1)} %shard_map.107), channel_id=1, source_target_pairs={{0,8},{8,0},{16,24},{24,16},{1,9},{9,1},{17,25},{25,17},{2,10},{10... | collective-permute-start | bytes 393224 | tf_op jit(solution)/shard_map/ppermute | solution.py:274
  32.2 19.2 %copy-start.6 = (s32[64]{0:T(128)S(1)}, s32[64]{0:T(128)}, u32[]{:S(2)}) copy-start(s32[64]{0:T(128)} %param.15) | copy-start | bytes 772
  32.2 20.6 %copy-start.1 = (f32[1024,256]{1,0:T(8,128)S(1)}, f32[1024,256]{1,0:T(8,128)}, u32[]{:S(2)}) copy-start(f32[1024,256]{1,0:T(8,128)} %table_ref.3) | copy-start | bytes 3145732
  32.2 20.6 %copy-start.7 = (f32[1024]{0:T(1024)S(1)}, f32[1024]{0:T(1024)}, u32[]{:S(2)}) copy-start(f32[1024]{0:T(1024)} %param.14) | copy-start | bytes 12292
  32.5 1.4 %collective-permute-start.1 = (bf16[8,32,256]{2,1,0:T(8,128)(2,1)S(1)}, bf16[8,32,256]{2,1,0:T(8,128)(2,1)S(1)}, u32[]{:S(2)}, u32[]{:S(2)}) collective-permute-start(bf16[8,32,256]{2,1,0:T(8,128)(2,1)S(1)} %bitcast.9), channel_id=1, source_target_pairs={{0,8},{8,0},{16,24},{24,16},{1,9},{9,1},{17,25},{25,17},{2,10},{10... | collective-permute-start | bytes 393224 | tf_op jit(solution)/shard_map/ppermute | solution.py:274
  46.2 5.3 %collective-permute-start.2 = (bf16[304,256]{1,0:T(8,128)(2,1)S(1)}, bf16[304,256]{1,0:T(8,128)(2,1)S(1)}, u32[]{:S(2)}, u32[]{:S(2)}) collective-permute-start(bf16[304,256]{1,0:T(8,128)(2,1)S(1)} %shard_map.112.refs_0_), channel_id=1, source_target_pairs={{0,16},{8,24},{16,0},{24,8},{1,17},{9,25},{17,1},{25,9},{2,18},{10... | collective-permute-start | bytes 466952 | tf_op jit(solution)/shard_map/ppermute | solution.py:274
  47.7 3.7 %collective-permute-start.3 = (bf16[304,256]{1,0:T(8,128)(2,1)S(1)}, bf16[304,256]{1,0:T(8,128)(2,1)S(1)}, u32[]{:S(2)}, u32[]{:S(2)}) collective-permute-start(bf16[304,256]{1,0:T(8,128)(2,1)S(1)} %shard_map.112.refs_0_), channel_id=1, source_target_pairs={{0,8},{8,0},{16,24},{24,16},{1,9},{9,1},{17,25},{25,17},{2,10},{10... | collective-permute-start | bytes 466952 | tf_op jit(solution)/shard_map/ppermute | solution.py:274
  51.4 1.4 %collective-permute-start.4 = (bf16[304,256]{1,0:T(8,128)(2,1)S(1)}, bf16[304,256]{1,0:T(8,128)(2,1)S(1)}, u32[]{:S(2)}, u32[]{:S(2)}) collective-permute-start(bf16[304,256]{1,0:T(8,128)(2,1)S(1)} %collective-permute-done.2.refs_1_), channel_id=1, source_target_pairs={{0,8},{8,0},{16,24},{24,16},{1,9},{9,1},{17,25},{25,17},{2,10},{10... | collective-permute-start | bytes 466952 | tf_op jit(solution)/shard_map/ppermute | solution.py:274

commit v12 on v11

--- a/solution.py
+++ b/solution.py
@@ -12,10 +12,10 @@
 f32, bf16, i32 = jnp.float32, jnp.bfloat16, jnp.int32
 VMEM = pl.BlockSpec(memory_space=pltpu.VMEM)
 HBM = pl.BlockSpec(memory_space=pltpu.HBM)
-SMEM = pl.BlockSpec(memory_space=pltpu.SMEM)
 FIELDS = 4
 FIELD_BITS = 8
 TAIL = 16
+FIRST = 2
 
 
 def call(body, outs, operands, scratch=(), in_specs=None, out_specs=None):
@@ -39,67 +39,87 @@
     return (lax.broadcasted_iota(i32, shape, axis) + start == ids).astype(f32).astype(bf16)
 
 
-def incidence_body(hot_dev, slot_cap, count_ref, slots_ref, out_ref, inc_t_ref):
-    vocab, batch = inc_t_ref.shape
-    owners = vocab // (hot_dev + slot_cap)
+def entries(hot_dev, counts, slots, field):
+    owners = counts.shape[1]
+    slot_cap = FIELDS * field // owners - hot_dev
     half = hot_dev // 2
     hot_cols = owners * hot_dev
-    me = core()
-    field = vocab // FIELDS
-    step = 128
-    row = lax.broadcasted_iota(i32, (field, step), 0)
-    for start in range(0, batch, step):
-        slots = slots_ref[:, start:start + step]
-        place = slots % hot_dev
-        hot = jnp.where(place // half == me, 0, owners * half) + (slots // hot_dev) * half + place % half
-        column = jnp.where(slots < hot_cols, hot, slots)
-        key = jnp.where(slots < 0, -1, column % field)
-        unit = jnp.left_shift(jnp.ones_like(slots), FIELD_BITS * (column // field))
-        packed = jnp.zeros((field, step), i32)
-        for entry in range(slots.shape[0]):
-            packed += jnp.where(row == key[entry:entry + 1, :], unit[entry:entry + 1, :], 0)
-        for k in range(FIELDS):
-            part = jnp.right_shift(packed, FIELD_BITS * k) & (2**FIELD_BITS - 1)
-            inc_t_ref[k * field:(k + 1) * field, start:start + step] = part.astype(f32).astype(bf16)
-    place = lax.broadcasted_iota(i32, (slot_cap, batch), 0)
-    for owner in range(owners):
-        rows = pl.ds(hot_cols + owner * slot_cap, slot_cap)
-        inc_t_ref[rows, :] = jnp.where(place < count_ref[0, owner], inc_t_ref[rows, :].astype(f32), 0.0).astype(bf16)
-    out_ref[...] = inc_t_ref[...].T
-
-
-def core():
-    return lax.rem(lax.axis_index("dp"), 2)
-
-
-def pick_hot_body(ids_ref, table_ref, hot_ref, table_bf_ref, ids, table, sems):
-    copies = [pltpu.make_async_copy(ids_ref, ids, sems.at[0]), pltpu.make_async_copy(table_ref, table, sems.at[1])]
+    place = slots % hot_dev
+    hot = jnp.where(place // half == core(), 0, owners * half) + (slots // hot_dev) * half + place % half
+    column = jnp.where(slots < hot_cols, hot, slots)
+    cold = slots - hot_cols
+    live = slots >= 0
+    for t in range(owners):
+        at = cold - t * slot_cap
+        live = live & ((at < counts[:, t:t + 1]) | (at >= slot_cap))
+    key = jnp.where(live, column % field, -1)
+    return key, jnp.left_shift(jnp.ones_like(slots), FIELD_BITS * (column // field))
+
+
+def count(key, unit, field):
+    row = lax.broadcasted_iota(i32, (field, key.shape[1]), 0)
+    packed = jnp.zeros(row.shape, i32)
+    for entry in range(key.shape[0]):
+        packed += jnp.where(row == key[entry:entry + 1, :], unit[entry:entry + 1, :], 0)
+    return packed
+
+
+def prepare_body(count_ref, slots_ref, ids_ref, table_ref, packed_ref, key_ref, unit_ref, hot_ref, table_bf_ref, *scratch):
+    counts, slots, ids, table, sems = scratch
+    pairs = [(count_ref, counts), (slots_ref, slots), (ids_ref, ids), (table_ref, table)]
+    copies = [pltpu.make_async_copy(src, dst, sems.at[k]) for k, (src, dst) in enumerate(pairs)]
     for copy in copies:
         copy.start()
-    for copy in copies:
-        copy.wait()
     hot_dev = ids.shape[1]
+    field, first = packed_ref.shape
+    copies[0].wait()
+    copies[1].wait()
+    for start in range(0, slots.shape[1], 128):
+        at = slice(start, start + 128)
+        key, unit = entries(hot_dev, counts[...], slots[:, at], field)
+        if start < first:
+            packed_ref[:, at] = count(key, unit, field)
+        else:
+            rest = slice(start - first, start - first + 128)
+            key_ref[:, rest], unit_ref[:, rest] = key, unit
+    copies[2].wait()
+    copies[3].wait()
     table_bf_ref[...] = table[...].astype(bf16)
     column = jnp.broadcast_to(ids[...], (8, hot_dev)).T[:, 0:1]
     pick = one_hot(column, (hot_dev, table.shape[0]), 1)
     hot_ref[...] = jnp.dot(pick, table_bf_ref[...], preferred_element_type=f32).astype(bf16)
 
 
-def serve_body(asked_ref, hot_ref, table_ref, out_ref, pick, staged, sem):
+def incidence_body(packed_ref, key_ref, unit_ref, out_ref, inc_t_ref):
+    field, first = packed_ref.shape
+    for start in range(0, out_ref.shape[0], 128):
+        at = slice(start, start + 128)
+        if start < first:
+            packed = packed_ref[:, at]
+        else:
+            rest = slice(start - first, start - first + 128)
+            packed = count(key_ref[:, rest], unit_ref[:, rest], field)
+        for k in range(FIELDS):
+            part = jnp.right_shift(packed, FIELD_BITS * k) & (2**FIELD_BITS - 1)
+            inc_t_ref[k * field:(k + 1) * field, at] = part.astype(f32).astype(bf16)
+    out_ref[...] = inc_t_ref[...].T
+
+
+def core():
+    return lax.rem(lax.axis_index("dp"), 2)
+
+
+def serve_body(asked_ref, hot_ref, table_ref, out_ref, pick):
     owners, slot_cap = asked_ref.shape
-    hot_dev = hot_ref.shape[0]
+    half = hot_ref.shape[0] // 2
     asked = asked_ref[...].T
     for t in range(owners):
         pick[t * slot_cap:(t + 1) * slot_cap, :] = one_hot(asked[:, t:t + 1], (slot_cap, table_ref.shape[0]), 1)
     picked = jnp.dot(pick[...], table_ref[...], preferred_element_type=f32).astype(bf16)
-    half = hot_dev // 2
     hot = hot_ref[pl.ds(pl.multiple_of(core() * half, half), half), :]
     for t in range(owners):
-        staged[t, 0:half, :] = hot
-        staged[t, half:, :] = picked[t * slot_cap:(t + 1) * slot_cap]
-    copy = pltpu.make_async_copy(staged, out_ref, sem)
-    copy.start()
-    copy.wait()
+        out_ref[t, 0:half, :] = hot
+        out_ref[t, half:, :] = picked[t * slot_cap:(t + 1) * slot_cap]
 
 
 def first_rows_body(rows_ref, out_ref):
@@ -288,33 +308,40 @@
 
     hot_row = hot_ids.reshape(1, hot_dev)
     asked = exchange(cold_ids[0])
-    inc = call(
-        functools.partial(incidence_body, hot_dev, slot_cap),
-        shape((batch, vocab), bf16),
-        (cold_count, bag_slots.T),
-        [pltpu.VMEM((vocab, batch), bf16)],
-        in_specs=[SMEM, VMEM],
-    )
-    hot, table_bf = call(
-        pick_hot_body,
-        (shape((hot_dev, width), bf16), shape((rows, width), bf16)),
-        (hot_row, table),
-        [pltpu.VMEM((1, hot_dev), i32), pltpu.VMEM((rows, width), f32), pltpu.SemaphoreType.DMA((2,))],
-        in_specs=[HBM, HBM],
-    )
+    slots = bag_slots.T
+    first = FIRST * batch // 4
+    rest = shape((slots.shape[0], batch - first), i32)
+    packed, key, unit, hot, table_bf = call(
+        prepare_body,
+        (
+            shape((vocab // FIELDS, first), i32),
+            rest,
+            rest,
+            shape((hot_dev, width), bf16),
+            shape((rows, width), bf16),
+        ),
+        tuple(pltpu.with_memory_space_constraint(x, pltpu.HBM) for x in (cold_count, slots, hot_row, table)),
+        [
+            pltpu.VMEM(cold_count.shape, i32),
+            pltpu.VMEM(slots.shape, i32),
+            pltpu.VMEM(hot_row.shape, i32),
+            pltpu.VMEM(table.shape, f32),
+            pltpu.SemaphoreType.DMA((4,)),
+        ],
+        in_specs=[HBM] * 4,
+    )
+    asked, packed = lax.optimization_barrier((asked, packed))
     served = call(
         serve_body,
         shape((owners, half + slot_cap, width), bf16),
         (asked, hot, table_bf),
-        [
-            pltpu.VMEM((owners * slot_cap, rows), bf16),
-            pltpu.VMEM((owners, half + slot_cap, width), bf16),
-            pltpu.SemaphoreType.DMA,
-        ],
-        out_specs=HBM,
-    )
-    own_rows, inc = lax.optimization_barrier((exchange(served), inc))
-    mate_rows = swap(call(first_rows_body, shape((owners, half, width), bf16), (own_rows,)), 1)
+        [pltpu.VMEM((owners * slot_cap, rows), bf16)],
+    )
+    own_rows = exchange(served)
+    first_rows = call(first_rows_body, shape((owners, half, width), bf16), (own_rows,))
+    first_rows, packed = lax.optimization_barrier((first_rows, packed))
+    mate_rows = swap(first_rows, 1)
+    inc = call(incidence_body, shape((batch, vocab), bf16), (packed, key, unit), [pltpu.VMEM((vocab, batch), bf16)])
     dpooled = call(
         top_body,
         shape((batch, width), bf16),

time: 55.1 us -> 53.6 us (0.973)
  blocking collectives: 12.1 us -> 23.1 us
  waiting for transfers between devices: 15.8 us -> 8.86 us
  starting transfers between devices: 12.7 us -> 9.4 us
  local copies, waits for them, and re-layouts: 1.92 us -> 0.03 us
    all_to_all x1 -> x2, blocking collectives: 12.1 us -> 23.1 us  [exchange(): return lax.all_to_all(x, 'table', split_axis=0, concat_axis=0, tiled=True)]
    all_to_all x2 -> x1, waiting for transfers between devices: 9.49 us -> 3.83 us  [exchange(): return lax.all_to_all(x, 'table', split_axis=0, concat_axis=0, tiled=True)]
    all_to_all x2 -> x1, starting transfers between devices: 10.8 us -> 7.4 us  [exchange(): return lax.all_to_all(x, 'table', split_axis=0, concat_axis=0, tiled=True)]
    unnamed x20 -> x12, local copies, waits for them, and re-layouts: 1.92 us -> 0.03 us
    ppermute x5, waiting for transfers between devices: 6.3 us -> 5.03 us  [swap(): lax.ppermute(x, 'dp', [(g, g ^ bit) for g in range(lax.axis_size('dp'))])]
  transfers between devices with their start and end apart: 7 -> 6, of which waited for: 6 -> 5; matrix products, arithmetic and copies ran while one was open for 0% -> 0% of each run, Pallas kernels for 8% -> 9%
where the time goes in v12:
time: 53.6 us; the launch traced here: 53.4 us
  blocking collectives  23.1 us (43%)
  Pallas kernels  11.3 us (21%)
  starting transfers between devices  9.4 us (18%)
  waiting for transfers between devices  8.86 us (17%)
  between operations  0.75 us (1%)
    all_to_all x2, blocking collectives, exchange(): return lax.all_to_all(x, 'table', split_axis=0, concat_axis=0, tiled=True)  23.1 us
    pallas_call x11, Pallas kernels, call(): pl.pallas_call(body, out_shape=outs, in_specs=in_specs or [VMEM] * len(op...  11.3 us
    all_to_all x1, starting transfers between devices, exchange(): return lax.all_to_all(x, 'table', split_axis=0, concat_axis=0, tiled=True)  7.4 us
    ppermute x5, waiting for transfers between devices, swap(): lax.ppermute(x, 'dp', [(g, g ^ bit) for g in range(lax.axis_size('dp'))])  5.03 us
    all_to_all x1, waiting for transfers between devices, exchange(): return lax.all_to_all(x, 'table', split_axis=0, concat_axis=0, tiled=True)  3.83 us
    ppermute x5, starting transfers between devices, swap(): lax.ppermute(x, 'dp', [(g, g ^ bit) for g in range(lax.axis_size('dp'))])  2 us
  transfers between devices with their start and end apart: 6, of which 5 were waited for; matrix products, arithmetic and copies ran while one was open for 0% of the time, Pallas kernels for 9%

profile of v12, /device:TPU:0, one launch (start us, length us, event | category | flops | bytes accessed | tf_op | source)
XLA Modules:
  0.0 53.4 jit_solution(4477010748467351991)
XLA Ops:
  0.7 7.4 %all-to-all-start = ((s32[8,1,32]{2,1,0:T(1,128)}), s32[8,1,32]{2,1,0:T(1,128)S(1)}, u32[]{:S(2)}, u32[]{:S(2)}) async-start(s32[8,1,32]{2,1,0:T(1,128)} %bitcast.19), calls=%async_computation | async-start | bytes 8192 | tf_op jit(solution)/shard_map/all_to_all | solution.py:290
  8.1 2.6 %shard_map.104 = (s32[192,256]{1,0:T(8,128)S(1)}, s32[32,256]{1,0:T(8,128)S(1)}, s32[32,256]{1,0:T(8,128)S(1)}, bf16[64,256]{1,0:T(8,128)(2,1)S(1)}, bf16[1024,256]{1,0:T(8,128)(2,1)S(1)}) custom-call(s32[1,8]{1,0:T(1,128)} %count_ref.1, s32[32,512]{1,0:T(8,128)} %bitcast.18, s32[1,64]{1,0:T(1,128)} %bitcast.13, f32[1024,256]{1,0:T(8,128)} %table_ref.3), custom_call_target="tpu_custom_call" | custom-call | tf_op jit(solution)/shard_map/pallas_call | solution.py:24
  10.6 3.8 %all-to-all-done = s32[8,1,32]{2,1,0:T(1,128)S(1)} async-done(((s32[8,1,32]{2,1,0:T(1,128)}), s32[8,1,32]{2,1,0:T(1,128)S(1)}, u32[]{:S(2)}, u32[]{:S(2)}) %all-to-all-start) | async-done | bytes 1056 | tf_op jit(solution)/shard_map/all_to_all | solution.py:290
  14.4 0.4 shard_map.105
  14.9 10.6 %all_to_all.22.rows_ref.own_ref = bf16[8,64,256]{2,1,0:T(8,128)(2,1)S(1)} all-to-all(bf16[8,64,256]{2,1,0:T(8,128)(2,1)S(1)} %shard_map.105), channel_id=1, replica_groups=mesh['dp'=4,'table'=8] {'table'}, dimensions={0} | all-to-all | bytes 524288 | tf_op jit(solution)/shard_map/all_to_all | solution.py:290
  25.5 0.1 collective-permute-start
  25.6 1.1 %shard_map.107.inc_ref = bf16[512,768]{1,0:T(8,128)(2,1)S(1)} custom-call(s32[192,256]{1,0:T(8,128)S(1)} %get-tuple-element.22.packed_ref, s32[32,256]{1,0:T(8,128)S(1)} %get-tuple-element.23.key_ref, s32[32,256]{1,0:T(8,128)S(1)} %get-tuple-element.24.unit_ref), custom_call_target="tpu_custom_call" | custom-call | tf_op jit(solution)/shard_map/pallas_call | solution.py:24
  26.7 0.2 collective-permute-done.mate_ref
  27.0 3.6 %shard_map.108.dpooled_ref = bf16[512,256]{1,0:T(8,128)(2,1)S(1)} custom-call(f32[4,128]{1,0:T(4,128)S(1)} %bitcast.17, bf16[512,768]{1,0:T(8,128)(2,1)S(1)} %shard_map.107.inc_ref, bf16[8,64,256]{2,1,0:T(8,128)(2,1)S(1)} %all_to_all.22.rows_ref.own_ref, bf16[8,32,256]{2,1,0:T(8,128)(2,1)S(1)} %collective-permute-done.mate_ref, ...), custom_call_target="tpu_custom_call" | custom-call | tf_op jit(solution)/shard_map/pallas_call | solution.py:24
  30.5 0.0 copy-start.3
  30.5 0.0 copy-start
  30.6 0.0 copy-start.4
  30.6 0.3 shard_map.110
  30.8 0.4 collective-permute-start.1
  31.2 0.3 shard_map.109
  31.5 0.7 %collective-permute-done.1.got_ref = bf16[8,32,256]{2,1,0:T(8,128)(2,1)S(1)} collective-permute-done((bf16[8,32,256]{2,1,0:T(8,128)(2,1)S(1)}, bf16[8,32,256]{2,1,0:T(8,128)(2,1)S(1)}, u32[]{:S(2)}, u32[]{:S(2)}) %collective-permute-start.1) | collective-permute-done | bytes 131104 | tf_op jit(solution)/shard_map/ppermute | solution.py:294
  32.3 12.5 %all_to_all.23.back_ref = bf16[8,64,256]{2,1,0:T(8,128)(2,1)S(1)} all-to-all(bf16[8,64,256]{2,1,0:T(8,128)(2,1)S(1)} %shard_map.111), channel_id=1, replica_groups=mesh['dp'=4,'table'=8] {'table'}, dimensions={0} | all-to-all | bytes 524288 | tf_op jit(solution)/shard_map/all_to_all | solution.py:290
  44.7 0.1 shard_map.112.refs_0_
  44.8 1.6 %collective-permute-start.2 = (bf16[304,256]{1,0:T(8,128)(2,1)S(1)}, bf16[304,256]{1,0:T(8,128)(2,1)S(1)}, u32[]{:S(2)}, u32[]{:S(2)}) collective-permute-start(bf16[304,256]{1,0:T(8,128)(2,1)S(1)} %shard_map.112.refs_0_), channel_id=1, source_target_pairs={{0,16},{8,24},{16,0},{24,8},{1,17},{9,25},{17,1},{25,9},{2,18},{10... | collective-permute-start | bytes 466952 | tf_op jit(solution)/shard_map/ppermute | solution.py:294
  46.4 0.0 collective-permute-start.3
  46.4 3.7 %collective-permute-done.2.refs_1_ = bf16[304,256]{1,0:T(8,128)(2,1)S(1)} collective-permute-done((bf16[304,256]{1,0:T(8,128)(2,1)S(1)}, bf16[304,256]{1,0:T(8,128)(2,1)S(1)}, u32[]{:S(2)}, u32[]{:S(2)}) %collective-permute-start.2) | collective-permute-done | bytes 155680 | tf_op jit(solution)/shard_map/ppermute | solution.py:294
  50.1 1.0 %shard_map.113 = (f32[1024,256]{1,0:T(8,128)S(1)}, f32[1024,256]{1,0:T(8,128)S(1)}) custom-call(s32[1,64]{1,0:T(1,128)S(1)} %bitcast.14, bf16[304,256]{1,0:T(8,128)(2,1)S(1)} %shard_map.112.refs_0_, bf16[304,256]{1,0:T(8,128)(2,1)S(1)} %collective-permute-done.2.refs_1_, bf16[304,256]{1,0:T(8,128)(2,1)S(1)} %collective-permute-done.3.refs_2_), custom_call_target="tpu_custom_call" | custom-call | tf_op jit(solution)/shard_map/pallas_call | solution.py:24
  51.1 0.4 collective-permute-done.4.part_ref
  51.5 1.9 %shard_map.114 = (f32[1024,256]{1,0:T(8,128)}, f32[8,128]{1,0:T(8,128)}) custom-call(s32[1,64]{1,0:T(1,128)S(1)} %bitcast.15, f32[8,128]{1,0:T(8,128)S(1)} %bitcast.16, f32[1024,256]{1,0:T(8,128)S(1)} %copy-done, f32[1024,256]{1,0:T(8,128)S(1)} %get-tuple-element.28.near_ref, f32[1024,256]{1,0:T(8,128)S(1)} %get-tuple-element.29.far_ref, ...), custom_call_target="tpu_custom_call" | custom-call | tf_op jit(solution)/shard_map/pallas_call | solution.py:24
  (13 shorter events, 0.1 us)
Async XLA Ops:
  0.6 26.3 %copy-start.2 = (bf16[4096]{0:T(1024)(128)(2,1)S(1)}, bf16[4096]{0:T(1024)(128)(2,1)}, u32[]{:S(2)}) copy-start(bf16[4096]{0:T(1024)(128)(2,1)} %param.17) | copy-start | bytes 24580
  0.6 26.3 %copy-start.1 = (bf16[256,4096]{1,0:T(8,128)(2,1)S(1)}, bf16[256,4096]{1,0:T(8,128)(2,1)}, u32[]{:S(2)}) copy-start(bf16[256,4096]{1,0:T(8,128)(2,1)} %w_in_ref.1) | copy-start | bytes 6291460
  0.7 26.3 %copy-start.5 = (f32[512]{0:T(512)S(1)}, f32[512]{0:T(512)}, u32[]{:S(2)}) copy-start(f32[512]{0:T(512)} %param.10) | copy-start | bytes 6148
  0.7 13.8 %all-to-all-start = ((s32[8,1,32]{2,1,0:T(1,128)}), s32[8,1,32]{2,1,0:T(1,128)S(1)}, u32[]{:S(2)}, u32[]{:S(2)}) async-start(s32[8,1,32]{2,1,0:T(1,128)} %bitcast.19), calls=%async_computation | async-start | bytes 8192 | tf_op jit(solution)/shard_map/all_to_all | solution.py:290
  25.5 1.4 %collective-permute-start = (bf16[8,32,256]{2,1,0:T(8,128)(2,1)S(1)}, bf16[8,32,256]{2,1,0:T(8,128)(2,1)S(1)}, u32[]{:S(2)}, u32[]{:S(2)}) collective-permute-start(bf16[8,32,256]{2,1,0:T(8,128)(2,1)S(1)} %shard_map.106), channel_id=1, source_target_pairs={{0,8},{8,0},{16,24},{24,16},{1,9},{9,1},{17,25},{25,17},{2,10},{10... | collective-permute-start | bytes 393224 | tf_op jit(solution)/shard_map/ppermute | solution.py:294
  30.5 19.6 %copy-start.3 = (s32[64]{0:T(128)S(1)}, s32[64]{0:T(128)}, u32[]{:S(2)}) copy-start(s32[64]{0:T(128)} %param.15) | copy-start | bytes 772
  30.5 20.9 %copy-start = (f32[1024,256]{1,0:T(8,128)S(1)}, f32[1024,256]{1,0:T(8,128)}, u32[]{:S(2)}) copy-start(f32[1024,256]{1,0:T(8,128)} %table_ref.3) | copy-start | bytes 3145732
  30.6 20.9 %copy-start.4 = (f32[1024]{0:T(1024)S(1)}, f32[1024]{0:T(1024)}, u32[]{:S(2)}) copy-start(f32[1024]{0:T(1024)} %param.14) | copy-start | bytes 12292
  30.8 1.4 %collective-permute-start.1 = (bf16[8,32,256]{2,1,0:T(8,128)(2,1)S(1)}, bf16[8,32,256]{2,1,0:T(8,128)(2,1)S(1)}, u32[]{:S(2)}, u32[]{:S(2)}) collective-permute-start(bf16[8,32,256]{2,1,0:T(8,128)(2,1)S(1)} %bitcast.9), channel_id=1, source_target_pairs={{0,8},{8,0},{16,24},{24,16},{1,9},{9,1},{17,25},{25,17},{2,10},{10... | collective-permute-start | bytes 393224 | tf_op jit(solution)/shard_map/ppermute | solution.py:294
  44.8 5.3 %collective-permute-start.2 = (bf16[304,256]{1,0:T(8,128)(2,1)S(1)}, bf16[304,256]{1,0:T(8,128)(2,1)S(1)}, u32[]{:S(2)}, u32[]{:S(2)}) collective-permute-start(bf16[304,256]{1,0:T(8,128)(2,1)S(1)} %shard_map.112.refs_0_), channel_id=1, source_target_pairs={{0,16},{8,24},{16,0},{24,8},{1,17},{9,25},{17,1},{25,9},{2,18},{10... | collective-permute-start | bytes 466952 | tf_op jit(solution)/shard_map/ppermute | solution.py:294
  46.4 3.7 %collective-permute-start.3 = (bf16[304,256]{1,0:T(8,128)(2,1)S(1)}, bf16[304,256]{1,0:T(8,128)(2,1)S(1)}, u32[]{:S(2)}, u32[]{:S(2)}) collective-permute-start(bf16[304,256]{1,0:T(8,128)(2,1)S(1)} %shard_map.112.refs_0_), channel_id=1, source_target_pairs={{0,8},{8,0},{16,24},{24,16},{1,9},{9,1},{17,25},{25,17},{2,10},{10... | collective-permute-start | bytes 466952 | tf_op jit(solution)/shard_map/ppermute | solution.py:294
  50.1 1.4 %collective-permute-start.4 = (bf16[304,256]{1,0:T(8,128)(2,1)S(1)}, bf16[304,256]{1,0:T(8,128)(2,1)S(1)}, u32[]{:S(2)}, u32[]{:S(2)}) collective-permute-start(bf16[304,256]{1,0:T(8,128)(2,1)S(1)} %collective-permute-done.2.refs_1_), channel_id=1, source_target_pairs={{0,8},{8,0},{16,24},{24,16},{1,9},{9,1},{17,25},{25,17},{2,10},{10... | collective-permute-start | bytes 466952 | tf_op jit(solution)/shard_map/ppermute | solution.py:294

commit v13 on v12

--- a/solution.py
+++ b/solution.py
@@ -62,6 +62,18 @@
     for entry in range(key.shape[0]):
         packed += jnp.where(row == key[entry:entry + 1, :], unit[entry:entry + 1, :], 0)
     return packed
+
+
+def turn_body(ids_ref, out_ref, sems):
+    half = ids_ref.shape[0] // 2
+    copies = [
+        pltpu.make_async_copy(ids_ref.at[k * half:(k + 1) * half], out_ref.at[(1 - k) * half:(2 - k) * half], sems.at[k])
+        for k in range(2)
+    ]
+    for copy in copies:
+        copy.start()
+    for copy in copies:
+        copy.wait()
 
 
 def prepare_body(count_ref, slots_ref, ids_ref, table_ref, packed_ref, key_ref, unit_ref, hot_ref, table_bf_ref, *scratch):
@@ -109,24 +121,24 @@
     return lax.rem(lax.axis_index("dp"), 2)
 
 
-def serve_body(asked_ref, hot_ref, table_ref, out_ref, pick):
+def serve_body(order, asked_ref, hot_ref, table_ref, out_ref, pick):
     owners, slot_cap = asked_ref.shape
     half = hot_ref.shape[0] // 2
     asked = asked_ref[...].T
-    for t in range(owners):
-        pick[t * slot_cap:(t + 1) * slot_cap, :] = one_hot(asked[:, t:t + 1], (slot_cap, table_ref.shape[0]), 1)
+    for k, t in enumerate(order):
+        pick[t * slot_cap:(t + 1) * slot_cap, :] = one_hot(asked[:, k:k + 1], (slot_cap, table_ref.shape[0]), 1)
     picked = jnp.dot(pick[...], table_ref[...], preferred_element_type=f32).astype(bf16)
     hot = hot_ref[pl.ds(pl.multiple_of(core() * half, half), half), :]
-    for t in range(owners):
-        out_ref[t, 0:half, :] = hot
-        out_ref[t, half:, :] = picked[t * slot_cap:(t + 1) * slot_cap]
+    for k, t in enumerate(order):
+        out_ref[k, 0:half, :] = hot
+        out_ref[k, half:, :] = picked[t * slot_cap:(t + 1) * slot_cap]
 
 
 def first_rows_body(rows_ref, out_ref):
     out_ref[...] = rows_ref[:, 0:out_ref.shape[1], :]
 
 
-def top_body(labels_ref, inc_ref, own_ref, mate_ref, w_in_ref, w_out_ref, out_ref, hidden, rows, pooled, total, dlogit):
+def top_body(order, labels_ref, inc_ref, own_ref, mate_ref, w_in_ref, w_out_ref, out_ref, hidden, rows, pooled, total, dlogit):
     batch = inc_ref.shape[0]
     hidden_units, width = w_in_ref.shape[1], w_in_ref.shape[0]
     owners, half, _ = mate_ref.shape
@@ -134,10 +146,10 @@
     slot_cap = own_ref.shape[1] - half
     size, step, wide = batch // 2, 512, 1024
     blocks = [slice(at, at + size) for at in range(0, batch, size)]
-    rows[hot_half:2 * hot_half, :] = mate_ref[...].reshape(hot_half, width)
-    for t in range(owners):
-        rows[t * half:(t + 1) * half, :] = own_ref[t, 0:half, :]
-        rows[2 * hot_half + t * slot_cap:2 * hot_half + (t + 1) * slot_cap, :] = own_ref[t, half:, :]
+    for k, t in enumerate(order):
+        rows[t * half:(t + 1) * half, :] = own_ref[k, 0:half, :]
+        rows[hot_half + t * half:hot_half + (t + 1) * half, :] = mate_ref[k]
+        rows[2 * hot_half + t * slot_cap:2 * hot_half + (t + 1) * slot_cap, :] = own_ref[k, half:, :]
     pooled[...] = jnp.dot(inc_ref[...], rows[...], preferred_element_type=f32).astype(bf16)
     w_out = w_out_ref[...].astype(f32)
     for samples in blocks:
@@ -187,22 +199,22 @@
     cold_ref[...] = jnp.dot(inc_ref[:, 2 * hot_half:].T, dpooled, preferred_element_type=f32).astype(bf16)
 
 
-def pack_grads_body(hot_ref, got_ref, cold_ref, out_ref):
+def pack_grads_body(order, hot_ref, got_ref, cold_ref, out_ref):
     owners, half, width = got_ref.shape
     hot = hot_ref[...] + got_ref[...].reshape(owners * half, width).astype(f32)
     slot_cap = out_ref.shape[1] - half
-    for t in range(owners):
-        out_ref[t, 0:half, :] = hot[t * half:(t + 1) * half].astype(bf16)
-        out_ref[t, half:, :] = cold_ref[t * slot_cap:(t + 1) * slot_cap, :]
-
-
-def collect_body(asked_ref, back_ref, out_ref):
+    for k, t in enumerate(order):
+        out_ref[k, 0:half, :] = hot[t * half:(t + 1) * half].astype(bf16)
+        out_ref[k, half:, :] = cold_ref[t * slot_cap:(t + 1) * slot_cap, :]
+
+
+def collect_body(order, asked_ref, back_ref, out_ref):
     owners, slot_cap = asked_ref.shape
     half = back_ref.shape[1] - slot_cap
     out_ref[0:half, :] = jnp.sum(back_ref[:, 0:half, :].astype(f32), axis=0).astype(bf16)
-    for t in range(owners):
-        out_ref[half + t * slot_cap:half + (t + 1) * slot_cap, :] = back_ref[t, half:, :]
-    asked = lanes([asked_ref[t:t + 1, :] for t in range(owners)])
+    for k, t in enumerate(order):
+        out_ref[half + t * slot_cap:half + (t + 1) * slot_cap, :] = back_ref[k, half:, :]
+    asked = lanes([asked_ref[order.index(t):order.index(t) + 1, :] for t in range(owners)])
     digit = lax.broadcasted_iota(i32, (TAIL, asked.shape[1]), 0)
     digits = jnp.where(digit == 0, asked >> 8, jnp.where(digit == 1, asked & 255, 0))
     out_ref[half + owners * slot_cap:, :] = digits.astype(f32).astype(bf16)
@@ -274,20 +286,20 @@
         copy.wait()
 
 
-def dense_body(hot_ref, asked_ref, back_ref, out_ref):
+def dense_body(order, hot_ref, asked_ref, back_ref, out_ref):
     owners, slot_cap = asked_ref.shape
     half = back_ref.shape[1] - slot_cap
     rows = out_ref.shape[0]
     hot = jnp.sum(back_ref[:, 0:half, :].astype(f32), axis=0).astype(bf16)
     grad = jnp.dot(one_hot(hot_half(hot_ref, core()), (rows, half), 0), hot, preferred_element_type=f32)
-    for t in range(owners):
-        pick = one_hot(asked_ref[t:t + 1, :], (rows, slot_cap), 0)
-        grad += jnp.dot(pick, back_ref[t, half:, :], preferred_element_type=f32)
+    for k, t in enumerate(order):
+        pick = one_hot(asked_ref[k:k + 1, :], (rows, slot_cap), 0)
+        grad += jnp.dot(pick, back_ref[k, half:, :], preferred_element_type=f32)
     out_ref[...] = grad.astype(bf16)
 
 
-def exchange(x):
-    return lax.all_to_all(x, "table", split_axis=0, concat_axis=0, tiled=True)
+def exchange(x, order):
+    return lax.all_to_all(x, "table", split_axis=0, concat_axis=0, tiled=True, axis_index_groups=[list(order)])
 
 
 def swap(x, bit):
@@ -307,7 +319,17 @@
     shape = jax.ShapeDtypeStruct
 
     hot_row = hot_ids.reshape(1, hot_dev)
-    asked = exchange(cold_ids[0])
+    straight = tuple(range(owners))
+    requests = call(
+        turn_body,
+        shape((owners, slot_cap), i32),
+        (pltpu.with_memory_space_constraint(cold_ids[0], pltpu.HBM),),
+        [pltpu.SemaphoreType.DMA((2,))],
+        in_specs=[HBM],
+        out_specs=HBM,
+    )
+    order = straight[owners // 2:] + straight[:owners // 2]
+    asked = exchange(requests, order)
     slots = bag_slots.T
     first = FIRST * batch // 4
     rest = shape((slots.shape[0], batch - first), i32)
@@ -332,18 +354,18 @@
     )
     asked, packed = lax.optimization_barrier((asked, packed))
     served = call(
-        serve_body,
+        functools.partial(serve_body, order),
         shape((owners, half + slot_cap, width), bf16),
         (asked, hot, table_bf),
         [pltpu.VMEM((owners * slot_cap, rows), bf16)],
     )
-    own_rows = exchange(served)
+    own_rows = exchange(served, order)
     first_rows = call(first_rows_body, shape((owners, half, width), bf16), (own_rows,))
     first_rows, packed = lax.optimization_barrier((first_rows, packed))
     mate_rows = swap(first_rows, 1)
     inc = call(incidence_body, shape((batch, vocab), bf16), (packed, key, unit), [pltpu.VMEM((vocab, batch), bf16)])
     dpooled = call(
-        top_body,
+        functools.partial(top_body, order),
         shape((batch, width), bf16),
         (labels.reshape(-1, 128), inc, own_rows, mate_rows, w_in, w_out.reshape(-1, 128)),
         [
@@ -362,11 +384,15 @@
         (shape((hot_half, width), f32), shape((owners * slot_cap, width), bf16)),
         (inc, dpooled),
     )
-    summed = call(pack_grads_body, shape((owners, half + slot_cap, width), bf16), (hot_grads, got, cold_grads))
-    returned = exchange(summed)
+    summed = call(
+        functools.partial(pack_grads_body, order),
+        shape((owners, half + slot_cap, width), bf16),
+        (hot_grads, got, cold_grads),
+    )
+    returned = exchange(summed, order)
     size = half + owners * slot_cap + TAIL
     if groups == 4 and 2 * size <= rows and owners * slot_cap == width:
-        own = call(collect_body, shape((size, width), bf16), (asked, returned))
+        own = call(functools.partial(collect_body, order), shape((size, width), bf16), (asked, returned))
         beside = swap(own, 2)
         far_own, far_beside = swap(own, 1), swap(beside, 1)
         dense = shape((rows, width), f32)
@@ -385,7 +411,7 @@
             out_specs=(HBM, HBM),
         )
         return new_table, new_sum.reshape(rows)
-    grad = call(dense_body, shape((rows, width), bf16), (hot_row, asked, returned))
+    grad = call(functools.partial(dense_body, order), shape((rows, width), bf16), (hot_row, asked, returned))
     grad = lax.psum(grad, "dp").astype(f32)
     new_sum = adagrad_sum + jnp.mean(grad * grad, axis=1)
     return table - learning_rate * grad / jnp.sqrt(new_sum)[:, None], new_sum

time: 53.6 us -> 51.3 us (0.957)
  waiting for transfers between devices: 8.86 us -> 6.49 us
  blocking collectives: 23.1 us -> 21.5 us
  Pallas kernels: 11.3 us -> 12.4 us
    all_to_all x1, waiting for transfers between devices: 3.83 us -> 1.47 us  [exchange(): lax.all_to_all(x, 'table', split_axis=0, concat_axis=0, tiled=True, axis_...]
    all_to_all x2, blocking collectives: 23.1 us -> 21.5 us  [exchange(): lax.all_to_all(x, 'table', split_axis=0, concat_axis=0, tiled=True, axis_...]
    pallas_call x11 -> x12, Pallas kernels: 11.3 us -> 12.4 us  [call(): pl.pallas_call(body, out_shape=outs, in_specs=in_specs or [VMEM] * len(op...]
  transfers between devices with their start and end apart: 6 -> 6, of which waited for: 5 -> 5; matrix products, arithmetic and copies ran while one was open for 0% -> 0% of each run, Pallas kernels for 9% -> 10%
where the time goes in v13:
time: 51.3 us; the launch traced here: 51 us
  blocking collectives  21.5 us (42%)
  Pallas kernels  12.4 us (24%)
  starting transfers between devices  9.83 us (19%)
  waiting for transfers between devices  6.49 us (13%)
  between operations  0.77 us (2%)
    all_to_all x2, blocking collectives, exchange(): lax.all_to_all(x, 'table', split_axis=0, concat_axis=0, tiled=True, axis_...  21.5 us
    pallas_call x12, Pallas kernels, call(): pl.pallas_call(body, out_shape=outs, in_specs=in_specs or [VMEM] * len(op...  12.4 us
    all_to_all x1, starting transfers between devices, exchange(): lax.all_to_all(x, 'table', split_axis=0, concat_axis=0, tiled=True, axis_...  7.83 us
    ppermute x5, waiting for transfers between devices, swap(): lax.ppermute(x, 'dp', [(g, g ^ bit) for g in range(lax.axis_size('dp'))])  5.02 us
    ppermute x5, starting transfers between devices, swap(): lax.ppermute(x, 'dp', [(g, g ^ bit) for g in range(lax.axis_size('dp'))])  2 us
    all_to_all x1, waiting for transfers between devices, exchange(): lax.all_to_all(x, 'table', split_axis=0, concat_axis=0, tiled=True, axis_...  1.47 us
  transfers between devices with their start and end apart: 6, of which 5 were waited for; matrix products, arithmetic and copies ran while one was open for 0% of the time, Pallas kernels for 10%

profile of v13, /device:TPU:0, one launch (start us, length us, event | category | flops | bytes accessed | tf_op | source)
XLA Modules:
  0.0 51.0 jit_solution(7251938766950388975)
XLA Ops:
  0.7 1.2 %shard_map.104 = s32[8,32]{1,0:T(8,128)} custom-call(s32[8,32]{1,0:T(8,128)} %bitcast.22), custom_call_target="tpu_custom_call" | custom-call | tf_op jit(solution)/shard_map/pallas_call | solution.py:24
  1.9 7.8 %all-to-all-start = ((s32[8,1,32]{2,1,0:T(1,128)}), s32[8,1,32]{2,1,0:T(1,128)S(1)}, u32[]{:S(2)}, u32[]{:S(2)}) async-start(s32[8,1,32]{2,1,0:T(1,128)} %bitcast.4), calls=%async_computation | async-start | bytes 8192 | tf_op jit(solution)/shard_map/all_to_all | solution.py:302
  9.7 2.6 %shard_map.105 = (s32[192,256]{1,0:T(8,128)S(1)}, s32[32,256]{1,0:T(8,128)S(1)}, s32[32,256]{1,0:T(8,128)S(1)}, bf16[64,256]{1,0:T(8,128)(2,1)S(1)}, bf16[1024,256]{1,0:T(8,128)(2,1)S(1)}) custom-call(s32[1,8]{1,0:T(1,128)} %count_ref.1, s32[32,512]{1,0:T(8,128)} %bitcast.21, s32[1,64]{1,0:T(1,128)} %bitcast.16, f32[1024,256]{1,0:T(8,128)} %table_ref.3), custom_call_target="tpu_custom_call" | custom-call | tf_op jit(solution)/shard_map/pallas_call | solution.py:24
  12.3 1.5 %all-to-all-done = s32[8,1,32]{2,1,0:T(1,128)S(1)} async-done(((s32[8,1,32]{2,1,0:T(1,128)}), s32[8,1,32]{2,1,0:T(1,128)S(1)}, u32[]{:S(2)}, u32[]{:S(2)}) %all-to-all-start) | async-done | bytes 1056 | tf_op jit(solution)/shard_map/all_to_all | solution.py:302
  13.8 0.4 shard_map.106
  14.2 9.9 %all_to_all.22.rows_ref.own_ref = bf16[8,64,256]{2,1,0:T(8,128)(2,1)S(1)} all-to-all(bf16[8,64,256]{2,1,0:T(8,128)(2,1)S(1)} %shard_map.106), channel_id=1, replica_groups={{4,5,6,7,0,1,2,3},{12,13,14,15,8,9,10,11},{20,21,22,23,16,17,18,19},{28..., dimensions={0} | all-to-all | bytes 524288 | tf_op jit(solution)/shard_map/all_to_all | solution.py:302
  24.1 0.1 collective-permute-start
  24.2 1.1 %shard_map.108.inc_ref = bf16[512,768]{1,0:T(8,128)(2,1)S(1)} custom-call(s32[192,256]{1,0:T(8,128)S(1)} %get-tuple-element.22.packed_ref, s32[32,256]{1,0:T(8,128)S(1)} %get-tuple-element.23.key_ref, s32[32,256]{1,0:T(8,128)S(1)} %get-tuple-element.24.unit_ref), custom_call_target="tpu_custom_call" | custom-call | tf_op jit(solution)/shard_map/pallas_call | solution.py:24
  25.3 0.2 collective-permute-done.mate_ref
  25.5 3.5 %shard_map.109.dpooled_ref = bf16[512,256]{1,0:T(8,128)(2,1)S(1)} custom-call(f32[4,128]{1,0:T(4,128)S(1)} %bitcast.20, bf16[512,768]{1,0:T(8,128)(2,1)S(1)} %shard_map.108.inc_ref, bf16[8,64,256]{2,1,0:T(8,128)(2,1)S(1)} %all_to_all.22.rows_ref.own_ref, bf16[8,32,256]{2,1,0:T(8,128)(2,1)S(1)} %collective-permute-done.mate_ref, ...), custom_call_target="tpu_custom_call" | custom-call | tf_op jit(solution)/shard_map/pallas_call | solution.py:24
  29.0 0.0 copy-start.3
  29.0 0.0 copy-start
  29.0 0.0 copy-start.4
  29.0 0.3 shard_map.111
  29.3 0.4 collective-permute-start.1
  29.7 0.3 shard_map.110
  30.0 0.7 %collective-permute-done.1.got_ref = bf16[8,32,256]{2,1,0:T(8,128)(2,1)S(1)} collective-permute-done((bf16[8,32,256]{2,1,0:T(8,128)(2,1)S(1)}, bf16[8,32,256]{2,1,0:T(8,128)(2,1)S(1)}, u32[]{:S(2)}, u32[]{:S(2)}) %collective-permute-start.1) | collective-permute-done | bytes 131104 | tf_op jit(solution)/shard_map/ppermute | solution.py:306
  30.8 11.6 %all_to_all.23.back_ref = bf16[8,64,256]{2,1,0:T(8,128)(2,1)S(1)} all-to-all(bf16[8,64,256]{2,1,0:T(8,128)(2,1)S(1)} %shard_map.112), channel_id=1, replica_groups={{4,5,6,7,0,1,2,3},{12,13,14,15,8,9,10,11},{20,21,22,23,16,17,18,19},{28..., dimensions={0} | all-to-all | bytes 524288 | tf_op jit(solution)/shard_map/all_to_all | solution.py:302
  42.4 0.1 shard_map.113.refs_0_
  42.5 1.6 %collective-permute-start.2 = (bf16[304,256]{1,0:T(8,128)(2,1)S(1)}, bf16[304,256]{1,0:T(8,128)(2,1)S(1)}, u32[]{:S(2)}, u32[]{:S(2)}) collective-permute-start(bf16[304,256]{1,0:T(8,128)(2,1)S(1)} %shard_map.113.refs_0_), channel_id=1, source_target_pairs={{0,16},{8,24},{16,0},{24,8},{1,17},{9,25},{17,1},{25,9},{2,18},{10... | collective-permute-start | bytes 466952 | tf_op jit(solution)/shard_map/ppermute | solution.py:306
  44.0 3.7 %collective-permute-done.2.refs_1_ = bf16[304,256]{1,0:T(8,128)(2,1)S(1)} collective-permute-done((bf16[304,256]{1,0:T(8,128)(2,1)S(1)}, bf16[304,256]{1,0:T(8,128)(2,1)S(1)}, u32[]{:S(2)}, u32[]{:S(2)}) %collective-permute-start.2) | collective-permute-done | bytes 155680 | tf_op jit(solution)/shard_map/ppermute | solution.py:306
  47.8 1.0 %shard_map.114 = (f32[1024,256]{1,0:T(8,128)S(1)}, f32[1024,256]{1,0:T(8,128)S(1)}) custom-call(s32[1,64]{1,0:T(1,128)S(1)} %bitcast.17, bf16[304,256]{1,0:T(8,128)(2,1)S(1)} %shard_map.113.refs_0_, bf16[304,256]{1,0:T(8,128)(2,1)S(1)} %collective-permute-done.2.refs_1_, bf16[304,256]{1,0:T(8,128)(2,1)S(1)} %collective-permute-done.3.refs_2_), custom_call_target="tpu_custom_call" | custom-call | tf_op jit(solution)/shard_map/pallas_call | solution.py:24
  48.8 0.4 collective-permute-done.4.part_ref
  49.1 1.9 %shard_map.115 = (f32[1024,256]{1,0:T(8,128)}, f32[8,128]{1,0:T(8,128)}) custom-call(s32[1,64]{1,0:T(1,128)S(1)} %bitcast.18, f32[8,128]{1,0:T(8,128)S(1)} %bitcast.19, f32[1024,256]{1,0:T(8,128)S(1)} %copy-done, f32[1024,256]{1,0:T(8,128)S(1)} %get-tuple-element.28.near_ref, f32[1024,256]{1,0:T(8,128)S(1)} %get-tuple-element.29.far_ref, ...), custom_call_target="tpu_custom_call" | custom-call | tf_op jit(solution)/shard_map/pallas_call | solution.py:24
  (14 shorter events, 0.1 us)
Async XLA Ops:
  0.6 24.9 %copy-start.2 = (bf16[4096]{0:T(1024)(128)(2,1)S(1)}, bf16[4096]{0:T(1024)(128)(2,1)}, u32[]{:S(2)}) copy-start(bf16[4096]{0:T(1024)(128)(2,1)} %param.17) | copy-start | bytes 24580
  0.6 24.9 %copy-start.1 = (bf16[256,4096]{1,0:T(8,128)(2,1)S(1)}, bf16[256,4096]{1,0:T(8,128)(2,1)}, u32[]{:S(2)}) copy-start(bf16[256,4096]{1,0:T(8,128)(2,1)} %w_in_ref.1) | copy-start | bytes 6291460
  0.7 24.9 %copy-start.5 = (f32[512]{0:T(512)S(1)}, f32[512]{0:T(512)}, u32[]{:S(2)}) copy-start(f32[512]{0:T(512)} %param.10) | copy-start | bytes 6148
  1.9 11.9 %all-to-all-start = ((s32[8,1,32]{2,1,0:T(1,128)}), s32[8,1,32]{2,1,0:T(1,128)S(1)}, u32[]{:S(2)}, u32[]{:S(2)}) async-start(s32[8,1,32]{2,1,0:T(1,128)} %bitcast.4), calls=%async_computation | async-start | bytes 8192 | tf_op jit(solution)/shard_map/all_to_all | solution.py:302
  24.1 1.4 %collective-permute-start = (bf16[8,32,256]{2,1,0:T(8,128)(2,1)S(1)}, bf16[8,32,256]{2,1,0:T(8,128)(2,1)S(1)}, u32[]{:S(2)}, u32[]{:S(2)}) collective-permute-start(bf16[8,32,256]{2,1,0:T(8,128)(2,1)S(1)} %shard_map.107), channel_id=1, source_target_pairs={{0,8},{8,0},{16,24},{24,16},{1,9},{9,1},{17,25},{25,17},{2,10},{10... | collective-permute-start | bytes 393224 | tf_op jit(solution)/shard_map/ppermute | solution.py:306
  29.0 18.8 %copy-start.3 = (s32[64]{0:T(128)S(1)}, s32[64]{0:T(128)}, u32[]{:S(2)}) copy-start(s32[64]{0:T(128)} %param.15) | copy-start | bytes 772
  29.0 20.1 %copy-start = (f32[1024,256]{1,0:T(8,128)S(1)}, f32[1024,256]{1,0:T(8,128)}, u32[]{:S(2)}) copy-start(f32[1024,256]{1,0:T(8,128)} %table_ref.3) | copy-start | bytes 3145732
  29.0 20.1 %copy-start.4 = (f32[1024]{0:T(1024)S(1)}, f32[1024]{0:T(1024)}, u32[]{:S(2)}) copy-start(f32[1024]{0:T(1024)} %param.14) | copy-start | bytes 12292
  29.3 1.4 %collective-permute-start.1 = (bf16[8,32,256]{2,1,0:T(8,128)(2,1)S(1)}, bf16[8,32,256]{2,1,0:T(8,128)(2,1)S(1)}, u32[]{:S(2)}, u32[]{:S(2)}) collective-permute-start(bf16[8,32,256]{2,1,0:T(8,128)(2,1)S(1)} %bitcast.12), channel_id=1, source_target_pairs={{0,8},{8,0},{16,24},{24,16},{1,9},{9,1},{17,25},{25,17},{2,10},{10... | collective-permute-start | bytes 393224 | tf_op jit(solution)/shard_map/ppermute | solution.py:306
  42.5 5.3 %collective-permute-start.2 = (bf16[304,256]{1,0:T(8,128)(2,1)S(1)}, bf16[304,256]{1,0:T(8,128)(2,1)S(1)}, u32[]{:S(2)}, u32[]{:S(2)}) collective-permute-start(bf16[304,256]{1,0:T(8,128)(2,1)S(1)} %shard_map.113.refs_0_), channel_id=1, source_target_pairs={{0,16},{8,24},{16,0},{24,8},{1,17},{9,25},{17,1},{25,9},{2,18},{10... | collective-permute-start | bytes 466952 | tf_op jit(solution)/shard_map/ppermute | solution.py:306
  44.0 3.7 %collective-permute-start.3 = (bf16[304,256]{1,0:T(8,128)(2,1)S(1)}, bf16[304,256]{1,0:T(8,128)(2,1)S(1)}, u32[]{:S(2)}, u32[]{:S(2)}) collective-permute-start(bf16[304,256]{1,0:T(8,128)(2,1)S(1)} %shard_map.113.refs_0_), channel_id=1, source_target_pairs={{0,8},{8,0},{16,24},{24,16},{1,9},{9,1},{17,25},{25,17},{2,10},{10... | collective-permute-start | bytes 466952 | tf_op jit(solution)/shard_map/ppermute | solution.py:306
  47.7 1.4 %collective-permute-start.4 = (bf16[304,256]{1,0:T(8,128)(2,1)S(1)}, bf16[304,256]{1,0:T(8,128)(2,1)S(1)}, u32[]{:S(2)}, u32[]{:S(2)}) collective-permute-start(bf16[304,256]{1,0:T(8,128)(2,1)S(1)} %collective-permute-done.2.refs_1_), channel_id=1, source_target_pairs={{0,8},{8,0},{16,24},{24,16},{1,9},{9,1},{17,25},{25,17},{2,10},{10... | collective-permute-start | bytes 466952 | tf_op jit(solution)/shard_map/ppermute | solution.py:306

commit v14 on v13

--- a/solution.py
+++ b/solution.py
@@ -138,13 +138,13 @@
     out_ref[...] = rows_ref[:, 0:out_ref.shape[1], :]
 
 
-def top_body(order, labels_ref, inc_ref, own_ref, mate_ref, w_in_ref, w_out_ref, out_ref, hidden, rows, pooled, total, dlogit):
+def top_body(order, labels_ref, inc_ref, own_ref, mate_ref, w_in_ref, w_out_ref, out_ref, to_mate_ref, hidden, rows, pooled, total, dlogit):
     batch = inc_ref.shape[0]
     hidden_units, width = w_in_ref.shape[1], w_in_ref.shape[0]
     owners, half, _ = mate_ref.shape
     hot_half = owners * half
     slot_cap = own_ref.shape[1] - half
-    size, step, wide = batch // 2, 512, 1024
+    size, step, wide = batch // 2, 512, 512
     blocks = [slice(at, at + size) for at in range(0, batch, size)]
     for k, t in enumerate(order):
         rows[t * half:(t + 1) * half, :] = own_ref[k, 0:half, :]
@@ -152,6 +152,7 @@
         rows[2 * hot_half + t * slot_cap:2 * hot_half + (t + 1) * slot_cap, :] = own_ref[k, half:, :]
     pooled[...] = jnp.dot(inc_ref[...], rows[...], preferred_element_type=f32).astype(bf16)
     w_out = w_out_ref[...].astype(f32)
+    labels = labels_ref[...].T
     for samples in blocks:
         acc = jnp.zeros((size, 128), f32)
         for start in range(0, hidden_units, step):
@@ -164,11 +165,11 @@
             for k in range(0, step, 128):
                 acc += term[:, k:k + 128]
         total[samples, :] = acc
-    lines = [slice(at, at + 128) for at in range(0, batch, 128)]
-    logit = lanes([jnp.sum(total[line, :], axis=1, keepdims=True) for line in lines])
-    delta = jax.nn.sigmoid(logit) - labels_ref[...].T
-    for k, line in enumerate(lines):
-        dlogit[line, :] = jnp.broadcast_to(delta[:, k:k + 1], (128, 128))
+        for k in range(samples.start // 128, samples.stop // 128):
+            line = slice(k * 128, (k + 1) * 128)
+            logit = jnp.sum(total[line, :], axis=1, keepdims=True)
+            dlogit[line, :] = jnp.broadcast_to(jax.nn.sigmoid(logit) - labels[:, k:k + 1], (128, 128))
+    mate = jnp.zeros((hot_half, width), f32)
     for samples in blocks:
         scale = dlogit[samples, :]
         grad = jnp.zeros((size, width), f32)
@@ -183,13 +184,10 @@
                 dhidden, w_in_ref[:, start:start + wide], (((1,), (1,)), ((), ())), preferred_element_type=f32
             )
         out_ref[samples, :] = grad.astype(bf16)
-
-
-def mate_grads_body(inc_ref, dpooled_ref, out_ref):
-    hot_half = out_ref.shape[0]
-    out_ref[...] = jnp.dot(
-        inc_ref[:, hot_half:2 * hot_half].T, dpooled_ref[...], preferred_element_type=f32
-    ).astype(bf16)
+        mate += jnp.dot(
+            inc_ref[samples, hot_half:2 * hot_half].T, out_ref[samples, :], preferred_element_type=f32
+        )
+    to_mate_ref[...] = mate.astype(bf16)
 
 
 def own_grads_body(inc_ref, dpooled_ref, hot_ref, cold_ref):
@@ -364,9 +362,10 @@
     first_rows, packed = lax.optimization_barrier((first_rows, packed))
     mate_rows = swap(first_rows, 1)
     inc = call(incidence_body, shape((batch, vocab), bf16), (packed, key, unit), [pltpu.VMEM((vocab, batch), bf16)])
-    dpooled = call(
+    hot_half = owners * half
+    dpooled, to_mate = call(
         functools.partial(top_body, order),
-        shape((batch, width), bf16),
+        (shape((batch, width), bf16), shape((hot_half, width), bf16)),
         (labels.reshape(-1, 128), inc, own_rows, mate_rows, w_in, w_out.reshape(-1, 128)),
         [
             pltpu.VMEM((batch, hidden_units), bf16),
@@ -376,8 +375,6 @@
             pltpu.VMEM((batch, 128), f32),
         ],
     )
-    hot_half = owners * half
-    to_mate = call(mate_grads_body, shape((hot_half, width), bf16), (inc, dpooled))
     got = swap(to_mate.reshape(owners, half, width), 1)
     hot_grads, cold_grads = call(
         own_grads_body,

time: 51.3 us -> 51.1 us (level)
    pallas_call x12 -> x11, Pallas kernels: 12.4 us -> 12.2 us  [call(): pl.pallas_call(body, out_shape=outs, in_specs=in_specs or [VMEM] * len(op...]
where the time goes in v14:
time: 51.1 us; the launch traced here: 50.8 us
  blocking collectives  21.5 us (42%)
  Pallas kernels  12.2 us (24%)
  starting transfers between devices  9.83 us (19%)
  waiting for transfers between devices  6.49 us (13%)
  between operations  0.76 us (1%)
    all_to_all x2, blocking collectives, exchange(): lax.all_to_all(x, 'table', split_axis=0, concat_axis=0, tiled=True, axis_...  21.5 us
    pallas_call x11, Pallas kernels, call(): pl.pallas_call(body, out_shape=outs, in_specs=in_specs or [VMEM] * len(op...  12.2 us
    all_to_all x1, starting transfers between devices, exchange(): lax.all_to_all(x, 'table', split_axis=0, concat_axis=0, tiled=True, axis_...  7.83 us
    ppermute x5, waiting for transfers between devices, swap(): lax.ppermute(x, 'dp', [(g, g ^ bit) for g in range(lax.axis_size('dp'))])  5.02 us
    ppermute x5, starting transfers between devices, swap(): lax.ppermute(x, 'dp', [(g, g ^ bit) for g in range(lax.axis_size('dp'))])  2 us
    all_to_all x1, waiting for transfers between devices, exchange(): lax.all_to_all(x, 'table', split_axis=0, concat_axis=0, tiled=True, axis_...  1.47 us
  transfers between devices with their start and end apart: 6, of which 5 were waited for; matrix products, arithmetic and copies ran while one was open for 0% of the time, Pallas kernels for 10%

profile of v14, /device:TPU:0, one launch (start us, length us, event | category | flops | bytes accessed | tf_op | source)
XLA Modules:
  0.0 50.8 jit_solution(13351755178771774428)
XLA Ops:
  0.7 1.2 %shard_map.104 = s32[8,32]{1,0:T(8,128)} custom-call(s32[8,32]{1,0:T(8,128)} %bitcast.22), custom_call_target="tpu_custom_call" | custom-call | tf_op jit(solution)/shard_map/pallas_call | solution.py:24
  1.9 7.8 %all-to-all-start = ((s32[8,1,32]{2,1,0:T(1,128)}), s32[8,1,32]{2,1,0:T(1,128)S(1)}, u32[]{:S(2)}, u32[]{:S(2)}) async-start(s32[8,1,32]{2,1,0:T(1,128)} %bitcast.4), calls=%async_computation | async-start | bytes 8192 | tf_op jit(solution)/shard_map/all_to_all | solution.py:300
  9.7 2.6 %shard_map.105 = (s32[192,256]{1,0:T(8,128)S(1)}, s32[32,256]{1,0:T(8,128)S(1)}, s32[32,256]{1,0:T(8,128)S(1)}, bf16[64,256]{1,0:T(8,128)(2,1)S(1)}, bf16[1024,256]{1,0:T(8,128)(2,1)S(1)}) custom-call(s32[1,8]{1,0:T(1,128)} %count_ref.1, s32[32,512]{1,0:T(8,128)} %bitcast.21, s32[1,64]{1,0:T(1,128)} %bitcast.15, f32[1024,256]{1,0:T(8,128)} %table_ref.3), custom_call_target="tpu_custom_call" | custom-call | tf_op jit(solution)/shard_map/pallas_call | solution.py:24
  12.3 1.5 %all-to-all-done = s32[8,1,32]{2,1,0:T(1,128)S(1)} async-done(((s32[8,1,32]{2,1,0:T(1,128)}), s32[8,1,32]{2,1,0:T(1,128)S(1)}, u32[]{:S(2)}, u32[]{:S(2)}) %all-to-all-start) | async-done | bytes 1056 | tf_op jit(solution)/shard_map/all_to_all | solution.py:300
  13.8 0.4 shard_map.106
  14.2 9.9 %all_to_all.22.rows_ref.own_ref = bf16[8,64,256]{2,1,0:T(8,128)(2,1)S(1)} all-to-all(bf16[8,64,256]{2,1,0:T(8,128)(2,1)S(1)} %shard_map.106), channel_id=1, replica_groups={{4,5,6,7,0,1,2,3},{12,13,14,15,8,9,10,11},{20,21,22,23,16,17,18,19},{28..., dimensions={0} | all-to-all | bytes 524288 | tf_op jit(solution)/shard_map/all_to_all | solution.py:300
  24.1 0.1 collective-permute-start
  24.2 1.1 %shard_map.108.inc_ref = bf16[512,768]{1,0:T(8,128)(2,1)S(1)} custom-call(s32[192,256]{1,0:T(8,128)S(1)} %get-tuple-element.24.packed_ref, s32[32,256]{1,0:T(8,128)S(1)} %get-tuple-element.25.key_ref, s32[32,256]{1,0:T(8,128)S(1)} %get-tuple-element.26.unit_ref), custom_call_target="tpu_custom_call" | custom-call | tf_op jit(solution)/shard_map/pallas_call | solution.py:24
  25.3 0.2 collective-permute-done.mate_ref
  25.5 3.6 %shard_map.109 = (bf16[512,256]{1,0:T(8,128)(2,1)S(1)}, bf16[256,256]{1,0:T(8,128)(2,1)S(1)}) custom-call(f32[4,128]{1,0:T(4,128)S(1)} %bitcast.19, bf16[512,768]{1,0:T(8,128)(2,1)S(1)} %shard_map.108.inc_ref, bf16[8,64,256]{2,1,0:T(8,128)(2,1)S(1)} %all_to_all.22.rows_ref.own_ref, bf16[8,32,256]{2,1,0:T(8,128)(2,1)S(1)} %collective-permute-done.mate_ref, ...), custom_call_target="tpu_custom_call" | custom-call | tf_op jit(solution)/shard_map/pallas_call | solution.py:24
  29.1 0.0 copy-start.3
  29.1 0.0 copy-start
  29.1 0.0 copy-start.4
  29.2 0.4 collective-permute-start.1
  29.5 0.3 shard_map.110
  29.9 0.7 %collective-permute-done.1.got_ref = bf16[8,32,256]{2,1,0:T(8,128)(2,1)S(1)} collective-permute-done((bf16[8,32,256]{2,1,0:T(8,128)(2,1)S(1)}, bf16[8,32,256]{2,1,0:T(8,128)(2,1)S(1)}, u32[]{:S(2)}, u32[]{:S(2)}) %collective-permute-start.1) | collective-permute-done | bytes 131104 | tf_op jit(solution)/shard_map/ppermute | solution.py:304
  30.6 11.6 %all_to_all.23.back_ref = bf16[8,64,256]{2,1,0:T(8,128)(2,1)S(1)} all-to-all(bf16[8,64,256]{2,1,0:T(8,128)(2,1)S(1)} %shard_map.111), channel_id=1, replica_groups={{4,5,6,7,0,1,2,3},{12,13,14,15,8,9,10,11},{20,21,22,23,16,17,18,19},{28..., dimensions={0} | all-to-all | bytes 524288 | tf_op jit(solution)/shard_map/all_to_all | solution.py:300
  42.2 0.1 shard_map.112.refs_0_
  42.3 1.6 %collective-permute-start.2 = (bf16[304,256]{1,0:T(8,128)(2,1)S(1)}, bf16[304,256]{1,0:T(8,128)(2,1)S(1)}, u32[]{:S(2)}, u32[]{:S(2)}) collective-permute-start(bf16[304,256]{1,0:T(8,128)(2,1)S(1)} %shard_map.112.refs_0_), channel_id=1, source_target_pairs={{0,16},{8,24},{16,0},{24,8},{1,17},{9,25},{17,1},{25,9},{2,18},{10... | collective-permute-start | bytes 466952 | tf_op jit(solution)/shard_map/ppermute | solution.py:304
  43.9 3.7 %collective-permute-done.2.refs_1_ = bf16[304,256]{1,0:T(8,128)(2,1)S(1)} collective-permute-done((bf16[304,256]{1,0:T(8,128)(2,1)S(1)}, bf16[304,256]{1,0:T(8,128)(2,1)S(1)}, u32[]{:S(2)}, u32[]{:S(2)}) %collective-permute-start.2) | collective-permute-done | bytes 155680 | tf_op jit(solution)/shard_map/ppermute | solution.py:304
  47.6 0.0 collective-permute-start.4
  47.6 1.0 %shard_map.113 = (f32[1024,256]{1,0:T(8,128)S(1)}, f32[1024,256]{1,0:T(8,128)S(1)}) custom-call(s32[1,64]{1,0:T(1,128)S(1)} %bitcast.16, bf16[304,256]{1,0:T(8,128)(2,1)S(1)} %shard_map.112.refs_0_, bf16[304,256]{1,0:T(8,128)(2,1)S(1)} %collective-permute-done.2.refs_1_, bf16[304,256]{1,0:T(8,128)(2,1)S(1)} %collective-permute-done.3.refs_2_), custom_call_target="tpu_custom_call" | custom-call | tf_op jit(solution)/shard_map/pallas_call | solution.py:24
  48.6 0.4 collective-permute-done.4.part_ref
  49.0 1.9 %shard_map.114 = (f32[1024,256]{1,0:T(8,128)}, f32[8,128]{1,0:T(8,128)}) custom-call(s32[1,64]{1,0:T(1,128)S(1)} %bitcast.17, f32[8,128]{1,0:T(8,128)S(1)} %bitcast.18, f32[1024,256]{1,0:T(8,128)S(1)} %copy-done, f32[1024,256]{1,0:T(8,128)S(1)} %get-tuple-element.32.near_ref, f32[1024,256]{1,0:T(8,128)S(1)} %get-tuple-element.33.far_ref, ...), custom_call_target="tpu_custom_call" | custom-call | tf_op jit(solution)/shard_map/pallas_call | solution.py:24
  (13 shorter events, 0.1 us)
Async XLA Ops:
  0.6 24.9 %copy-start.2 = (bf16[4096]{0:T(1024)(128)(2,1)S(1)}, bf16[4096]{0:T(1024)(128)(2,1)}, u32[]{:S(2)}) copy-start(bf16[4096]{0:T(1024)(128)(2,1)} %param.17) | copy-start | bytes 24580
  0.6 24.9 %copy-start.1 = (bf16[256,4096]{1,0:T(8,128)(2,1)S(1)}, bf16[256,4096]{1,0:T(8,128)(2,1)}, u32[]{:S(2)}) copy-start(bf16[256,4096]{1,0:T(8,128)(2,1)} %w_in_ref.1) | copy-start | bytes 6291460
  0.7 24.9 %copy-start.5 = (f32[512]{0:T(512)S(1)}, f32[512]{0:T(512)}, u32[]{:S(2)}) copy-start(f32[512]{0:T(512)} %param.10) | copy-start | bytes 6148
  1.9 11.9 %all-to-all-start = ((s32[8,1,32]{2,1,0:T(1,128)}), s32[8,1,32]{2,1,0:T(1,128)S(1)}, u32[]{:S(2)}, u32[]{:S(2)}) async-start(s32[8,1,32]{2,1,0:T(1,128)} %bitcast.4), calls=%async_computation | async-start | bytes 8192 | tf_op jit(solution)/shard_map/all_to_all | solution.py:300
  24.1 1.4 %collective-permute-start = (bf16[8,32,256]{2,1,0:T(8,128)(2,1)S(1)}, bf16[8,32,256]{2,1,0:T(8,128)(2,1)S(1)}, u32[]{:S(2)}, u32[]{:S(2)}) collective-permute-start(bf16[8,32,256]{2,1,0:T(8,128)(2,1)S(1)} %shard_map.107), channel_id=1, source_target_pairs={{0,8},{8,0},{16,24},{24,16},{1,9},{9,1},{17,25},{25,17},{2,10},{10... | collective-permute-start | bytes 393224 | tf_op jit(solution)/shard_map/ppermute | solution.py:304
  29.1 18.5 %copy-start.3 = (s32[64]{0:T(128)S(1)}, s32[64]{0:T(128)}, u32[]{:S(2)}) copy-start(s32[64]{0:T(128)} %param.15) | copy-start | bytes 772
  29.1 19.9 %copy-start = (f32[1024,256]{1,0:T(8,128)S(1)}, f32[1024,256]{1,0:T(8,128)}, u32[]{:S(2)}) copy-start(f32[1024,256]{1,0:T(8,128)} %table_ref.3) | copy-start | bytes 3145732
  29.1 19.8 %copy-start.4 = (f32[1024]{0:T(1024)S(1)}, f32[1024]{0:T(1024)}, u32[]{:S(2)}) copy-start(f32[1024]{0:T(1024)} %param.14) | copy-start | bytes 12292
  29.2 1.4 %collective-permute-start.1 = (bf16[8,32,256]{2,1,0:T(8,128)(2,1)S(1)}, bf16[8,32,256]{2,1,0:T(8,128)(2,1)S(1)}, u32[]{:S(2)}, u32[]{:S(2)}) collective-permute-start(bf16[8,32,256]{2,1,0:T(8,128)(2,1)S(1)} %bitcast.20), channel_id=1, source_target_pairs={{0,8},{8,0},{16,24},{24,16},{1,9},{9,1},{17,25},{25,17},{2,10},{10... | collective-permute-start | bytes 393224 | tf_op jit(solution)/shard_map/ppermute | solution.py:304
  42.3 5.3 %collective-permute-start.2 = (bf16[304,256]{1,0:T(8,128)(2,1)S(1)}, bf16[304,256]{1,0:T(8,128)(2,1)S(1)}, u32[]{:S(2)}, u32[]{:S(2)}) collective-permute-start(bf16[304,256]{1,0:T(8,128)(2,1)S(1)} %shard_map.112.refs_0_), channel_id=1, source_target_pairs={{0,16},{8,24},{16,0},{24,8},{1,17},{9,25},{17,1},{25,9},{2,18},{10... | collective-permute-start | bytes 466952 | tf_op jit(solution)/shard_map/ppermute | solution.py:304
  43.9 3.7 %collective-permute-start.3 = (bf16[304,256]{1,0:T(8,128)(2,1)S(1)}, bf16[304,256]{1,0:T(8,128)(2,1)S(1)}, u32[]{:S(2)}, u32[]{:S(2)}) collective-permute-start(bf16[304,256]{1,0:T(8,128)(2,1)S(1)} %shard_map.112.refs_0_), channel_id=1, source_target_pairs={{0,8},{8,0},{16,24},{24,16},{1,9},{9,1},{17,25},{25,17},{2,10},{10... | collective-permute-start | bytes 466952 | tf_op jit(solution)/shard_map/ppermute | solution.py:304
  47.6 1.4 %collective-permute-start.4 = (bf16[304,256]{1,0:T(8,128)(2,1)S(1)}, bf16[304,256]{1,0:T(8,128)(2,1)S(1)}, u32[]{:S(2)}, u32[]{:S(2)}) collective-permute-start(bf16[304,256]{1,0:T(8,128)(2,1)S(1)} %collective-permute-done.2.refs_1_), channel_id=1, source_target_pairs={{0,8},{8,0},{16,24},{24,16},{1,9},{9,1},{17,25},{25,17},{2,10},{10... | collective-permute-start | bytes 466952 | tf_op jit(solution)/shard_map/ppermute | solution.py:304

commit v15 on v14

--- a/solution.py
+++ b/solution.py
@@ -121,11 +121,11 @@
     return lax.rem(lax.axis_index("dp"), 2)
 
 
-def serve_body(order, asked_ref, hot_ref, table_ref, out_ref, pick):
+def serve_body(ask_order, order, asked_ref, hot_ref, table_ref, out_ref, pick):
     owners, slot_cap = asked_ref.shape
     half = hot_ref.shape[0] // 2
     asked = asked_ref[...].T
-    for k, t in enumerate(order):
+    for k, t in enumerate(ask_order):
         pick[t * slot_cap:(t + 1) * slot_cap, :] = one_hot(asked[:, k:k + 1], (slot_cap, table_ref.shape[0]), 1)
     picked = jnp.dot(pick[...], table_ref[...], preferred_element_type=f32).astype(bf16)
     hot = hot_ref[pl.ds(pl.multiple_of(core() * half, half), half), :]
@@ -206,13 +206,13 @@
         out_ref[k, half:, :] = cold_ref[t * slot_cap:(t + 1) * slot_cap, :]
 
 
-def collect_body(order, asked_ref, back_ref, out_ref):
+def collect_body(ask_order, order, asked_ref, back_ref, out_ref):
     owners, slot_cap = asked_ref.shape
     half = back_ref.shape[1] - slot_cap
     out_ref[0:half, :] = jnp.sum(back_ref[:, 0:half, :].astype(f32), axis=0).astype(bf16)
     for k, t in enumerate(order):
         out_ref[half + t * slot_cap:half + (t + 1) * slot_cap, :] = back_ref[k, half:, :]
-    asked = lanes([asked_ref[order.index(t):order.index(t) + 1, :] for t in range(owners)])
+    asked = lanes([asked_ref[ask_order.index(t):ask_order.index(t) + 1, :] for t in range(owners)])
     digit = lax.broadcasted_iota(i32, (TAIL, asked.shape[1]), 0)
     digits = jnp.where(digit == 0, asked >> 8, jnp.where(digit == 1, asked & 255, 0))
     out_ref[half + owners * slot_cap:, :] = digits.astype(f32).astype(bf16)
@@ -284,14 +284,15 @@
         copy.wait()
 
 
-def dense_body(order, hot_ref, asked_ref, back_ref, out_ref):
+def dense_body(ask_order, order, hot_ref, asked_ref, back_ref, out_ref):
     owners, slot_cap = asked_ref.shape
     half = back_ref.shape[1] - slot_cap
     rows = out_ref.shape[0]
     hot = jnp.sum(back_ref[:, 0:half, :].astype(f32), axis=0).astype(bf16)
     grad = jnp.dot(one_hot(hot_half(hot_ref, core()), (rows, half), 0), hot, preferred_element_type=f32)
     for k, t in enumerate(order):
-        pick = one_hot(asked_ref[k:k + 1, :], (rows, slot_cap), 0)
+        at = ask_order.index(t)
+        pick = one_hot(asked_ref[at:at + 1, :], (rows, slot_cap), 0)
         grad += jnp.dot(pick, back_ref[k, half:, :], preferred_element_type=f32)
     out_ref[...] = grad.astype(bf16)
 
@@ -317,7 +318,6 @@
     shape = jax.ShapeDtypeStruct
 
     hot_row = hot_ids.reshape(1, hot_dev)
-    straight = tuple(range(owners))
     requests = call(
         turn_body,
         shape((owners, slot_cap), i32),
@@ -326,8 +326,9 @@
         in_specs=[HBM],
         out_specs=HBM,
     )
-    order = straight[owners // 2:] + straight[:owners // 2]
-    asked = exchange(requests, order)
+    ask_order = tuple((t + owners // 2) % owners for t in range(owners))
+    order = tuple(t if t % 2 else ask_order[t] for t in range(owners))
+    asked = exchange(requests, ask_order)
     slots = bag_slots.T
     first = FIRST * batch // 4
     rest = shape((slots.shape[0], batch - first), i32)
@@ -352,7 +353,7 @@
     )
     asked, packed = lax.optimization_barrier((asked, packed))
     served = call(
-        functools.partial(serve_body, order),
+        functools.partial(serve_body, ask_order, order),
         shape((owners, half + slot_cap, width), bf16),
         (asked, hot, table_bf),
         [pltpu.VMEM((owners * slot_cap, rows), bf16)],
@@ -389,7 +390,7 @@
     returned = exchange(summed, order)
     size = half + owners * slot_cap + TAIL
     if groups == 4 and 2 * size <= rows and owners * slot_cap == width:
-        own = call(functools.partial(collect_body, order), shape((size, width), bf16), (asked, returned))
+        own = call(functools.partial(collect_body, ask_order, order), shape((size, width), bf16), (asked, returned))
         beside = swap(own, 2)
         far_own, far_beside = swap(own, 1), swap(beside, 1)
         dense = shape((rows, width), f32)
@@ -408,7 +409,7 @@
             out_specs=(HBM, HBM),
         )
         return new_table, new_sum.reshape(rows)
-    grad = call(functools.partial(dense_body, order), shape((rows, width), bf16), (hot_row, asked, returned))
+    grad = call(functools.partial(dense_body, ask_order, order), shape((rows, width), bf16), (hot_row, asked, returned))
     grad = lax.psum(grad, "dp").astype(f32)
     new_sum = adagrad_sum + jnp.mean(grad * grad, axis=1)
     return table - learning_rate * grad / jnp.sqrt(new_sum)[:, None], new_sum

time: 51.1 us -> 50.8 us (level)
  no operation moved by 1% of the time
where the time goes in v15:
time: 50.8 us; the launch traced here: 50.6 us
  blocking collectives  21.3 us (42%)
  Pallas kernels  12.2 us (24%)
  starting transfers between devices  9.83 us (19%)
  waiting for transfers between devices  6.48 us (13%)
  between operations  0.76 us (1%)
    all_to_all x2, blocking collectives, exchange(): lax.all_to_all(x, 'table', split_axis=0, concat_axis=0, tiled=True, axis_...  21.3 us
    pallas_call x11, Pallas kernels, call(): pl.pallas_call(body, out_shape=outs, in_specs=in_specs or [VMEM] * len(op...  12.2 us
    all_to_all x1, starting transfers between devices, exchange(): lax.all_to_all(x, 'table', split_axis=0, concat_axis=0, tiled=True, axis_...  7.83 us
    ppermute x5, waiting for transfers between devices, swap(): lax.ppermute(x, 'dp', [(g, g ^ bit) for g in range(lax.axis_size('dp'))])  5.02 us
    ppermute x5, starting transfers between devices, swap(): lax.ppermute(x, 'dp', [(g, g ^ bit) for g in range(lax.axis_size('dp'))])  2.01 us
    all_to_all x1, waiting for transfers between devices, exchange(): lax.all_to_all(x, 'table', split_axis=0, concat_axis=0, tiled=True, axis_...  1.47 us
  transfers between devices with their start and end apart: 6, of which 5 were waited for; matrix products, arithmetic and copies ran while one was open for 0% of the time, Pallas kernels for 10%

profile of v15, /device:TPU:0, one launch (start us, length us, event | category | flops | bytes accessed | tf_op | source)
XLA Modules:
  0.0 50.6 jit_solution(5410829901626829154)
XLA Ops:
  0.7 1.2 %shard_map.104 = s32[8,32]{1,0:T(8,128)} custom-call(s32[8,32]{1,0:T(8,128)} %bitcast.22), custom_call_target="tpu_custom_call" | custom-call | tf_op jit(solution)/shard_map/pallas_call | solution.py:24
  1.9 7.8 %all-to-all-start = ((s32[8,1,32]{2,1,0:T(1,128)}), s32[8,1,32]{2,1,0:T(1,128)S(1)}, u32[]{:S(2)}, u32[]{:S(2)}) async-start(s32[8,1,32]{2,1,0:T(1,128)} %bitcast.4), calls=%async_computation | async-start | bytes 8192 | tf_op jit(solution)/shard_map/all_to_all | solution.py:301
  9.7 2.6 %shard_map.105 = (s32[192,256]{1,0:T(8,128)S(1)}, s32[32,256]{1,0:T(8,128)S(1)}, s32[32,256]{1,0:T(8,128)S(1)}, bf16[64,256]{1,0:T(8,128)(2,1)S(1)}, bf16[1024,256]{1,0:T(8,128)(2,1)S(1)}) custom-call(s32[1,8]{1,0:T(1,128)} %count_ref.1, s32[32,512]{1,0:T(8,128)} %bitcast.21, s32[1,64]{1,0:T(1,128)} %bitcast.15, f32[1024,256]{1,0:T(8,128)} %table_ref.3), custom_call_target="tpu_custom_call" | custom-call | tf_op jit(solution)/shard_map/pallas_call | solution.py:24
  12.3 1.5 %all-to-all-done = s32[8,1,32]{2,1,0:T(1,128)S(1)} async-done(((s32[8,1,32]{2,1,0:T(1,128)}), s32[8,1,32]{2,1,0:T(1,128)S(1)}, u32[]{:S(2)}, u32[]{:S(2)}) %all-to-all-start) | async-done | bytes 1056 | tf_op jit(solution)/shard_map/all_to_all | solution.py:301
  13.8 0.4 shard_map.106
  14.2 9.6 %all_to_all.22.rows_ref.own_ref = bf16[8,64,256]{2,1,0:T(8,128)(2,1)S(1)} all-to-all(bf16[8,64,256]{2,1,0:T(8,128)(2,1)S(1)} %shard_map.106), channel_id=1, replica_groups={{4,1,6,3,0,5,2,7},{12,9,14,11,8,13,10,15},{20,17,22,19,16,21,18,23},{28..., dimensions={0} | all-to-all | bytes 524288 | tf_op jit(solution)/shard_map/all_to_all | solution.py:301
  23.8 0.1 collective-permute-start
  23.9 1.1 %shard_map.108.inc_ref = bf16[512,768]{1,0:T(8,128)(2,1)S(1)} custom-call(s32[192,256]{1,0:T(8,128)S(1)} %get-tuple-element.24.packed_ref, s32[32,256]{1,0:T(8,128)S(1)} %get-tuple-element.25.key_ref, s32[32,256]{1,0:T(8,128)S(1)} %get-tuple-element.26.unit_ref), custom_call_target="tpu_custom_call" | custom-call | tf_op jit(solution)/shard_map/pallas_call | solution.py:24
  25.0 0.2 collective-permute-done.mate_ref
  25.2 3.6 %shard_map.109 = (bf16[512,256]{1,0:T(8,128)(2,1)S(1)}, bf16[256,256]{1,0:T(8,128)(2,1)S(1)}) custom-call(f32[4,128]{1,0:T(4,128)S(1)} %bitcast.19, bf16[512,768]{1,0:T(8,128)(2,1)S(1)} %shard_map.108.inc_ref, bf16[8,64,256]{2,1,0:T(8,128)(2,1)S(1)} %all_to_all.22.rows_ref.own_ref, bf16[8,32,256]{2,1,0:T(8,128)(2,1)S(1)} %collective-permute-done.mate_ref, ...), custom_call_target="tpu_custom_call" | custom-call | tf_op jit(solution)/shard_map/pallas_call | solution.py:24
  28.8 0.0 copy-start.3
  28.8 0.0 copy-start
  28.9 0.0 copy-start.4
  28.9 0.4 collective-permute-start.1
  29.2 0.3 shard_map.110
  29.6 0.7 %collective-permute-done.1.got_ref = bf16[8,32,256]{2,1,0:T(8,128)(2,1)S(1)} collective-permute-done((bf16[8,32,256]{2,1,0:T(8,128)(2,1)S(1)}, bf16[8,32,256]{2,1,0:T(8,128)(2,1)S(1)}, u32[]{:S(2)}, u32[]{:S(2)}) %collective-permute-start.1) | collective-permute-done | bytes 131104 | tf_op jit(solution)/shard_map/ppermute | solution.py:305
  30.3 11.7 %all_to_all.23.back_ref = bf16[8,64,256]{2,1,0:T(8,128)(2,1)S(1)} all-to-all(bf16[8,64,256]{2,1,0:T(8,128)(2,1)S(1)} %shard_map.111), channel_id=1, replica_groups={{4,1,6,3,0,5,2,7},{12,9,14,11,8,13,10,15},{20,17,22,19,16,21,18,23},{28..., dimensions={0} | all-to-all | bytes 524288 | tf_op jit(solution)/shard_map/all_to_all | solution.py:301
  42.0 0.1 shard_map.112.refs_0_
  42.1 1.6 %collective-permute-start.2 = (bf16[304,256]{1,0:T(8,128)(2,1)S(1)}, bf16[304,256]{1,0:T(8,128)(2,1)S(1)}, u32[]{:S(2)}, u32[]{:S(2)}) collective-permute-start(bf16[304,256]{1,0:T(8,128)(2,1)S(1)} %shard_map.112.refs_0_), channel_id=1, source_target_pairs={{0,16},{8,24},{16,0},{24,8},{1,17},{9,25},{17,1},{25,9},{2,18},{10... | collective-permute-start | bytes 466952 | tf_op jit(solution)/shard_map/ppermute | solution.py:305
  43.6 3.7 %collective-permute-done.2.refs_1_ = bf16[304,256]{1,0:T(8,128)(2,1)S(1)} collective-permute-done((bf16[304,256]{1,0:T(8,128)(2,1)S(1)}, bf16[304,256]{1,0:T(8,128)(2,1)S(1)}, u32[]{:S(2)}, u32[]{:S(2)}) %collective-permute-start.2) | collective-permute-done | bytes 155680 | tf_op jit(solution)/shard_map/ppermute | solution.py:305
  47.3 0.0 collective-permute-start.4
  47.4 1.0 %shard_map.113 = (f32[1024,256]{1,0:T(8,128)S(1)}, f32[1024,256]{1,0:T(8,128)S(1)}) custom-call(s32[1,64]{1,0:T(1,128)S(1)} %bitcast.16, bf16[304,256]{1,0:T(8,128)(2,1)S(1)} %shard_map.112.refs_0_, bf16[304,256]{1,0:T(8,128)(2,1)S(1)} %collective-permute-done.2.refs_1_, bf16[304,256]{1,0:T(8,128)(2,1)S(1)} %collective-permute-done.3.refs_2_), custom_call_target="tpu_custom_call" | custom-call | tf_op jit(solution)/shard_map/pallas_call | solution.py:24
  48.4 0.4 collective-permute-done.4.part_ref
  48.7 1.9 %shard_map.114 = (f32[1024,256]{1,0:T(8,128)}, f32[8,128]{1,0:T(8,128)}) custom-call(s32[1,64]{1,0:T(1,128)S(1)} %bitcast.17, f32[8,128]{1,0:T(8,128)S(1)} %bitcast.18, f32[1024,256]{1,0:T(8,128)S(1)} %copy-done, f32[1024,256]{1,0:T(8,128)S(1)} %get-tuple-element.32.near_ref, f32[1024,256]{1,0:T(8,128)S(1)} %get-tuple-element.33.far_ref, ...), custom_call_target="tpu_custom_call" | custom-call | tf_op jit(solution)/shard_map/pallas_call | solution.py:24
  (13 shorter events, 0.1 us)
Async XLA Ops:
  0.6 24.6 %copy-start.2 = (bf16[4096]{0:T(1024)(128)(2,1)S(1)}, bf16[4096]{0:T(1024)(128)(2,1)}, u32[]{:S(2)}) copy-start(bf16[4096]{0:T(1024)(128)(2,1)} %param.17) | copy-start | bytes 24580
  0.6 24.6 %copy-start.1 = (bf16[256,4096]{1,0:T(8,128)(2,1)S(1)}, bf16[256,4096]{1,0:T(8,128)(2,1)}, u32[]{:S(2)}) copy-start(bf16[256,4096]{1,0:T(8,128)(2,1)} %w_in_ref.1) | copy-start | bytes 6291460
  0.7 24.6 %copy-start.5 = (f32[512]{0:T(512)S(1)}, f32[512]{0:T(512)}, u32[]{:S(2)}) copy-start(f32[512]{0:T(512)} %param.10) | copy-start | bytes 6148
  1.9 11.9 %all-to-all-start = ((s32[8,1,32]{2,1,0:T(1,128)}), s32[8,1,32]{2,1,0:T(1,128)S(1)}, u32[]{:S(2)}, u32[]{:S(2)}) async-start(s32[8,1,32]{2,1,0:T(1,128)} %bitcast.4), calls=%async_computation | async-start | bytes 8192 | tf_op jit(solution)/shard_map/all_to_all | solution.py:301
  23.8 1.4 %collective-permute-start = (bf16[8,32,256]{2,1,0:T(8,128)(2,1)S(1)}, bf16[8,32,256]{2,1,0:T(8,128)(2,1)S(1)}, u32[]{:S(2)}, u32[]{:S(2)}) collective-permute-start(bf16[8,32,256]{2,1,0:T(8,128)(2,1)S(1)} %shard_map.107), channel_id=1, source_target_pairs={{0,8},{8,0},{16,24},{24,16},{1,9},{9,1},{17,25},{25,17},{2,10},{10... | collective-permute-start | bytes 393224 | tf_op jit(solution)/shard_map/ppermute | solution.py:305
  28.8 18.5 %copy-start.3 = (s32[64]{0:T(128)S(1)}, s32[64]{0:T(128)}, u32[]{:S(2)}) copy-start(s32[64]{0:T(128)} %param.15) | copy-start | bytes 772
  28.8 19.9 %copy-start = (f32[1024,256]{1,0:T(8,128)S(1)}, f32[1024,256]{1,0:T(8,128)}, u32[]{:S(2)}) copy-start(f32[1024,256]{1,0:T(8,128)} %table_ref.3) | copy-start | bytes 3145732
  28.9 19.9 %copy-start.4 = (f32[1024]{0:T(1024)S(1)}, f32[1024]{0:T(1024)}, u32[]{:S(2)}) copy-start(f32[1024]{0:T(1024)} %param.14) | copy-start | bytes 12292
  28.9 1.4 %collective-permute-start.1 = (bf16[8,32,256]{2,1,0:T(8,128)(2,1)S(1)}, bf16[8,32,256]{2,1,0:T(8,128)(2,1)S(1)}, u32[]{:S(2)}, u32[]{:S(2)}) collective-permute-start(bf16[8,32,256]{2,1,0:T(8,128)(2,1)S(1)} %bitcast.20), channel_id=1, source_target_pairs={{0,8},{8,0},{16,24},{24,16},{1,9},{9,1},{17,25},{25,17},{2,10},{10... | collective-permute-start | bytes 393224 | tf_op jit(solution)/shard_map/ppermute | solution.py:305
  42.1 5.3 %collective-permute-start.2 = (bf16[304,256]{1,0:T(8,128)(2,1)S(1)}, bf16[304,256]{1,0:T(8,128)(2,1)S(1)}, u32[]{:S(2)}, u32[]{:S(2)}) collective-permute-start(bf16[304,256]{1,0:T(8,128)(2,1)S(1)} %shard_map.112.refs_0_), channel_id=1, source_target_pairs={{0,16},{8,24},{16,0},{24,8},{1,17},{9,25},{17,1},{25,9},{2,18},{10... | collective-permute-start | bytes 466952 | tf_op jit(solution)/shard_map/ppermute | solution.py:305
  43.6 3.7 %collective-permute-start.3 = (bf16[304,256]{1,0:T(8,128)(2,1)S(1)}, bf16[304,256]{1,0:T(8,128)(2,1)S(1)}, u32[]{:S(2)}, u32[]{:S(2)}) collective-permute-start(bf16[304,256]{1,0:T(8,128)(2,1)S(1)} %shard_map.112.refs_0_), channel_id=1, source_target_pairs={{0,8},{8,0},{16,24},{24,16},{1,9},{9,1},{17,25},{25,17},{2,10},{10... | collective-permute-start | bytes 466952 | tf_op jit(solution)/shard_map/ppermute | solution.py:305
  47.3 1.4 %collective-permute-start.4 = (bf16[304,256]{1,0:T(8,128)(2,1)S(1)}, bf16[304,256]{1,0:T(8,128)(2,1)S(1)}, u32[]{:S(2)}, u32[]{:S(2)}) collective-permute-start(bf16[304,256]{1,0:T(8,128)(2,1)S(1)} %collective-permute-done.2.refs_1_), channel_id=1, source_target_pairs={{0,8},{8,0},{16,24},{24,16},{1,9},{9,1},{17,25},{25,17},{2,10},{10... | collective-permute-start | bytes 466952 | tf_op jit(solution)/shard_map/ppermute | solution.py:305

commit v16 on v15

--- a/solution.py
+++ b/solution.py
@@ -267,19 +267,21 @@
         squares[at.start // step:at.stop // step, :] = jnp.sum(square, axis=0, keepdims=True)
 
     row_grads(1 - core(), hot_ref, [part_ref], put, rows)
-    new_sum = sum_ref[...] + squares[...] * (1.0 / width)
-    sums[...] = new_sum
-    scale = (learning_rate / jnp.sqrt(new_sum)).T
-    for start in range(0, rows, step):
-        at = slice(start, start + step)
-        k = start // step
-        staged[at, :] = table_ref[at, :] - grads[at, :] * scale[:, k:k + 1]
-    copies = [
-        pltpu.make_async_copy(staged, new_table_ref, sems.at[0]),
-        pltpu.make_async_copy(sums, new_sum_ref, sems.at[1]),
-    ]
-    for copy in copies:
-        copy.start()
+    lines = rows // 128 // 2
+    copies = []
+    for h in range(2):
+        own = slice(h * lines, (h + 1) * lines)
+        new_sum = sum_ref[own, :] + squares[own, :] * (1.0 / width)
+        sums[own, :] = new_sum
+        scale = (learning_rate / jnp.sqrt(new_sum)).T
+        for k in range(lines):
+            at = slice((h * lines + k) * step, (h * lines + k + 1) * step)
+            staged[at, :] = table_ref[at, :] - grads[at, :] * scale[:, k:k + 1]
+        done = slice(h * lines * step, (h + 1) * lines * step)
+        copies.append(pltpu.make_async_copy(staged.at[done], new_table_ref.at[done], sems.at[h]))
+        copies[-1].start()
+    copies.append(pltpu.make_async_copy(sums, new_sum_ref, sems.at[2]))
+    copies[-1].start()
     for copy in copies:
         copy.wait()
 
@@ -404,7 +406,7 @@
                 pltpu.VMEM((rows, width), f32),
                 pltpu.VMEM((rows, width), f32),
                 pltpu.VMEM((rows // 128, 128), f32),
-                pltpu.SemaphoreType.DMA((2,)),
+                pltpu.SemaphoreType.DMA((3,)),
             ],
             out_specs=(HBM, HBM),
         )

time: 50.8 us -> 50.8 us (level)
  no operation moved by 1% of the time
where the time goes in v16:
time: 50.8 us; the launch traced here: 50.5 us
  blocking collectives  21.3 us (42%)
  Pallas kernels  12.2 us (24%)
  starting transfers between devices  9.83 us (19%)
  waiting for transfers between devices  6.48 us (13%)
  between operations  0.76 us (1%)
    all_to_all x2, blocking collectives, exchange(): lax.all_to_all(x, 'table', split_axis=0, concat_axis=0, tiled=True, axis_...  21.3 us
    pallas_call x11, Pallas kernels, call(): pl.pallas_call(body, out_shape=outs, in_specs=in_specs or [VMEM] * len(op...  12.2 us
    all_to_all x1, starting transfers between devices, exchange(): lax.all_to_all(x, 'table', split_axis=0, concat_axis=0, tiled=True, axis_...  7.83 us
    ppermute x5, waiting for transfers between devices, swap(): lax.ppermute(x, 'dp', [(g, g ^ bit) for g in range(lax.axis_size('dp'))])  5.02 us
    ppermute x5, starting transfers between devices, swap(): lax.ppermute(x, 'dp', [(g, g ^ bit) for g in range(lax.axis_size('dp'))])  2.01 us
    all_to_all x1, waiting for transfers between devices, exchange(): lax.all_to_all(x, 'table', split_axis=0, concat_axis=0, tiled=True, axis_...  1.47 us
  transfers between devices with their start and end apart: 6, of which 5 were waited for; matrix products, arithmetic and copies ran while one was open for 0% of the time, Pallas kernels for 10%

profile of v16, /device:TPU:0, one launch (start us, length us, event | category | flops | bytes accessed | tf_op | source)
XLA Modules:
  0.0 50.5 jit_solution(8965883242166967665)
XLA Ops:
  0.7 1.2 %shard_map.104 = s32[8,32]{1,0:T(8,128)} custom-call(s32[8,32]{1,0:T(8,128)} %bitcast.22), custom_call_target="tpu_custom_call" | custom-call | tf_op jit(solution)/shard_map/pallas_call | solution.py:24
  1.9 7.8 %all-to-all-start = ((s32[8,1,32]{2,1,0:T(1,128)}), s32[8,1,32]{2,1,0:T(1,128)S(1)}, u32[]{:S(2)}, u32[]{:S(2)}) async-start(s32[8,1,32]{2,1,0:T(1,128)} %bitcast.4), calls=%async_computation | async-start | bytes 8192 | tf_op jit(solution)/shard_map/all_to_all | solution.py:303
  9.7 2.6 %shard_map.105 = (s32[192,256]{1,0:T(8,128)S(1)}, s32[32,256]{1,0:T(8,128)S(1)}, s32[32,256]{1,0:T(8,128)S(1)}, bf16[64,256]{1,0:T(8,128)(2,1)S(1)}, bf16[1024,256]{1,0:T(8,128)(2,1)S(1)}) custom-call(s32[1,8]{1,0:T(1,128)} %count_ref.1, s32[32,512]{1,0:T(8,128)} %bitcast.21, s32[1,64]{1,0:T(1,128)} %bitcast.15, f32[1024,256]{1,0:T(8,128)} %table_ref.3), custom_call_target="tpu_custom_call" | custom-call | tf_op jit(solution)/shard_map/pallas_call | solution.py:24
  12.3 1.5 %all-to-all-done = s32[8,1,32]{2,1,0:T(1,128)S(1)} async-done(((s32[8,1,32]{2,1,0:T(1,128)}), s32[8,1,32]{2,1,0:T(1,128)S(1)}, u32[]{:S(2)}, u32[]{:S(2)}) %all-to-all-start) | async-done | bytes 1056 | tf_op jit(solution)/shard_map/all_to_all | solution.py:303
  13.8 0.4 shard_map.106
  14.2 9.6 %all_to_all.22.rows_ref.own_ref = bf16[8,64,256]{2,1,0:T(8,128)(2,1)S(1)} all-to-all(bf16[8,64,256]{2,1,0:T(8,128)(2,1)S(1)} %shard_map.106), channel_id=1, replica_groups={{4,1,6,3,0,5,2,7},{12,9,14,11,8,13,10,15},{20,17,22,19,16,21,18,23},{28..., dimensions={0} | all-to-all | bytes 524288 | tf_op jit(solution)/shard_map/all_to_all | solution.py:303
  23.8 0.1 collective-permute-start
  23.9 1.1 %shard_map.108.inc_ref = bf16[512,768]{1,0:T(8,128)(2,1)S(1)} custom-call(s32[192,256]{1,0:T(8,128)S(1)} %get-tuple-element.24.packed_ref, s32[32,256]{1,0:T(8,128)S(1)} %get-tuple-element.25.key_ref, s32[32,256]{1,0:T(8,128)S(1)} %get-tuple-element.26.unit_ref), custom_call_target="tpu_custom_call" | custom-call | tf_op jit(solution)/shard_map/pallas_call | solution.py:24
  25.0 0.2 collective-permute-done.mate_ref
  25.2 3.6 %shard_map.109 = (bf16[512,256]{1,0:T(8,128)(2,1)S(1)}, bf16[256,256]{1,0:T(8,128)(2,1)S(1)}) custom-call(f32[4,128]{1,0:T(4,128)S(1)} %bitcast.19, bf16[512,768]{1,0:T(8,128)(2,1)S(1)} %shard_map.108.inc_ref, bf16[8,64,256]{2,1,0:T(8,128)(2,1)S(1)} %all_to_all.22.rows_ref.own_ref, bf16[8,32,256]{2,1,0:T(8,128)(2,1)S(1)} %collective-permute-done.mate_ref, ...), custom_call_target="tpu_custom_call" | custom-call | tf_op jit(solution)/shard_map/pallas_call | solution.py:24
  28.8 0.0 copy-start.3
  28.8 0.0 copy-start
  28.9 0.0 copy-start.4
  28.9 0.4 collective-permute-start.1
  29.2 0.3 shard_map.110
  29.6 0.7 %collective-permute-done.1.got_ref = bf16[8,32,256]{2,1,0:T(8,128)(2,1)S(1)} collective-permute-done((bf16[8,32,256]{2,1,0:T(8,128)(2,1)S(1)}, bf16[8,32,256]{2,1,0:T(8,128)(2,1)S(1)}, u32[]{:S(2)}, u32[]{:S(2)}) %collective-permute-start.1) | collective-permute-done | bytes 131104 | tf_op jit(solution)/shard_map/ppermute | solution.py:307
  30.3 11.7 %all_to_all.23.back_ref = bf16[8,64,256]{2,1,0:T(8,128)(2,1)S(1)} all-to-all(bf16[8,64,256]{2,1,0:T(8,128)(2,1)S(1)} %shard_map.111), channel_id=1, replica_groups={{4,1,6,3,0,5,2,7},{12,9,14,11,8,13,10,15},{20,17,22,19,16,21,18,23},{28..., dimensions={0} | all-to-all | bytes 524288 | tf_op jit(solution)/shard_map/all_to_all | solution.py:303
  42.0 0.1 shard_map.112.refs_0_
  42.1 1.6 %collective-permute-start.2 = (bf16[304,256]{1,0:T(8,128)(2,1)S(1)}, bf16[304,256]{1,0:T(8,128)(2,1)S(1)}, u32[]{:S(2)}, u32[]{:S(2)}) collective-permute-start(bf16[304,256]{1,0:T(8,128)(2,1)S(1)} %shard_map.112.refs_0_), channel_id=1, source_target_pairs={{0,16},{8,24},{16,0},{24,8},{1,17},{9,25},{17,1},{25,9},{2,18},{10... | collective-permute-start | bytes 466952 | tf_op jit(solution)/shard_map/ppermute | solution.py:307
  43.6 3.7 %collective-permute-done.2.refs_1_ = bf16[304,256]{1,0:T(8,128)(2,1)S(1)} collective-permute-done((bf16[304,256]{1,0:T(8,128)(2,1)S(1)}, bf16[304,256]{1,0:T(8,128)(2,1)S(1)}, u32[]{:S(2)}, u32[]{:S(2)}) %collective-permute-start.2) | collective-permute-done | bytes 155680 | tf_op jit(solution)/shard_map/ppermute | solution.py:307
  47.3 0.0 collective-permute-start.4
  47.4 1.0 %shard_map.113 = (f32[1024,256]{1,0:T(8,128)S(1)}, f32[1024,256]{1,0:T(8,128)S(1)}) custom-call(s32[1,64]{1,0:T(1,128)S(1)} %bitcast.16, bf16[304,256]{1,0:T(8,128)(2,1)S(1)} %shard_map.112.refs_0_, bf16[304,256]{1,0:T(8,128)(2,1)S(1)} %collective-permute-done.2.refs_1_, bf16[304,256]{1,0:T(8,128)(2,1)S(1)} %collective-permute-done.3.refs_2_), custom_call_target="tpu_custom_call" | custom-call | tf_op jit(solution)/shard_map/pallas_call | solution.py:24
  48.4 0.4 collective-permute-done.4.part_ref
  48.7 1.8 %shard_map.114 = (f32[1024,256]{1,0:T(8,128)}, f32[8,128]{1,0:T(8,128)}) custom-call(s32[1,64]{1,0:T(1,128)S(1)} %bitcast.17, f32[8,128]{1,0:T(8,128)S(1)} %bitcast.18, f32[1024,256]{1,0:T(8,128)S(1)} %copy-done, f32[1024,256]{1,0:T(8,128)S(1)} %get-tuple-element.32.near_ref, f32[1024,256]{1,0:T(8,128)S(1)} %get-tuple-element.33.far_ref, ...), custom_call_target="tpu_custom_call" | custom-call | tf_op jit(solution)/shard_map/pallas_call | solution.py:24
  (13 shorter events, 0.1 us)
Async XLA Ops:
  0.6 24.6 %copy-start.2 = (bf16[4096]{0:T(1024)(128)(2,1)S(1)}, bf16[4096]{0:T(1024)(128)(2,1)}, u32[]{:S(2)}) copy-start(bf16[4096]{0:T(1024)(128)(2,1)} %param.17) | copy-start | bytes 24580
  0.6 24.6 %copy-start.1 = (bf16[256,4096]{1,0:T(8,128)(2,1)S(1)}, bf16[256,4096]{1,0:T(8,128)(2,1)}, u32[]{:S(2)}) copy-start(bf16[256,4096]{1,0:T(8,128)(2,1)} %w_in_ref.1) | copy-start | bytes 6291460
  0.7 24.6 %copy-start.5 = (f32[512]{0:T(512)S(1)}, f32[512]{0:T(512)}, u32[]{:S(2)}) copy-start(f32[512]{0:T(512)} %param.10) | copy-start | bytes 6148
  1.9 11.9 %all-to-all-start = ((s32[8,1,32]{2,1,0:T(1,128)}), s32[8,1,32]{2,1,0:T(1,128)S(1)}, u32[]{:S(2)}, u32[]{:S(2)}) async-start(s32[8,1,32]{2,1,0:T(1,128)} %bitcast.4), calls=%async_computation | async-start | bytes 8192 | tf_op jit(solution)/shard_map/all_to_all | solution.py:303
  23.8 1.4 %collective-permute-start = (bf16[8,32,256]{2,1,0:T(8,128)(2,1)S(1)}, bf16[8,32,256]{2,1,0:T(8,128)(2,1)S(1)}, u32[]{:S(2)}, u32[]{:S(2)}) collective-permute-start(bf16[8,32,256]{2,1,0:T(8,128)(2,1)S(1)} %shard_map.107), channel_id=1, source_target_pairs={{0,8},{8,0},{16,24},{24,16},{1,9},{9,1},{17,25},{25,17},{2,10},{10... | collective-permute-start | bytes 393224 | tf_op jit(solution)/shard_map/ppermute | solution.py:307
  28.8 18.5 %copy-start.3 = (s32[64]{0:T(128)S(1)}, s32[64]{0:T(128)}, u32[]{:S(2)}) copy-start(s32[64]{0:T(128)} %param.15) | copy-start | bytes 772
  28.8 19.9 %copy-start = (f32[1024,256]{1,0:T(8,128)S(1)}, f32[1024,256]{1,0:T(8,128)}, u32[]{:S(2)}) copy-start(f32[1024,256]{1,0:T(8,128)} %table_ref.3) | copy-start | bytes 3145732
  28.9 19.9 %copy-start.4 = (f32[1024]{0:T(1024)S(1)}, f32[1024]{0:T(1024)}, u32[]{:S(2)}) copy-start(f32[1024]{0:T(1024)} %param.14) | copy-start | bytes 12292
  28.9 1.4 %collective-permute-start.1 = (bf16[8,32,256]{2,1,0:T(8,128)(2,1)S(1)}, bf16[8,32,256]{2,1,0:T(8,128)(2,1)S(1)}, u32[]{:S(2)}, u32[]{:S(2)}) collective-permute-start(bf16[8,32,256]{2,1,0:T(8,128)(2,1)S(1)} %bitcast.20), channel_id=1, source_target_pairs={{0,8},{8,0},{16,24},{24,16},{1,9},{9,1},{17,25},{25,17},{2,10},{10... | collective-permute-start | bytes 393224 | tf_op jit(solution)/shard_map/ppermute | solution.py:307
  42.1 5.3 %collective-permute-start.2 = (bf16[304,256]{1,0:T(8,128)(2,1)S(1)}, bf16[304,256]{1,0:T(8,128)(2,1)S(1)}, u32[]{:S(2)}, u32[]{:S(2)}) collective-permute-start(bf16[304,256]{1,0:T(8,128)(2,1)S(1)} %shard_map.112.refs_0_), channel_id=1, source_target_pairs={{0,16},{8,24},{16,0},{24,8},{1,17},{9,25},{17,1},{25,9},{2,18},{10... | collective-permute-start | bytes 466952 | tf_op jit(solution)/shard_map/ppermute | solution.py:307
  43.6 3.7 %collective-permute-start.3 = (bf16[304,256]{1,0:T(8,128)(2,1)S(1)}, bf16[304,256]{1,0:T(8,128)(2,1)S(1)}, u32[]{:S(2)}, u32[]{:S(2)}) collective-permute-start(bf16[304,256]{1,0:T(8,128)(2,1)S(1)} %shard_map.112.refs_0_), channel_id=1, source_target_pairs={{0,8},{8,0},{16,24},{24,16},{1,9},{9,1},{17,25},{25,17},{2,10},{10... | collective-permute-start | bytes 466952 | tf_op jit(solution)/shard_map/ppermute | solution.py:307
  47.3 1.4 %collective-permute-start.4 = (bf16[304,256]{1,0:T(8,128)(2,1)S(1)}, bf16[304,256]{1,0:T(8,128)(2,1)S(1)}, u32[]{:S(2)}, u32[]{:S(2)}) collective-permute-start(bf16[304,256]{1,0:T(8,128)(2,1)S(1)} %collective-permute-done.2.refs_1_), channel_id=1, source_target_pairs={{0,8},{8,0},{16,24},{24,16},{1,9},{9,1},{17,25},{25,17},{2,10},{10... | collective-permute-start | bytes 466952 | tf_op jit(solution)/shard_map/ppermute | solution.py:307

commit v17 on v16

--- a/solution.py
+++ b/solution.py
@@ -144,7 +144,7 @@
     owners, half, _ = mate_ref.shape
     hot_half = owners * half
     slot_cap = own_ref.shape[1] - half
-    size, step, wide = batch // 2, 512, 512
+    size, step, wide = batch // 2, 256, 256
     blocks = [slice(at, at + size) for at in range(0, batch, size)]
     for k, t in enumerate(order):
         rows[t * half:(t + 1) * half, :] = own_ref[k, 0:half, :]

time: 50.8 us -> 50.8 us (level)
  no operation moved by 1% of the time
where the time goes in v17:
time: 50.8 us; the launch traced here: 50.5 us
  blocking collectives  21.3 us (42%)
  Pallas kernels  12.2 us (24%)
  starting transfers between devices  9.83 us (19%)
  waiting for transfers between devices  6.48 us (13%)
  between operations  0.76 us (1%)
    all_to_all x2, blocking collectives, exchange(): lax.all_to_all(x, 'table', split_axis=0, concat_axis=0, tiled=True, axis_...  21.3 us
    pallas_call x11, Pallas kernels, call(): pl.pallas_call(body, out_shape=outs, in_specs=in_specs or [VMEM] * len(op...  12.2 us
    all_to_all x1, starting transfers between devices, exchange(): lax.all_to_all(x, 'table', split_axis=0, concat_axis=0, tiled=True, axis_...  7.83 us
    ppermute x5, waiting for transfers between devices, swap(): lax.ppermute(x, 'dp', [(g, g ^ bit) for g in range(lax.axis_size('dp'))])  5.01 us
    ppermute x5, starting transfers between devices, swap(): lax.ppermute(x, 'dp', [(g, g ^ bit) for g in range(lax.axis_size('dp'))])  2.01 us
    all_to_all x1, waiting for transfers between devices, exchange(): lax.all_to_all(x, 'table', split_axis=0, concat_axis=0, tiled=True, axis_...  1.47 us
  transfers between devices with their start and end apart: 6, of which 5 were waited for; matrix products, arithmetic and copies ran while one was open for 0% of the time, Pallas kernels for 10%

profile of v17, /device:TPU:0, one launch (start us, length us, event | category | flops | bytes accessed | tf_op | source)
XLA Modules:
  0.0 50.5 jit_solution(10314744192601169551)
XLA Ops:
  0.7 1.2 %shard_map.104 = s32[8,32]{1,0:T(8,128)} custom-call(s32[8,32]{1,0:T(8,128)} %bitcast.22), custom_call_target="tpu_custom_call" | custom-call | tf_op jit(solution)/shard_map/pallas_call | solution.py:24
  1.9 7.8 %all-to-all-start = ((s32[8,1,32]{2,1,0:T(1,128)}), s32[8,1,32]{2,1,0:T(1,128)S(1)}, u32[]{:S(2)}, u32[]{:S(2)}) async-start(s32[8,1,32]{2,1,0:T(1,128)} %bitcast.4), calls=%async_computation | async-start | bytes 8192 | tf_op jit(solution)/shard_map/all_to_all | solution.py:303
  9.7 2.6 %shard_map.105 = (s32[192,256]{1,0:T(8,128)S(1)}, s32[32,256]{1,0:T(8,128)S(1)}, s32[32,256]{1,0:T(8,128)S(1)}, bf16[64,256]{1,0:T(8,128)(2,1)S(1)}, bf16[1024,256]{1,0:T(8,128)(2,1)S(1)}) custom-call(s32[1,8]{1,0:T(1,128)} %count_ref.1, s32[32,512]{1,0:T(8,128)} %bitcast.21, s32[1,64]{1,0:T(1,128)} %bitcast.15, f32[1024,256]{1,0:T(8,128)} %table_ref.3), custom_call_target="tpu_custom_call" | custom-call | tf_op jit(solution)/shard_map/pallas_call | solution.py:24
  12.3 1.5 %all-to-all-done = s32[8,1,32]{2,1,0:T(1,128)S(1)} async-done(((s32[8,1,32]{2,1,0:T(1,128)}), s32[8,1,32]{2,1,0:T(1,128)S(1)}, u32[]{:S(2)}, u32[]{:S(2)}) %all-to-all-start) | async-done | bytes 1056 | tf_op jit(solution)/shard_map/all_to_all | solution.py:303
  13.8 0.4 shard_map.106
  14.2 9.6 %all_to_all.22.rows_ref.own_ref = bf16[8,64,256]{2,1,0:T(8,128)(2,1)S(1)} all-to-all(bf16[8,64,256]{2,1,0:T(8,128)(2,1)S(1)} %shard_map.106), channel_id=1, replica_groups={{4,1,6,3,0,5,2,7},{12,9,14,11,8,13,10,15},{20,17,22,19,16,21,18,23},{28..., dimensions={0} | all-to-all | bytes 524288 | tf_op jit(solution)/shard_map/all_to_all | solution.py:303
  23.8 0.1 collective-permute-start
  23.9 1.1 %shard_map.108.inc_ref = bf16[512,768]{1,0:T(8,128)(2,1)S(1)} custom-call(s32[192,256]{1,0:T(8,128)S(1)} %get-tuple-element.24.packed_ref, s32[32,256]{1,0:T(8,128)S(1)} %get-tuple-element.25.key_ref, s32[32,256]{1,0:T(8,128)S(1)} %get-tuple-element.26.unit_ref), custom_call_target="tpu_custom_call" | custom-call | tf_op jit(solution)/shard_map/pallas_call | solution.py:24
  25.0 0.2 collective-permute-done.mate_ref
  25.2 3.6 %shard_map.109 = (bf16[512,256]{1,0:T(8,128)(2,1)S(1)}, bf16[256,256]{1,0:T(8,128)(2,1)S(1)}) custom-call(f32[4,128]{1,0:T(4,128)S(1)} %bitcast.19, bf16[512,768]{1,0:T(8,128)(2,1)S(1)} %shard_map.108.inc_ref, bf16[8,64,256]{2,1,0:T(8,128)(2,1)S(1)} %all_to_all.22.rows_ref.own_ref, bf16[8,32,256]{2,1,0:T(8,128)(2,1)S(1)} %collective-permute-done.mate_ref, ...), custom_call_target="tpu_custom_call" | custom-call | tf_op jit(solution)/shard_map/pallas_call | solution.py:24
  28.8 0.0 copy-start.3
  28.8 0.0 copy-start
  28.9 0.0 copy-start.4
  28.9 0.4 collective-permute-start.1
  29.2 0.3 shard_map.110
  29.6 0.7 %collective-permute-done.1.got_ref = bf16[8,32,256]{2,1,0:T(8,128)(2,1)S(1)} collective-permute-done((bf16[8,32,256]{2,1,0:T(8,128)(2,1)S(1)}, bf16[8,32,256]{2,1,0:T(8,128)(2,1)S(1)}, u32[]{:S(2)}, u32[]{:S(2)}) %collective-permute-start.1) | collective-permute-done | bytes 131104 | tf_op jit(solution)/shard_map/ppermute | solution.py:307
  30.3 11.7 %all_to_all.23.back_ref = bf16[8,64,256]{2,1,0:T(8,128)(2,1)S(1)} all-to-all(bf16[8,64,256]{2,1,0:T(8,128)(2,1)S(1)} %shard_map.111), channel_id=1, replica_groups={{4,1,6,3,0,5,2,7},{12,9,14,11,8,13,10,15},{20,17,22,19,16,21,18,23},{28..., dimensions={0} | all-to-all | bytes 524288 | tf_op jit(solution)/shard_map/all_to_all | solution.py:303
  42.0 0.1 shard_map.112.refs_0_
  42.1 1.6 %collective-permute-start.2 = (bf16[304,256]{1,0:T(8,128)(2,1)S(1)}, bf16[304,256]{1,0:T(8,128)(2,1)S(1)}, u32[]{:S(2)}, u32[]{:S(2)}) collective-permute-start(bf16[304,256]{1,0:T(8,128)(2,1)S(1)} %shard_map.112.refs_0_), channel_id=1, source_target_pairs={{0,16},{8,24},{16,0},{24,8},{1,17},{9,25},{17,1},{25,9},{2,18},{10... | collective-permute-start | bytes 466952 | tf_op jit(solution)/shard_map/ppermute | solution.py:307
  43.6 3.7 %collective-permute-done.2.refs_1_ = bf16[304,256]{1,0:T(8,128)(2,1)S(1)} collective-permute-done((bf16[304,256]{1,0:T(8,128)(2,1)S(1)}, bf16[304,256]{1,0:T(8,128)(2,1)S(1)}, u32[]{:S(2)}, u32[]{:S(2)}) %collective-permute-start.2) | collective-permute-done | bytes 155680 | tf_op jit(solution)/shard_map/ppermute | solution.py:307
  47.3 0.0 collective-permute-start.4
  47.3 1.0 %shard_map.113 = (f32[1024,256]{1,0:T(8,128)S(1)}, f32[1024,256]{1,0:T(8,128)S(1)}) custom-call(s32[1,64]{1,0:T(1,128)S(1)} %bitcast.16, bf16[304,256]{1,0:T(8,128)(2,1)S(1)} %shard_map.112.refs_0_, bf16[304,256]{1,0:T(8,128)(2,1)S(1)} %collective-permute-done.2.refs_1_, bf16[304,256]{1,0:T(8,128)(2,1)S(1)} %collective-permute-done.3.refs_2_), custom_call_target="tpu_custom_call" | custom-call | tf_op jit(solution)/shard_map/pallas_call | solution.py:24
  48.3 0.4 collective-permute-done.4.part_ref
  48.7 1.8 %shard_map.114 = (f32[1024,256]{1,0:T(8,128)}, f32[8,128]{1,0:T(8,128)}) custom-call(s32[1,64]{1,0:T(1,128)S(1)} %bitcast.17, f32[8,128]{1,0:T(8,128)S(1)} %bitcast.18, f32[1024,256]{1,0:T(8,128)S(1)} %copy-done, f32[1024,256]{1,0:T(8,128)S(1)} %get-tuple-element.32.near_ref, f32[1024,256]{1,0:T(8,128)S(1)} %get-tuple-element.33.far_ref, ...), custom_call_target="tpu_custom_call" | custom-call | tf_op jit(solution)/shard_map/pallas_call | solution.py:24
  (13 shorter events, 0.1 us)
Async XLA Ops:
  0.6 24.6 %copy-start.2 = (bf16[4096]{0:T(1024)(128)(2,1)S(1)}, bf16[4096]{0:T(1024)(128)(2,1)}, u32[]{:S(2)}) copy-start(bf16[4096]{0:T(1024)(128)(2,1)} %param.17) | copy-start | bytes 24580
  0.6 24.6 %copy-start.1 = (bf16[256,4096]{1,0:T(8,128)(2,1)S(1)}, bf16[256,4096]{1,0:T(8,128)(2,1)}, u32[]{:S(2)}) copy-start(bf16[256,4096]{1,0:T(8,128)(2,1)} %w_in_ref.1) | copy-start | bytes 6291460
  0.7 24.6 %copy-start.5 = (f32[512]{0:T(512)S(1)}, f32[512]{0:T(512)}, u32[]{:S(2)}) copy-start(f32[512]{0:T(512)} %param.10) | copy-start | bytes 6148
  1.9 11.9 %all-to-all-start = ((s32[8,1,32]{2,1,0:T(1,128)}), s32[8,1,32]{2,1,0:T(1,128)S(1)}, u32[]{:S(2)}, u32[]{:S(2)}) async-start(s32[8,1,32]{2,1,0:T(1,128)} %bitcast.4), calls=%async_computation | async-start | bytes 8192 | tf_op jit(solution)/shard_map/all_to_all | solution.py:303
  23.8 1.4 %collective-permute-start = (bf16[8,32,256]{2,1,0:T(8,128)(2,1)S(1)}, bf16[8,32,256]{2,1,0:T(8,128)(2,1)S(1)}, u32[]{:S(2)}, u32[]{:S(2)}) collective-permute-start(bf16[8,32,256]{2,1,0:T(8,128)(2,1)S(1)} %shard_map.107), channel_id=1, source_target_pairs={{0,8},{8,0},{16,24},{24,16},{1,9},{9,1},{17,25},{25,17},{2,10},{10... | collective-permute-start | bytes 393224 | tf_op jit(solution)/shard_map/ppermute | solution.py:307
  28.8 18.5 %copy-start.3 = (s32[64]{0:T(128)S(1)}, s32[64]{0:T(128)}, u32[]{:S(2)}) copy-start(s32[64]{0:T(128)} %param.15) | copy-start | bytes 772
  28.8 19.9 %copy-start = (f32[1024,256]{1,0:T(8,128)S(1)}, f32[1024,256]{1,0:T(8,128)}, u32[]{:S(2)}) copy-start(f32[1024,256]{1,0:T(8,128)} %table_ref.3) | copy-start | bytes 3145732
  28.9 19.9 %copy-start.4 = (f32[1024]{0:T(1024)S(1)}, f32[1024]{0:T(1024)}, u32[]{:S(2)}) copy-start(f32[1024]{0:T(1024)} %param.14) | copy-start | bytes 12292
  28.9 1.4 %collective-permute-start.1 = (bf16[8,32,256]{2,1,0:T(8,128)(2,1)S(1)}, bf16[8,32,256]{2,1,0:T(8,128)(2,1)S(1)}, u32[]{:S(2)}, u32[]{:S(2)}) collective-permute-start(bf16[8,32,256]{2,1,0:T(8,128)(2,1)S(1)} %bitcast.20), channel_id=1, source_target_pairs={{0,8},{8,0},{16,24},{24,16},{1,9},{9,1},{17,25},{25,17},{2,10},{10... | collective-permute-start | bytes 393224 | tf_op jit(solution)/shard_map/ppermute | solution.py:307
  42.1 5.3 %collective-permute-start.2 = (bf16[304,256]{1,0:T(8,128)(2,1)S(1)}, bf16[304,256]{1,0:T(8,128)(2,1)S(1)}, u32[]{:S(2)}, u32[]{:S(2)}) collective-permute-start(bf16[304,256]{1,0:T(8,128)(2,1)S(1)} %shard_map.112.refs_0_), channel_id=1, source_target_pairs={{0,16},{8,24},{16,0},{24,8},{1,17},{9,25},{17,1},{25,9},{2,18},{10... | collective-permute-start | bytes 466952 | tf_op jit(solution)/shard_map/ppermute | solution.py:307
  43.6 3.7 %collective-permute-start.3 = (bf16[304,256]{1,0:T(8,128)(2,1)S(1)}, bf16[304,256]{1,0:T(8,128)(2,1)S(1)}, u32[]{:S(2)}, u32[]{:S(2)}) collective-permute-start(bf16[304,256]{1,0:T(8,128)(2,1)S(1)} %shard_map.112.refs_0_), channel_id=1, source_target_pairs={{0,8},{8,0},{16,24},{24,16},{1,9},{9,1},{17,25},{25,17},{2,10},{10... | collective-permute-start | bytes 466952 | tf_op jit(solution)/shard_map/ppermute | solution.py:307
  47.3 1.4 %collective-permute-start.4 = (bf16[304,256]{1,0:T(8,128)(2,1)S(1)}, bf16[304,256]{1,0:T(8,128)(2,1)S(1)}, u32[]{:S(2)}, u32[]{:S(2)}) collective-permute-start(bf16[304,256]{1,0:T(8,128)(2,1)S(1)} %collective-permute-done.2.refs_1_), channel_id=1, source_target_pairs={{0,8},{8,0},{16,24},{24,16},{1,9},{9,1},{17,25},{25,17},{2,10},{10... | collective-permute-start | bytes 466952 | tf_op jit(solution)/shard_map/ppermute | solution.py:307
